TPU v7x, 256 devices: a whole 4x4x8 slice. The times are simulated.
256 devices in a mesh: gx: 16 (over x, y), gy: 16 (over z, core).
Axes of the slice: x: 4, y: 4, z: 8, core: 2. Of those that a mesh axis runs over, the one named last changes fastest.
Arguments:
- right_side: float32 [256, 512, 128], P('gx', 'gy'), may hold values from -8 to 8
- kappa: float32 [256, 512, 128], P('gx', 'gy'), may hold values from 0.5 to 5
- owners: int32 [16, 16], replicated, may hold values from 240 to 255, as said below
Outputs:
- solution_field: float32 [256, 512, 128], P('gx', 'gy')
- residual: float32 [256, 512, 128], P('gx', 'gy')
Inputs may be any that keep to these rules, and one draw needn't show every extreme that they name: Each agglomerate holds all tiles of 1 to 4 neighbouring tile columns (tiles sharing their second index), with widths drawn from the seed; owners[i, j] is the largest flat index i' * 16 + j' of a tile (i', j') in the agglomerate of tile (i, j).
All inputs are finite; a program needn't handle non-finite values.
Results may differ from a plain program's by a relative error of at most 0.0003.
Values sent between devices are 32-bit elements; how exact they have to be, the bound alone decides.
No kernel may reach another device: no remote copies, remote signals or barrier semaphores. Data moves between devices by JAX's collectives and lax.ppermute only.
A program may use at most 128 MiB of HBM per device.

v0:
```python
import functools

import jax
import jax.numpy as jnp
import numpy as np
from jax import lax
from jax.experimental import pallas as pl
from jax.experimental.pallas import tpu as pltpu
from jax.sharding import PartitionSpec as P

SIGMA = 0.02
F32 = jnp.float32
BF16 = jnp.bfloat16
TX, TY = 16, 32
HX = 10
HY = 12
PX, RY = TX + 2 * HX, TY + 2 * HY
UX, UR = TX + 10, TY + 16
VMEM_BYTES = 56 * 1024 * 1024


def cheb_steps(degree, lower):
    centre = 0.5 * (2.0 + lower)
    half = 0.5 * (2.0 - lower)
    sharp = centre / half
    ratio = 1.0 / sharp
    steps = []
    for _ in range(degree - 1):
        nxt = 1.0 / (2.0 * sharp - ratio)
        steps.append((nxt * ratio, 2.0 * nxt / half))
        ratio = nxt
    return 1.0 / centre, steps


SMOOTH = cheb_steps(3, 0.3)
COARSE = cheb_steps(24, 0.05)


def lane_map(z):
    groups = 128 // z
    out = np.zeros((4, 128, 128), np.float32)
    for q in range(4):
        for lane in range(128):
            cell = (lane // z + groups * q) // 2
            out[q, lane, cell * (z // 2) + (lane % z) // 2] = 1.0
    return out


def restrict_map(z):
    return jnp.asarray(lane_map(z).reshape(512, 128), BF16)


def prolong_map(z):
    return jnp.asarray(np.concatenate([m.T for m in lane_map(z)], axis=1), BF16)


def pair_dot(value, matrix):
    high = value.astype(BF16)
    rest = value - high.astype(F32)
    mid = rest.astype(BF16)
    low = (rest - mid.astype(F32)).astype(BF16)
    dot = functools.partial(jnp.dot, preferred_element_type=F32)
    return dot(high, matrix) + (dot(mid, matrix) + dot(low, matrix))


def lanes(shape):
    return lax.broadcasted_iota(jnp.int32, shape, len(shape) - 1)


def turn(value, shift, axis):
    return pltpu.roll(value, shift % value.shape[axis], axis)


def next_x(v, z):
    if z == 128:
        return jnp.concatenate([v[1:], v[:1]], axis=0)
    a = turn(v, -z, 2)
    b = jnp.concatenate([a[1:], a[:1]], axis=0)
    return jnp.where(lanes(v.shape) < 128 - z, a, b)


def prev_x(v, z):
    if z == 128:
        return jnp.concatenate([v[-1:], v[:-1]], axis=0)
    a = turn(v, z, 2)
    b = jnp.concatenate([a[-1:], a[:-1]], axis=0)
    return jnp.where(lanes(v.shape) >= z, a, b)


def faces_of(k, step, scale, low, high):
    own = (0.5 * scale) * k
    both = own + (0.5 * scale) * step
    if low is None:
        return both, None
    edge = jnp.where(low | high, own, 0.0)
    return jnp.where(high, 0.0, both), edge


def build(k, scale, z, inside=None, edge_x=(None, None), edge_y=(None, None)):
    shape = k.shape
    cell = lanes(shape) & (z - 1)
    wx, ex = faces_of(k, next_x(k, z), scale, *edge_x)
    wy, ey = faces_of(k, turn(k, -1, 1), scale, *edge_y)
    wz, ez = faces_of(k, turn(k, -1, 2), scale, cell == 0, cell == z - 1)
    s = ez + SIGMA * scale
    if ex is not None:
        s = s + ex
    if ey is not None:
        s = s + ey
    diagonal = s + wx + prev_x(wx, z) + wy + turn(wy, 1, 1) + wz + turn(wz, 1, 2)
    rd = 1.0 / diagonal
    if inside is not None:
        rd = jnp.where(inside, rd, 0.0)
    return wx, wy, wz, s, rd


def remain(v, b, level, z):
    wx, wy, wz, s, _ = level
    fx = wx * (next_x(v, z) - v)
    fy = wy * (turn(v, -1, 1) - v)
    fz = wz * (turn(v, -1, 2) - v)
    total = (fx - prev_x(fx, z)) + (fy - turn(fy, 1, 1)) + (fz - turn(fz, 1, 2))
    return (b - s * v) + total


def smooth(x, b, level, z):
    first, steps = SMOOTH
    rd = level[4]
    if x is None:
        d = (b * rd) * first
        x = d
    else:
        d = (remain(x, b, level, z) * rd) * first
        x = x + d
    for keep, gain in steps:
        d = keep * d + gain * (remain(x, b, level, z) * rd)
        x = x + d
    return x


def within(shape, first_x, first_y, z, size_x, size_y):
    plane = lax.broadcasted_iota(jnp.int32, shape, 0)
    cx = first_x + plane * (128 // z) + lanes(shape) // z
    cy = first_y + lax.broadcasted_iota(jnp.int32, shape, 1)
    return (cx >= 0) & (cx < size_x) & (cy >= 0) & (cy < size_y)


def pair_rows(ref, plane, start, count):
    return ref[plane, pl.ds(start, count, stride=2), :] + ref[plane, pl.ds(start + 1, count, stride=2), :]


def spread_rows(ref, plane, start, value):
    count = value.shape[0]
    ref[plane, pl.ds(start, count, stride=2), :] = value
    ref[plane, pl.ds(start + 1, count, stride=2), :] = value


def build_top(k_ref, wx, wy, wz, s, rd, planes, inside_at, body):
    rows = k_ref.shape[1]
    shape = (rows, 128)
    lane = lanes(shape)

    def step(p, carry):
        k, wxp = carry
        kn = k_ref[jnp.minimum(p + 1, planes - 1)]
        own = 0.5 * k
        fx = 0.5 * kn + own
        fy = turn(own, -1, 0) + own
        fz = jnp.where(lane == 127, 0.0, turn(own, -1, 1) + own)
        sv = SIGMA + jnp.where((lane == 0) | (lane == 127), own, 0.0)
        diagonal = sv + (fx + wxp) + (fy + turn(fy, 1, 0)) + (fz + turn(fz, 1, 1))
        rdv = jnp.where(inside_at(p), 1.0 / diagonal, 0.0)
        wx[p], wy[p], wz[p], s[p], rd[p] = fx, fy, fz, sv, rdv
        body(p, rdv)
        return kn, fx

    lax.fori_loop(0, planes, step, (k_ref[0], jnp.zeros(shape, F32)))


def sweep_top(x, wx, wy, wz, s, low, high, body):
    v0 = x[low]
    fx0 = wx[low - 1] * (v0 - x[low - 1])

    def step(p, carry):
        v, fxp = carry
        vn = x[p + 1]
        fx = wx[p] * (vn - v)
        fy = wy[p] * (turn(v, -1, 0) - v)
        fz = wz[p] * (turn(v, -1, 1) - v)
        total = (fx - fxp) + (fy - turn(fy, 1, 0)) + (fz - turn(fz, 1, 1))
        body(p, v, s[p] * v - total)
        return vn, fx

    lax.fori_loop(low, high, step, (v0, fx0))


def fill_top(dst, tile, left, right, below, above):
    dst[:, 0:2, :] = jnp.zeros((PX, 2, 128), F32)
    dst[:, RY - 2 : RY, :] = jnp.zeros((PX, 2, 128), F32)
    dst[0:HX, HY : HY + TY, :] = left
    dst[HX : HX + TX, HY : HY + TY, :] = tile
    dst[HX + TX :, HY : HY + TY, :] = right
    dst[:, 2:HY, :] = below
    dst[:, HY + TY : RY - 2, :] = above


def down_kernel(first, pos, tile, left, right, below, above, *refs):
    if first:
        ktile, r0, r1, xup, bup, kup, kx, one, two = refs[:9]
        scratch = refs[9:]
    else:
        kx, r0, r1, xup, bup, one, two = refs[:7]
        scratch = refs[7:]
    bx, wx, wy, wz, s, rd, d, x, rs, b1s, x1s, k1s = scratch
    gx, gy = pos[0], pos[1]
    row = lax.broadcasted_iota(jnp.int32, (RY, 128), 0) + (gy * TY - HY)
    row_in = (row >= 0) & (row < 512)

    def inside_at(p):
        at = gx * TX - HX + p
        return row_in & ((at >= 0) & (at < 256))

    fill_top(bx, tile[...], left[0], right[0], below[0], above[0])
    if first:
        fill_top(kx, ktile[...], left[1], right[1], below[1], above[1])

        def clear(p, _):
            kx[p] = jnp.where(inside_at(p), kx[p], 0.0)
            return 0

        lax.fori_loop(0, PX, clear, 0)

    start, steps = SMOOTH

    def begin(p, rdv):
        v = (bx[p] * rdv) * start
        d[p] = v
        x[p] = v

    build_top(kx, wx, wy, wz, s, rd, PX, inside_at, begin)
    for number, (keep, gain) in enumerate(steps):

        def advance(p, v, av):
            dv = keep * d[p] + gain * ((bx[p] - av) * rd[p])
            d[p] = dv
            x[p] = v + dv

        sweep_top(x, wx, wy, wz, s, 2 + number, PX - 2 - number, advance)

    def residual(p, v, av):
        d[p] = bx[p] - av

    sweep_top(x, wx, wy, wz, s, 4, PX - 4, residual)
    xup[...] = x[5 : 5 + UX, 4 : 4 + UR, :]
    bup[...] = bx[5 : 5 + UX, 4 : 4 + UR, :]
    if first:
        kup[...] = kx[5 : 5 + UX, 4 : 4 + UR, :]

    def coarse(src):
        for c in range(16):
            rs[c] = src[2 + 2 * c] + src[3 + 2 * c]
        flat = [
            jnp.concatenate([pair_rows(rs, 2 * c, 4, 24), pair_rows(rs, 2 * c + 1, 4, 24)], axis=1)
            for c in range(8)
        ]
        return (0.125 * pair_dot(jnp.concatenate(flat, axis=0), r0[...])).reshape(8, 24, 128)

    d[2] = jnp.zeros((RY, 128), F32)
    d[3] = jnp.zeros((RY, 128), F32)
    d[PX - 4] = jnp.zeros((RY, 128), F32)
    d[PX - 3] = jnp.zeros((RY, 128), F32)
    b1 = coarse(d)
    k1 = coarse(kx)
    level = build(k1, 0.25, 64, within(k1.shape, gx * 8 - 4, gy * 16 - 4, 64, 128, 256))
    x1 = smooth(None, b1, level, 64)
    res = remain(x1, b1, level, 64)
    b1s[...] = b1
    x1s[...] = x1
    k1s[...] = k1
    one[0] = b1s[2:6, 4:20, :]
    one[1] = x1s[2:6, 4:20, :]
    if first:
        one[2] = k1s[2:6, 4:20, :]
    b1s[...] = res

    def coarse_tile(src):
        return jnp.concatenate([pair_rows(src, 2 + q, 4, 8) for q in range(4)], axis=1)

    flat = [coarse_tile(b1s)]
    if first:
        flat.append(coarse_tile(k1s))
    out = 0.125 * pair_dot(jnp.concatenate(flat, axis=0), r1[...])
    two[...] = out.reshape(len(flat), 8, 128)


def call(kernel, outs, scratch, *args, flops=1e7):
    specs = [pl.BlockSpec(memory_space=pltpu.SMEM)]
    specs += [pl.BlockSpec(memory_space=pltpu.VMEM)] * (len(args) - 1)
    return pl.pallas_call(
        kernel,
        out_shape=[jax.ShapeDtypeStruct(o, F32) for o in outs],
        in_specs=specs,
        out_specs=[pl.BlockSpec(memory_space=pltpu.VMEM)] * len(outs),
        scratch_shapes=[pltpu.VMEM(o, F32) for o in scratch],
        compiler_params=pltpu.CompilerParams(vmem_limit_bytes=VMEM_BYTES),
        cost_estimate=pl.CostEstimate(flops=int(flops), bytes_accessed=8 << 20, transcendentals=0),
    )(*args)


def go_down(first, pos, tile, left, right, below, above, kappa, r0, r1):
    top, up = (PX, RY, 128), (UX, UR, 128)
    outs = [up, up] + ([up, top] if first else []) + [(3 if first else 2, 4, 16, 128), (2 if first else 1, 8, 128)]
    scratch = [top] * 8 + [(16, RY, 128)] + [(8, 24, 128)] * 3
    kernel = functools.partial(down_kernel, first)
    return call(kernel, outs, scratch, pos, tile, left, right, below, above, kappa, r0, r1)


def mid_kernel(first, pos, mid, below, above, *refs):
    if first:
        r2, near, three, k2 = refs[:4]
        scratch = refs[4:]
    else:
        k2, r2, near, three = refs[:4]
        scratch = refs[4:]
    hold, rs, cs = scratch
    gx, gy = pos[0], pos[1]
    skip = below.shape[0] - mid.shape[0]
    shape = (16, 24, 128)
    inside = within(shape, 0, gy * 8 - 8, 32, 64, 128)

    def rows(dst, at):
        dst[:, 0:8, :] = below[skip + at : skip + at + 16]
        dst[:, 8:16, :] = mid[at : at + 16]
        dst[:, 16:24, :] = above[skip + at : skip + at + 16]

    rows(rs, 0)
    b = rs[...]
    if first:
        rows(k2, 16)
        k2[...] = jnp.where(inside, k2[...], 0.0)
    k = k2[...]
    plane = lax.broadcasted_iota(jnp.int32, shape, 0)
    lane = lanes(shape)
    edge_x = ((plane == 0) & (lane < 32), (plane == 15) & (lane >= 96))
    level = build(k, 0.25**2, 32, inside, edge_x)
    x = smooth(None, b, level, 32)
    rs[...] = remain(x, b, level, 32)
    for number, value in enumerate((b, x) + level):
        hold[number] = value
    for i in range(5):
        at = gx - 2 + i
        ok = (at >= 0) & (at < 16)
        from_plane = jnp.clip(at, 0, 15)
        for number in range(7):
            near[number, i] = jnp.where(ok, hold[number, from_plane], 0.0)

    def coarse(src, out):
        flat = [
            jnp.concatenate([pair_rows(src, 4 * c + q, 4, 8) for q in range(4)], axis=1) for c in range(4)
        ]
        cs[...] = (0.125 * pair_dot(jnp.concatenate(flat, axis=0), r2[...])).reshape(4, 8, 128)
        for c in range(4):
            three[out + c // 2, 4 * (c % 2) : 4 * (c % 2) + 4, :] = cs[c, 2:6, :]

    coarse(rs, 0)
    if first:
        coarse(k2, 2)


def go_mid(first, pos, mid, below, above, k2, r2):
    outs = [(7, 5, 24, 128), (4 if first else 2, 8, 128)] + ([(16, 24, 128)] if first else [])
    scratch = [(7, 16, 24, 128), (16, 24, 128), (4, 8, 128)]
    args = (mid, below, above) + (() if first else (k2,)) + (r2,)
    return call(functools.partial(mid_kernel, first), outs, scratch, pos, *args)


def solve_last(b, k, owned):
    shape = k.shape
    scale = 0.25**4
    lane = lanes(shape)
    row = lax.broadcasted_iota(jnp.int32, shape, 0)
    moves = (
        (8, 1, lane < 8, True),
        (-8, 1, lane >= 120, True),
        (1, 0, row == 0, True),
        (-1, 0, row == 31, True),
        (1, 1, (lane & 7) == 0, False),
        (-1, 1, (lane & 7) == 7, False),
    )
    diagonal = jnp.full(shape, SIGMA * scale, F32)
    pulls = []
    for shift, axis, edge, masked in moves:
        weight = (0.5 * scale) * (k + jnp.where(edge, 0.0, turn(k, shift, axis)))
        diagonal = diagonal + weight
        keep = jnp.where(edge, 0.0, weight)
        if masked:
            keep = jnp.where(owned == turn(owned, shift, axis), keep, 0.0)
        pulls.append(keep)
    rd = 1.0 / diagonal
    pulls = [keep * rd for keep in pulls]
    g = b * rd
    first, steps = COARSE
    d = g * first
    x = d
    for keep, gain in steps:
        total = [pull * turn(x, move[0], move[1]) for pull, move in zip(pulls, moves)]
        near = (total[0] + total[1]) + (total[2] + total[3]) + (total[4] + total[5])
        d = keep * d + gain * ((g - x) + near)
        x = x + d
    return x


def up_kernel(first, pos, owned, b3g, k3g, near, one, left, right, below, above, x0, b0, k0, *refs):
    if first:
        r3, t3, t2, t1, t0, xout, rout, k1 = refs[:8]
        scratch = refs[8:]
    else:
        k1, xbefore, borig, r3, t3, t2, t1, t0, xout, rout = refs[:10]
        scratch = refs[10:]
    b3, k3, s3, e2, s2, b1s, s1, e0, wx, wy, wz, s, rd, d, x = scratch
    gx, gy = pos[0], pos[1]

    for g in range(16):
        for c in range(4):
            part = slice(4 * (c % 2), 4 * (c % 2) + 4)
            b3[c, 4 * g : 4 * g + 4, :] = b3g[g, c // 2, part, :]
            k3[c, 4 * g : 4 * g + 4, :] = k3g[g, c // 2, part, :]
    shape = (4, 64, 128)
    plane = lax.broadcasted_iota(jnp.int32, shape, 0)
    rown = lax.broadcasted_iota(jnp.int32, shape, 1)
    lane = lanes(shape)
    level = build(
        k3[...],
        0.25**3,
        16,
        None,
        ((plane == 0) & (lane < 16), (plane == 3) & (lane >= 112)),
        (rown == 0, rown == 63),
    )
    b = b3[...]
    x3 = smooth(None, b, level, 16)
    s3[...] = remain(x3, b, level, 16)

    flat = [
        jnp.concatenate([pair_rows(src, q, 0, 32) for q in range(4)], axis=1) for src in (s3, k3)
    ]
    fine = 0.125 * pair_dot(jnp.concatenate(flat, axis=0), r3[...])
    x4 = solve_last(fine[:32], fine[32:], owned[...])

    back = pair_dot(x4, t3[...])
    for q in range(4):
        spread_rows(s3, q, 0, back[:, 128 * q : 128 * q + 128])
    s3[...] = smooth(x3 + s3[...], b, level, 16)

    for i in range(5):
        at = jnp.clip(gx - 2 + i, 0, 15)
        back = pair_dot(s3[at // 4], t2[at % 4])
        spread_rows(e2, i, 8, back)
    e = e2[:, pl.ds(pl.multiple_of(gy * 8, 8), 24), :]
    level = tuple(near[number] for number in range(2, 7))
    x2 = near[1] + jnp.where(level[4] > 0.0, e, 0.0)
    s2[...] = smooth(x2, near[0], level, 32)

    shape = (12, 32, 128)
    inside = within(shape, gx * 8 - 8, gy * 16 - 8, 64, 128, 256)

    def fill(dst, number):
        dst[0:4, 8:24, :] = left[number]
        dst[4:8, 8:24, :] = one[number]
        dst[8:12, 8:24, :] = right[number]
        dst[:, 0:8, :] = below[12 * number : 12 * number + 12]
        dst[:, 24:32, :] = above[12 * number : 12 * number + 12]

    fill(b1s, 0)
    fill(s1, 1)
    x1 = jnp.where(inside, s1[...], 0.0)
    if first:
        fill(k1, 2)
        k1[...] = jnp.where(inside, k1[...], 0.0)
    flat = jnp.concatenate([s2[i, 4:20, :] for i in range(1, 4)], axis=0)
    back = pair_dot(flat, t1[...])
    for i in range(3):
        for q in range(4):
            spread_rows(s1, 4 * i + q, 0, back[16 * i : 16 * i + 16, 128 * q : 128 * q + 128])
    level = build(k1[...], 0.25, 64, inside)
    x1 = x1 + jnp.where(inside, s1[...], 0.0)
    s1[...] = smooth(x1, b1s[...], level, 64)

    flat = jnp.concatenate([s1[i, 4:28, :] for i in range(3, 9)], axis=0)
    back = pair_dot(flat, t0[...])
    for i in range(6):
        for q in range(2):
            spread_rows(e0, 2 * i + q, 0, back[24 * i : 24 * i + 24, 128 * q : 128 * q + 128])
    row = lax.broadcasted_iota(jnp.int32, (UR, 128), 0) + (gy * TY - 8)
    row_in = (row >= 0) & (row < 512)

    def inside_at(p):
        at = gx * TX - 5 + p
        return row_in & ((at >= 0) & (at < 256))

    def begin(p, rdv):
        correction = e0[jnp.clip((p - 1) // 2, 0, 11)]
        x[p] = x0[p] + jnp.where(rdv > 0.0, correction, 0.0)

    build_top(k0, wx, wy, wz, s, rd, UX, inside_at, begin)
    start, steps = SMOOTH

    def open_up(p, v, av):
        dv = ((b0[p] - av) * rd[p]) * start
        d[p] = dv
        x[p] = v + dv

    sweep_top(x, wx, wy, wz, s, 2, UX - 2, open_up)
    for number, (keep, gain) in enumerate(steps):

        def advance(p, v, av):
            dv = keep * d[p] + gain * ((b0[p] - av) * rd[p])
            d[p] = dv
            x[p] = v + dv

        sweep_top(x, wx, wy, wz, s, 3 + number, UX - 3 - number, advance)

    if first:
        xout[...] = x[4 : UX - 4]

        def residual(p, v, av):
            rout[p - 5] = b0[p, 8 : 8 + TY, :] - av[8 : 8 + TY]
    else:

        def add(p, _):
            x[p] = x[p] + xbefore[p - 4]
            return 0

        lax.fori_loop(4, UX - 4, add, 0)

        def residual(p, v, av):
            xout[p - 5] = v[8 : 8 + TY]
            rout[p - 5] = borig[p - 5] - av[8 : 8 + TY]

    sweep_top(x, wx, wy, wz, s, 5, UX - 5, residual)


def go_up(first, *args):
    tile = (TX, TY, 128)
    outs = [(TX + 2, UR, 128), tile, (12, 32, 128)] if first else [tile, tile]
    up = (UX, UR, 128)
    scratch = [(4, 64, 128)] * 3 + [(5, 144, 128), (5, 24, 128), (12, 32, 128), (12, 32, 128), (12, UR, 128)]
    return call(functools.partial(up_kernel, first), outs, scratch + [up] * 7, *args)


def shift(value, axis, step):
    count = lax.axis_size(axis)
    return lax.ppermute(value, axis, [(i, (i + step) % count) for i in range(count)])


def gather(value, axis):
    count = lax.axis_size(axis)
    return lax.all_to_all(jnp.broadcast_to(value[None], (count,) + value.shape), axis, 0, 0, tiled=True)


def local(right_side, kappa, owners):
    pos = jnp.stack([lax.axis_index("gx"), lax.axis_index("gy")]).astype(jnp.int32)
    owned = jnp.repeat(jnp.repeat(owners.T, 2, 0), 8, 1).astype(F32)
    r0 = restrict_map(128)[128:384]
    r1, r2, r3 = restrict_map(64), restrict_map(32), restrict_map(16)
    t0 = prolong_map(128)[:, 128:384]
    t1, t3 = prolong_map(64), prolong_map(16)
    t2 = jnp.asarray(np.transpose(lane_map(32), (0, 2, 1)), BF16)

    source = right_side
    keep = {}
    for first in (True, False):
        mid = jnp.stack([source, kappa]) if first else source[None]
        left = shift(mid[:, TX - HX :], "gx", 1)
        right = shift(mid[:, :HX], "gx", -1)
        wide = jnp.concatenate([left, mid, right], axis=1)
        below = shift(wide[:, :, TY - HX :], "gy", 1)
        above = shift(wide[:, :, :HX], "gy", -1)
        out = go_down(first, pos, source, left, right, below, above, kappa if first else keep["kx"], r0, r1)
        if first:
            xup, bup, keep["kup"], keep["kx"], one, two = out
        else:
            xup, bup, one, two = out
        left = shift(one, "gx", 1)
        right = shift(one, "gx", -1)
        rows = jnp.swapaxes(gather(two, "gx"), 0, 1).reshape(-1, 8, 128)
        wide = jnp.concatenate([left, one, right], axis=1)
        low = wide[:, :, :8].reshape(-1, 8, 128)
        high = wide[:, :, 8:].reshape(-1, 8, 128)
        below = shift(jnp.concatenate([high, rows]), "gy", 1)
        above = shift(jnp.concatenate([low, rows]), "gy", -1)
        out = go_mid(first, pos, rows, below, above, keep.get("k2"), r2)
        if first:
            near, three, keep["k2"] = out
        else:
            near, three = out
        spread = gather(three, "gy")
        if first:
            keep["k3"] = spread[:, 2:]
            spread = spread[:, :2]
        args = (pos, owned, spread, keep["k3"], near, one, left, right, below, above, xup, bup, keep["kup"])
        if first:
            keep["x"], source, keep["k1"] = go_up(True, *args, r3, t3, t2, t1, t0)
        else:
            field, residual = go_up(False, *args, keep["k1"], keep["x"], right_side, r3, t3, t2, t1, t0)
    return field, residual


def solution(mesh):
    spec = P("gx", "gy", None)
    return jax.shard_map(
        local, mesh=mesh, in_specs=(spec, spec, P()), out_specs=(spec, spec), check_vma=False
    )
```

profile of v0, /device:TPU:1, one launch (start us, length us, event | category | flops | bytes accessed | tf_op | source)
XLA Modules:
  0.0 243.5 jit_solution(757839841931993587)
XLA Ops:
  0.7 1.3 pad_maximum_fusion.4
  1.9 5.8 %collective-permute-start.1 = (f32[2,10,32,128]{3,2,1,0:T(8,128)S(1)}, f32[2,10,32,128]{3,2,1,0:T(8,128)S(1)}, u32[]{:S(2)}, u32[]{:S(2)}) collective-permute-start(f32[2,10,32,128]{3,2,1,0:T(8,128)S(1)} %get-tuple-element.42), channel_id=1, source_target_pairs={{0,240},{16,0},{32,16},{48,32},{64,48},{80,64},{96,80},{112,96},{1... | collective-permute-start | bytes 983048 | tf_op jit(solution)/shard_map/ppermute | solution.py:553
  7.7 6.4 %collective-permute-done.1.right = f32[2,10,32,128]{3,2,1,0:T(8,128)S(1)} collective-permute-done((f32[2,10,32,128]{3,2,1,0:T(8,128)S(1)}, f32[2,10,32,128]{3,2,1,0:T(8,128)S(1)}, u32[]{:S(2)}, u32[]{:S(2)}) %collective-permute-start.1) | collective-permute-done | bytes 327712 | tf_op jit(solution)/shard_map/ppermute | solution.py:553
  14.1 5.2 %collective-permute-done.left = f32[2,10,32,128]{3,2,1,0:T(8,128)S(1)} collective-permute-done((f32[2,10,32,128]{3,2,1,0:T(8,128)S(1)}, f32[2,10,32,128]{3,2,1,0:T(8,128)S(1)}, u32[]{:S(2)}, u32[]{:S(2)}) %collective-permute-start) | collective-permute-done | bytes 327712 | tf_op jit(solution)/shard_map/ppermute | solution.py:553
  19.4 0.6 copy-done.3
  20.5 3.4 %collective-permute-start.2 = (f32[2,36,10,128]{3,0,2,1:T(2,128)S(1)}, f32[2,36,10,128]{3,0,2,1:T(2,128)S(1)}, u32[]{:S(2)}, u32[]{:S(2)}) collective-permute-start(f32[2,36,10,128]{3,0,2,1:T(2,128)S(1)} %copy.22), channel_id=1, source_target_pairs={{0,1},{1,2},{2,3},{3,4},{4,5},{5,6},{6,7},{7,8},{8,9},{9,10},{10,1... | collective-permute-start | bytes 1105928 | tf_op jit(solution)/shard_map/ppermute | solution.py:553
  24.8 3.6 %collective-permute-done.2 = f32[2,36,10,128]{3,0,2,1:T(2,128)S(1)} collective-permute-done((f32[2,36,10,128]{3,0,2,1:T(2,128)S(1)}, f32[2,36,10,128]{3,0,2,1:T(2,128)S(1)}, u32[]{:S(2)}, u32[]{:S(2)}) %collective-permute-start.2) | collective-permute-done | bytes 368672 | tf_op jit(solution)/shard_map/ppermute | solution.py:553
  28.3 0.9 copy.24.below
  29.2 2.1 collective-permute-done.3
  31.2 0.9 copy.25.above
  32.1 24.0 %shard_map.122 = (f32[26,48,128]{2,1,0:T(8,128)}, f32[26,48,128]{2,1,0:T(8,128)}, f32[26,48,128]{2,1,0:T(8,128)}, f32[36,56,128]{2,1,0:T(8,128)}, f32[3,4,16,128]{3,2,1,0:T(8,128)}, /*index=5*/f32[2,8,128]{2,1,0:T(8,128)}) custom-call(s32[2]{0:T(128)} %pad_add_fusion.pos, f32[16,32,128]{2,1,0:T(8,128)} %refs_2_.4, f32[2,10,32,128]{3,2,1,0:T(8,128)} %copy-done.3, ...), custom_call_target="tpu_custom_call" | custom-call | flops 10000000 | bytes 8388608 | tf_op jit(solution)/shard_map/pallas_call | solution.py:299
  56.1 4.8 %collective-permute-start.5 = (f32[3,4,16,128]{3,2,1,0:T(8,128)}, f32[3,4,16,128]{3,2,1,0:T(8,128)S(1)}, u32[]{:S(2)}, u32[]{:S(2)}) collective-permute-start(f32[3,4,16,128]{3,2,1,0:T(8,128)} %get-tuple-element.21.one), channel_id=1, source_target_pairs={{0,240},{16,0},{32,16},{48,32},{64,48},{80,64},{96,80},{112,96},{1... | collective-permute-start | bytes 294920 | tf_op jit(solution)/shard_map/ppermute | solution.py:553
  60.9 1.4 broadcast_in_dim.18
  62.3 3.5 %all-to-all-start = ((f32[16,2,8,128]{3,2,1,0:T(8,128)}), f32[16,2,8,128]{3,2,1,0:T(8,128)S(1)}, u32[]{:S(2)}, u32[]{:S(2)}) async-start(f32[16,2,8,128]{3,2,1,0:T(8,128)} %broadcast_in_dim.18), calls=%async_computation | async-start | bytes 262144 | tf_op jit(solution)/shard_map/all_to_all | solution.py:558
  65.8 0.9 constant_dynamic-update-slice_fusion.1
  66.8 5.7 %all-to-all-done = f32[16,2,8,128]{3,2,1,0:T(8,128)S(1)} async-done(((f32[16,2,8,128]{3,2,1,0:T(8,128)}), f32[16,2,8,128]{3,2,1,0:T(8,128)S(1)}, u32[]{:S(2)}, u32[]{:S(2)}) %all-to-all-start) | async-done | bytes 131104 | tf_op jit(solution)/shard_map/all_to_all | solution.py:558
  72.6 2.9 %collective-permute-start.7 = (f32[68,8,128]{2,1,0:T(8,128)S(1)}, f32[68,8,128]{2,1,0:T(8,128)S(1)}, u32[]{:S(2)}, u32[]{:S(2)}) collective-permute-start(f32[68,8,128]{2,1,0:T(8,128)S(1)} %get-tuple-element.52), channel_id=1, source_target_pairs={{0,15},{1,0},{2,1},{3,2},{4,3},{5,4},{6,5},{7,6},{8,7},{9,8},{10,9... | collective-permute-start | bytes 835592 | tf_op jit(solution)/shard_map/ppermute | solution.py:553
  75.5 3.9 %collective-permute-done.7.above = f32[68,8,128]{2,1,0:T(8,128)S(1)} collective-permute-done((f32[68,8,128]{2,1,0:T(8,128)S(1)}, f32[68,8,128]{2,1,0:T(8,128)S(1)}, u32[]{:S(2)}, u32[]{:S(2)}) %collective-permute-start.7) | collective-permute-done | bytes 278560 | tf_op jit(solution)/shard_map/ppermute | solution.py:553
  79.5 0.7 copy-done.5
  80.2 0.7 copy-done.6
  80.9 3.2 %shard_map.123 = (f32[7,5,24,128]{3,2,1,0:T(8,128)}, f32[4,8,128]{2,1,0:T(8,128)}, f32[16,24,128]{2,1,0:T(8,128)}) custom-call(s32[2]{0:T(128)} %pad_add_fusion.pos, f32[32,8,128]{2,1,0:T(8,128)} %bitcast.25, f32[68,8,128]{2,1,0:T(8,128)} %copy-done.6, f32[68,8,128]{2,1,0:T(8,128)} %copy-done.5, bf16[512,128]{1,0:T(8,128)(2,1)} %constant.25.clone.refs_0_.refs_1_), custom_call_target="tpu_custom_call" | custom-call | flops 10000000 | bytes 8388608 | tf_op jit(solution)/shard_map/pallas_call | solution.py:299
  84.0 1.4 broadcast_in_dim.38
  85.5 10.5 %all-to-all-start.1 = ((f32[16,4,8,128]{3,2,1,0:T(8,128)}), f32[16,4,8,128]{3,2,1,0:T(8,128)S(1)}, u32[]{:S(2)}, u32[]{:S(2)}) async-start(f32[16,4,8,128]{3,2,1,0:T(8,128)} %broadcast_in_dim.38), calls=%async_computation.1 | async-start | bytes 524288 | tf_op jit(solution)/shard_map/all_to_all | solution.py:558
  96.2 0.7 copy.28.owned
  96.9 10.9 %all-to-all-done.1 = f32[16,4,8,128]{3,2,1,0:T(8,128)S(1)} async-done(((f32[16,4,8,128]{3,2,1,0:T(8,128)}), f32[16,4,8,128]{3,2,1,0:T(8,128)S(1)}, u32[]{:S(2)}, u32[]{:S(2)}) %all-to-all-start.1) | async-done | bytes 262176 | tf_op jit(solution)/shard_map/all_to_all | solution.py:558
  107.7 0.7 fusion.5
  108.5 24.4 %shard_map.124 = (f32[18,48,128]{2,1,0:T(8,128)}, f32[16,32,128]{2,1,0:T(8,128)}, f32[12,32,128]{2,1,0:T(8,128)}) custom-call(s32[2]{0:T(128)} %pad_add_fusion.pos, f32[32,128]{1,0:T(8,128)} %copy.28.owned, f32[16,2,8,128]{3,2,1,0:T(8,128)} %get-tuple-element.49.b3g, f32[16,2,8,128]{3,2,1,0:T(8,128)} %get-tuple-element.48.k3g, ...), custom_call_target="tpu_custom_call" | custom-call | flops 10000000 | bytes 8388608 | tf_op jit(solution)/shard_map/pallas_call | solution.py:299
  132.9 1.0 fusion.4
  133.9 1.4 collective-permute-start.9
  135.4 4.7 %collective-permute-done.9.right = f32[1,10,32,128]{3,2,1,0:T(8,128)S(1)} collective-permute-done((f32[1,10,32,128]{3,2,1,0:T(8,128)S(1)}, f32[1,10,32,128]{3,2,1,0:T(8,128)S(1)}, u32[]{:S(2)}, u32[]{:S(2)}) %collective-permute-start.9) | collective-permute-done | bytes 163872 | tf_op jit(solution)/shard_map/ppermute | solution.py:553
  140.2 4.4 %collective-permute-done.8.left = f32[1,10,32,128]{3,2,1,0:T(8,128)S(1)} collective-permute-done((f32[1,10,32,128]{3,2,1,0:T(8,128)S(1)}, f32[1,10,32,128]{3,2,1,0:T(8,128)S(1)}, u32[]{:S(2)}, u32[]{:S(2)}) %collective-permute-start.8) | collective-permute-done | bytes 163872 | tf_op jit(solution)/shard_map/ppermute | solution.py:553
  144.6 1.0 pad_maximum_fusion.1
  145.7 0.7 collective-permute-start.11
  146.4 1.0 collective-permute-start.10
  147.5 4.7 %collective-permute-done.11.above = f32[1,36,10,128]{3,2,1,0:T(8,128)S(1)} collective-permute-done((f32[1,36,10,128]{3,2,1,0:T(8,128)S(1)}, f32[1,36,10,128]{3,2,1,0:T(8,128)S(1)}, u32[]{:S(2)}, u32[]{:S(2)}) %collective-permute-start.11) | collective-permute-done | bytes 184352 | tf_op jit(solution)/shard_map/ppermute | solution.py:553
  152.2 0.7 copy-done.14
  153.0 23.4 %shard_map.125 = (f32[26,48,128]{2,1,0:T(8,128)}, f32[26,48,128]{2,1,0:T(8,128)}, f32[2,4,16,128]{3,2,1,0:T(8,128)}, f32[1,8,128]{2,1,0:T(8,128)}) custom-call(s32[2]{0:T(128)} %pad_add_fusion.pos, f32[16,32,128]{2,1,0:T(8,128)} %get-tuple-element.27.tile, f32[1,10,32,128]{3,2,1,0:T(8,128)} %copy-done.10, f32[1,10,32,128]{3,2,1,0:T(8,128)} %copy-done.9, ...), custom_call_target="tpu_custom_call" | custom-call | flops 10000000 | bytes 8388608 | tf_op jit(solution)/shard_map/pallas_call | solution.py:299
  176.4 4.8 %collective-permute-start.13 = (f32[2,4,16,128]{3,2,1,0:T(8,128)}, f32[2,4,16,128]{3,2,1,0:T(8,128)S(1)}, u32[]{:S(2)}, u32[]{:S(2)}) collective-permute-start(f32[2,4,16,128]{3,2,1,0:T(8,128)} %get-tuple-element.30.one), channel_id=1, source_target_pairs={{0,240},{16,0},{32,16},{48,32},{64,48},{80,64},{96,80},{112,96},{1... | collective-permute-start | bytes 196616 | tf_op jit(solution)/shard_map/ppermute | solution.py:553
  181.2 1.3 broadcast_in_dim.41
  182.5 3.5 %all-to-all-start.2 = ((f32[16,1,8,128]{3,2,1,0:T(8,128)}), f32[16,1,8,128]{3,2,1,0:T(8,128)S(1)}, u32[]{:S(2)}, u32[]{:S(2)}) async-start(f32[16,1,8,128]{3,2,1,0:T(8,128)} %broadcast_in_dim.41), calls=%async_computation.2 | async-start | bytes 131072 | tf_op jit(solution)/shard_map/all_to_all | solution.py:558
  186.0 0.9 constant_dynamic-update-slice_fusion.4
  186.9 5.5 %all-to-all-done.2 = f32[16,1,8,128]{3,2,1,0:T(8,128)S(1)} async-done(((f32[16,1,8,128]{3,2,1,0:T(8,128)}), f32[16,1,8,128]{3,2,1,0:T(8,128)S(1)}, u32[]{:S(2)}, u32[]{:S(2)}) %all-to-all-start.2) | async-done | bytes 65568 | tf_op jit(solution)/shard_map/all_to_all | solution.py:558
  192.5 3.2 %collective-permute-start.15 = (f32[40,8,128]{2,1,0:T(8,128)S(1)}, f32[40,8,128]{2,1,0:T(8,128)S(1)}, u32[]{:S(2)}, u32[]{:S(2)}) collective-permute-start(f32[40,8,128]{2,1,0:T(8,128)S(1)} %get-tuple-element.54), channel_id=1, source_target_pairs={{0,15},{1,0},{2,1},{3,2},{4,3},{5,4},{6,5},{7,6},{8,7},{9,8},{10,9... | collective-permute-start | bytes 491528 | tf_op jit(solution)/shard_map/ppermute | solution.py:553
  195.7 2.8 %collective-permute-done.15.above = f32[40,8,128]{2,1,0:T(8,128)S(1)} collective-permute-done((f32[40,8,128]{2,1,0:T(8,128)S(1)}, f32[40,8,128]{2,1,0:T(8,128)S(1)}, u32[]{:S(2)}, u32[]{:S(2)}) %collective-permute-start.15) | collective-permute-done | bytes 163872 | tf_op jit(solution)/shard_map/ppermute | solution.py:553
  199.3 3.1 %shard_map.126 = (f32[7,5,24,128]{3,2,1,0:T(8,128)}, f32[2,8,128]{2,1,0:T(8,128)}) custom-call(s32[2]{0:T(128)} %pad_add_fusion.pos, f32[16,8,128]{2,1,0:T(8,128)} %bitcast.27, f32[40,8,128]{2,1,0:T(8,128)} %copy-done.8, f32[40,8,128]{2,1,0:T(8,128)} %copy-done.7, f32[16,24,128]{2,1,0:T(8,128)} %get-tuple-element.31.refs_0_, ...), custom_call_target="tpu_custom_call" | custom-call | flops 10000000 | bytes 8388608 | tf_op jit(solution)/shard_map/pallas_call | solution.py:299
  202.3 0.7 broadcast_in_dim.42
  203.0 15.8 %all_to_all.20.b3g = f32[16,2,8,128]{3,2,1,0:T(8,128)} all-to-all(f32[16,2,8,128]{3,2,1,0:T(8,128)S(1)} %broadcast_in_dim.42), channel_id=1, replica_groups=mesh['gx'=16,'gy'=16] {'gy'}, dimensions={0} | all-to-all | bytes 262144 | tf_op jit(solution)/shard_map/all_to_all | solution.py:558
  218.8 24.6 %shard_map.127 = (f32[16,32,128]{2,1,0:T(8,128)}, f32[16,32,128]{2,1,0:T(8,128)}) custom-call(s32[2]{0:T(128)} %pad_add_fusion.pos, f32[32,128]{1,0:T(8,128)} %copy.28.owned, f32[16,2,8,128]{3,2,1,0:T(8,128)} %all_to_all.20.b3g, f32[16,2,8,128]{3,2,1,0:T(8,128)} %get-tuple-element.48.k3g, f32[7,5,24,128]{3,2,1,0:T(8,128)} %get-tuple-element.33.near, ...), custom_call_target="tpu_custom_call" | custom-call | flops 10000000 | bytes 8388608 | tf_op jit(solution)/shard_map/pallas_call | solution.py:299
  (68 shorter events, 2.7 us)
Async XLA Ops:
  0.6 18.7 %copy-start = (f32[16,32,128]{2,1,0:T(8,128)S(1)}, f32[16,32,128]{2,1,0:T(8,128)}, u32[]{:S(2)}) copy-start(f32[16,32,128]{2,1,0:T(8,128)} %refs_2_.4) | copy-start | bytes 786436
  0.6 18.7 %copy-start.1 = (f32[16,32,128]{2,1,0:T(8,128)S(1)}, f32[16,32,128]{2,1,0:T(8,128)}, u32[]{:S(2)}) copy-start(f32[16,32,128]{2,1,0:T(8,128)} %refs_0_.3) | copy-start | bytes 786436
  1.9 12.2 %collective-permute-start.1 = (f32[2,10,32,128]{3,2,1,0:T(8,128)S(1)}, f32[2,10,32,128]{3,2,1,0:T(8,128)S(1)}, u32[]{:S(2)}, u32[]{:S(2)}) collective-permute-start(f32[2,10,32,128]{3,2,1,0:T(8,128)S(1)} %get-tuple-element.42), channel_id=1, source_target_pairs={{0,240},{16,0},{32,16},{48,32},{64,48},{80,64},{96,80},{112,96},{1... | collective-permute-start | bytes 983048 | tf_op jit(solution)/shard_map/ppermute | solution.py:553
  7.7 11.6 %collective-permute-start = (f32[2,10,32,128]{3,2,1,0:T(8,128)S(1)}, f32[2,10,32,128]{3,2,1,0:T(8,128)S(1)}, u32[]{:S(2)}, u32[]{:S(2)}) collective-permute-start(f32[2,10,32,128]{3,2,1,0:T(8,128)S(1)} %get-tuple-element.43), channel_id=1, source_target_pairs={{0,16},{16,32},{32,48},{48,64},{64,80},{80,96},{96,112},{112,128},... | collective-permute-start | bytes 983048 | tf_op jit(solution)/shard_map/ppermute | solution.py:553
  14.1 5.3 %copy-start.2 = (f32[2,10,32,128]{3,2,1,0:T(8,128)}, f32[2,10,32,128]{3,2,1,0:T(8,128)S(1)}, u32[]{:S(2)}) copy-start(f32[2,10,32,128]{3,2,1,0:T(8,128)S(1)} %collective-permute-done.1.right) | copy-start | bytes 983044
  19.3 0.7 copy-start.3
  20.5 7.9 %collective-permute-start.2 = (f32[2,36,10,128]{3,0,2,1:T(2,128)S(1)}, f32[2,36,10,128]{3,0,2,1:T(2,128)S(1)}, u32[]{:S(2)}, u32[]{:S(2)}) collective-permute-start(f32[2,36,10,128]{3,0,2,1:T(2,128)S(1)} %copy.22), channel_id=1, source_target_pairs={{0,1},{1,2},{2,3},{3,4},{4,5},{5,6},{6,7},{7,8},{8,9},{9,10},{10,1... | collective-permute-start | bytes 1105928 | tf_op jit(solution)/shard_map/ppermute | solution.py:553
  24.1 7.1 %collective-permute-start.3 = (f32[2,36,10,128]{3,0,2,1:T(2,128)S(1)}, f32[2,36,10,128]{3,0,2,1:T(2,128)S(1)}, u32[]{:S(2)}, u32[]{:S(2)}) collective-permute-start(f32[2,36,10,128]{3,0,2,1:T(2,128)S(1)} %copy.23), channel_id=1, source_target_pairs={{0,15},{1,0},{2,1},{3,2},{4,3},{5,4},{6,5},{7,6},{8,7},{9,8},{10,9... | collective-permute-start | bytes 1105928 | tf_op jit(solution)/shard_map/ppermute | solution.py:553
  56.1 9.7 %collective-permute-start.4 = (f32[3,4,16,128]{3,2,1,0:T(8,128)}, f32[3,4,16,128]{3,2,1,0:T(8,128)S(1)}, u32[]{:S(2)}, u32[]{:S(2)}) collective-permute-start(f32[3,4,16,128]{3,2,1,0:T(8,128)} %get-tuple-element.21.one), channel_id=1, source_target_pairs={{0,16},{16,32},{32,48},{48,64},{64,80},{80,96},{96,112},{112,128},... | collective-permute-start | bytes 294920 | tf_op jit(solution)/shard_map/ppermute | solution.py:553
  56.1 10.6 %collective-permute-start.5 = (f32[3,4,16,128]{3,2,1,0:T(8,128)}, f32[3,4,16,128]{3,2,1,0:T(8,128)S(1)}, u32[]{:S(2)}, u32[]{:S(2)}) collective-permute-start(f32[3,4,16,128]{3,2,1,0:T(8,128)} %get-tuple-element.21.one), channel_id=1, source_target_pairs={{0,240},{16,0},{32,16},{48,32},{64,48},{80,64},{96,80},{112,96},{1... | collective-permute-start | bytes 294920 | tf_op jit(solution)/shard_map/ppermute | solution.py:553
  62.3 10.2 %all-to-all-start = ((f32[16,2,8,128]{3,2,1,0:T(8,128)}), f32[16,2,8,128]{3,2,1,0:T(8,128)S(1)}, u32[]{:S(2)}, u32[]{:S(2)}) async-start(f32[16,2,8,128]{3,2,1,0:T(8,128)} %broadcast_in_dim.18), calls=%async_computation | async-start | bytes 262144 | tf_op jit(solution)/shard_map/all_to_all | solution.py:558
  65.8 6.8 %copy-start.12 = (f32[3,4,16,128]{3,2,1,0:T(8,128)}, f32[3,4,16,128]{3,2,1,0:T(8,128)S(1)}, u32[]{:S(2)}) copy-start(f32[3,4,16,128]{3,2,1,0:T(8,128)S(1)} %collective-permute-done.4.left) | copy-start | bytes 294916
  66.8 17.3 %copy-start.13 = (f32[3,4,16,128]{3,2,1,0:T(8,128)}, f32[3,4,16,128]{3,2,1,0:T(8,128)S(1)}, u32[]{:S(2)}) copy-start(f32[3,4,16,128]{3,2,1,0:T(8,128)S(1)} %collective-permute-done.5.right) | copy-start | bytes 294916
  72.5 6.9 %copy-start.4 = (f32[2,16,8,128]{3,2,1,0:T(8,128)}, f32[2,16,8,128]{3,2,1,0:T(8,128)S(1)}, u32[]{:S(2)}) copy-start(f32[2,16,8,128]{3,2,1,0:T(8,128)S(1)} %copy.26) | copy-start | bytes 393220
  72.5 23.5 %copy-start.18 = (s32[16,16]{1,0:T(8,128)S(1)}, s32[16,16]{1,0:T(8,128)}, u32[]{:S(2)}) copy-start(s32[16,16]{1,0:T(8,128)} %param.13) | copy-start | bytes 3076
  72.6 6.8 %collective-permute-start.7 = (f32[68,8,128]{2,1,0:T(8,128)S(1)}, f32[68,8,128]{2,1,0:T(8,128)S(1)}, u32[]{:S(2)}, u32[]{:S(2)}) collective-permute-start(f32[68,8,128]{2,1,0:T(8,128)S(1)} %get-tuple-element.52), channel_id=1, source_target_pairs={{0,15},{1,0},{2,1},{3,2},{4,3},{5,4},{6,5},{7,6},{8,7},{9,8},{10,9... | collective-permute-start | bytes 835592 | tf_op jit(solution)/shard_map/ppermute | solution.py:553
  75.5 3.9 %collective-permute-start.6 = (f32[68,8,128]{2,1,0:T(8,128)S(1)}, f32[68,8,128]{2,1,0:T(8,128)S(1)}, u32[]{:S(2)}, u32[]{:S(2)}) collective-permute-start(f32[68,8,128]{2,1,0:T(8,128)S(1)} %get-tuple-element.53), channel_id=1, source_target_pairs={{0,1},{1,2},{2,3},{3,4},{4,5},{5,6},{6,7},{7,8},{8,9},{9,10},{10,1... | collective-permute-start | bytes 835592 | tf_op jit(solution)/shard_map/ppermute | solution.py:553
  79.5 0.7 copy-start.5
  80.2 0.7 copy-start.6
  85.5 22.3 %all-to-all-start.1 = ((f32[16,4,8,128]{3,2,1,0:T(8,128)}), f32[16,4,8,128]{3,2,1,0:T(8,128)S(1)}, u32[]{:S(2)}, u32[]{:S(2)}) async-start(f32[16,4,8,128]{3,2,1,0:T(8,128)} %broadcast_in_dim.38), calls=%async_computation.1 | async-start | bytes 524288 | tf_op jit(solution)/shard_map/all_to_all | solution.py:558
  133.9 6.3 %collective-permute-start.9 = (f32[1,10,32,128]{3,2,1,0:T(8,128)S(1)}, f32[1,10,32,128]{3,2,1,0:T(8,128)S(1)}, u32[]{:S(2)}, u32[]{:S(2)}) collective-permute-start(f32[1,10,32,128]{3,2,1,0:T(8,128)S(1)} %get-tuple-element.46), channel_id=1, source_target_pairs={{0,240},{16,0},{32,16},{48,32},{64,48},{80,64},{96,80},{112,96},{1... | collective-permute-start | bytes 491528 | tf_op jit(solution)/shard_map/ppermute | solution.py:553
  135.4 9.2 %collective-permute-start.8 = (f32[1,10,32,128]{3,2,1,0:T(8,128)S(1)}, f32[1,10,32,128]{3,2,1,0:T(8,128)S(1)}, u32[]{:S(2)}, u32[]{:S(2)}) collective-permute-start(f32[1,10,32,128]{3,2,1,0:T(8,128)S(1)} %get-tuple-element.47), channel_id=1, source_target_pairs={{0,16},{16,32},{32,48},{48,64},{64,80},{80,96},{96,112},{112,128},... | collective-permute-start | bytes 491528 | tf_op jit(solution)/shard_map/ppermute | solution.py:553
  140.2 5.5 %copy-start.9 = (f32[1,10,32,128]{3,2,1,0:T(8,128)}, f32[1,10,32,128]{3,2,1,0:T(8,128)S(1)}, u32[]{:S(2)}) copy-start(f32[1,10,32,128]{3,2,1,0:T(8,128)S(1)} %collective-permute-done.9.right) | copy-start | bytes 491524
  144.6 1.1 copy-start.10
  145.7 6.5 %collective-permute-start.11 = (f32[1,36,10,128]{3,2,1,0:T(8,128)S(1)}, f32[1,36,10,128]{3,2,1,0:T(8,128)S(1)}, u32[]{:S(2)}, u32[]{:S(2)}) collective-permute-start(f32[1,36,10,128]{3,2,1,0:T(8,128)S(1)} %get-tuple-element.40), channel_id=1, source_target_pairs={{0,15},{1,0},{2,1},{3,2},{4,3},{5,4},{6,5},{7,6},{8,7},{9,8},{10,9... | collective-permute-start | bytes 552968 | tf_op jit(solution)/shard_map/ppermute | solution.py:553
  146.4 5.7 %collective-permute-start.10 = (f32[1,36,10,128]{3,2,1,0:T(8,128)S(1)}, f32[1,36,10,128]{3,2,1,0:T(8,128)S(1)}, u32[]{:S(2)}, u32[]{:S(2)}) collective-permute-start(f32[1,36,10,128]{3,2,1,0:T(8,128)S(1)} %get-tuple-element.41), channel_id=1, source_target_pairs={{0,1},{1,2},{2,3},{3,4},{4,5},{5,6},{6,7},{7,8},{8,9},{9,10},{10,1... | collective-permute-start | bytes 552968 | tf_op jit(solution)/shard_map/ppermute | solution.py:553
  152.2 0.7 copy-start.14
  152.2 0.8 copy-start.15
  176.4 9.6 %collective-permute-start.12 = (f32[2,4,16,128]{3,2,1,0:T(8,128)}, f32[2,4,16,128]{3,2,1,0:T(8,128)S(1)}, u32[]{:S(2)}, u32[]{:S(2)}) collective-permute-start(f32[2,4,16,128]{3,2,1,0:T(8,128)} %get-tuple-element.30.one), channel_id=1, source_target_pairs={{0,16},{16,32},{32,48},{48,64},{64,80},{80,96},{96,112},{112,128},... | collective-permute-start | bytes 196616 | tf_op jit(solution)/shard_map/ppermute | solution.py:553
  176.4 10.5 %collective-permute-start.13 = (f32[2,4,16,128]{3,2,1,0:T(8,128)}, f32[2,4,16,128]{3,2,1,0:T(8,128)S(1)}, u32[]{:S(2)}, u32[]{:S(2)}) collective-permute-start(f32[2,4,16,128]{3,2,1,0:T(8,128)} %get-tuple-element.30.one), channel_id=1, source_target_pairs={{0,240},{16,0},{32,16},{48,32},{64,48},{80,64},{96,80},{112,96},{1... | collective-permute-start | bytes 196616 | tf_op jit(solution)/shard_map/ppermute | solution.py:553
  182.5 10.0 %all-to-all-start.2 = ((f32[16,1,8,128]{3,2,1,0:T(8,128)}), f32[16,1,8,128]{3,2,1,0:T(8,128)S(1)}, u32[]{:S(2)}, u32[]{:S(2)}) async-start(f32[16,1,8,128]{3,2,1,0:T(8,128)} %broadcast_in_dim.41), calls=%async_computation.2 | async-start | bytes 131072 | tf_op jit(solution)/shard_map/all_to_all | solution.py:558
  186.0 32.8 %copy-start.16 = (f32[2,4,16,128]{3,2,1,0:T(8,128)}, f32[2,4,16,128]{3,2,1,0:T(8,128)S(1)}, u32[]{:S(2)}) copy-start(f32[2,4,16,128]{3,2,1,0:T(8,128)S(1)} %collective-permute-done.12.left) | copy-start | bytes 196612
  186.9 31.9 %copy-start.17 = (f32[2,4,16,128]{3,2,1,0:T(8,128)}, f32[2,4,16,128]{3,2,1,0:T(8,128)S(1)}, u32[]{:S(2)}) copy-start(f32[2,4,16,128]{3,2,1,0:T(8,128)S(1)} %collective-permute-done.13.right) | copy-start | bytes 196612
  192.4 6.1 %copy-start.11 = (f32[16,1,8,128]{3,2,1,0:T(8,128)}, f32[16,1,8,128]{3,2,1,0:T(8,128)S(1)}, u32[]{:S(2)}) copy-start(f32[16,1,8,128]{3,2,1,0:T(8,128)S(1)} %all-to-all-done.2) | copy-start | bytes 196612
  192.5 6.1 %collective-permute-start.15 = (f32[40,8,128]{2,1,0:T(8,128)S(1)}, f32[40,8,128]{2,1,0:T(8,128)S(1)}, u32[]{:S(2)}, u32[]{:S(2)}) collective-permute-start(f32[40,8,128]{2,1,0:T(8,128)S(1)} %get-tuple-element.54), channel_id=1, source_target_pairs={{0,15},{1,0},{2,1},{3,2},{4,3},{5,4},{6,5},{7,6},{8,7},{9,8},{10,9... | collective-permute-start | bytes 491528 | tf_op jit(solution)/shard_map/ppermute | solution.py:553
  195.7 2.8 %collective-permute-start.14 = (f32[40,8,128]{2,1,0:T(8,128)S(1)}, f32[40,8,128]{2,1,0:T(8,128)S(1)}, u32[]{:S(2)}, u32[]{:S(2)}) collective-permute-start(f32[40,8,128]{2,1,0:T(8,128)S(1)} %get-tuple-element.55), channel_id=1, source_target_pairs={{0,1},{1,2},{2,3},{3,4},{4,5},{5,6},{6,7},{7,8},{8,9},{9,10},{10,1... | collective-permute-start | bytes 491528 | tf_op jit(solution)/shard_map/ppermute | solution.py:553
  198.5 0.6 copy-start.7
  198.5 0.7 copy-start.8
where the time goes:
time: 244 us; the launch traced here: 243 us
  Pallas kernels  103 us (42%)
  waiting for transfers between devices  59.8 us (25%)
  starting transfers between devices  45.8 us (19%)
  blocking collectives  15.8 us (6%)
  local copies, waits for them, and re-layouts  15.4 us (6%)
  other arithmetic  3.02 us (1%)
    pallas_call x6, Pallas kernels, call(): pl.pallas_call(kernel, out_shape=[jax.ShapeDtypeStruct(o, F32) for o in o...  103 us
    ppermute x16, waiting for transfers between devices, shift(): lax.ppermute(value, axis, [(i, (i + step) % count) for i in range(count)])  37.8 us
    ppermute x16, starting transfers between devices, shift(): lax.ppermute(value, axis, [(i, (i + step) % count) for i in range(count)])  28.3 us
    all_to_all x3, waiting for transfers between devices, gather(): lax.all_to_all(jnp.broadcast_to(value[None], (count,) + value.shape), axi...  22.1 us
    all_to_all x3, starting transfers between devices, gather(): lax.all_to_all(jnp.broadcast_to(value[None], (count,) + value.shape), axi...  17.6 us
    all_to_all x1, blocking collectives, gather(): lax.all_to_all(jnp.broadcast_to(value[None], (count,) + value.shape), axi...  15.8 us
    unnamed x42, local copies, waits for them, and re-layouts  5.47 us
  transfers between devices with their start and end apart: 19, of which 12 were waited for; matrix products, arithmetic and copies ran while one was open for 3% of the time, Pallas kernels for 0%

commit v1 on v0

--- a/solution.py
+++ b/solution.py
@@ -15,7 +15,8 @@
 HX = 10
 HY = 12
 PX, RY = TX + 2 * HX, TY + 2 * HY
-UX, UR = TX + 10, TY + 16
+UX, UR = TX + 12, TY + 16
+CHUNK = 4
 VMEM_BYTES = 56 * 1024 * 1024
 
 
@@ -155,43 +156,56 @@
     ref[plane, pl.ds(start + 1, count, stride=2), :] = value
 
 
+def insider(rows, first_x, first_y):
+    row = lax.broadcasted_iota(jnp.int32, (CHUNK, rows, 128), 1) + first_y
+    row_in = (row >= 0) & (row < 512)
+    plane = lax.broadcasted_iota(jnp.int32, (CHUNK, rows, 128), 0) + first_x
+    return lambda p: row_in & (plane >= -p) & (plane < 256 - p)
+
+
 def build_top(k_ref, wx, wy, wz, s, rd, planes, inside_at, body):
     rows = k_ref.shape[1]
-    shape = (rows, 128)
+    shape = (CHUNK, rows, 128)
     lane = lanes(shape)
 
-    def step(p, carry):
-        k, wxp = carry
-        kn = k_ref[jnp.minimum(p + 1, planes - 1)]
+    def step(i, wxp):
+        p = i * CHUNK
+        k = k_ref[pl.ds(p, CHUNK)]
+        kn = jnp.concatenate([k[1:], k_ref[pl.ds(jnp.minimum(p + CHUNK, planes - 1), 1)]], axis=0)
         own = 0.5 * k
         fx = 0.5 * kn + own
-        fy = turn(own, -1, 0) + own
-        fz = jnp.where(lane == 127, 0.0, turn(own, -1, 1) + own)
+        fy = turn(own, -1, 1) + own
+        fz = jnp.where(lane == 127, 0.0, turn(own, -1, 2) + own)
         sv = SIGMA + jnp.where((lane == 0) | (lane == 127), own, 0.0)
-        diagonal = sv + (fx + wxp) + (fy + turn(fy, 1, 0)) + (fz + turn(fz, 1, 1))
+        fxp = jnp.concatenate([wxp, fx[:-1]], axis=0)
+        diagonal = sv + (fx + fxp) + (fy + turn(fy, 1, 1)) + (fz + turn(fz, 1, 2))
         rdv = jnp.where(inside_at(p), 1.0 / diagonal, 0.0)
-        wx[p], wy[p], wz[p], s[p], rd[p] = fx, fy, fz, sv, rdv
+        at = pl.ds(p, CHUNK)
+        wx[at], wy[at], wz[at], s[at], rd[at] = fx, fy, fz, sv, rdv
         body(p, rdv)
-        return kn, fx
-
-    lax.fori_loop(0, planes, step, (k_ref[0], jnp.zeros(shape, F32)))
+        return fx[-1:]
+
+    lax.fori_loop(0, planes // CHUNK, step, jnp.zeros((1, rows, 128), F32))
 
 
 def sweep_top(x, wx, wy, wz, s, low, high, body):
-    v0 = x[low]
-    fx0 = wx[low - 1] * (v0 - x[low - 1])
-
-    def step(p, carry):
-        v, fxp = carry
-        vn = x[p + 1]
-        fx = wx[p] * (vn - v)
-        fy = wy[p] * (turn(v, -1, 0) - v)
-        fz = wz[p] * (turn(v, -1, 1) - v)
-        total = (fx - fxp) + (fy - turn(fy, 1, 0)) + (fz - turn(fz, 1, 1))
-        body(p, v, s[p] * v - total)
-        return vn, fx
-
-    lax.fori_loop(low, high, step, (v0, fx0))
+    fx0 = wx[low - 1 : low] * (x[low : low + 1] - x[low - 1 : low])
+
+    def step(i, fxp):
+        p = low + i * CHUNK
+        at = pl.ds(p, CHUNK)
+        v = x[at]
+        vn = jnp.concatenate([v[1:], x[pl.ds(p + CHUNK, 1)]], axis=0)
+        fx = wx[at] * (vn - v)
+        fy = wy[at] * (turn(v, -1, 1) - v)
+        fz = wz[at] * (turn(v, -1, 2) - v)
+        fxp = jnp.concatenate([fxp, fx[:-1]], axis=0)
+        total = (fx - fxp) + (fy - turn(fy, 1, 1)) + (fz - turn(fz, 1, 2))
+        body(p, at, v, s[at] * v - total)
+        return fx[-1:]
+
+    assert (high - low) % CHUNK == 0
+    lax.fori_loop(0, (high - low) // CHUNK, step, fx0)
 
 
 def fill_top(dst, tile, left, right, below, above):
@@ -213,48 +227,45 @@
         scratch = refs[7:]
     bx, wx, wy, wz, s, rd, d, x, rs, b1s, x1s, k1s = scratch
     gx, gy = pos[0], pos[1]
-    row = lax.broadcasted_iota(jnp.int32, (RY, 128), 0) + (gy * TY - HY)
-    row_in = (row >= 0) & (row < 512)
-
-    def inside_at(p):
-        at = gx * TX - HX + p
-        return row_in & ((at >= 0) & (at < 256))
+    inside_at = insider(RY, gx * TX - HX, gy * TY - HY)
 
     fill_top(bx, tile[...], left[0], right[0], below[0], above[0])
     if first:
         fill_top(kx, ktile[...], left[1], right[1], below[1], above[1])
 
-        def clear(p, _):
-            kx[p] = jnp.where(inside_at(p), kx[p], 0.0)
+        def clear(i, _):
+            at = pl.ds(i * CHUNK, CHUNK)
+            kx[at] = jnp.where(inside_at(i * CHUNK), kx[at], 0.0)
             return 0
 
-        lax.fori_loop(0, PX, clear, 0)
+        lax.fori_loop(0, PX // CHUNK, clear, 0)
 
     start, steps = SMOOTH
 
     def begin(p, rdv):
-        v = (bx[p] * rdv) * start
-        d[p] = v
-        x[p] = v
+        at = pl.ds(p, CHUNK)
+        v = (bx[at] * rdv) * start
+        d[at] = v
+        x[at] = v
 
     build_top(kx, wx, wy, wz, s, rd, PX, inside_at, begin)
     for number, (keep, gain) in enumerate(steps):
 
-        def advance(p, v, av):
-            dv = keep * d[p] + gain * ((bx[p] - av) * rd[p])
-            d[p] = dv
-            x[p] = v + dv
-
-        sweep_top(x, wx, wy, wz, s, 2 + number, PX - 2 - number, advance)
-
-    def residual(p, v, av):
-        d[p] = bx[p] - av
+        def advance(p, at, v, av):
+            dv = keep * d[at] + gain * ((bx[at] - av) * rd[at])
+            d[at] = dv
+            x[at] = v + dv
+
+        sweep_top(x, wx, wy, wz, s, 2, PX - 2, advance)
+
+    def residual(p, at, v, av):
+        d[at] = bx[at] - av
 
     sweep_top(x, wx, wy, wz, s, 4, PX - 4, residual)
-    xup[...] = x[5 : 5 + UX, 4 : 4 + UR, :]
-    bup[...] = bx[5 : 5 + UX, 4 : 4 + UR, :]
-    if first:
-        kup[...] = kx[5 : 5 + UX, 4 : 4 + UR, :]
+    xup[...] = x[4 : 4 + UX, 4 : 4 + UR, :]
+    bup[...] = bx[4 : 4 + UX, 4 : 4 + UR, :]
+    if first:
+        kup[...] = kx[4 : 4 + UX, 4 : 4 + UR, :]
 
     def coarse(src):
         for c in range(16):
@@ -491,53 +502,48 @@
     for i in range(6):
         for q in range(2):
             spread_rows(e0, 2 * i + q, 0, back[24 * i : 24 * i + 24, 128 * q : 128 * q + 128])
-    row = lax.broadcasted_iota(jnp.int32, (UR, 128), 0) + (gy * TY - 8)
-    row_in = (row >= 0) & (row < 512)
-
-    def inside_at(p):
-        at = gx * TX - 5 + p
-        return row_in & ((at >= 0) & (at < 256))
+    inside_at = insider(UR, gx * TX - 6, gy * TY - 8)
 
     def begin(p, rdv):
-        correction = e0[jnp.clip((p - 1) // 2, 0, 11)]
-        x[p] = x0[p] + jnp.where(rdv > 0.0, correction, 0.0)
+        at = pl.ds(p, CHUNK)
+        low = jnp.maximum(p // 2 - 1, 0)
+        high = jnp.minimum(p // 2, 11)
+        pair = (e0[pl.ds(low, 1)], e0[pl.ds(high, 1)])
+        correction = jnp.concatenate([pair[0], pair[0], pair[1], pair[1]], axis=0)
+        x[at] = x0[at] + jnp.where(rdv > 0.0, correction, 0.0)
 
     build_top(k0, wx, wy, wz, s, rd, UX, inside_at, begin)
     start, steps = SMOOTH
 
-    def open_up(p, v, av):
-        dv = ((b0[p] - av) * rd[p]) * start
-        d[p] = dv
-        x[p] = v + dv
+    def open_up(p, at, v, av):
+        dv = ((b0[at] - av) * rd[at]) * start
+        d[at] = dv
+        x[at] = v + dv
 
     sweep_top(x, wx, wy, wz, s, 2, UX - 2, open_up)
     for number, (keep, gain) in enumerate(steps):
 
-        def advance(p, v, av):
-            dv = keep * d[p] + gain * ((b0[p] - av) * rd[p])
-            d[p] = dv
-            x[p] = v + dv
-
-        sweep_top(x, wx, wy, wz, s, 3 + number, UX - 3 - number, advance)
-
-    if first:
-        xout[...] = x[4 : UX - 4]
-
-        def residual(p, v, av):
-            rout[p - 5] = b0[p, 8 : 8 + TY, :] - av[8 : 8 + TY]
+        def advance(p, at, v, av):
+            dv = keep * d[at] + gain * ((b0[at] - av) * rd[at])
+            d[at] = dv
+            x[at] = v + dv
+
+        sweep_top(x, wx, wy, wz, s, 4, UX - 4, advance)
+
+    if first:
+        xout[...] = x[5 : UX - 5]
+
+        def residual(p, at, v, av):
+            rout[pl.ds(p - 6, CHUNK)] = b0[at, 8 : 8 + TY, :] - av[:, 8 : 8 + TY]
     else:
-
-        def add(p, _):
-            x[p] = x[p] + xbefore[p - 4]
-            return 0
-
-        lax.fori_loop(4, UX - 4, add, 0)
-
-        def residual(p, v, av):
-            xout[p - 5] = v[8 : 8 + TY]
-            rout[p - 5] = borig[p - 5] - av[8 : 8 + TY]
-
-    sweep_top(x, wx, wy, wz, s, 5, UX - 5, residual)
+        x[5 : UX - 5] = x[5 : UX - 5] + xbefore[...]
+
+        def residual(p, at, v, av):
+            out = pl.ds(p - 6, CHUNK)
+            xout[out] = v[:, 8 : 8 + TY]
+            rout[out] = borig[out] - av[:, 8 : 8 + TY]
+
+    sweep_top(x, wx, wy, wz, s, 6, UX - 6, residual)
 
 
 def go_up(first, *args):

time: 244 us -> 196 us (0.80)
  Pallas kernels: 103 us -> 53.9 us
    pallas_call x6, Pallas kernels: 103 us -> 53.9 us  [call(): pl.pallas_call(kernel, out_shape=[jax.ShapeDtypeStruct(o, F32) for o in o...]
  transfers between devices with their start and end apart: 19 -> 19, of which waited for: 12 -> 12; matrix products, arithmetic and copies ran while one was open for 3% -> 4% of each run, Pallas kernels for 0% -> 0%
where the time goes in v1:
time: 196 us; the launch traced here: 195 us
  waiting for transfers between devices  59.7 us (30%)
  Pallas kernels  53.9 us (28%)
  starting transfers between devices  45.8 us (23%)
  blocking collectives  15.8 us (8%)
  local copies, waits for them, and re-layouts  15.4 us (8%)
  other arithmetic  3.1 us (2%)
    pallas_call x6, Pallas kernels, call(): pl.pallas_call(kernel, out_shape=[jax.ShapeDtypeStruct(o, F32) for o in o...  53.9 us
    ppermute x16, waiting for transfers between devices, shift(): lax.ppermute(value, axis, [(i, (i + step) % count) for i in range(count)])  37.7 us
    ppermute x16, starting transfers between devices, shift(): lax.ppermute(value, axis, [(i, (i + step) % count) for i in range(count)])  28.3 us
    all_to_all x3, waiting for transfers between devices, gather(): lax.all_to_all(jnp.broadcast_to(value[None], (count,) + value.shape), axi...  22.1 us
    all_to_all x3, starting transfers between devices, gather(): lax.all_to_all(jnp.broadcast_to(value[None], (count,) + value.shape), axi...  17.6 us
    all_to_all x1, blocking collectives, gather(): lax.all_to_all(jnp.broadcast_to(value[None], (count,) + value.shape), axi...  15.8 us
    unnamed x42, local copies, waits for them, and re-layouts  5.47 us
    broadcast_in_dim x4, local copies, waits for them, and re-layouts, gather(): jnp.broadcast_to(value[None], (count,) + value.shape)  4.82 us
  transfers between devices with their start and end apart: 19, of which 12 were waited for; matrix products, arithmetic and copies ran while one was open for 4% of the time, Pallas kernels for 0%

profile of v1, /device:TPU:1, one launch (start us, length us, event | category | flops | bytes accessed | tf_op | source)
XLA Modules:
  0.0 194.8 jit_solution(15884019308276351186)
XLA Ops:
  0.7 1.3 pad_maximum_fusion.4
  1.9 5.8 %collective-permute-start.1 = (f32[2,10,32,128]{3,2,1,0:T(8,128)S(1)}, f32[2,10,32,128]{3,2,1,0:T(8,128)S(1)}, u32[]{:S(2)}, u32[]{:S(2)}) collective-permute-start(f32[2,10,32,128]{3,2,1,0:T(8,128)S(1)} %get-tuple-element.42), channel_id=1, source_target_pairs={{0,240},{16,0},{32,16},{48,32},{64,48},{80,64},{96,80},{112,96},{1... | collective-permute-start | bytes 983048 | tf_op jit(solution)/shard_map/ppermute | solution.py:559
  7.7 6.4 %collective-permute-done.1.right = f32[2,10,32,128]{3,2,1,0:T(8,128)S(1)} collective-permute-done((f32[2,10,32,128]{3,2,1,0:T(8,128)S(1)}, f32[2,10,32,128]{3,2,1,0:T(8,128)S(1)}, u32[]{:S(2)}, u32[]{:S(2)}) %collective-permute-start.1) | collective-permute-done | bytes 327712 | tf_op jit(solution)/shard_map/ppermute | solution.py:559
  14.1 5.2 %collective-permute-done.left = f32[2,10,32,128]{3,2,1,0:T(8,128)S(1)} collective-permute-done((f32[2,10,32,128]{3,2,1,0:T(8,128)S(1)}, f32[2,10,32,128]{3,2,1,0:T(8,128)S(1)}, u32[]{:S(2)}, u32[]{:S(2)}) %collective-permute-start) | collective-permute-done | bytes 327712 | tf_op jit(solution)/shard_map/ppermute | solution.py:559
  20.5 3.4 %collective-permute-start.2 = (f32[2,36,10,128]{3,0,2,1:T(2,128)S(1)}, f32[2,36,10,128]{3,0,2,1:T(2,128)S(1)}, u32[]{:S(2)}, u32[]{:S(2)}) collective-permute-start(f32[2,36,10,128]{3,0,2,1:T(2,128)S(1)} %copy.22), channel_id=1, source_target_pairs={{0,1},{1,2},{2,3},{3,4},{4,5},{5,6},{6,7},{7,8},{8,9},{9,10},{10,1... | collective-permute-start | bytes 1105928 | tf_op jit(solution)/shard_map/ppermute | solution.py:559
  24.2 0.7 pad_add_fusion.pos
  24.8 3.5 %collective-permute-done.2 = f32[2,36,10,128]{3,0,2,1:T(2,128)S(1)} collective-permute-done((f32[2,36,10,128]{3,0,2,1:T(2,128)S(1)}, f32[2,36,10,128]{3,0,2,1:T(2,128)S(1)}, u32[]{:S(2)}, u32[]{:S(2)}) %collective-permute-start.2) | collective-permute-done | bytes 368672 | tf_op jit(solution)/shard_map/ppermute | solution.py:559
  28.3 0.9 copy.24.below
  29.2 2.1 %collective-permute-done.3 = f32[2,36,10,128]{3,0,2,1:T(2,128)S(1)} collective-permute-done((f32[2,36,10,128]{3,0,2,1:T(2,128)S(1)}, f32[2,36,10,128]{3,0,2,1:T(2,128)S(1)}, u32[]{:S(2)}, u32[]{:S(2)}) %collective-permute-start.3) | collective-permute-done | bytes 368672 | tf_op jit(solution)/shard_map/ppermute | solution.py:559
  31.2 0.9 copy.25.above
  32.1 10.3 %shard_map.122 = (f32[28,48,128]{2,1,0:T(8,128)}, f32[28,48,128]{2,1,0:T(8,128)}, f32[28,48,128]{2,1,0:T(8,128)}, f32[36,56,128]{2,1,0:T(8,128)}, f32[3,4,16,128]{3,2,1,0:T(8,128)}, /*index=5*/f32[2,8,128]{2,1,0:T(8,128)}) custom-call(s32[2]{0:T(128)} %pad_add_fusion.pos, f32[16,32,128]{2,1,0:T(8,128)} %refs_2_.4, f32[2,10,32,128]{3,2,1,0:T(8,128)} %copy-done.3, ...), custom_call_target="tpu_custom_call" | custom-call | flops 10000000 | bytes 8388608 | tf_op jit(solution)/shard_map/pallas_call | solution.py:310
  42.4 4.8 %collective-permute-start.5 = (f32[3,4,16,128]{3,2,1,0:T(8,128)}, f32[3,4,16,128]{3,2,1,0:T(8,128)S(1)}, u32[]{:S(2)}, u32[]{:S(2)}) collective-permute-start(f32[3,4,16,128]{3,2,1,0:T(8,128)} %get-tuple-element.21.one), channel_id=1, source_target_pairs={{0,240},{16,0},{32,16},{48,32},{64,48},{80,64},{96,80},{112,96},{1... | collective-permute-start | bytes 294920 | tf_op jit(solution)/shard_map/ppermute | solution.py:559
  47.2 1.4 broadcast_in_dim.18
  48.6 3.5 %all-to-all-start = ((f32[16,2,8,128]{3,2,1,0:T(8,128)}), f32[16,2,8,128]{3,2,1,0:T(8,128)S(1)}, u32[]{:S(2)}, u32[]{:S(2)}) async-start(f32[16,2,8,128]{3,2,1,0:T(8,128)} %broadcast_in_dim.18), calls=%async_computation | async-start | bytes 262144 | tf_op jit(solution)/shard_map/all_to_all | solution.py:564
  52.1 0.9 constant_dynamic-update-slice_fusion.1
  53.1 5.7 %all-to-all-done = f32[16,2,8,128]{3,2,1,0:T(8,128)S(1)} async-done(((f32[16,2,8,128]{3,2,1,0:T(8,128)}), f32[16,2,8,128]{3,2,1,0:T(8,128)S(1)}, u32[]{:S(2)}, u32[]{:S(2)}) %all-to-all-start) | async-done | bytes 131104 | tf_op jit(solution)/shard_map/all_to_all | solution.py:564
  58.9 2.9 %collective-permute-start.7 = (f32[68,8,128]{2,1,0:T(8,128)S(1)}, f32[68,8,128]{2,1,0:T(8,128)S(1)}, u32[]{:S(2)}, u32[]{:S(2)}) collective-permute-start(f32[68,8,128]{2,1,0:T(8,128)S(1)} %get-tuple-element.52), channel_id=1, source_target_pairs={{0,15},{1,0},{2,1},{3,2},{4,3},{5,4},{6,5},{7,6},{8,7},{9,8},{10,9... | collective-permute-start | bytes 835592 | tf_op jit(solution)/shard_map/ppermute | solution.py:559
  61.8 3.9 %collective-permute-done.7.above = f32[68,8,128]{2,1,0:T(8,128)S(1)} collective-permute-done((f32[68,8,128]{2,1,0:T(8,128)S(1)}, f32[68,8,128]{2,1,0:T(8,128)S(1)}, u32[]{:S(2)}, u32[]{:S(2)}) %collective-permute-start.7) | collective-permute-done | bytes 278560 | tf_op jit(solution)/shard_map/ppermute | solution.py:559
  65.8 0.7 copy-done.5
  66.4 0.7 copy-done.6
  67.2 3.2 %shard_map.123 = (f32[7,5,24,128]{3,2,1,0:T(8,128)}, f32[4,8,128]{2,1,0:T(8,128)}, f32[16,24,128]{2,1,0:T(8,128)}) custom-call(s32[2]{0:T(128)} %pad_add_fusion.pos, f32[32,8,128]{2,1,0:T(8,128)} %bitcast.25, f32[68,8,128]{2,1,0:T(8,128)} %copy-done.6, f32[68,8,128]{2,1,0:T(8,128)} %copy-done.5, bf16[512,128]{1,0:T(8,128)(2,1)} %constant.25.clone.refs_0_.refs_1_), custom_call_target="tpu_custom_call" | custom-call | flops 10000000 | bytes 8388608 | tf_op jit(solution)/shard_map/pallas_call | solution.py:310
  70.3 1.4 broadcast_in_dim.38
  71.8 10.5 %all-to-all-start.1 = ((f32[16,4,8,128]{3,2,1,0:T(8,128)}), f32[16,4,8,128]{3,2,1,0:T(8,128)S(1)}, u32[]{:S(2)}, u32[]{:S(2)}) async-start(f32[16,4,8,128]{3,2,1,0:T(8,128)} %broadcast_in_dim.38), calls=%async_computation.1 | async-start | bytes 524288 | tf_op jit(solution)/shard_map/all_to_all | solution.py:564
  82.5 0.7 copy.28.owned
  83.2 10.8 %all-to-all-done.1 = f32[16,4,8,128]{3,2,1,0:T(8,128)S(1)} async-done(((f32[16,4,8,128]{3,2,1,0:T(8,128)}), f32[16,4,8,128]{3,2,1,0:T(8,128)S(1)}, u32[]{:S(2)}, u32[]{:S(2)}) %all-to-all-start.1) | async-done | bytes 262176 | tf_op jit(solution)/shard_map/all_to_all | solution.py:564
  94.0 0.7 fusion.5
  94.8 13.7 %shard_map.124 = (f32[18,48,128]{2,1,0:T(8,128)}, f32[16,32,128]{2,1,0:T(8,128)}, f32[12,32,128]{2,1,0:T(8,128)}) custom-call(s32[2]{0:T(128)} %pad_add_fusion.pos, f32[32,128]{1,0:T(8,128)} %copy.28.owned, f32[16,2,8,128]{3,2,1,0:T(8,128)} %get-tuple-element.49.b3g, f32[16,2,8,128]{3,2,1,0:T(8,128)} %get-tuple-element.48.k3g, ...), custom_call_target="tpu_custom_call" | custom-call | flops 10000000 | bytes 8388608 | tf_op jit(solution)/shard_map/pallas_call | solution.py:310
  108.5 1.0 fusion.4
  109.5 1.4 collective-permute-start.9
  111.0 4.7 %collective-permute-done.9.right = f32[1,10,32,128]{3,2,1,0:T(8,128)S(1)} collective-permute-done((f32[1,10,32,128]{3,2,1,0:T(8,128)S(1)}, f32[1,10,32,128]{3,2,1,0:T(8,128)S(1)}, u32[]{:S(2)}, u32[]{:S(2)}) %collective-permute-start.9) | collective-permute-done | bytes 163872 | tf_op jit(solution)/shard_map/ppermute | solution.py:559
  115.8 4.4 %collective-permute-done.8.left = f32[1,10,32,128]{3,2,1,0:T(8,128)S(1)} collective-permute-done((f32[1,10,32,128]{3,2,1,0:T(8,128)S(1)}, f32[1,10,32,128]{3,2,1,0:T(8,128)S(1)}, u32[]{:S(2)}, u32[]{:S(2)}) %collective-permute-start.8) | collective-permute-done | bytes 163872 | tf_op jit(solution)/shard_map/ppermute | solution.py:559
  120.2 1.0 pad_maximum_fusion.1
  121.3 0.7 collective-permute-start.11
  122.0 1.0 collective-permute-start.10
  123.1 4.7 %collective-permute-done.11.above = f32[1,36,10,128]{3,2,1,0:T(8,128)S(1)} collective-permute-done((f32[1,36,10,128]{3,2,1,0:T(8,128)S(1)}, f32[1,36,10,128]{3,2,1,0:T(8,128)S(1)}, u32[]{:S(2)}, u32[]{:S(2)}) %collective-permute-start.11) | collective-permute-done | bytes 184352 | tf_op jit(solution)/shard_map/ppermute | solution.py:559
  127.8 0.7 copy-done.14
  128.6 9.8 %shard_map.125 = (f32[28,48,128]{2,1,0:T(8,128)}, f32[28,48,128]{2,1,0:T(8,128)}, f32[2,4,16,128]{3,2,1,0:T(8,128)}, f32[1,8,128]{2,1,0:T(8,128)}) custom-call(s32[2]{0:T(128)} %pad_add_fusion.pos, f32[16,32,128]{2,1,0:T(8,128)} %get-tuple-element.27.tile, f32[1,10,32,128]{3,2,1,0:T(8,128)} %copy-done.10, f32[1,10,32,128]{3,2,1,0:T(8,128)} %copy-done.9, ...), custom_call_target="tpu_custom_call" | custom-call | flops 10000000 | bytes 8388608 | tf_op jit(solution)/shard_map/pallas_call | solution.py:310
  138.4 4.8 %collective-permute-start.13 = (f32[2,4,16,128]{3,2,1,0:T(8,128)}, f32[2,4,16,128]{3,2,1,0:T(8,128)S(1)}, u32[]{:S(2)}, u32[]{:S(2)}) collective-permute-start(f32[2,4,16,128]{3,2,1,0:T(8,128)} %get-tuple-element.30.one), channel_id=1, source_target_pairs={{0,240},{16,0},{32,16},{48,32},{64,48},{80,64},{96,80},{112,96},{1... | collective-permute-start | bytes 196616 | tf_op jit(solution)/shard_map/ppermute | solution.py:559
  143.2 1.3 broadcast_in_dim.41
  144.5 3.5 %all-to-all-start.2 = ((f32[16,1,8,128]{3,2,1,0:T(8,128)}), f32[16,1,8,128]{3,2,1,0:T(8,128)S(1)}, u32[]{:S(2)}, u32[]{:S(2)}) async-start(f32[16,1,8,128]{3,2,1,0:T(8,128)} %broadcast_in_dim.41), calls=%async_computation.2 | async-start | bytes 131072 | tf_op jit(solution)/shard_map/all_to_all | solution.py:564
  148.1 0.9 constant_dynamic-update-slice_fusion.4
  149.0 5.5 %all-to-all-done.2 = f32[16,1,8,128]{3,2,1,0:T(8,128)S(1)} async-done(((f32[16,1,8,128]{3,2,1,0:T(8,128)}), f32[16,1,8,128]{3,2,1,0:T(8,128)S(1)}, u32[]{:S(2)}, u32[]{:S(2)}) %all-to-all-start.2) | async-done | bytes 65568 | tf_op jit(solution)/shard_map/all_to_all | solution.py:564
  154.5 3.3 %collective-permute-start.15 = (f32[40,8,128]{2,1,0:T(8,128)S(1)}, f32[40,8,128]{2,1,0:T(8,128)S(1)}, u32[]{:S(2)}, u32[]{:S(2)}) collective-permute-start(f32[40,8,128]{2,1,0:T(8,128)S(1)} %get-tuple-element.54), channel_id=1, source_target_pairs={{0,15},{1,0},{2,1},{3,2},{4,3},{5,4},{6,5},{7,6},{8,7},{9,8},{10,9... | collective-permute-start | bytes 491528 | tf_op jit(solution)/shard_map/ppermute | solution.py:559
  157.8 2.8 %collective-permute-done.15.above = f32[40,8,128]{2,1,0:T(8,128)S(1)} collective-permute-done((f32[40,8,128]{2,1,0:T(8,128)S(1)}, f32[40,8,128]{2,1,0:T(8,128)S(1)}, u32[]{:S(2)}, u32[]{:S(2)}) %collective-permute-start.15) | collective-permute-done | bytes 163872 | tf_op jit(solution)/shard_map/ppermute | solution.py:559
  161.3 3.1 %shard_map.126 = (f32[7,5,24,128]{3,2,1,0:T(8,128)}, f32[2,8,128]{2,1,0:T(8,128)}) custom-call(s32[2]{0:T(128)} %pad_add_fusion.pos, f32[16,8,128]{2,1,0:T(8,128)} %bitcast.27, f32[40,8,128]{2,1,0:T(8,128)} %copy-done.8, f32[40,8,128]{2,1,0:T(8,128)} %copy-done.7, f32[16,24,128]{2,1,0:T(8,128)} %get-tuple-element.31.refs_0_, ...), custom_call_target="tpu_custom_call" | custom-call | flops 10000000 | bytes 8388608 | tf_op jit(solution)/shard_map/pallas_call | solution.py:310
  164.4 0.7 broadcast_in_dim.42
  165.1 15.8 %all_to_all.20.b3g = f32[16,2,8,128]{3,2,1,0:T(8,128)} all-to-all(f32[16,2,8,128]{3,2,1,0:T(8,128)S(1)} %broadcast_in_dim.42), channel_id=1, replica_groups=mesh['gx'=16,'gy'=16] {'gy'}, dimensions={0} | all-to-all | bytes 262144 | tf_op jit(solution)/shard_map/all_to_all | solution.py:564
  180.9 13.9 %shard_map.127 = (f32[16,32,128]{2,1,0:T(8,128)}, f32[16,32,128]{2,1,0:T(8,128)}) custom-call(s32[2]{0:T(128)} %pad_add_fusion.pos, f32[32,128]{1,0:T(8,128)} %copy.28.owned, f32[16,2,8,128]{3,2,1,0:T(8,128)} %all_to_all.20.b3g, f32[16,2,8,128]{3,2,1,0:T(8,128)} %get-tuple-element.48.k3g, f32[7,5,24,128]{3,2,1,0:T(8,128)} %get-tuple-element.33.near, ...), custom_call_target="tpu_custom_call" | custom-call | flops 10000000 | bytes 8388608 | tf_op jit(solution)/shard_map/pallas_call | solution.py:310
  (68 shorter events, 2.8 us)
Async XLA Ops:
  0.6 18.7 %copy-start = (f32[16,32,128]{2,1,0:T(8,128)S(1)}, f32[16,32,128]{2,1,0:T(8,128)}, u32[]{:S(2)}) copy-start(f32[16,32,128]{2,1,0:T(8,128)} %refs_2_.4) | copy-start | bytes 786436
  0.6 18.7 %copy-start.1 = (f32[16,32,128]{2,1,0:T(8,128)S(1)}, f32[16,32,128]{2,1,0:T(8,128)}, u32[]{:S(2)}) copy-start(f32[16,32,128]{2,1,0:T(8,128)} %refs_0_.3) | copy-start | bytes 786436
  1.9 12.2 %collective-permute-start.1 = (f32[2,10,32,128]{3,2,1,0:T(8,128)S(1)}, f32[2,10,32,128]{3,2,1,0:T(8,128)S(1)}, u32[]{:S(2)}, u32[]{:S(2)}) collective-permute-start(f32[2,10,32,128]{3,2,1,0:T(8,128)S(1)} %get-tuple-element.42), channel_id=1, source_target_pairs={{0,240},{16,0},{32,16},{48,32},{64,48},{80,64},{96,80},{112,96},{1... | collective-permute-start | bytes 983048 | tf_op jit(solution)/shard_map/ppermute | solution.py:559
  7.7 11.6 %collective-permute-start = (f32[2,10,32,128]{3,2,1,0:T(8,128)S(1)}, f32[2,10,32,128]{3,2,1,0:T(8,128)S(1)}, u32[]{:S(2)}, u32[]{:S(2)}) collective-permute-start(f32[2,10,32,128]{3,2,1,0:T(8,128)S(1)} %get-tuple-element.43), channel_id=1, source_target_pairs={{0,16},{16,32},{32,48},{48,64},{64,80},{80,96},{96,112},{112,128},... | collective-permute-start | bytes 983048 | tf_op jit(solution)/shard_map/ppermute | solution.py:559
  14.1 5.3 %copy-start.2 = (f32[2,10,32,128]{3,2,1,0:T(8,128)}, f32[2,10,32,128]{3,2,1,0:T(8,128)S(1)}, u32[]{:S(2)}) copy-start(f32[2,10,32,128]{3,2,1,0:T(8,128)S(1)} %collective-permute-done.1.right) | copy-start | bytes 983044
  19.3 0.7 copy-start.3
  20.5 7.9 %collective-permute-start.2 = (f32[2,36,10,128]{3,0,2,1:T(2,128)S(1)}, f32[2,36,10,128]{3,0,2,1:T(2,128)S(1)}, u32[]{:S(2)}, u32[]{:S(2)}) collective-permute-start(f32[2,36,10,128]{3,0,2,1:T(2,128)S(1)} %copy.22), channel_id=1, source_target_pairs={{0,1},{1,2},{2,3},{3,4},{4,5},{5,6},{6,7},{7,8},{8,9},{9,10},{10,1... | collective-permute-start | bytes 1105928 | tf_op jit(solution)/shard_map/ppermute | solution.py:559
  24.1 7.1 %collective-permute-start.3 = (f32[2,36,10,128]{3,0,2,1:T(2,128)S(1)}, f32[2,36,10,128]{3,0,2,1:T(2,128)S(1)}, u32[]{:S(2)}, u32[]{:S(2)}) collective-permute-start(f32[2,36,10,128]{3,0,2,1:T(2,128)S(1)} %copy.23), channel_id=1, source_target_pairs={{0,15},{1,0},{2,1},{3,2},{4,3},{5,4},{6,5},{7,6},{8,7},{9,8},{10,9... | collective-permute-start | bytes 1105928 | tf_op jit(solution)/shard_map/ppermute | solution.py:559
  42.4 9.7 %collective-permute-start.4 = (f32[3,4,16,128]{3,2,1,0:T(8,128)}, f32[3,4,16,128]{3,2,1,0:T(8,128)S(1)}, u32[]{:S(2)}, u32[]{:S(2)}) collective-permute-start(f32[3,4,16,128]{3,2,1,0:T(8,128)} %get-tuple-element.21.one), channel_id=1, source_target_pairs={{0,16},{16,32},{32,48},{48,64},{64,80},{80,96},{96,112},{112,128},... | collective-permute-start | bytes 294920 | tf_op jit(solution)/shard_map/ppermute | solution.py:559
  42.4 10.6 %collective-permute-start.5 = (f32[3,4,16,128]{3,2,1,0:T(8,128)}, f32[3,4,16,128]{3,2,1,0:T(8,128)S(1)}, u32[]{:S(2)}, u32[]{:S(2)}) collective-permute-start(f32[3,4,16,128]{3,2,1,0:T(8,128)} %get-tuple-element.21.one), channel_id=1, source_target_pairs={{0,240},{16,0},{32,16},{48,32},{64,48},{80,64},{96,80},{112,96},{1... | collective-permute-start | bytes 294920 | tf_op jit(solution)/shard_map/ppermute | solution.py:559
  48.6 10.3 %all-to-all-start = ((f32[16,2,8,128]{3,2,1,0:T(8,128)}), f32[16,2,8,128]{3,2,1,0:T(8,128)S(1)}, u32[]{:S(2)}, u32[]{:S(2)}) async-start(f32[16,2,8,128]{3,2,1,0:T(8,128)} %broadcast_in_dim.18), calls=%async_computation | async-start | bytes 262144 | tf_op jit(solution)/shard_map/all_to_all | solution.py:564
  52.1 6.8 %copy-start.12 = (f32[3,4,16,128]{3,2,1,0:T(8,128)}, f32[3,4,16,128]{3,2,1,0:T(8,128)S(1)}, u32[]{:S(2)}) copy-start(f32[3,4,16,128]{3,2,1,0:T(8,128)S(1)} %collective-permute-done.4.left) | copy-start | bytes 294916
  53.1 17.3 %copy-start.13 = (f32[3,4,16,128]{3,2,1,0:T(8,128)}, f32[3,4,16,128]{3,2,1,0:T(8,128)S(1)}, u32[]{:S(2)}) copy-start(f32[3,4,16,128]{3,2,1,0:T(8,128)S(1)} %collective-permute-done.5.right) | copy-start | bytes 294916
  58.8 6.9 %copy-start.4 = (f32[2,16,8,128]{3,2,1,0:T(8,128)}, f32[2,16,8,128]{3,2,1,0:T(8,128)S(1)}, u32[]{:S(2)}) copy-start(f32[2,16,8,128]{3,2,1,0:T(8,128)S(1)} %copy.26) | copy-start | bytes 393220
  58.8 23.5 %copy-start.18 = (s32[16,16]{1,0:T(8,128)S(1)}, s32[16,16]{1,0:T(8,128)}, u32[]{:S(2)}) copy-start(s32[16,16]{1,0:T(8,128)} %param.13) | copy-start | bytes 3076
  58.9 6.8 %collective-permute-start.7 = (f32[68,8,128]{2,1,0:T(8,128)S(1)}, f32[68,8,128]{2,1,0:T(8,128)S(1)}, u32[]{:S(2)}, u32[]{:S(2)}) collective-permute-start(f32[68,8,128]{2,1,0:T(8,128)S(1)} %get-tuple-element.52), channel_id=1, source_target_pairs={{0,15},{1,0},{2,1},{3,2},{4,3},{5,4},{6,5},{7,6},{8,7},{9,8},{10,9... | collective-permute-start | bytes 835592 | tf_op jit(solution)/shard_map/ppermute | solution.py:559
  61.8 3.9 %collective-permute-start.6 = (f32[68,8,128]{2,1,0:T(8,128)S(1)}, f32[68,8,128]{2,1,0:T(8,128)S(1)}, u32[]{:S(2)}, u32[]{:S(2)}) collective-permute-start(f32[68,8,128]{2,1,0:T(8,128)S(1)} %get-tuple-element.53), channel_id=1, source_target_pairs={{0,1},{1,2},{2,3},{3,4},{4,5},{5,6},{6,7},{7,8},{8,9},{9,10},{10,1... | collective-permute-start | bytes 835592 | tf_op jit(solution)/shard_map/ppermute | solution.py:559
  65.7 0.7 copy-start.5
  66.4 0.7 copy-start.6
  71.8 22.3 %all-to-all-start.1 = ((f32[16,4,8,128]{3,2,1,0:T(8,128)}), f32[16,4,8,128]{3,2,1,0:T(8,128)S(1)}, u32[]{:S(2)}, u32[]{:S(2)}) async-start(f32[16,4,8,128]{3,2,1,0:T(8,128)} %broadcast_in_dim.38), calls=%async_computation.1 | async-start | bytes 524288 | tf_op jit(solution)/shard_map/all_to_all | solution.py:564
  109.5 6.3 %collective-permute-start.9 = (f32[1,10,32,128]{3,2,1,0:T(8,128)S(1)}, f32[1,10,32,128]{3,2,1,0:T(8,128)S(1)}, u32[]{:S(2)}, u32[]{:S(2)}) collective-permute-start(f32[1,10,32,128]{3,2,1,0:T(8,128)S(1)} %get-tuple-element.46), channel_id=1, source_target_pairs={{0,240},{16,0},{32,16},{48,32},{64,48},{80,64},{96,80},{112,96},{1... | collective-permute-start | bytes 491528 | tf_op jit(solution)/shard_map/ppermute | solution.py:559
  110.9 9.2 %collective-permute-start.8 = (f32[1,10,32,128]{3,2,1,0:T(8,128)S(1)}, f32[1,10,32,128]{3,2,1,0:T(8,128)S(1)}, u32[]{:S(2)}, u32[]{:S(2)}) collective-permute-start(f32[1,10,32,128]{3,2,1,0:T(8,128)S(1)} %get-tuple-element.47), channel_id=1, source_target_pairs={{0,16},{16,32},{32,48},{48,64},{64,80},{80,96},{96,112},{112,128},... | collective-permute-start | bytes 491528 | tf_op jit(solution)/shard_map/ppermute | solution.py:559
  115.8 5.5 %copy-start.9 = (f32[1,10,32,128]{3,2,1,0:T(8,128)}, f32[1,10,32,128]{3,2,1,0:T(8,128)S(1)}, u32[]{:S(2)}) copy-start(f32[1,10,32,128]{3,2,1,0:T(8,128)S(1)} %collective-permute-done.9.right) | copy-start | bytes 491524
  120.2 1.1 copy-start.10
  121.3 6.5 %collective-permute-start.11 = (f32[1,36,10,128]{3,2,1,0:T(8,128)S(1)}, f32[1,36,10,128]{3,2,1,0:T(8,128)S(1)}, u32[]{:S(2)}, u32[]{:S(2)}) collective-permute-start(f32[1,36,10,128]{3,2,1,0:T(8,128)S(1)} %get-tuple-element.40), channel_id=1, source_target_pairs={{0,15},{1,0},{2,1},{3,2},{4,3},{5,4},{6,5},{7,6},{8,7},{9,8},{10,9... | collective-permute-start | bytes 552968 | tf_op jit(solution)/shard_map/ppermute | solution.py:559
  122.0 5.7 %collective-permute-start.10 = (f32[1,36,10,128]{3,2,1,0:T(8,128)S(1)}, f32[1,36,10,128]{3,2,1,0:T(8,128)S(1)}, u32[]{:S(2)}, u32[]{:S(2)}) collective-permute-start(f32[1,36,10,128]{3,2,1,0:T(8,128)S(1)} %get-tuple-element.41), channel_id=1, source_target_pairs={{0,1},{1,2},{2,3},{3,4},{4,5},{5,6},{6,7},{7,8},{8,9},{9,10},{10,1... | collective-permute-start | bytes 552968 | tf_op jit(solution)/shard_map/ppermute | solution.py:559
  127.8 0.7 copy-start.14
  127.8 0.8 copy-start.15
  138.4 9.6 %collective-permute-start.12 = (f32[2,4,16,128]{3,2,1,0:T(8,128)}, f32[2,4,16,128]{3,2,1,0:T(8,128)S(1)}, u32[]{:S(2)}, u32[]{:S(2)}) collective-permute-start(f32[2,4,16,128]{3,2,1,0:T(8,128)} %get-tuple-element.30.one), channel_id=1, source_target_pairs={{0,16},{16,32},{32,48},{48,64},{64,80},{80,96},{96,112},{112,128},... | collective-permute-start | bytes 196616 | tf_op jit(solution)/shard_map/ppermute | solution.py:559
  138.4 10.5 %collective-permute-start.13 = (f32[2,4,16,128]{3,2,1,0:T(8,128)}, f32[2,4,16,128]{3,2,1,0:T(8,128)S(1)}, u32[]{:S(2)}, u32[]{:S(2)}) collective-permute-start(f32[2,4,16,128]{3,2,1,0:T(8,128)} %get-tuple-element.30.one), channel_id=1, source_target_pairs={{0,240},{16,0},{32,16},{48,32},{64,48},{80,64},{96,80},{112,96},{1... | collective-permute-start | bytes 196616 | tf_op jit(solution)/shard_map/ppermute | solution.py:559
  144.5 10.0 %all-to-all-start.2 = ((f32[16,1,8,128]{3,2,1,0:T(8,128)}), f32[16,1,8,128]{3,2,1,0:T(8,128)S(1)}, u32[]{:S(2)}, u32[]{:S(2)}) async-start(f32[16,1,8,128]{3,2,1,0:T(8,128)} %broadcast_in_dim.41), calls=%async_computation.2 | async-start | bytes 131072 | tf_op jit(solution)/shard_map/all_to_all | solution.py:564
  148.0 32.8 %copy-start.16 = (f32[2,4,16,128]{3,2,1,0:T(8,128)}, f32[2,4,16,128]{3,2,1,0:T(8,128)S(1)}, u32[]{:S(2)}) copy-start(f32[2,4,16,128]{3,2,1,0:T(8,128)S(1)} %collective-permute-done.12.left) | copy-start | bytes 196612
  148.9 32.0 %copy-start.17 = (f32[2,4,16,128]{3,2,1,0:T(8,128)}, f32[2,4,16,128]{3,2,1,0:T(8,128)S(1)}, u32[]{:S(2)}) copy-start(f32[2,4,16,128]{3,2,1,0:T(8,128)S(1)} %collective-permute-done.13.right) | copy-start | bytes 196612
  154.5 6.1 %copy-start.11 = (f32[16,1,8,128]{3,2,1,0:T(8,128)}, f32[16,1,8,128]{3,2,1,0:T(8,128)S(1)}, u32[]{:S(2)}) copy-start(f32[16,1,8,128]{3,2,1,0:T(8,128)S(1)} %all-to-all-done.2) | copy-start | bytes 196612
  154.5 6.1 %collective-permute-start.15 = (f32[40,8,128]{2,1,0:T(8,128)S(1)}, f32[40,8,128]{2,1,0:T(8,128)S(1)}, u32[]{:S(2)}, u32[]{:S(2)}) collective-permute-start(f32[40,8,128]{2,1,0:T(8,128)S(1)} %get-tuple-element.54), channel_id=1, source_target_pairs={{0,15},{1,0},{2,1},{3,2},{4,3},{5,4},{6,5},{7,6},{8,7},{9,8},{10,9... | collective-permute-start | bytes 491528 | tf_op jit(solution)/shard_map/ppermute | solution.py:559
  157.8 2.8 %collective-permute-start.14 = (f32[40,8,128]{2,1,0:T(8,128)S(1)}, f32[40,8,128]{2,1,0:T(8,128)S(1)}, u32[]{:S(2)}, u32[]{:S(2)}) collective-permute-start(f32[40,8,128]{2,1,0:T(8,128)S(1)} %get-tuple-element.55), channel_id=1, source_target_pairs={{0,1},{1,2},{2,3},{3,4},{4,5},{5,6},{6,7},{7,8},{8,9},{9,10},{10,1... | collective-permute-start | bytes 491528 | tf_op jit(solution)/shard_map/ppermute | solution.py:559
  160.6 0.6 copy-start.7
  160.6 0.7 copy-start.8

commit v2 on v1

v2 whole, which is shorter than its diff:
```python
import functools

import jax
import jax.numpy as jnp
import numpy as np
from jax import lax
from jax.experimental import pallas as pl
from jax.experimental.pallas import tpu as pltpu
from jax.sharding import PartitionSpec as P

SIGMA = 0.02
F32 = jnp.float32
BF16 = jnp.bfloat16
TX, TY = 16, 32
HX = 10
HY = 12
PX, RY = TX + 2 * HX, TY + 2 * HY
UX, UR = TX + 16, TY + 16
CHUNK = 4
VMEM_BYTES = 56 * 1024 * 1024


def cheb_steps(degree, lower):
    centre = 0.5 * (2.0 + lower)
    half = 0.5 * (2.0 - lower)
    sharp = centre / half
    ratio = 1.0 / sharp
    steps = []
    for _ in range(degree - 1):
        nxt = 1.0 / (2.0 * sharp - ratio)
        steps.append((nxt * ratio, 2.0 * nxt / half))
        ratio = nxt
    return 1.0 / centre, steps


SMOOTH = cheb_steps(3, 0.3)
COARSE = cheb_steps(24, 0.05)


def lane_map(z):
    groups = 128 // z
    out = np.zeros((4, 128, 128), np.float32)
    for q in range(4):
        for lane in range(128):
            cell = (lane // z + groups * q) // 2
            out[q, lane, cell * (z // 2) + (lane % z) // 2] = 1.0
    return out


def restrict_map(z):
    return jnp.asarray(lane_map(z).reshape(512, 128), BF16)


def prolong_map(z):
    return jnp.asarray(np.concatenate([m.T for m in lane_map(z)], axis=1), BF16)


def pair_dot(value, matrix):
    high = value.astype(BF16)
    rest = value - high.astype(F32)
    mid = rest.astype(BF16)
    low = (rest - mid.astype(F32)).astype(BF16)
    dot = functools.partial(jnp.dot, preferred_element_type=F32)
    return dot(high, matrix) + (dot(mid, matrix) + dot(low, matrix))


def lanes(shape):
    return lax.broadcasted_iota(jnp.int32, shape, len(shape) - 1)


def turn(value, shift, axis):
    return pltpu.roll(value, shift % value.shape[axis], axis)


def next_x(v, z):
    if z == 128:
        return jnp.concatenate([v[1:], v[:1]], axis=0)
    a = turn(v, -z, 2)
    b = jnp.concatenate([a[1:], a[:1]], axis=0)
    return jnp.where(lanes(v.shape) < 128 - z, a, b)


def prev_x(v, z):
    if z == 128:
        return jnp.concatenate([v[-1:], v[:-1]], axis=0)
    a = turn(v, z, 2)
    b = jnp.concatenate([a[-1:], a[:-1]], axis=0)
    return jnp.where(lanes(v.shape) >= z, a, b)


def faces_of(k, step, scale, low, high):
    own = (0.5 * scale) * k
    both = own + (0.5 * scale) * step
    if low is None:
        return both, None
    edge = jnp.where(low | high, own, 0.0)
    return jnp.where(high, 0.0, both), edge


def build(k, scale, z, inside=None, edge_x=(None, None), edge_y=(None, None)):
    shape = k.shape
    cell = lanes(shape) & (z - 1)
    wx, ex = faces_of(k, next_x(k, z), scale, *edge_x)
    wy, ey = faces_of(k, turn(k, -1, 1), scale, *edge_y)
    wz, ez = faces_of(k, turn(k, -1, 2), scale, cell == 0, cell == z - 1)
    s = ez + SIGMA * scale
    if ex is not None:
        s = s + ex
    if ey is not None:
        s = s + ey
    diagonal = s + wx + prev_x(wx, z) + wy + turn(wy, 1, 1) + wz + turn(wz, 1, 2)
    rd = 1.0 / diagonal
    if inside is not None:
        rd = jnp.where(inside, rd, 0.0)
    return wx, wy, wz, s, rd


def remain(v, b, level, z):
    wx, wy, wz, s, _ = level
    fx = wx * (next_x(v, z) - v)
    fy = wy * (turn(v, -1, 1) - v)
    fz = wz * (turn(v, -1, 2) - v)
    total = (fx - prev_x(fx, z)) + (fy - turn(fy, 1, 1)) + (fz - turn(fz, 1, 2))
    return (b - s * v) + total


def smooth(x, b, level, z):
    first, steps = SMOOTH
    rd = level[4]
    if x is None:
        d = (b * rd) * first
        x = d
    else:
        d = (remain(x, b, level, z) * rd) * first
        x = x + d
    for keep, gain in steps:
        d = keep * d + gain * (remain(x, b, level, z) * rd)
        x = x + d
    return x


def within(shape, first_x, first_y, z, size_x, size_y):
    plane = lax.broadcasted_iota(jnp.int32, shape, 0)
    cx = first_x + plane * (128 // z) + lanes(shape) // z
    cy = first_y + lax.broadcasted_iota(jnp.int32, shape, 1)
    return (cx >= 0) & (cx < size_x) & (cy >= 0) & (cy < size_y)


def pair_rows(ref, plane, start, count):
    return ref[plane, pl.ds(start, count, stride=2), :] + ref[plane, pl.ds(start + 1, count, stride=2), :]


def spread_rows(ref, plane, start, value):
    count = value.shape[0]
    ref[plane, pl.ds(start, count, stride=2), :] = value
    ref[plane, pl.ds(start + 1, count, stride=2), :] = value


def insider(rows, first_x, first_y):
    row = lax.broadcasted_iota(jnp.int32, (CHUNK, rows, 128), 1) + first_y
    row_in = (row >= 0) & (row < 512)
    plane = lax.broadcasted_iota(jnp.int32, (CHUNK, rows, 128), 0) + first_x
    return lambda p: row_in & (plane >= -p) & (plane < 256 - p)


def build_top(k_ref, wx, wy, wz, s, rd, low, high, inside_at, body):
    rows = k_ref.shape[1]
    shape = (CHUNK, rows, 128)
    lane = lanes(shape)

    def step(i, wxp):
        p = low + i * CHUNK
        k = k_ref[pl.ds(p, CHUNK)]
        kn = jnp.concatenate([k[1:], k_ref[pl.ds(jnp.minimum(p + CHUNK, k_ref.shape[0] - 1), 1)]], axis=0)
        own = 0.5 * k
        fx = 0.5 * kn + own
        fy = turn(own, -1, 1) + own
        fz = jnp.where(lane == 127, 0.0, turn(own, -1, 2) + own)
        sv = SIGMA + jnp.where((lane == 0) | (lane == 127), own, 0.0)
        fxp = jnp.concatenate([wxp, fx[:-1]], axis=0)
        diagonal = sv + (fx + fxp) + (fy + turn(fy, 1, 1)) + (fz + turn(fz, 1, 2))
        rdv = jnp.where(inside_at(p), 1.0 / diagonal, 0.0)
        at = pl.ds(p, CHUNK)
        wx[at], wy[at], wz[at], s[at], rd[at] = fx, fy, fz, sv, rdv
        body(p, rdv)
        return fx[-1:]

    assert (high - low) % CHUNK == 0
    lax.fori_loop(0, (high - low) // CHUNK, step, jnp.zeros((1, rows, 128), F32))


def sweep_top(x, wx, wy, wz, s, low, high, body):
    fx0 = wx[low - 1 : low] * (x[low : low + 1] - x[low - 1 : low])

    def step(i, fxp):
        p = low + i * CHUNK
        at = pl.ds(p, CHUNK)
        v = x[at]
        vn = jnp.concatenate([v[1:], x[pl.ds(p + CHUNK, 1)]], axis=0)
        fx = wx[at] * (vn - v)
        fy = wy[at] * (turn(v, -1, 1) - v)
        fz = wz[at] * (turn(v, -1, 2) - v)
        fxp = jnp.concatenate([fxp, fx[:-1]], axis=0)
        total = (fx - fxp) + (fy - turn(fy, 1, 1)) + (fz - turn(fz, 1, 2))
        body(p, at, v, s[at] * v - total)
        return fx[-1:]

    assert (high - low) % CHUNK == 0
    lax.fori_loop(0, (high - low) // CHUNK, step, fx0)


def fill_top(dst, tile, left, right, below, above):
    dst[:, 0:2, :] = jnp.zeros((PX, 2, 128), F32)
    dst[:, RY - 2 : RY, :] = jnp.zeros((PX, 2, 128), F32)
    dst[0:HX, HY : HY + TY, :] = left
    dst[HX : HX + TX, HY : HY + TY, :] = tile
    dst[HX + TX :, HY : HY + TY, :] = right
    dst[:, 2:HY, :] = below
    dst[:, HY + TY : RY - 2, :] = above


def down_kernel(pos, tile, left, right, below, above, ktile, r0, r1, xup, bup, kup, one, two, *scratch):
    bx, kx, wx, wy, wz, s, rd, d, x, rs, b1s, x1s, k1s = scratch
    gx, gy = pos[0], pos[1]
    inside_at = insider(RY, gx * TX - HX, gy * TY - HY)
    fill_top(bx, tile[...], left[0], right[0], below[0], above[0])
    fill_top(kx, ktile[...], left[1], right[1], below[1], above[1])

    def clear(i, _):
        at = pl.ds(i * CHUNK, CHUNK)
        kx[at] = jnp.where(inside_at(i * CHUNK), kx[at], 0.0)
        return 0

    lax.fori_loop(0, PX // CHUNK, clear, 0)
    start, steps = SMOOTH

    def begin(p, rdv):
        at = pl.ds(p, CHUNK)
        v = (bx[at] * rdv) * start
        d[at] = v
        x[at] = v

    build_top(kx, wx, wy, wz, s, rd, 0, PX, inside_at, begin)
    for keep, gain in steps:
        sweep_top(x, wx, wy, wz, s, 2, PX - 2, advance_top(keep, gain, bx, 0, rd, d, x))

    def residual(p, at, v, av):
        d[at] = bx[at] - av

    sweep_top(x, wx, wy, wz, s, 4, PX - 4, residual)
    region = (slice(2, 2 + UX), slice(4, 4 + UR))
    xup[...] = x[region]
    bup[...] = bx[region]
    kup[...] = kx[region]

    def coarse(src):
        for c in range(16):
            rs[c] = src[2 + 2 * c] + src[3 + 2 * c]
        return pair_planes(rs, 8, 4, 24, r0)

    for p in (2, 3, PX - 4, PX - 3):
        d[p] = jnp.zeros((RY, 128), F32)
    b1 = coarse(d)
    k1 = coarse(kx)
    level = build(k1, 0.25, 64, within(k1.shape, gx * 8 - 4, gy * 16 - 4, 64, 128, 256))
    x1 = smooth(None, b1, level, 64)
    b1s[...] = b1
    x1s[...] = x1
    k1s[...] = k1
    for number, src in enumerate((b1s, x1s, k1s)):
        one[number] = src[2:6, 4:20, :]
    b1s[...] = remain(x1, b1, level, 64)
    send_all(two, coarse_tile((b1s, k1s), 2, 4, r1))


def pair_planes(rs, planes, start, rows, r0):
    flat = [
        jnp.concatenate([pair_rows(rs, 2 * c, start, rows), pair_rows(rs, 2 * c + 1, start, rows)], axis=1)
        for c in range(planes)
    ]
    return (0.125 * pair_dot(jnp.concatenate(flat, axis=0), r0[...])).reshape(planes, rows, 128)


def coarse_tile(sources, plane, row, r1):
    flat = [
        jnp.concatenate([pair_rows(src, plane + q, row, 8) for q in range(4)], axis=1) for src in sources
    ]
    out = 0.125 * pair_dot(jnp.concatenate(flat, axis=0), r1[...])
    return out.reshape(len(sources), 8, 128)


def send_all(out, value):
    for g in range(16):
        out[g] = value


def advance_top(keep, gain, b, shift_b, rd, d, x):
    def advance(p, at, v, av):
        dv = keep * d[at] + gain * ((b[pl.ds(p - shift_b, CHUNK)] - av) * rd[at])
        d[at] = dv
        x[at] = v + dv

    return advance


def open_top(b, shift_b, rd, d, x):
    def advance(p, at, v, av):
        dv = ((b[pl.ds(p - shift_b, CHUNK)] - av) * rd[at]) * SMOOTH[0]
        d[at] = dv
        x[at] = v + dv

    return advance


def call(kernel, outs, scratch, *args, flops=1e7):
    specs = [pl.BlockSpec(memory_space=pltpu.SMEM)]
    specs += [pl.BlockSpec(memory_space=pltpu.VMEM)] * (len(args) - 1)
    return pl.pallas_call(
        kernel,
        out_shape=[jax.ShapeDtypeStruct(o, F32) for o in outs],
        in_specs=specs,
        out_specs=[pl.BlockSpec(memory_space=pltpu.VMEM)] * len(outs),
        scratch_shapes=[pltpu.VMEM(o, F32) for o in scratch],
        compiler_params=pltpu.CompilerParams(vmem_limit_bytes=VMEM_BYTES),
        cost_estimate=pl.CostEstimate(flops=int(flops), bytes_accessed=8 << 20, transcendentals=0),
    )(*args)


def go_down(*args):
    top, up = (PX, RY, 128), (UX, UR, 128)
    outs = [up, up, up, (3, 4, 16, 128), (16, 2, 8, 128)]
    scratch = [top] * 9 + [(16, RY, 128)] + [(8, 24, 128)] * 3
    return call(down_kernel, outs, scratch, *args)


def one_kernel(pos, mid, left, right, below, above, k1, r1, bout, xout, two, res):
    gx, gy = pos[0], pos[1]
    fill_one(bout, left[:, 0:16], mid[...], right[:, 0:16], below[...], above[...])
    b = bout[...]
    inside = within(b.shape, gx * 8 - 8, gy * 16 - 8, 64, 128, 256)
    level = build(k1[...], 0.25, 64, inside)
    x = smooth(None, b, level, 64)
    xout[...] = x
    res[...] = remain(x, b, level, 64)
    send_all(two, coarse_tile((res,), 4, 8, r1))


def fill_one(dst, left, tile, right, below, above):
    dst[0:4, 8:24, :] = left
    dst[4:8, 8:24, :] = tile
    dst[8:12, 8:24, :] = right
    dst[:, 0:8, :] = below
    dst[:, 24:32, :] = above


def go_one(*args):
    wide = (12, 32, 128)
    return call(one_kernel, [wide, wide, (16, 1, 8, 128)], [wide], *args)


def mid_kernel(first, pos, mid, below, above, *refs):
    if first:
        r2, near, three, k2, x2 = refs[:5]
        scratch = refs[5:]
    else:
        k2, r2, near, three = refs[:4]
        scratch = refs[4:]
    hold, rs, cs = scratch
    gx, gy = pos[0], pos[1]
    shape = (16, 24, 128)
    inside = within(shape, 0, gy * 8 - 8, 32, 64, 128)

    def rows(dst, number):
        part = slice(16 * number, 16 * number + 16)
        dst[:, 0:8, :] = below[part]
        dst[:, 8:16, :] = mid[:, number]
        dst[:, 16:24, :] = above[part]

    rows(rs, 0)
    b = rs[...]
    if first:
        rows(k2, 1)
        k2[...] = jnp.where(inside, k2[...], 0.0)
    k = k2[...]
    plane = lax.broadcasted_iota(jnp.int32, shape, 0)
    lane = lanes(shape)
    edge_x = ((plane == 0) & (lane < 32), (plane == 15) & (lane >= 96))
    level = build(k, 0.25**2, 32, inside, edge_x)
    x = smooth(None, b, level, 32)
    rs[...] = remain(x, b, level, 32)
    for number, value in enumerate((b, x) + level):
        hold[number] = value
    for i in range(5):
        at = gx - 2 + i
        ok = (at >= 0) & (at < 16)
        from_plane = jnp.clip(at, 0, 15)
        for number in range(7):
            near[number, i] = jnp.where(ok, hold[number, from_plane], 0.0)

    if first:
        x2[...] = near[1, :, 8:16, :]

    def coarse(src, out):
        flat = [
            jnp.concatenate([pair_rows(src, 4 * c + q, 4, 8) for q in range(4)], axis=1) for c in range(4)
        ]
        cs[...] = (0.125 * pair_dot(jnp.concatenate(flat, axis=0), r2[...])).reshape(4, 8, 128)
        for c in range(4):
            part = cs[c, 2:6, :]
            for g in range(16):
                three[g, out + c // 2, 4 * (c % 2) : 4 * (c % 2) + 4, :] = part

    coarse(rs, 0)
    if first:
        coarse(k2, 2)


def go_mid(first, pos, mid, below, above, k2, r2):
    outs = [(7, 5, 24, 128), (16, 4 if first else 2, 8, 128)]
    outs += [(16, 24, 128), (5, 8, 128)] if first else []
    scratch = [(7, 16, 24, 128), (16, 24, 128), (4, 8, 128)]
    args = (mid, below, above) + (() if first else (k2,)) + (r2,)
    return call(functools.partial(mid_kernel, first), outs, scratch, pos, *args)


def solve_last(b, k, owned):
    shape = k.shape
    scale = 0.25**4
    lane = lanes(shape)
    row = lax.broadcasted_iota(jnp.int32, shape, 0)
    moves = (
        (8, 1, lane < 8, True),
        (-8, 1, lane >= 120, True),
        (1, 0, row == 0, True),
        (-1, 0, row == 31, True),
        (1, 1, (lane & 7) == 0, False),
        (-1, 1, (lane & 7) == 7, False),
    )
    diagonal = jnp.full(shape, SIGMA * scale, F32)
    pulls = []
    for shift, axis, edge, masked in moves:
        weight = (0.5 * scale) * (k + jnp.where(edge, 0.0, turn(k, shift, axis)))
        diagonal = diagonal + weight
        keep = jnp.where(edge, 0.0, weight)
        if masked:
            keep = jnp.where(owned == turn(owned, shift, axis), keep, 0.0)
        pulls.append(keep)
    rd = 1.0 / diagonal
    pulls = [keep * rd for keep in pulls]
    g = b * rd
    first, steps = COARSE
    d = g * first
    x = d
    for keep, gain in steps:
        total = [pull * turn(x, move[0], move[1]) for pull, move in zip(pulls, moves)]
        near = (total[0] + total[1]) + (total[2] + total[3]) + (total[4] + total[5])
        d = keep * d + gain * ((g - x) + near)
        x = x + d
    return x


def fill_three(dst, gathered, first):
    for g in range(16):
        for c in range(4):
            part = gathered[g, first + c // 2, 4 * (c % 2) : 4 * (c % 2) + 4, :]
            dst[c, 4 * g : 4 * g + 4, :] = part


def solve_three(b_ref, k_ref, owned, s3, r3, t3):
    shape = (4, 64, 128)
    plane = lax.broadcasted_iota(jnp.int32, shape, 0)
    row = lax.broadcasted_iota(jnp.int32, shape, 1)
    lane = lanes(shape)
    edge_x = ((plane == 0) & (lane < 16), (plane == 3) & (lane >= 112))
    level = build(k_ref[...], 0.25**3, 16, None, edge_x, (row == 0, row == 63))
    b = b_ref[...]
    x = smooth(None, b, level, 16)
    s3[...] = remain(x, b, level, 16)
    flat = [
        jnp.concatenate([pair_rows(src, q, 0, 32) for q in range(4)], axis=1) for src in (s3, k_ref)
    ]
    fine = 0.125 * pair_dot(jnp.concatenate(flat, axis=0), r3[...])
    last = solve_last(fine[:32], fine[32:], owned[...])
    back = pair_dot(last, t3[...])
    for q in range(4):
        spread_rows(s3, q, 0, back[:, 128 * q : 128 * q + 128])
    s3[...] = smooth(x + s3[...], b, level, 16)


def rise_two(gx, gy, near, x2, s3, t2, e2, s2):
    for i in range(5):
        at = jnp.clip(gx - 2 + i, 0, 15)
        spread_rows(e2, i, 8, pair_dot(s3[at // 4], t2[at % 4]))
    e = e2[:, pl.ds(pl.multiple_of(gy * 8, 8), 24), :]
    level = tuple(near[number] for number in range(2, 7))
    x = jnp.where(level[4] > 0.0, x2 + e, 0.0)
    s2[...] = smooth(x, near[0], level, 32)


def rise_one(x1, b1, k1, inside, s2, t1, s1):
    flat = jnp.concatenate([s2[i, 4:20, :] for i in range(1, 4)], axis=0)
    back = pair_dot(flat, t1[...])
    for i in range(3):
        for q in range(4):
            spread_rows(s1, 4 * i + q, 0, back[16 * i : 16 * i + 16, 128 * q : 128 * q + 128])
    level = build(k1, 0.25, 64, inside)
    s1[...] = smooth(jnp.where(inside, x1 + s1[...], 0.0), b1, level, 64)


def spread_one(s1, low, high, t0, e0):
    flat = jnp.concatenate([s1[i, 4:28, :] for i in range(low, high)], axis=0)
    back = pair_dot(flat, t0[...])
    for i in range(high - low):
        for q in range(2):
            part = back[24 * i : 24 * i + 24, 128 * q : 128 * q + 128]
            spread_rows(e0, 2 * (low - 2 + i) + q, 0, part)


def add_top(x0, e0, x):
    def begin(p, rdv):
        c = p // 2
        pair = (e0[pl.ds(c, 1)], e0[pl.ds(c + 1, 1)])
        correction = jnp.concatenate([pair[0], pair[0], pair[1], pair[1]], axis=0)
        at = pl.ds(p, CHUNK)
        x[at] = jnp.where(rdv > 0.0, x0[at] + correction, 0.0)

    return begin


def turn_kernel(
    pos, owned, three, near, x2low, x2high, one, left, right, below, above, x0, b0, k0, r0, r3, t3, t2, t1, t0,
    k3, k1, xout, rout, x0n, b1n, east, west,
    b3, s3, e2, s2, x2s, b1s, s1, e0, wx, wy, wz, s, rd, d, x, rs
):
    gx, gy = pos[0], pos[1]
    fill_three(b3, three, 0)
    fill_three(k3, three, 2)
    solve_three(b3, k3, owned, s3, r3, t3)
    x2s[:, 0:8, :] = x2low[...]
    x2s[:, 8:16, :] = near[1, :, 8:16, :]
    x2s[:, 16:24, :] = x2high[...]
    rise_two(gx, gy, near, x2s[...], s3, t2, e2, s2)

    inside = within((12, 32, 128), gx * 8 - 8, gy * 16 - 8, 64, 128, 256)
    for number, dst in enumerate((b1s, s1, k1)):
        part = slice(32 + 12 * number, 44 + 12 * number)
        fill_one(dst, left[number], one[number], right[number], below[part], above[part])
    k1[...] = jnp.where(inside, k1[...], 0.0)
    rise_one(s1[...], b1s[...], k1[...], inside, s2, t1, s1)

    spread_one(s1, 2, 10, t0, e0)
    inside_at = insider(UR, gx * TX - 8, gy * TY - 8)
    build_top(k0, wx, wy, wz, s, rd, 0, UX, inside_at, add_top(x0, e0, x))
    start, steps = SMOOTH
    sweep_top(x, wx, wy, wz, s, 2, UX - 2, open_top(b0, 0, rd, d, x))
    for (keep, gain), edge in zip(steps, (2, 4)):
        sweep_top(x, wx, wy, wz, s, edge, UX - edge, advance_top(keep, gain, b0, 0, rd, d, x))

    def residual(p, at, v, av):
        rout[pl.ds(p - 4, CHUNK)] = b0[at] - av

    sweep_top(x, wx, wy, wz, s, 4, UX - 4, residual)
    xout[...] = x[7 : UX - 7]

    def begin(i, _):
        at = pl.ds(4 + i * CHUNK, CHUNK)
        v = (rout[pl.ds(i * CHUNK, CHUNK)] * rd[at]) * start
        d[at] = v
        x[at] = v
        return 0

    lax.fori_loop(0, (UX - 8) // CHUNK, begin, 0)
    for keep, gain in steps:
        sweep_top(x, wx, wy, wz, s, 6, UX - 6, advance_top(keep, gain, rout, 4, rd, d, x))

    def again(p, at, v, av):
        d[at] = rout[pl.ds(p - 4, CHUNK)] - av

    sweep_top(x, wx, wy, wz, s, 8, UX - 8, again)
    x0n[...] = x[8:24, 8:40, :]
    for c in range(8):
        rs[c] = d[8 + 2 * c] + d[9 + 2 * c]
    b1 = pair_planes(rs, 4, 8, 16, r0)
    b1n[...] = b1
    for side, plane in ((east, 20), (west, 8)):
        side[:, 0:16, :] = b1
        side[:, 16:48, :] = x[plane : plane + 4, 8:40, :]


def go_turn(*args):
    up, wide = (UX, UR, 128), (12, 32, 128)
    outs = [(4, 64, 128), wide, (TX + 2, UR, 128), (TX + 8, UR, 128), (TX, TY, 128), (4, 16, 128)]
    outs += [(4, 48, 128)] * 2
    scratch = [(4, 64, 128)] * 2 + [(5, 144, 128), (5, 24, 128), (5, 24, 128), wide, wide, (16, UR, 128)]
    return call(turn_kernel, outs, scratch + [up] * 7 + [(8, UR, 128)], *args)


def last_kernel(
    pos, owned, three, k3, near, b1, x1, k1, x0n, left, right, below, above, r, k0, xbefore, borig,
    r3, t3, t2, t1, t0, xout, rout,
    b3, s3, e2, s2, s1, e0, wx, wy, wz, s, rd, d, x
):
    gx, gy = pos[0], pos[1]
    fill_three(b3, three, 0)
    solve_three(b3, k3, owned, s3, r3, t3)
    rise_two(gx, gy, near, near[1], s3, t2, e2, s2)
    inside = within((12, 32, 128), gx * 8 - 8, gy * 16 - 8, 64, 128, 256)
    rise_one(x1[...], b1[...], k1[...], inside, s2, t1, s1)

    spread_one(s1, 3, 9, t0, e0)
    x[4:8, 8:40, :] = left[:, 16:48, :]
    x[8:24, 8:40, :] = x0n[...]
    x[24:28, 8:40, :] = right[:, 16:48, :]
    x[4:28, 0:8, :] = below[16:40]
    x[4:28, 40:48, :] = above[16:40]
    inside_at = insider(UR, gx * TX - 8, gy * TY - 8)
    build_top(k0, wx, wy, wz, s, rd, 4, UX - 4, inside_at, add_top(x, e0, x))
    sweep_top(x, wx, wy, wz, s, 4, UX - 4, open_top(r, 4, rd, d, x))
    for keep, gain in SMOOTH[1]:
        sweep_top(x, wx, wy, wz, s, 6, UX - 6, advance_top(keep, gain, r, 4, rd, d, x))
    x[7 : UX - 7] = x[7 : UX - 7] + xbefore[...]

    def residual(p, at, v, av):
        out = pl.ds(p - 8, CHUNK)
        xout[out] = v[:, 8 : 8 + TY]
        rout[out] = borig[out] - av[:, 8 : 8 + TY]

    sweep_top(x, wx, wy, wz, s, 8, UX - 8, residual)


def go_last(*args):
    up, wide, tile = (UX, UR, 128), (12, 32, 128), (TX, TY, 128)
    scratch = [(4, 64, 128)] * 2 + [(5, 144, 128), (5, 24, 128), wide, (16, UR, 128)]
    return call(last_kernel, [tile, tile], scratch + [up] * 7, *args)


def shift(value, axis, step):
    count = lax.axis_size(axis)
    return lax.ppermute(value, axis, [(i, (i + step) % count) for i in range(count)])


def gather(copies, axis):
    return lax.all_to_all(copies, axis, 0, 0, tiled=True)


def local(right_side, kappa, owners):
    pos = jnp.stack([lax.axis_index("gx"), lax.axis_index("gy")]).astype(jnp.int32)
    owned = jnp.repeat(jnp.repeat(owners.T, 2, 0), 8, 1).astype(F32)
    r0 = restrict_map(128)[128:384]
    r1, r2, r3 = restrict_map(64), restrict_map(32), restrict_map(16)
    t0 = prolong_map(128)[:, 128:384]
    t1, t3 = prolong_map(64), prolong_map(16)
    t2 = jnp.asarray(np.transpose(lane_map(32), (0, 2, 1)), BF16)

    mid = jnp.stack([right_side, kappa])
    left = shift(mid[:, TX - HX :], "gx", 1)
    right = shift(mid[:, :HX], "gx", -1)
    wide = jnp.concatenate([left, mid, right], axis=1)
    below = shift(wide[:, :, TY - HX :], "gy", 1)
    above = shift(wide[:, :, :HX], "gy", -1)
    xup, bup, kup, one, two = go_down(pos, right_side, left, right, below, above, kappa, r0, r1)
    left = shift(one, "gx", 1)
    right = shift(one, "gx", -1)
    two = gather(two, "gx")
    rows = jnp.swapaxes(two, 0, 1).reshape(-1, 8, 128)
    wide = jnp.concatenate([left, one, right], axis=1)
    below = shift(jnp.concatenate([rows, wide[:, :, 8:].reshape(-1, 8, 128)]), "gy", 1)
    above = shift(jnp.concatenate([rows, wide[:, :, :8].reshape(-1, 8, 128)]), "gy", -1)
    near, three, k2, x2 = go_mid(True, pos, two, below, above, None, r2)
    x2low = shift(x2, "gy", 1)
    x2high = shift(x2, "gy", -1)
    three = gather(three, "gy")
    k3, k1, xbefore, source, x0n, b1n, east, west = go_turn(
        pos, owned, three, near, x2low, x2high, one, left, right, below, above, xup, bup, kup, r0, r3, t3, t2, t1, t0
    )

    left = shift(east, "gx", 1)
    right = shift(west, "gx", -1)
    wide = jnp.concatenate([left[:, :16], b1n, right[:, :16]])
    below = shift(wide[:, 8:], "gy", 1)
    above = shift(wide[:, :8], "gy", -1)
    b1, x1, two = go_one(pos, b1n, left, right, below, above, k1, r1)
    two = gather(two, "gx")
    wide = jnp.concatenate([left[:, 16:], x0n, right[:, 16:]])
    below = shift(jnp.concatenate([two[:, 0], wide[:, 24:]]), "gy", 1)
    above = shift(jnp.concatenate([two[:, 0], wide[:, :8]]), "gy", -1)
    near, three = go_mid(False, pos, two, below, above, k2, r2)
    three = gather(three, "gy")
    field, residual = go_last(
        pos, owned, three, k3, near, b1, x1, k1, x0n, left, right, below, above, source, kup, xbefore, right_side,
        r3, t3, t2, t1, t0
    )
    return field, residual


def solution(mesh):
    spec = P("gx", "gy", None)
    return jax.shard_map(
        local, mesh=mesh, in_specs=(spec, spec, P()), out_specs=(spec, spec), check_vma=False
    )
```

time: 196 us -> 180 us (0.918)
  waiting for transfers between devices: 59.7 us -> 48.9 us
  local copies, waits for them, and re-layouts: 15.4 us -> 10 us
  starting transfers between devices: 45.8 us -> 49 us
  Pallas kernels: 53.9 us -> 51.6 us
    all_to_all x3, waiting for transfers between devices: 22.1 us -> 13.9 us  [gather(): return lax.all_to_all(copies, axis, 0, 0, tiled=True)]
    broadcast_in_dim x4 -> x0, local copies, waits for them, and re-layouts: 4.82 us -> none  [gather(): jnp.broadcast_to(value[None], (count,) + value.shape)]
    all_to_all x3, starting transfers between devices: 17.6 us -> 20.5 us  [gather(): return lax.all_to_all(copies, axis, 0, 0, tiled=True)]
    ppermute x16, waiting for transfers between devices: 37.7 us -> 35.1 us  [shift(): lax.ppermute(value, axis, [(i, (i + step) % count) for i in range(count)])]
    pallas_call x6, Pallas kernels: 53.9 us -> 51.6 us  [call(): pl.pallas_call(kernel, out_shape=[jax.ShapeDtypeStruct(o, F32) for o in o...]
    unnamed x42 -> x44, local copies, waits for them, and re-layouts: 5.47 us -> 5.06 us
  transfers between devices with their start and end apart: 19 -> 19, of which waited for: 12 -> 12; matrix products, arithmetic and copies ran while one was open for 4% -> 3% of each run, Pallas kernels for 0% -> 0%
where the time goes in v2:
time: 180 us; the launch traced here: 179 us
  Pallas kernels  51.6 us (29%)
  starting transfers between devices  49 us (27%)
  waiting for transfers between devices  48.9 us (27%)
  blocking collectives  16.1 us (9%)
  local copies, waits for them, and re-layouts  10 us (6%)
  other arithmetic  2.8 us (2%)
    pallas_call x6, Pallas kernels, call(): pl.pallas_call(kernel, out_shape=[jax.ShapeDtypeStruct(o, F32) for o in o...  51.6 us
    ppermute x16, waiting for transfers between devices, shift(): lax.ppermute(value, axis, [(i, (i + step) % count) for i in range(count)])  35.1 us
    ppermute x16, starting transfers between devices, shift(): lax.ppermute(value, axis, [(i, (i + step) % count) for i in range(count)])  28.4 us
    all_to_all x3, starting transfers between devices, gather(): return lax.all_to_all(copies, axis, 0, 0, tiled=True)  20.5 us
    all_to_all x1, blocking collectives, gather(): return lax.all_to_all(copies, axis, 0, 0, tiled=True)  16.1 us
    all_to_all x3, waiting for transfers between devices, gather(): return lax.all_to_all(copies, axis, 0, 0, tiled=True)  13.9 us
    unnamed x44, local copies, waits for them, and re-layouts  5.06 us
  transfers between devices with their start and end apart: 19, of which 12 were waited for; matrix products, arithmetic and copies ran while one was open for 3% of the time, Pallas kernels for 0%

profile of v2, /device:TPU:1, one launch (start us, length us, event | category | flops | bytes accessed | tf_op | source)
XLA Modules:
  0.0 179.2 jit_solution(7521683165243869355)
XLA Ops:
  0.7 1.3 pad_maximum_fusion.3
  1.9 5.8 %collective-permute-start.1 = (f32[2,10,32,128]{3,2,1,0:T(8,128)S(1)}, f32[2,10,32,128]{3,2,1,0:T(8,128)S(1)}, u32[]{:S(2)}, u32[]{:S(2)}) collective-permute-start(f32[2,10,32,128]{3,2,1,0:T(8,128)S(1)} %get-tuple-element.48), channel_id=1, source_target_pairs={{0,240},{16,0},{32,16},{48,32},{64,48},{80,64},{96,80},{112,96},{1... | collective-permute-start | bytes 983048 | tf_op jit(solution)/shard_map/ppermute | solution.py:639
  7.7 6.4 %collective-permute-done.1.right = f32[2,10,32,128]{3,2,1,0:T(8,128)S(1)} collective-permute-done((f32[2,10,32,128]{3,2,1,0:T(8,128)S(1)}, f32[2,10,32,128]{3,2,1,0:T(8,128)S(1)}, u32[]{:S(2)}, u32[]{:S(2)}) %collective-permute-start.1) | collective-permute-done | bytes 327712 | tf_op jit(solution)/shard_map/ppermute | solution.py:639
  14.1 5.2 %collective-permute-done.left = f32[2,10,32,128]{3,2,1,0:T(8,128)S(1)} collective-permute-done((f32[2,10,32,128]{3,2,1,0:T(8,128)S(1)}, f32[2,10,32,128]{3,2,1,0:T(8,128)S(1)}, u32[]{:S(2)}, u32[]{:S(2)}) %collective-permute-start) | collective-permute-done | bytes 327712 | tf_op jit(solution)/shard_map/ppermute | solution.py:639
  19.4 0.6 copy-done.3
  20.2 0.3 copy.31
  20.5 3.4 %collective-permute-start.2 = (f32[2,36,10,128]{3,0,2,1:T(2,128)S(1)}, f32[2,36,10,128]{3,0,2,1:T(2,128)S(1)}, u32[]{:S(2)}, u32[]{:S(2)}) collective-permute-start(f32[2,36,10,128]{3,0,2,1:T(2,128)S(1)} %copy.31), channel_id=1, source_target_pairs={{0,1},{1,2},{2,3},{3,4},{4,5},{5,6},{6,7},{7,8},{8,9},{9,10},{10,1... | collective-permute-start | bytes 1105928 | tf_op jit(solution)/shard_map/ppermute | solution.py:639
  23.9 0.3 copy.32
  24.2 0.6 pad_add_fusion.pos
  24.8 3.5 %collective-permute-done.2 = f32[2,36,10,128]{3,0,2,1:T(2,128)S(1)} collective-permute-done((f32[2,36,10,128]{3,0,2,1:T(2,128)S(1)}, f32[2,36,10,128]{3,0,2,1:T(2,128)S(1)}, u32[]{:S(2)}, u32[]{:S(2)}) %collective-permute-start.2) | collective-permute-done | bytes 368672 | tf_op jit(solution)/shard_map/ppermute | solution.py:639
  28.3 0.9 copy.33.below
  29.2 2.1 %collective-permute-done.3 = f32[2,36,10,128]{3,0,2,1:T(2,128)S(1)} collective-permute-done((f32[2,36,10,128]{3,0,2,1:T(2,128)S(1)}, f32[2,36,10,128]{3,0,2,1:T(2,128)S(1)}, u32[]{:S(2)}, u32[]{:S(2)}) %collective-permute-start.3) | collective-permute-done | bytes 368672 | tf_op jit(solution)/shard_map/ppermute | solution.py:639
  31.2 0.9 copy.34.above
  32.1 10.4 %shard_map.122 = (f32[32,48,128]{2,1,0:T(8,128)}, f32[32,48,128]{2,1,0:T(8,128)}, f32[32,48,128]{2,1,0:T(8,128)}, f32[3,4,16,128]{3,2,1,0:T(8,128)}, f32[16,2,8,128]{3,2,1,0:T(8,128)}) custom-call(s32[2]{0:T(128)} %pad_add_fusion.pos, f32[16,32,128]{2,1,0:T(8,128)} %borig.1, f32[2,10,32,128]{3,2,1,0:T(8,128)} %copy-done.3, f32[2,10,32,128]{3,2,1,0:T(8,128)} %copy-done.2, ...), custom_call_target="tpu_custom_call" | custom-call | flops 10000000 | bytes 8388608 | tf_op jit(solution)/shard_map/pallas_call | solution.py:318
  42.5 4.8 %collective-permute-start.5 = (f32[3,4,16,128]{3,2,1,0:T(8,128)}, f32[3,4,16,128]{3,2,1,0:T(8,128)S(1)}, u32[]{:S(2)}, u32[]{:S(2)}) collective-permute-start(f32[3,4,16,128]{3,2,1,0:T(8,128)} %get-tuple-element.25.one), channel_id=1, source_target_pairs={{0,240},{16,0},{32,16},{48,32},{64,48},{80,64},{96,80},{112,96},{1... | collective-permute-start | bytes 294920 | tf_op jit(solution)/shard_map/ppermute | solution.py:639
  47.3 3.5 %all-to-all-start = ((f32[16,2,8,128]{3,2,1,0:T(8,128)}), f32[16,2,8,128]{3,2,1,0:T(8,128)S(1)}, u32[]{:S(2)}, u32[]{:S(2)}) async-start(f32[16,2,8,128]{3,2,1,0:T(8,128)} %get-tuple-element.24), calls=%async_computation | async-start | bytes 262144 | tf_op jit(solution)/shard_map/all_to_all | solution.py:643
  50.9 0.9 constant_dynamic-update-slice_fusion.1
  51.9 5.7 %all-to-all-done.mid = f32[16,2,8,128]{3,2,1,0:T(8,128)S(1)} async-done(((f32[16,2,8,128]{3,2,1,0:T(8,128)}), f32[16,2,8,128]{3,2,1,0:T(8,128)S(1)}, u32[]{:S(2)}, u32[]{:S(2)}) %all-to-all-start) | async-done | bytes 131104 | tf_op jit(solution)/shard_map/all_to_all | solution.py:643
  57.7 2.9 %collective-permute-start.7 = (f32[68,8,128]{2,1,0:T(8,128)S(1)}, f32[68,8,128]{2,1,0:T(8,128)S(1)}, u32[]{:S(2)}, u32[]{:S(2)}) collective-permute-start(f32[68,8,128]{2,1,0:T(8,128)S(1)} %get-tuple-element.54), channel_id=1, source_target_pairs={{0,15},{1,0},{2,1},{3,2},{4,3},{5,4},{6,5},{7,6},{8,7},{9,8},{10,9... | collective-permute-start | bytes 835592 | tf_op jit(solution)/shard_map/ppermute | solution.py:639
  60.6 3.9 %collective-permute-done.7.above = f32[68,8,128]{2,1,0:T(8,128)S(1)} collective-permute-done((f32[68,8,128]{2,1,0:T(8,128)S(1)}, f32[68,8,128]{2,1,0:T(8,128)S(1)}, u32[]{:S(2)}, u32[]{:S(2)}) %collective-permute-start.7) | collective-permute-done | bytes 278560 | tf_op jit(solution)/shard_map/ppermute | solution.py:639
  64.5 0.7 copy-done.5
  65.2 0.7 copy-done.6
  65.9 3.3 %shard_map.123 = (f32[7,5,24,128]{3,2,1,0:T(8,128)}, f32[16,4,8,128]{3,2,1,0:T(8,128)}, f32[16,24,128]{2,1,0:T(8,128)}, f32[5,8,128]{2,1,0:T(8,128)}) custom-call(s32[2]{0:T(128)} %pad_add_fusion.pos, f32[16,2,8,128]{3,2,1,0:T(8,128)} %copy-done.4, f32[68,8,128]{2,1,0:T(8,128)} %copy-done.6, f32[68,8,128]{2,1,0:T(8,128)} %copy-done.5, ...), custom_call_target="tpu_custom_call" | custom-call | flops 10000000 | bytes 8388608 | tf_op jit(solution)/shard_map/pallas_call | solution.py:318
  69.2 10.5 %all-to-all-start.1 = ((f32[16,4,8,128]{3,2,1,0:T(8,128)}), f32[16,4,8,128]{3,2,1,0:T(8,128)S(1)}, u32[]{:S(2)}, u32[]{:S(2)}) async-start(f32[16,4,8,128]{3,2,1,0:T(8,128)} %get-tuple-element.26), calls=%async_computation.1 | async-start | bytes 524288 | tf_op jit(solution)/shard_map/all_to_all | solution.py:643
  80.0 1.6 collective-permute-start.8
  81.7 0.7 copy.37.owned
  82.3 6.1 %collective-permute-done.9.x2high = f32[5,8,128]{2,1,0:T(8,128)S(1)} collective-permute-done((f32[5,8,128]{2,1,0:T(8,128)}, f32[5,8,128]{2,1,0:T(8,128)S(1)}, u32[]{:S(2)}, u32[]{:S(2)}) %collective-permute-start.9) | collective-permute-done | bytes 20512 | tf_op jit(solution)/shard_map/ppermute | solution.py:639
  88.4 3.3 %all-to-all-done.1.three = f32[16,4,8,128]{3,2,1,0:T(8,128)S(1)} async-done(((f32[16,4,8,128]{3,2,1,0:T(8,128)}), f32[16,4,8,128]{3,2,1,0:T(8,128)S(1)}, u32[]{:S(2)}, u32[]{:S(2)}) %all-to-all-start.1) | async-done | bytes 262176 | tf_op jit(solution)/shard_map/all_to_all | solution.py:643
  91.7 0.7 copy-done.8
  92.4 18.1 %shard_map.124 = (f32[4,64,128]{2,1,0:T(8,128)}, f32[12,32,128]{2,1,0:T(8,128)}, f32[18,48,128]{2,1,0:T(8,128)}, f32[24,48,128]{2,1,0:T(8,128)}, f32[16,32,128]{...) custom-call(s32[2]{0:T(128)} %pad_add_fusion.pos, f32[32,128]{1,0:T(8,128)} %copy.37.owned, ...), custom_call_target="tpu_custom_call" | custom-call | flops 10000000 | bytes 8388608 | tf_op jit(solution)/shard_map/pallas_call | solution.py:318
  110.8 4.6 %collective-permute-start.11 = (f32[4,48,128]{2,1,0:T(8,128)}, f32[4,48,128]{2,1,0:T(8,128)S(1)}, u32[]{:S(2)}, u32[]{:S(2)}) collective-permute-start(f32[4,48,128]{2,1,0:T(8,128)} %get-tuple-element.34), channel_id=1, source_target_pairs={{0,240},{16,0},{32,16},{48,32},{64,48},{80,64},{96,80},{112,96},{1... | collective-permute-start | bytes 294920 | tf_op jit(solution)/shard_map/ppermute | solution.py:639
  115.4 3.1 %collective-permute-done.10.left = f32[4,48,128]{2,1,0:T(8,128)S(1)} collective-permute-done((f32[4,48,128]{2,1,0:T(8,128)}, f32[4,48,128]{2,1,0:T(8,128)S(1)}, u32[]{:S(2)}, u32[]{:S(2)}) %collective-permute-start.10) | collective-permute-done | bytes 98336 | tf_op jit(solution)/shard_map/ppermute | solution.py:639
  118.6 0.8 pad_maximum_fusion.10
  119.4 0.4 collective-permute-start.13
  119.8 1.4 collective-permute-start.12
  121.1 1.8 collective-permute-done.13.above
  122.9 0.6 copy-done.16
  123.5 3.0 %shard_map.125 = (f32[12,32,128]{2,1,0:T(8,128)}, f32[12,32,128]{2,1,0:T(8,128)}, f32[16,1,8,128]{3,2,1,0:T(8,128)}) custom-call(s32[2]{0:T(128)} %pad_add_fusion.pos, f32[4,16,128]{2,1,0:T(8,128)} %get-tuple-element.32.mid, f32[4,48,128]{2,1,0:T(8,128)} %copy-done.9, f32[4,48,128]{2,1,0:T(8,128)} %copy-done.10, f32[12,8,128]{2,1,0:T(8,128)} %copy-done.17, ...), custom_call_target="tpu_custom_call" | custom-call | flops 10000000 | bytes 8388608 | tf_op jit(solution)/shard_map/pallas_call | solution.py:318
  126.5 6.5 %all-to-all-start.2 = ((f32[16,1,8,128]{3,2,1,0:T(8,128)}), f32[16,1,8,128]{3,2,1,0:T(8,128)S(1)}, u32[]{:S(2)}, u32[]{:S(2)}) async-start(f32[16,1,8,128]{3,2,1,0:T(8,128)} %get-tuple-element.36), calls=%async_computation.2 | async-start | bytes 131072 | tf_op jit(solution)/shard_map/all_to_all | solution.py:643
  133.0 0.9 slice.74
  133.8 0.8 slice.75
  134.7 4.9 %all-to-all-done.2.mid = f32[16,1,8,128]{3,2,1,0:T(8,128)S(1)} async-done(((f32[16,1,8,128]{3,2,1,0:T(8,128)}), f32[16,1,8,128]{3,2,1,0:T(8,128)S(1)}, u32[]{:S(2)}, u32[]{:S(2)}) %all-to-all-start.2) | async-done | bytes 65568 | tf_op jit(solution)/shard_map/all_to_all | solution.py:643
  139.6 3.1 %collective-permute-start.15 = (f32[40,8,128]{2,1,0:T(8,128)S(1)}, f32[40,8,128]{2,1,0:T(8,128)S(1)}, u32[]{:S(2)}, u32[]{:S(2)}) collective-permute-start(f32[40,8,128]{2,1,0:T(8,128)S(1)} %get-tuple-element.50), channel_id=1, source_target_pairs={{0,15},{1,0},{2,1},{3,2},{4,3},{5,4},{6,5},{7,6},{8,7},{9,8},{10,9... | collective-permute-start | bytes 491528 | tf_op jit(solution)/shard_map/ppermute | solution.py:639
  142.7 3.0 %collective-permute-done.15.above = f32[40,8,128]{2,1,0:T(8,128)S(1)} collective-permute-done((f32[40,8,128]{2,1,0:T(8,128)S(1)}, f32[40,8,128]{2,1,0:T(8,128)S(1)}, u32[]{:S(2)}, u32[]{:S(2)}) %collective-permute-start.15) | collective-permute-done | bytes 163872 | tf_op jit(solution)/shard_map/ppermute | solution.py:639
  145.7 0.7 copy-done.11
  146.4 3.1 %shard_map.126 = (f32[7,5,24,128]{3,2,1,0:T(8,128)}, f32[16,2,8,128]{3,2,1,0:T(8,128)}) custom-call(s32[2]{0:T(128)} %pad_add_fusion.pos, f32[16,1,8,128]{3,2,1,0:T(8,128)} %copy-done.13, f32[40,8,128]{2,1,0:T(8,128)} %copy-done.12, f32[40,8,128]{2,1,0:T(8,128)} %copy-done.11, f32[16,24,128]{2,1,0:T(8,128)} %get-tuple-element.38.refs_0_, ...), custom_call_target="tpu_custom_call" | custom-call | flops 10000000 | bytes 8388608 | tf_op jit(solution)/shard_map/pallas_call | solution.py:318
  149.6 16.1 %all_to_all.20.three = f32[16,2,8,128]{3,2,1,0:T(8,128)} all-to-all(f32[16,2,8,128]{3,2,1,0:T(8,128)} %get-tuple-element.39), channel_id=1, replica_groups=mesh['gx'=16,'gy'=16] {'gy'}, dimensions={0} | all-to-all | bytes 262144 | tf_op jit(solution)/shard_map/all_to_all | solution.py:643
  165.7 13.6 %shard_map.127 = (f32[16,32,128]{2,1,0:T(8,128)}, f32[16,32,128]{2,1,0:T(8,128)}) custom-call(s32[2]{0:T(128)} %pad_add_fusion.pos, f32[32,128]{1,0:T(8,128)} %copy.37.owned, f32[16,2,8,128]{3,2,1,0:T(8,128)} %all_to_all.20.three, f32[4,64,128]{2,1,0:T(8,128)} %get-tuple-element.40.k3, f32[7,5,24,128]{3,2,1,0:T(8,128)} %get-tuple-element.41.near, ...), custom_call_target="tpu_custom_call" | custom-call | flops 10000000 | bytes 8388608 | tf_op jit(solution)/shard_map/pallas_call | solution.py:318
  (66 shorter events, 1.1 us)
Async XLA Ops:
  0.6 18.7 %copy-start = (f32[16,32,128]{2,1,0:T(8,128)S(1)}, f32[16,32,128]{2,1,0:T(8,128)}, u32[]{:S(2)}) copy-start(f32[16,32,128]{2,1,0:T(8,128)} %borig.1) | copy-start | bytes 786436
  0.6 18.7 %copy-start.1 = (f32[16,32,128]{2,1,0:T(8,128)S(1)}, f32[16,32,128]{2,1,0:T(8,128)}, u32[]{:S(2)}) copy-start(f32[16,32,128]{2,1,0:T(8,128)} %ktile.1) | copy-start | bytes 786436
  1.9 12.2 %collective-permute-start.1 = (f32[2,10,32,128]{3,2,1,0:T(8,128)S(1)}, f32[2,10,32,128]{3,2,1,0:T(8,128)S(1)}, u32[]{:S(2)}, u32[]{:S(2)}) collective-permute-start(f32[2,10,32,128]{3,2,1,0:T(8,128)S(1)} %get-tuple-element.48), channel_id=1, source_target_pairs={{0,240},{16,0},{32,16},{48,32},{64,48},{80,64},{96,80},{112,96},{1... | collective-permute-start | bytes 983048 | tf_op jit(solution)/shard_map/ppermute | solution.py:639
  7.7 11.6 %collective-permute-start = (f32[2,10,32,128]{3,2,1,0:T(8,128)S(1)}, f32[2,10,32,128]{3,2,1,0:T(8,128)S(1)}, u32[]{:S(2)}, u32[]{:S(2)}) collective-permute-start(f32[2,10,32,128]{3,2,1,0:T(8,128)S(1)} %get-tuple-element.49), channel_id=1, source_target_pairs={{0,16},{16,32},{32,48},{48,64},{64,80},{80,96},{96,112},{112,128},... | collective-permute-start | bytes 983048 | tf_op jit(solution)/shard_map/ppermute | solution.py:639
  14.1 5.3 %copy-start.2 = (f32[2,10,32,128]{3,2,1,0:T(8,128)}, f32[2,10,32,128]{3,2,1,0:T(8,128)S(1)}, u32[]{:S(2)}) copy-start(f32[2,10,32,128]{3,2,1,0:T(8,128)S(1)} %collective-permute-done.1.right) | copy-start | bytes 983044
  19.3 0.7 copy-start.3
  20.5 7.9 %collective-permute-start.2 = (f32[2,36,10,128]{3,0,2,1:T(2,128)S(1)}, f32[2,36,10,128]{3,0,2,1:T(2,128)S(1)}, u32[]{:S(2)}, u32[]{:S(2)}) collective-permute-start(f32[2,36,10,128]{3,0,2,1:T(2,128)S(1)} %copy.31), channel_id=1, source_target_pairs={{0,1},{1,2},{2,3},{3,4},{4,5},{5,6},{6,7},{7,8},{8,9},{9,10},{10,1... | collective-permute-start | bytes 1105928 | tf_op jit(solution)/shard_map/ppermute | solution.py:639
  24.1 7.1 %collective-permute-start.3 = (f32[2,36,10,128]{3,0,2,1:T(2,128)S(1)}, f32[2,36,10,128]{3,0,2,1:T(2,128)S(1)}, u32[]{:S(2)}, u32[]{:S(2)}) collective-permute-start(f32[2,36,10,128]{3,0,2,1:T(2,128)S(1)} %copy.32), channel_id=1, source_target_pairs={{0,15},{1,0},{2,1},{3,2},{4,3},{5,4},{6,5},{7,6},{8,7},{9,8},{10,9... | collective-permute-start | bytes 1105928 | tf_op jit(solution)/shard_map/ppermute | solution.py:639
  42.5 8.3 %collective-permute-start.4 = (f32[3,4,16,128]{3,2,1,0:T(8,128)}, f32[3,4,16,128]{3,2,1,0:T(8,128)S(1)}, u32[]{:S(2)}, u32[]{:S(2)}) collective-permute-start(f32[3,4,16,128]{3,2,1,0:T(8,128)} %get-tuple-element.25.one), channel_id=1, source_target_pairs={{0,16},{16,32},{32,48},{48,64},{64,80},{80,96},{96,112},{112,128},... | collective-permute-start | bytes 294920 | tf_op jit(solution)/shard_map/ppermute | solution.py:639
  42.5 9.3 %collective-permute-start.5 = (f32[3,4,16,128]{3,2,1,0:T(8,128)}, f32[3,4,16,128]{3,2,1,0:T(8,128)S(1)}, u32[]{:S(2)}, u32[]{:S(2)}) collective-permute-start(f32[3,4,16,128]{3,2,1,0:T(8,128)} %get-tuple-element.25.one), channel_id=1, source_target_pairs={{0,240},{16,0},{32,16},{48,32},{64,48},{80,64},{96,80},{112,96},{1... | collective-permute-start | bytes 294920 | tf_op jit(solution)/shard_map/ppermute | solution.py:639
  47.3 10.2 %all-to-all-start = ((f32[16,2,8,128]{3,2,1,0:T(8,128)}), f32[16,2,8,128]{3,2,1,0:T(8,128)S(1)}, u32[]{:S(2)}, u32[]{:S(2)}) async-start(f32[16,2,8,128]{3,2,1,0:T(8,128)} %get-tuple-element.24), calls=%async_computation | async-start | bytes 262144 | tf_op jit(solution)/shard_map/all_to_all | solution.py:643
  50.9 6.8 %copy-start.14 = (f32[3,4,16,128]{3,2,1,0:T(8,128)}, f32[3,4,16,128]{3,2,1,0:T(8,128)S(1)}, u32[]{:S(2)}) copy-start(f32[3,4,16,128]{3,2,1,0:T(8,128)S(1)} %collective-permute-done.4.left) | copy-start | bytes 294916
  51.8 17.4 %copy-start.15 = (f32[3,4,16,128]{3,2,1,0:T(8,128)}, f32[3,4,16,128]{3,2,1,0:T(8,128)S(1)}, u32[]{:S(2)}) copy-start(f32[3,4,16,128]{3,2,1,0:T(8,128)S(1)} %collective-permute-done.5.right) | copy-start | bytes 294916
  57.6 6.9 %copy-start.4 = (f32[16,2,8,128]{3,2,1,0:T(8,128)}, f32[16,2,8,128]{3,2,1,0:T(8,128)S(1)}, u32[]{:S(2)}) copy-start(f32[16,2,8,128]{3,2,1,0:T(8,128)S(1)} %all-to-all-done.mid) | copy-start | bytes 393220
  57.6 22.1 %copy-start.20 = (s32[16,16]{1,0:T(8,128)S(1)}, s32[16,16]{1,0:T(8,128)}, u32[]{:S(2)}) copy-start(s32[16,16]{1,0:T(8,128)} %param.13) | copy-start | bytes 3076
  57.7 6.8 %collective-permute-start.7 = (f32[68,8,128]{2,1,0:T(8,128)S(1)}, f32[68,8,128]{2,1,0:T(8,128)S(1)}, u32[]{:S(2)}, u32[]{:S(2)}) collective-permute-start(f32[68,8,128]{2,1,0:T(8,128)S(1)} %get-tuple-element.54), channel_id=1, source_target_pairs={{0,15},{1,0},{2,1},{3,2},{4,3},{5,4},{6,5},{7,6},{8,7},{9,8},{10,9... | collective-permute-start | bytes 835592 | tf_op jit(solution)/shard_map/ppermute | solution.py:639
  60.6 3.9 %collective-permute-start.6 = (f32[68,8,128]{2,1,0:T(8,128)S(1)}, f32[68,8,128]{2,1,0:T(8,128)S(1)}, u32[]{:S(2)}, u32[]{:S(2)}) collective-permute-start(f32[68,8,128]{2,1,0:T(8,128)S(1)} %get-tuple-element.55), channel_id=1, source_target_pairs={{0,1},{1,2},{2,3},{3,4},{4,5},{5,6},{6,7},{7,8},{8,9},{9,10},{10,1... | collective-permute-start | bytes 835592 | tf_op jit(solution)/shard_map/ppermute | solution.py:639
  64.5 0.7 copy-start.5
  65.2 0.7 copy-start.6
  69.2 22.5 %all-to-all-start.1 = ((f32[16,4,8,128]{3,2,1,0:T(8,128)}), f32[16,4,8,128]{3,2,1,0:T(8,128)S(1)}, u32[]{:S(2)}, u32[]{:S(2)}) async-start(f32[16,4,8,128]{3,2,1,0:T(8,128)} %get-tuple-element.26), calls=%async_computation.1 | async-start | bytes 524288 | tf_op jit(solution)/shard_map/all_to_all | solution.py:643
  79.9 8.5 %collective-permute-start.9 = (f32[5,8,128]{2,1,0:T(8,128)}, f32[5,8,128]{2,1,0:T(8,128)S(1)}, u32[]{:S(2)}, u32[]{:S(2)}) collective-permute-start(f32[5,8,128]{2,1,0:T(8,128)} %get-tuple-element.28), channel_id=1, source_target_pairs={{0,15},{1,0},{2,1},{3,2},{4,3},{5,4},{6,5},{7,6},{8,7},{9,8},{10,9... | collective-permute-start | bytes 61448 | tf_op jit(solution)/shard_map/ppermute | solution.py:639
  80.0 8.4 %collective-permute-start.8 = (f32[5,8,128]{2,1,0:T(8,128)}, f32[5,8,128]{2,1,0:T(8,128)S(1)}, u32[]{:S(2)}, u32[]{:S(2)}) collective-permute-start(f32[5,8,128]{2,1,0:T(8,128)} %get-tuple-element.28), channel_id=1, source_target_pairs={{0,1},{1,2},{2,3},{3,4},{4,5},{5,6},{6,7},{7,8},{8,9},{9,10},{10,1... | collective-permute-start | bytes 61448 | tf_op jit(solution)/shard_map/ppermute | solution.py:639
  88.4 3.3 %copy-start.18 = (f32[5,8,128]{2,1,0:T(8,128)}, f32[5,8,128]{2,1,0:T(8,128)S(1)}, u32[]{:S(2)}) copy-start(f32[5,8,128]{2,1,0:T(8,128)S(1)} %collective-permute-done.9.x2high) | copy-start | bytes 61444
  88.4 3.3 %copy-start.19 = (f32[5,8,128]{2,1,0:T(8,128)}, f32[5,8,128]{2,1,0:T(8,128)S(1)}, u32[]{:S(2)}) copy-start(f32[5,8,128]{2,1,0:T(8,128)S(1)} %collective-permute-done.8.x2low) | copy-start | bytes 61444
  91.7 0.7 copy-start.8
  110.5 29.1 %copy-start.7 = (f32[16,32,128]{2,1,0:T(8,128)S(1)}, f32[16,32,128]{2,1,0:T(8,128)}, u32[]{:S(2)}) copy-start(f32[16,32,128]{2,1,0:T(8,128)} %get-tuple-element.37.x0n) | copy-start | bytes 786436
  110.5 8.0 %collective-permute-start.10 = (f32[4,48,128]{2,1,0:T(8,128)}, f32[4,48,128]{2,1,0:T(8,128)S(1)}, u32[]{:S(2)}, u32[]{:S(2)}) collective-permute-start(f32[4,48,128]{2,1,0:T(8,128)} %get-tuple-element.33), channel_id=1, source_target_pairs={{0,16},{16,32},{32,48},{48,64},{64,80},{80,96},{96,112},{112,128},... | collective-permute-start | bytes 294920 | tf_op jit(solution)/shard_map/ppermute | solution.py:639
  110.8 7.7 %collective-permute-start.11 = (f32[4,48,128]{2,1,0:T(8,128)}, f32[4,48,128]{2,1,0:T(8,128)S(1)}, u32[]{:S(2)}, u32[]{:S(2)}) collective-permute-start(f32[4,48,128]{2,1,0:T(8,128)} %get-tuple-element.34), channel_id=1, source_target_pairs={{0,240},{16,0},{32,16},{48,32},{64,48},{80,64},{96,80},{112,96},{1... | collective-permute-start | bytes 294920 | tf_op jit(solution)/shard_map/ppermute | solution.py:639
  118.5 4.4 %copy-start.9 = (f32[4,48,128]{2,1,0:T(8,128)}, f32[4,48,128]{2,1,0:T(8,128)S(1)}, u32[]{:S(2)}) copy-start(f32[4,48,128]{2,1,0:T(8,128)S(1)} %collective-permute-done.10.left) | copy-start | bytes 294916
  118.6 4.4 %copy-start.10 = (f32[4,48,128]{2,1,0:T(8,128)}, f32[4,48,128]{2,1,0:T(8,128)S(1)}, u32[]{:S(2)}) copy-start(f32[4,48,128]{2,1,0:T(8,128)S(1)} %collective-permute-done.11.right) | copy-start | bytes 294916
  119.4 3.5 %collective-permute-start.13 = (f32[12,8,128]{2,1,0:T(8,128)S(1)}, f32[12,8,128]{2,1,0:T(8,128)S(1)}, u32[]{:S(2)}, u32[]{:S(2)}) collective-permute-start(f32[12,8,128]{2,1,0:T(8,128)S(1)} %get-tuple-element.56), channel_id=1, source_target_pairs={{0,15},{1,0},{2,1},{3,2},{4,3},{5,4},{6,5},{7,6},{8,7},{9,8},{10,9... | collective-permute-start | bytes 147464 | tf_op jit(solution)/shard_map/ppermute | solution.py:639
  119.8 3.1 %collective-permute-start.12 = (f32[12,8,128]{2,1,0:T(8,128)S(1)}, f32[12,8,128]{2,1,0:T(8,128)S(1)}, u32[]{:S(2)}, u32[]{:S(2)}) collective-permute-start(f32[12,8,128]{2,1,0:T(8,128)S(1)} %get-tuple-element.57), channel_id=1, source_target_pairs={{0,1},{1,2},{2,3},{3,4},{4,5},{5,6},{6,7},{7,8},{8,9},{9,10},{10,1... | collective-permute-start | bytes 147464 | tf_op jit(solution)/shard_map/ppermute | solution.py:639
  122.9 0.6 copy-start.16
  122.9 0.6 copy-start.17
  126.5 13.1 %all-to-all-start.2 = ((f32[16,1,8,128]{3,2,1,0:T(8,128)}), f32[16,1,8,128]{3,2,1,0:T(8,128)S(1)}, u32[]{:S(2)}, u32[]{:S(2)}) async-start(f32[16,1,8,128]{3,2,1,0:T(8,128)} %get-tuple-element.36), calls=%async_computation.2 | async-start | bytes 131072 | tf_op jit(solution)/shard_map/all_to_all | solution.py:643
  139.6 6.1 %copy-start.13 = (f32[16,1,8,128]{3,2,1,0:T(8,128)}, f32[16,1,8,128]{3,2,1,0:T(8,128)S(1)}, u32[]{:S(2)}) copy-start(f32[16,1,8,128]{3,2,1,0:T(8,128)S(1)} %all-to-all-done.2.mid) | copy-start | bytes 196612
  139.6 6.1 %collective-permute-start.15 = (f32[40,8,128]{2,1,0:T(8,128)S(1)}, f32[40,8,128]{2,1,0:T(8,128)S(1)}, u32[]{:S(2)}, u32[]{:S(2)}) collective-permute-start(f32[40,8,128]{2,1,0:T(8,128)S(1)} %get-tuple-element.50), channel_id=1, source_target_pairs={{0,15},{1,0},{2,1},{3,2},{4,3},{5,4},{6,5},{7,6},{8,7},{9,8},{10,9... | collective-permute-start | bytes 491528 | tf_op jit(solution)/shard_map/ppermute | solution.py:639
  142.7 3.0 %collective-permute-start.14 = (f32[40,8,128]{2,1,0:T(8,128)S(1)}, f32[40,8,128]{2,1,0:T(8,128)S(1)}, u32[]{:S(2)}, u32[]{:S(2)}) collective-permute-start(f32[40,8,128]{2,1,0:T(8,128)S(1)} %get-tuple-element.51), channel_id=1, source_target_pairs={{0,1},{1,2},{2,3},{3,4},{4,5},{5,6},{6,7},{7,8},{8,9},{9,10},{10,1... | collective-permute-start | bytes 491528 | tf_op jit(solution)/shard_map/ppermute | solution.py:639
  145.7 0.7 copy-start.11
  145.7 0.7 copy-start.12

commit v3 on v2

--- a/solution.py
+++ b/solution.py
@@ -15,9 +15,8 @@
 HX = 10
 HY = 12
 PX, RY = TX + 2 * HX, TY + 2 * HY
-UX, UR = TX + 16, TY + 16
 CHUNK = 4
-VMEM_BYTES = 56 * 1024 * 1024
+VMEM_BYTES = 24 * 1024 * 1024
 
 
 def cheb_steps(degree, lower):
@@ -219,8 +218,8 @@
     dst[:, HY + TY : RY - 2, :] = above
 
 
-def down_kernel(pos, tile, left, right, below, above, ktile, r0, r1, xup, bup, kup, one, two, *scratch):
-    bx, kx, wx, wy, wz, s, rd, d, x, rs, b1s, x1s, k1s = scratch
+def down_kernel(pos, tile, left, right, below, above, ktile, r0, r1, bx, x, wx, wy, wz, s, rd, one, two, *scratch):
+    kx, d, rs, b1s, x1s, k1s = scratch
     gx, gy = pos[0], pos[1]
     inside_at = insider(RY, gx * TX - HX, gy * TY - HY)
     fill_top(bx, tile[...], left[0], right[0], below[0], above[0])
@@ -248,10 +247,6 @@
         d[at] = bx[at] - av
 
     sweep_top(x, wx, wy, wz, s, 4, PX - 4, residual)
-    region = (slice(2, 2 + UX), slice(4, 4 + UR))
-    xup[...] = x[region]
-    bup[...] = bx[region]
-    kup[...] = kx[region]
 
     def coarse(src):
         for c in range(16):
@@ -327,9 +322,9 @@
 
 
 def go_down(*args):
-    top, up = (PX, RY, 128), (UX, UR, 128)
-    outs = [up, up, up, (3, 4, 16, 128), (16, 2, 8, 128)]
-    scratch = [top] * 9 + [(16, RY, 128)] + [(8, 24, 128)] * 3
+    top = (PX, RY, 128)
+    outs = [top] * 7 + [(3, 4, 16, 128), (16, 2, 8, 128)]
+    scratch = [top] * 2 + [(16, RY, 128)] + [(8, 24, 128)] * 3
     return call(down_kernel, outs, scratch, *args)
 
 
@@ -513,24 +508,28 @@
     for i in range(high - low):
         for q in range(2):
             part = back[24 * i : 24 * i + 24, 128 * q : 128 * q + 128]
-            spread_rows(e0, 2 * (low - 2 + i) + q, 0, part)
-
-
-def add_top(x0, e0, x):
-    def begin(p, rdv):
-        c = p // 2
+            spread_rows(e0, 2 * (low - 2 + i) + q, 4, part)
+    e0[:, 0:4, :] = jnp.zeros((16, 4, 128), F32)
+    e0[:, RY - 4 : RY, :] = jnp.zeros((16, 4, 128), F32)
+
+
+def add_top(x0, e0, rd, x, low, high):
+    def step(i, _):
+        p = low + i * CHUNK
+        c = (p - 2) // 2
         pair = (e0[pl.ds(c, 1)], e0[pl.ds(c + 1, 1)])
         correction = jnp.concatenate([pair[0], pair[0], pair[1], pair[1]], axis=0)
         at = pl.ds(p, CHUNK)
-        x[at] = jnp.where(rdv > 0.0, x0[at] + correction, 0.0)
-
-    return begin
+        x[at] = jnp.where(rd[at] > 0.0, x0[at] + correction, 0.0)
+        return 0
+
+    lax.fori_loop(0, (high - low) // CHUNK, step, 0)
 
 
 def turn_kernel(
-    pos, owned, three, near, x2low, x2high, one, left, right, below, above, x0, b0, k0, r0, r3, t3, t2, t1, t0,
+    pos, owned, three, near, x2low, x2high, one, left, right, below, above, b0, x0, wx, wy, wz, s, rd, r0, r3, t3, t2, t1, t0,
     k3, k1, xout, rout, x0n, b1n, east, west,
-    b3, s3, e2, s2, x2s, b1s, s1, e0, wx, wy, wz, s, rd, d, x, rs
+    b3, s3, e2, s2, x2s, b1s, s1, e0, d, x, rs
 ):
     gx, gy = pos[0], pos[1]
     fill_three(b3, three, 0)
@@ -549,56 +548,55 @@
     rise_one(s1[...], b1s[...], k1[...], inside, s2, t1, s1)
 
     spread_one(s1, 2, 10, t0, e0)
-    inside_at = insider(UR, gx * TX - 8, gy * TY - 8)
-    build_top(k0, wx, wy, wz, s, rd, 0, UX, inside_at, add_top(x0, e0, x))
+    add_top(x0, e0, rd, x, 2, PX - 2)
     start, steps = SMOOTH
-    sweep_top(x, wx, wy, wz, s, 2, UX - 2, open_top(b0, 0, rd, d, x))
-    for (keep, gain), edge in zip(steps, (2, 4)):
-        sweep_top(x, wx, wy, wz, s, edge, UX - edge, advance_top(keep, gain, b0, 0, rd, d, x))
+    sweep_top(x, wx, wy, wz, s, 4, PX - 4, open_top(b0, 0, rd, d, x))
+    for (keep, gain), edge in zip(steps, (4, 6)):
+        sweep_top(x, wx, wy, wz, s, edge, PX - edge, advance_top(keep, gain, b0, 0, rd, d, x))
 
     def residual(p, at, v, av):
-        rout[pl.ds(p - 4, CHUNK)] = b0[at] - av
-
-    sweep_top(x, wx, wy, wz, s, 4, UX - 4, residual)
-    xout[...] = x[7 : UX - 7]
+        rout[pl.ds(p - 6, CHUNK)] = b0[at] - av
+
+    sweep_top(x, wx, wy, wz, s, 6, PX - 6, residual)
+    xout[...] = x[9 : PX - 9]
 
     def begin(i, _):
-        at = pl.ds(4 + i * CHUNK, CHUNK)
+        at = pl.ds(6 + i * CHUNK, CHUNK)
         v = (rout[pl.ds(i * CHUNK, CHUNK)] * rd[at]) * start
         d[at] = v
         x[at] = v
         return 0
 
-    lax.fori_loop(0, (UX - 8) // CHUNK, begin, 0)
+    lax.fori_loop(0, (PX - 12) // CHUNK, begin, 0)
     for keep, gain in steps:
-        sweep_top(x, wx, wy, wz, s, 6, UX - 6, advance_top(keep, gain, rout, 4, rd, d, x))
+        sweep_top(x, wx, wy, wz, s, 8, PX - 8, advance_top(keep, gain, rout, 6, rd, d, x))
 
     def again(p, at, v, av):
-        d[at] = rout[pl.ds(p - 4, CHUNK)] - av
-
-    sweep_top(x, wx, wy, wz, s, 8, UX - 8, again)
-    x0n[...] = x[8:24, 8:40, :]
+        d[at] = rout[pl.ds(p - 6, CHUNK)] - av
+
+    sweep_top(x, wx, wy, wz, s, HX, HX + TX, again)
+    x0n[...] = x[HX : HX + TX, HY : HY + TY, :]
     for c in range(8):
-        rs[c] = d[8 + 2 * c] + d[9 + 2 * c]
-    b1 = pair_planes(rs, 4, 8, 16, r0)
+        rs[c] = d[HX + 2 * c] + d[HX + 1 + 2 * c]
+    b1 = pair_planes(rs, 4, HY, 16, r0)
     b1n[...] = b1
-    for side, plane in ((east, 20), (west, 8)):
+    for side, plane in ((east, HX + TX - 4), (west, HX)):
         side[:, 0:16, :] = b1
-        side[:, 16:48, :] = x[plane : plane + 4, 8:40, :]
+        side[:, 16:48, :] = x[plane : plane + 4, HY : HY + TY, :]
 
 
 def go_turn(*args):
-    up, wide = (UX, UR, 128), (12, 32, 128)
-    outs = [(4, 64, 128), wide, (TX + 2, UR, 128), (TX + 8, UR, 128), (TX, TY, 128), (4, 16, 128)]
+    top, wide = (PX, RY, 128), (12, 32, 128)
+    outs = [(4, 64, 128), wide, (TX + 2, RY, 128), (TX + 8, RY, 128), (TX, TY, 128), (4, 16, 128)]
     outs += [(4, 48, 128)] * 2
-    scratch = [(4, 64, 128)] * 2 + [(5, 144, 128), (5, 24, 128), (5, 24, 128), wide, wide, (16, UR, 128)]
-    return call(turn_kernel, outs, scratch + [up] * 7 + [(8, UR, 128)], *args)
+    scratch = [(4, 64, 128)] * 2 + [(5, 144, 128), (5, 24, 128), (5, 24, 128), wide, wide, (16, RY, 128)]
+    return call(turn_kernel, outs, scratch + [top] * 2 + [(8, RY, 128)], *args)
 
 
 def last_kernel(
-    pos, owned, three, k3, near, b1, x1, k1, x0n, left, right, below, above, r, k0, xbefore, borig,
-    r3, t3, t2, t1, t0, xout, rout,
-    b3, s3, e2, s2, s1, e0, wx, wy, wz, s, rd, d, x
+    pos, owned, three, k3, near, b1, x1, k1, x0n, left, right, below, above, r, xbefore,
+    b0, wx, wy, wz, s, rd, r3, t3, t2, t1, t0, xout, rout,
+    b3, s3, e2, s2, s1, e0, d, x
 ):
     gx, gy = pos[0], pos[1]
     fill_three(b3, three, 0)
@@ -608,30 +606,32 @@
     rise_one(x1[...], b1[...], k1[...], inside, s2, t1, s1)
 
     spread_one(s1, 3, 9, t0, e0)
-    x[4:8, 8:40, :] = left[:, 16:48, :]
-    x[8:24, 8:40, :] = x0n[...]
-    x[24:28, 8:40, :] = right[:, 16:48, :]
-    x[4:28, 0:8, :] = below[16:40]
-    x[4:28, 40:48, :] = above[16:40]
-    inside_at = insider(UR, gx * TX - 8, gy * TY - 8)
-    build_top(k0, wx, wy, wz, s, rd, 4, UX - 4, inside_at, add_top(x, e0, x))
-    sweep_top(x, wx, wy, wz, s, 4, UX - 4, open_top(r, 4, rd, d, x))
+    low, high = HX - 4, HX + TX + 4
+    x[low:HX, HY : HY + TY, :] = left[:, 16:48, :]
+    x[HX : HX + TX, HY : HY + TY, :] = x0n[...]
+    x[HX + TX : high, HY : HY + TY, :] = right[:, 16:48, :]
+    x[low:high, HY - 8 : HY, :] = below[16:40]
+    x[low:high, HY + TY : HY + TY + 8, :] = above[16:40]
+    x[low:high, 0 : HY - 8, :] = jnp.zeros((high - low, HY - 8, 128), F32)
+    x[low:high, RY - 4 : RY, :] = jnp.zeros((high - low, 4, 128), F32)
+    add_top(x, e0, rd, x, low, high)
+    sweep_top(x, wx, wy, wz, s, low, high, open_top(r, low, rd, d, x))
     for keep, gain in SMOOTH[1]:
-        sweep_top(x, wx, wy, wz, s, 6, UX - 6, advance_top(keep, gain, r, 4, rd, d, x))
-    x[7 : UX - 7] = x[7 : UX - 7] + xbefore[...]
+        sweep_top(x, wx, wy, wz, s, 8, PX - 8, advance_top(keep, gain, r, low, rd, d, x))
+    x[9 : PX - 9] = x[9 : PX - 9] + xbefore[...]
 
     def residual(p, at, v, av):
-        out = pl.ds(p - 8, CHUNK)
-        xout[out] = v[:, 8 : 8 + TY]
-        rout[out] = borig[out] - av[:, 8 : 8 + TY]
-
-    sweep_top(x, wx, wy, wz, s, 8, UX - 8, residual)
+        d[at] = b0[at] - av
+
+    sweep_top(x, wx, wy, wz, s, HX, HX + TX, residual)
+    xout[...] = x[HX : HX + TX, HY : HY + TY, :]
+    rout[...] = d[HX : HX + TX, HY : HY + TY, :]
 
 
 def go_last(*args):
-    up, wide, tile = (UX, UR, 128), (12, 32, 128), (TX, TY, 128)
-    scratch = [(4, 64, 128)] * 2 + [(5, 144, 128), (5, 24, 128), wide, (16, UR, 128)]
-    return call(last_kernel, [tile, tile], scratch + [up] * 7, *args)
+    top, wide, tile = (PX, RY, 128), (12, 32, 128), (TX, TY, 128)
+    scratch = [(4, 64, 128)] * 2 + [(5, 144, 128), (5, 24, 128), wide, (16, RY, 128)]
+    return call(last_kernel, [tile, tile], scratch + [top] * 2, *args)
 
 
 def shift(value, axis, step):
@@ -658,7 +658,8 @@
     wide = jnp.concatenate([left, mid, right], axis=1)
     below = shift(wide[:, :, TY - HX :], "gy", 1)
     above = shift(wide[:, :, :HX], "gy", -1)
-    xup, bup, kup, one, two = go_down(pos, right_side, left, right, below, above, kappa, r0, r1)
+    b0, x0, wx, wy, wz, s, rd, one, two = go_down(pos, right_side, left, right, below, above, kappa, r0, r1)
+    top = (wx, wy, wz, s, rd)
     left = shift(one, "gx", 1)
     right = shift(one, "gx", -1)
     two = gather(two, "gx")
@@ -671,7 +672,8 @@
     x2high = shift(x2, "gy", -1)
     three = gather(three, "gy")
     k3, k1, xbefore, source, x0n, b1n, east, west = go_turn(
-        pos, owned, three, near, x2low, x2high, one, left, right, below, above, xup, bup, kup, r0, r3, t3, t2, t1, t0
+        pos, owned, three, near, x2low, x2high, one, left, right, below, above, b0, x0, *top,
+        r0, r3, t3, t2, t1, t0
     )
 
     left = shift(east, "gx", 1)
@@ -687,8 +689,8 @@
     near, three = go_mid(False, pos, two, below, above, k2, r2)
     three = gather(three, "gy")
     field, residual = go_last(
-        pos, owned, three, k3, near, b1, x1, k1, x0n, left, right, below, above, source, kup, xbefore, right_side,
-        r3, t3, t2, t1, t0
+        pos, owned, three, k3, near, b1, x1, k1, x0n, left, right, below, above, source, xbefore, b0,
+        *top, r3, t3, t2, t1, t0
     )
     return field, residual
 

time: 180 us -> 207 us (1.15)
  local copies, waits for them, and re-layouts: 10 us -> 44.6 us
  Pallas kernels: 51.6 us -> 40.9 us
    unnamed x44 -> x140, local copies, waits for them, and re-layouts: 5.06 us -> 41.6 us
    pallas_call x6, Pallas kernels: 51.6 us -> 40.9 us  [call(): pl.pallas_call(kernel, out_shape=[jax.ShapeDtypeStruct(o, F32) for o in o...]
  transfers between devices with their start and end apart: 19 -> 19, of which waited for: 12 -> 12; matrix products, arithmetic and copies ran while one was open for 3% -> 2% of each run, Pallas kernels for 0% -> 0%
where the time goes in v3:
time: 207 us; the launch traced here: 205 us
  waiting for transfers between devices  50.2 us (24%)
  starting transfers between devices  50.1 us (24%)
  local copies, waits for them, and re-layouts  44.6 us (22%)
  Pallas kernels  40.9 us (20%)
  blocking collectives  15.1 us (7%)
  other arithmetic  3.43 us (2%)
    unnamed x140, local copies, waits for them, and re-layouts  41.6 us
    pallas_call x6, Pallas kernels, call(): pl.pallas_call(kernel, out_shape=[jax.ShapeDtypeStruct(o, F32) for o in o...  40.9 us
    ppermute x16, waiting for transfers between devices, shift(): lax.ppermute(value, axis, [(i, (i + step) % count) for i in range(count)])  36.7 us
    ppermute x16, starting transfers between devices, shift(): lax.ppermute(value, axis, [(i, (i + step) % count) for i in range(count)])  27.8 us
    all_to_all x3, starting transfers between devices, gather(): return lax.all_to_all(copies, axis, 0, 0, tiled=True)  22.3 us
    all_to_all x1, blocking collectives, gather(): return lax.all_to_all(copies, axis, 0, 0, tiled=True)  15.1 us
    all_to_all x3, waiting for transfers between devices, gather(): return lax.all_to_all(copies, axis, 0, 0, tiled=True)  13.5 us
  transfers between devices with their start and end apart: 19, of which 12 were waited for; matrix products, arithmetic and copies ran while one was open for 2% of the time, Pallas kernels for 0%

profile of v3, /device:TPU:1, one launch (start us, length us, event | category | flops | bytes accessed | tf_op | source)
XLA Modules:
  0.0 205.4 jit_solution(4135248517661254560)
XLA Ops:
  0.7 1.3 pad_maximum_fusion.3
  1.9 5.8 %collective-permute-start.1 = (f32[2,10,32,128]{3,2,1,0:T(8,128)S(1)}, f32[2,10,32,128]{3,2,1,0:T(8,128)S(1)}, u32[]{:S(2)}, u32[]{:S(2)}) collective-permute-start(f32[2,10,32,128]{3,2,1,0:T(8,128)S(1)} %get-tuple-element.56), channel_id=1, source_target_pairs={{0,240},{16,0},{32,16},{48,32},{64,48},{80,64},{96,80},{112,96},{1... | collective-permute-start | bytes 983048 | tf_op jit(solution)/shard_map/ppermute | solution.py:639
  7.8 6.4 %collective-permute-done.1.right = f32[2,10,32,128]{3,2,1,0:T(8,128)S(1)} collective-permute-done((f32[2,10,32,128]{3,2,1,0:T(8,128)S(1)}, f32[2,10,32,128]{3,2,1,0:T(8,128)S(1)}, u32[]{:S(2)}, u32[]{:S(2)}) %collective-permute-start.1) | collective-permute-done | bytes 327712 | tf_op jit(solution)/shard_map/ppermute | solution.py:639
  14.1 5.2 %collective-permute-done.left = f32[2,10,32,128]{3,2,1,0:T(8,128)S(1)} collective-permute-done((f32[2,10,32,128]{3,2,1,0:T(8,128)S(1)}, f32[2,10,32,128]{3,2,1,0:T(8,128)S(1)}, u32[]{:S(2)}, u32[]{:S(2)}) %collective-permute-start) | collective-permute-done | bytes 327712 | tf_op jit(solution)/shard_map/ppermute | solution.py:639
  20.4 3.4 %collective-permute-start.2 = (f32[2,36,10,128]{3,0,2,1:T(2,128)S(1)}, f32[2,36,10,128]{3,0,2,1:T(2,128)S(1)}, u32[]{:S(2)}, u32[]{:S(2)}) collective-permute-start(f32[2,36,10,128]{3,0,2,1:T(2,128)S(1)} %copy.31), channel_id=1, source_target_pairs={{0,1},{1,2},{2,3},{3,4},{4,5},{5,6},{6,7},{7,8},{8,9},{9,10},{10,1... | collective-permute-start | bytes 1105928 | tf_op jit(solution)/shard_map/ppermute | solution.py:639
  24.3 4.0 %collective-permute-done.2 = f32[2,36,10,128]{3,0,2,1:T(2,128)S(1)} collective-permute-done((f32[2,36,10,128]{3,0,2,1:T(2,128)S(1)}, f32[2,36,10,128]{3,0,2,1:T(2,128)S(1)}, u32[]{:S(2)}, u32[]{:S(2)}) %collective-permute-start.2) | collective-permute-done | bytes 368672 | tf_op jit(solution)/shard_map/ppermute | solution.py:639
  28.4 2.9 %collective-permute-done.3 = f32[2,36,10,128]{3,0,2,1:T(2,128)S(1)} collective-permute-done((f32[2,36,10,128]{3,0,2,1:T(2,128)S(1)}, f32[2,36,10,128]{3,0,2,1:T(2,128)S(1)}, u32[]{:S(2)}, u32[]{:S(2)}) %collective-permute-start.3) | collective-permute-done | bytes 368672 | tf_op jit(solution)/shard_map/ppermute | solution.py:639
  32.3 1.0 copy-done.13
  33.2 1.0 copy-done.15
  34.2 8.7 %shard_map.122 = (f32[36,56,128]{2,1,0:T(8,128)S(1)}, f32[36,56,128]{2,1,0:T(8,128)S(1)}, f32[36,56,128]{2,1,0:T(8,128)S(1)}, f32[36,56,128]{2,1,0:T(8,128)S(1)}...) custom-call(s32[2]{0:T(128)S(1)} %pad_add_fusion.pos, ...), custom_call_target="tpu_custom_call" | custom-call | flops 10000000 | bytes 8388608 | tf_op jit(solution)/shard_map/pallas_call | solution.py:313
  42.9 1.0 copy-done
  44.8 1.0 copy-done.6
  45.8 1.0 copy-done.20
  47.5 4.8 %collective-permute-start.5 = (f32[3,4,16,128]{3,2,1,0:T(8,128)}, f32[3,4,16,128]{3,2,1,0:T(8,128)S(1)}, u32[]{:S(2)}, u32[]{:S(2)}) collective-permute-start(f32[3,4,16,128]{3,2,1,0:T(8,128)} %get-tuple-element.29.one), channel_id=1, source_target_pairs={{0,240},{16,0},{32,16},{48,32},{64,48},{80,64},{96,80},{112,96},{1... | collective-permute-start | bytes 294920 | tf_op jit(solution)/shard_map/ppermute | solution.py:639
  52.3 3.5 %all-to-all-start = ((f32[16,2,8,128]{3,2,1,0:T(8,128)}), f32[16,2,8,128]{3,2,1,0:T(8,128)S(1)}, u32[]{:S(2)}, u32[]{:S(2)}) async-start(f32[16,2,8,128]{3,2,1,0:T(8,128)} %copy-done.61), calls=%async_computation | async-start | bytes 262144 | tf_op jit(solution)/shard_map/all_to_all | solution.py:643
  57.5 4.9 %all-to-all-done.mid = f32[16,2,8,128]{3,2,1,0:T(8,128)S(1)} async-done(((f32[16,2,8,128]{3,2,1,0:T(8,128)}), f32[16,2,8,128]{3,2,1,0:T(8,128)S(1)}, u32[]{:S(2)}, u32[]{:S(2)}) %all-to-all-start) | async-done | bytes 131104 | tf_op jit(solution)/shard_map/all_to_all | solution.py:643
  62.4 1.0 pad_maximum_fusion.1
  63.5 2.3 %collective-permute-start.7 = (f32[68,8,128]{2,1,0:T(8,128)S(1)}, f32[68,8,128]{2,1,0:T(8,128)S(1)}, u32[]{:S(2)}, u32[]{:S(2)}) collective-permute-start(f32[68,8,128]{2,1,0:T(8,128)S(1)} %get-tuple-element.62), channel_id=1, source_target_pairs={{0,15},{1,0},{2,1},{3,2},{4,3},{5,4},{6,5},{7,6},{8,7},{9,8},{10,9... | collective-permute-start | bytes 835592 | tf_op jit(solution)/shard_map/ppermute | solution.py:639
  65.8 3.7 %collective-permute-done.7.above = f32[68,8,128]{2,1,0:T(8,128)S(1)} collective-permute-done((f32[68,8,128]{2,1,0:T(8,128)S(1)}, f32[68,8,128]{2,1,0:T(8,128)S(1)}, u32[]{:S(2)}, u32[]{:S(2)}) %collective-permute-start.7) | collective-permute-done | bytes 278560 | tf_op jit(solution)/shard_map/ppermute | solution.py:639
  70.4 1.9 shard_map.123
  74.5 12.2 %all-to-all-start.1 = ((f32[16,4,8,128]{3,2,1,0:T(8,128)}), f32[16,4,8,128]{3,2,1,0:T(8,128)}, u32[]{:S(2)}, u32[]{:S(2)}) async-start(f32[16,4,8,128]{3,2,1,0:T(8,128)} %copy-done.50), calls=%async_computation.1 | async-start | bytes 524288 | tf_op jit(solution)/shard_map/all_to_all | solution.py:643
  87.0 1.6 collective-permute-start.8
  88.7 6.8 %collective-permute-done.9.x2high = f32[5,8,128]{2,1,0:T(8,128)S(1)} collective-permute-done((f32[5,8,128]{2,1,0:T(8,128)S(1)}, f32[5,8,128]{2,1,0:T(8,128)S(1)}, u32[]{:S(2)}, u32[]{:S(2)}) %collective-permute-start.9) | collective-permute-done | bytes 20512 | tf_op jit(solution)/shard_map/ppermute | solution.py:639
  95.5 3.3 %all-to-all-done.1.three = f32[16,4,8,128]{3,2,1,0:T(8,128)} async-done(((f32[16,4,8,128]{3,2,1,0:T(8,128)}), f32[16,4,8,128]{3,2,1,0:T(8,128)}, u32[]{:S(2)}, u32[]{:S(2)}) %all-to-all-start.1) | async-done | bytes 262176 | tf_op jit(solution)/shard_map/all_to_all | solution.py:643
  98.7 1.2 copy-done.1
  100.0 1.2 copy-done.4
  101.2 1.2 copy-done.7
  102.4 1.0 copy-done.17
  103.4 1.2 copy-done.21
  108.2 1.0 copy-done.41
  112.7 15.1 %shard_map.124 = (f32[4,64,128]{2,1,0:T(8,128)S(1)}, f32[12,32,128]{2,1,0:T(8,128)S(1)}, f32[18,56,128]{2,1,0:T(8,128)S(1)}, f32[24,56,128]{2,1,0:T(8,128)S(1)},...) custom-call(s32[2]{0:T(128)S(1)} %copy-done.64, ...), custom_call_target="tpu_custom_call" | custom-call | flops 10000000 | bytes 8388608 | tf_op jit(solution)/shard_map/pallas_call | solution.py:313
  129.7 4.6 %collective-permute-start.11 = (f32[4,48,128]{2,1,0:T(8,128)S(1)}, f32[4,48,128]{2,1,0:T(8,128)S(1)}, u32[]{:S(2)}, u32[]{:S(2)}) collective-permute-start(f32[4,48,128]{2,1,0:T(8,128)S(1)} %get-tuple-element.42), channel_id=1, source_target_pairs={{0,240},{16,0},{32,16},{48,32},{64,48},{80,64},{96,80},{112,96},{1... | collective-permute-start | bytes 294920 | tf_op jit(solution)/shard_map/ppermute | solution.py:639
  134.3 2.9 %collective-permute-done.10.left = f32[4,48,128]{2,1,0:T(8,128)S(1)} collective-permute-done((f32[4,48,128]{2,1,0:T(8,128)S(1)}, f32[4,48,128]{2,1,0:T(8,128)S(1)}, u32[]{:S(2)}, u32[]{:S(2)}) %collective-permute-start.10) | collective-permute-done | bytes 98336 | tf_op jit(solution)/shard_map/ppermute | solution.py:639
  137.7 1.4 collective-permute-start.12
  139.0 1.8 collective-permute-done.13.above
  140.8 1.8 shard_map.125
  144.6 6.5 %all-to-all-start.2 = ((f32[16,1,8,128]{3,2,1,0:T(8,128)}), f32[16,1,8,128]{3,2,1,0:T(8,128)}, u32[]{:S(2)}, u32[]{:S(2)}) async-start(f32[16,1,8,128]{3,2,1,0:T(8,128)} %copy-done.62), calls=%async_computation.2 | async-start | bytes 131072 | tf_op jit(solution)/shard_map/all_to_all | solution.py:643
  152.4 5.4 %all-to-all-done.2.mid = f32[16,1,8,128]{3,2,1,0:T(8,128)} async-done(((f32[16,1,8,128]{3,2,1,0:T(8,128)}), f32[16,1,8,128]{3,2,1,0:T(8,128)}, u32[]{:S(2)}, u32[]{:S(2)}) %all-to-all-start.2) | async-done | bytes 65568 | tf_op jit(solution)/shard_map/all_to_all | solution.py:643
  157.8 1.0 pad_maximum_fusion.4
  158.8 3.1 %collective-permute-start.15 = (f32[40,8,128]{2,1,0:T(8,128)S(1)}, f32[40,8,128]{2,1,0:T(8,128)S(1)}, u32[]{:S(2)}, u32[]{:S(2)}) collective-permute-start(f32[40,8,128]{2,1,0:T(8,128)S(1)} %get-tuple-element.58), channel_id=1, source_target_pairs={{0,15},{1,0},{2,1},{3,2},{4,3},{5,4},{6,5},{7,6},{8,7},{9,8},{10,9... | collective-permute-start | bytes 491528 | tf_op jit(solution)/shard_map/ppermute | solution.py:639
  161.9 3.0 %collective-permute-done.15.above = f32[40,8,128]{2,1,0:T(8,128)S(1)} collective-permute-done((f32[40,8,128]{2,1,0:T(8,128)S(1)}, f32[40,8,128]{2,1,0:T(8,128)S(1)}, u32[]{:S(2)}, u32[]{:S(2)}) %collective-permute-start.15) | collective-permute-done | bytes 163872 | tf_op jit(solution)/shard_map/ppermute | solution.py:639
  167.4 2.1 %shard_map.126 = (f32[7,5,24,128]{3,2,1,0:T(8,128)S(1)}, f32[16,2,8,128]{3,2,1,0:T(8,128)S(1)}) custom-call(s32[2]{0:T(128)S(1)} %copy-done.66, f32[16,1,8,128]{3,2,1,0:T(8,128)} %all-to-all-done.2.mid, f32[40,8,128]{2,1,0:T(8,128)S(1)} %collective-permute-done.14.below, f32[40,8,128]{2,1,0:T(8,128)S(1)} %collective-permute-done.15.above, ...), custom_call_target="tpu_custom_call" | custom-call | flops 10000000 | bytes 8388608 | tf_op jit(solution)/shard_map/pallas_call | solution.py:313
  169.5 15.1 %all_to_all.20.three = f32[16,2,8,128]{3,2,1,0:T(8,128)S(1)} all-to-all(f32[16,2,8,128]{3,2,1,0:T(8,128)S(1)} %get-tuple-element.47), channel_id=1, replica_groups=mesh['gx'=16,'gy'=16] {'gy'}, dimensions={0} | all-to-all | bytes 262144 | tf_op jit(solution)/shard_map/all_to_all | solution.py:643
  184.7 1.2 copy-done.5
  185.9 1.2 copy-done.8
  187.1 1.1 copy-done.25
  188.2 1.0 copy-done.39
  194.2 11.2 %shard_map.127 = (f32[16,32,128]{2,1,0:T(8,128)}, f32[16,32,128]{2,1,0:T(8,128)}) custom-call(s32[2]{0:T(128)S(1)} %copy-done.67, f32[32,128]{1,0:T(8,128)S(1)} %copy-done.58, f32[16,2,8,128]{3,2,1,0:T(8,128)S(1)} %all_to_all.20.three, f32[4,64,128]{2,1,0:T(8,128)S(1)} %copy-done.60, f32[7,5,24,128]{3,2,1,0:T(8,128)S(1)} %get-tuple-element.49.near, ...), custom_call_target="tpu_custom_call" | custom-call | flops 10000000 | bytes 8388608 | tf_op jit(solution)/shard_map/pallas_call | solution.py:313
  (162 shorter events, 29.4 us)
Async XLA Ops:
  0.6 18.7 %copy-start.10 = (f32[16,32,128]{2,1,0:T(8,128)S(1)}, f32[16,32,128]{2,1,0:T(8,128)}, u32[]{:S(2)}) copy-start(f32[16,32,128]{2,1,0:T(8,128)} %ktile.1) | copy-start | bytes 786436
  0.6 18.7 %copy-start.9 = (f32[16,32,128]{2,1,0:T(8,128)S(1)}, f32[16,32,128]{2,1,0:T(8,128)}, u32[]{:S(2)}) copy-start(f32[16,32,128]{2,1,0:T(8,128)} %tile.1) | copy-start | bytes 786436
  1.9 12.2 %collective-permute-start.1 = (f32[2,10,32,128]{3,2,1,0:T(8,128)S(1)}, f32[2,10,32,128]{3,2,1,0:T(8,128)S(1)}, u32[]{:S(2)}, u32[]{:S(2)}) collective-permute-start(f32[2,10,32,128]{3,2,1,0:T(8,128)S(1)} %get-tuple-element.56), channel_id=1, source_target_pairs={{0,240},{16,0},{32,16},{48,32},{64,48},{80,64},{96,80},{112,96},{1... | collective-permute-start | bytes 983048 | tf_op jit(solution)/shard_map/ppermute | solution.py:639
  7.7 11.6 %collective-permute-start = (f32[2,10,32,128]{3,2,1,0:T(8,128)S(1)}, f32[2,10,32,128]{3,2,1,0:T(8,128)S(1)}, u32[]{:S(2)}, u32[]{:S(2)}) collective-permute-start(f32[2,10,32,128]{3,2,1,0:T(8,128)S(1)} %get-tuple-element.57), channel_id=1, source_target_pairs={{0,16},{16,32},{32,48},{48,64},{64,80},{80,96},{96,112},{112,128},... | collective-permute-start | bytes 983048 | tf_op jit(solution)/shard_map/ppermute | solution.py:639
  14.1 5.3 %copy-start.12 = (f32[2,10,32,128]{3,2,1,0:T(8,128)}, f32[2,10,32,128]{3,2,1,0:T(8,128)S(1)}, u32[]{:S(2)}) copy-start(f32[2,10,32,128]{3,2,1,0:T(8,128)S(1)} %collective-permute-done.1.right) | copy-start | bytes 983044
  20.4 7.9 %collective-permute-start.2 = (f32[2,36,10,128]{3,0,2,1:T(2,128)S(1)}, f32[2,36,10,128]{3,0,2,1:T(2,128)S(1)}, u32[]{:S(2)}, u32[]{:S(2)}) collective-permute-start(f32[2,36,10,128]{3,0,2,1:T(2,128)S(1)} %copy.31), channel_id=1, source_target_pairs={{0,1},{1,2},{2,3},{3,4},{4,5},{5,6},{6,7},{7,8},{8,9},{9,10},{10,1... | collective-permute-start | bytes 1105928 | tf_op jit(solution)/shard_map/ppermute | solution.py:639
  24.1 7.2 %copy-start.36 = (bf16[512,128]{1,0:T(8,128)(2,1)S(1)}, bf16[512,128]{1,0:T(8,128)(2,1)}, u32[]{:S(2)}) copy-start(bf16[512,128]{1,0:T(8,128)(2,1)} %constant.24.clone.r1) | copy-start | bytes 393220
  24.1 7.2 %copy-start.48 = (bf16[256,128]{1,0:T(8,128)(2,1)S(1)}, bf16[256,128]{1,0:T(8,128)(2,1)}, u32[]{:S(2)}) copy-start(bf16[256,128]{1,0:T(8,128)(2,1)} %constant.31.r0) | copy-start | bytes 196612
  24.2 7.1 %collective-permute-start.3 = (f32[2,36,10,128]{3,0,2,1:T(2,128)S(1)}, f32[2,36,10,128]{3,0,2,1:T(2,128)S(1)}, u32[]{:S(2)}, u32[]{:S(2)}) collective-permute-start(f32[2,36,10,128]{3,0,2,1:T(2,128)S(1)} %copy.32), channel_id=1, source_target_pairs={{0,15},{1,0},{2,1},{3,2},{4,3},{5,4},{6,5},{7,6},{8,7},{9,8},{10,9... | collective-permute-start | bytes 1105928 | tf_op jit(solution)/shard_map/ppermute | solution.py:639
  24.3 18.6 %copy-start.63 = (s32[2]{0:T(128)}, s32[2]{0:T(128)S(1)}, u32[]{:S(2)}) copy-start(s32[2]{0:T(128)S(1)} %pad_add_fusion.pos) | copy-start | bytes 28
  47.5 8.3 %collective-permute-start.4 = (f32[3,4,16,128]{3,2,1,0:T(8,128)}, f32[3,4,16,128]{3,2,1,0:T(8,128)S(1)}, u32[]{:S(2)}, u32[]{:S(2)}) collective-permute-start(f32[3,4,16,128]{3,2,1,0:T(8,128)} %get-tuple-element.29.one), channel_id=1, source_target_pairs={{0,16},{16,32},{32,48},{48,64},{64,80},{80,96},{96,112},{112,128},... | collective-permute-start | bytes 294920 | tf_op jit(solution)/shard_map/ppermute | solution.py:639
  47.5 9.3 %collective-permute-start.5 = (f32[3,4,16,128]{3,2,1,0:T(8,128)}, f32[3,4,16,128]{3,2,1,0:T(8,128)S(1)}, u32[]{:S(2)}, u32[]{:S(2)}) collective-permute-start(f32[3,4,16,128]{3,2,1,0:T(8,128)} %get-tuple-element.29.one), channel_id=1, source_target_pairs={{0,240},{16,0},{32,16},{48,32},{64,48},{80,64},{96,80},{112,96},{1... | collective-permute-start | bytes 294920 | tf_op jit(solution)/shard_map/ppermute | solution.py:639
  52.3 10.1 %all-to-all-start = ((f32[16,2,8,128]{3,2,1,0:T(8,128)}), f32[16,2,8,128]{3,2,1,0:T(8,128)S(1)}, u32[]{:S(2)}, u32[]{:S(2)}) async-start(f32[16,2,8,128]{3,2,1,0:T(8,128)} %copy-done.61), calls=%async_computation | async-start | bytes 262144 | tf_op jit(solution)/shard_map/all_to_all | solution.py:643
  55.8 13.7 %copy-start.64 = (s32[2]{0:T(128)S(1)}, s32[2]{0:T(128)}, u32[]{:S(2)}) copy-start(s32[2]{0:T(128)} %copy-done.63) | copy-start | bytes 28
  55.8 7.7 %copy-start.42 = (f32[3,4,16,128]{3,2,1,0:T(8,128)}, f32[3,4,16,128]{3,2,1,0:T(8,128)S(1)}, u32[]{:S(2)}) copy-start(f32[3,4,16,128]{3,2,1,0:T(8,128)S(1)} %collective-permute-done.4.left) | copy-start | bytes 294916
  56.8 6.7 %copy-start.44 = (f32[3,4,16,128]{3,2,1,0:T(8,128)}, f32[3,4,16,128]{3,2,1,0:T(8,128)S(1)}, u32[]{:S(2)}) copy-start(f32[3,4,16,128]{3,2,1,0:T(8,128)S(1)} %collective-permute-done.5.right) | copy-start | bytes 294916
  62.4 24.3 %copy-start.68 = (s32[16,16]{1,0:T(8,128)S(1)}, s32[16,16]{1,0:T(8,128)}, u32[]{:S(2)}) copy-start(s32[16,16]{1,0:T(8,128)} %param.13) | copy-start | bytes 3076
  63.5 6.0 %collective-permute-start.7 = (f32[68,8,128]{2,1,0:T(8,128)S(1)}, f32[68,8,128]{2,1,0:T(8,128)S(1)}, u32[]{:S(2)}, u32[]{:S(2)}) collective-permute-start(f32[68,8,128]{2,1,0:T(8,128)S(1)} %get-tuple-element.62), channel_id=1, source_target_pairs={{0,15},{1,0},{2,1},{3,2},{4,3},{5,4},{6,5},{7,6},{8,7},{9,8},{10,9... | collective-permute-start | bytes 835592 | tf_op jit(solution)/shard_map/ppermute | solution.py:639
  65.8 3.7 %collective-permute-start.6 = (f32[68,8,128]{2,1,0:T(8,128)S(1)}, f32[68,8,128]{2,1,0:T(8,128)S(1)}, u32[]{:S(2)}, u32[]{:S(2)}) collective-permute-start(f32[68,8,128]{2,1,0:T(8,128)S(1)} %get-tuple-element.63), channel_id=1, source_target_pairs={{0,1},{1,2},{2,3},{3,4},{4,5},{5,6},{6,7},{7,8},{8,9},{9,10},{10,1... | collective-permute-start | bytes 835592 | tf_op jit(solution)/shard_map/ppermute | solution.py:639
  70.4 1.9 copy-start.16
  74.5 24.3 %all-to-all-start.1 = ((f32[16,4,8,128]{3,2,1,0:T(8,128)}), f32[16,4,8,128]{3,2,1,0:T(8,128)}, u32[]{:S(2)}, u32[]{:S(2)}) async-start(f32[16,4,8,128]{3,2,1,0:T(8,128)} %copy-done.50), calls=%async_computation.1 | async-start | bytes 524288 | tf_op jit(solution)/shard_map/all_to_all | solution.py:643
  86.9 8.6 %collective-permute-start.9 = (f32[5,8,128]{2,1,0:T(8,128)S(1)}, f32[5,8,128]{2,1,0:T(8,128)S(1)}, u32[]{:S(2)}, u32[]{:S(2)}) collective-permute-start(f32[5,8,128]{2,1,0:T(8,128)S(1)} %get-tuple-element.32), channel_id=1, source_target_pairs={{0,15},{1,0},{2,1},{3,2},{4,3},{5,4},{6,5},{7,6},{8,7},{9,8},{10,9... | collective-permute-start | bytes 61448 | tf_op jit(solution)/shard_map/ppermute | solution.py:639
  87.0 8.4 %collective-permute-start.8 = (f32[5,8,128]{2,1,0:T(8,128)S(1)}, f32[5,8,128]{2,1,0:T(8,128)S(1)}, u32[]{:S(2)}, u32[]{:S(2)}) collective-permute-start(f32[5,8,128]{2,1,0:T(8,128)S(1)} %get-tuple-element.32), channel_id=1, source_target_pairs={{0,1},{1,2},{2,3},{3,4},{4,5},{5,6},{6,7},{7,8},{8,9},{9,10},{10,1... | collective-permute-start | bytes 61448 | tf_op jit(solution)/shard_map/ppermute | solution.py:639
  88.7 39.2 %copy-start.57 = (f32[32,128]{1,0:T(8,128)}, f32[32,128]{1,0:T(8,128)S(1)}, u32[]{:S(2)}) copy-start(f32[32,128]{1,0:T(8,128)S(1)} %copy.37.owned) | copy-start | bytes 49156
  98.7 1.2 copy-start.1
  100.0 1.2 copy-start.4
  101.2 1.2 copy-start.7
  103.4 1.2 copy-start.21
  112.7 28.1 %copy-start.37 = (bf16[512,128]{1,0:T(8,128)(2,1)S(1)}, bf16[512,128]{1,0:T(8,128)(2,1)}, u32[]{:S(2)}) copy-start(bf16[512,128]{1,0:T(8,128)(2,1)} %constant.24.clone.r1) | copy-start | bytes 393220
  112.7 28.1 %copy-start.65 = (s32[2]{0:T(128)S(1)}, s32[2]{0:T(128)}, u32[]{:S(2)}) copy-start(s32[2]{0:T(128)} %copy-done.63) | copy-start | bytes 28
  129.4 11.4 %copy-start.22 = (f32[12,32,128]{2,1,0:T(8,128)}, f32[12,32,128]{2,1,0:T(8,128)S(1)}, u32[]{:S(2)}) copy-start(f32[12,32,128]{2,1,0:T(8,128)S(1)} %get-tuple-element.43.k1) | copy-start | bytes 589828
  129.4 13.2 %copy-start.24 = (f32[24,56,128]{2,1,0:T(8,128)}, f32[24,56,128]{2,1,0:T(8,128)S(1)}, u32[]{:S(2)}) copy-start(f32[24,56,128]{2,1,0:T(8,128)S(1)} %get-tuple-element.52.r) | copy-start | bytes 2064388
  129.4 13.2 %copy-start.59 = (f32[4,64,128]{2,1,0:T(8,128)}, f32[4,64,128]{2,1,0:T(8,128)S(1)}, u32[]{:S(2)}) copy-start(f32[4,64,128]{2,1,0:T(8,128)S(1)} %get-tuple-element.48.k3) | copy-start | bytes 393220
  129.4 28.4 %copy-start.19 = (f32[16,32,128]{2,1,0:T(8,128)S(1)}, f32[16,32,128]{2,1,0:T(8,128)}, u32[]{:S(2)}) copy-start(f32[16,32,128]{2,1,0:T(8,128)} %copy-done.18) | copy-start | bytes 786436
  129.4 7.8 %collective-permute-start.10 = (f32[4,48,128]{2,1,0:T(8,128)S(1)}, f32[4,48,128]{2,1,0:T(8,128)S(1)}, u32[]{:S(2)}, u32[]{:S(2)}) collective-permute-start(f32[4,48,128]{2,1,0:T(8,128)S(1)} %get-tuple-element.41), channel_id=1, source_target_pairs={{0,16},{16,32},{32,48},{48,64},{64,80},{80,96},{96,112},{112,128},... | collective-permute-start | bytes 294920 | tf_op jit(solution)/shard_map/ppermute | solution.py:639
  129.7 7.5 %collective-permute-start.11 = (f32[4,48,128]{2,1,0:T(8,128)S(1)}, f32[4,48,128]{2,1,0:T(8,128)S(1)}, u32[]{:S(2)}, u32[]{:S(2)}) collective-permute-start(f32[4,48,128]{2,1,0:T(8,128)S(1)} %get-tuple-element.42), channel_id=1, source_target_pairs={{0,240},{16,0},{32,16},{48,32},{64,48},{80,64},{96,80},{112,96},{1... | collective-permute-start | bytes 294920 | tf_op jit(solution)/shard_map/ppermute | solution.py:639
  137.2 3.5 %collective-permute-start.13 = (f32[12,8,128]{2,1,0:T(8,128)S(1)}, f32[12,8,128]{2,1,0:T(8,128)S(1)}, u32[]{:S(2)}, u32[]{:S(2)}) collective-permute-start(f32[12,8,128]{2,1,0:T(8,128)S(1)} %get-tuple-element.64), channel_id=1, source_target_pairs={{0,15},{1,0},{2,1},{3,2},{4,3},{5,4},{6,5},{7,6},{8,7},{9,8},{10,9... | collective-permute-start | bytes 147464 | tf_op jit(solution)/shard_map/ppermute | solution.py:639
  137.7 3.1 %collective-permute-start.12 = (f32[12,8,128]{2,1,0:T(8,128)S(1)}, f32[12,8,128]{2,1,0:T(8,128)S(1)}, u32[]{:S(2)}, u32[]{:S(2)}) collective-permute-start(f32[12,8,128]{2,1,0:T(8,128)S(1)} %get-tuple-element.65), channel_id=1, source_target_pairs={{0,1},{1,2},{2,3},{3,4},{4,5},{5,6},{6,7},{7,8},{8,9},{9,10},{10,1... | collective-permute-start | bytes 147464 | tf_op jit(solution)/shard_map/ppermute | solution.py:639
  144.6 13.2 %all-to-all-start.2 = ((f32[16,1,8,128]{3,2,1,0:T(8,128)}), f32[16,1,8,128]{3,2,1,0:T(8,128)}, u32[]{:S(2)}, u32[]{:S(2)}) async-start(f32[16,1,8,128]{3,2,1,0:T(8,128)} %copy-done.62), calls=%async_computation.2 | async-start | bytes 131072 | tf_op jit(solution)/shard_map/all_to_all | solution.py:643
  157.8 26.9 %copy-start.2 = (f32[36,56,128]{2,1,0:T(8,128)S(1)}, f32[36,56,128]{2,1,0:T(8,128)}, u32[]{:S(2)}) copy-start(f32[36,56,128]{2,1,0:T(8,128)} %copy-done) | copy-start | bytes 3096580
  157.8 26.9 %copy-start.23 = (f32[12,32,128]{2,1,0:T(8,128)S(1)}, f32[12,32,128]{2,1,0:T(8,128)}, u32[]{:S(2)}) copy-start(f32[12,32,128]{2,1,0:T(8,128)} %copy-done.22) | copy-start | bytes 589828
  157.8 26.9 %copy-start.27 = (bf16[4,128,128]{2,1,0:T(8,128)(2,1)S(1)}, bf16[4,128,128]{2,1,0:T(8,128)(2,1)}, u32[]{:S(2)}) copy-start(bf16[4,128,128]{2,1,0:T(8,128)(2,1)} %constant.30.clone.t2) | copy-start | bytes 393220
  157.8 26.9 %copy-start.29 = (bf16[128,512]{1,0:T(8,128)(2,1)S(1)}, bf16[128,512]{1,0:T(8,128)(2,1)}, u32[]{:S(2)}) copy-start(bf16[128,512]{1,0:T(8,128)(2,1)} %constant.29.clone.t3) | copy-start | bytes 393220
  157.8 26.9 %copy-start.31 = (bf16[128,512]{1,0:T(8,128)(2,1)S(1)}, bf16[128,512]{1,0:T(8,128)(2,1)}, u32[]{:S(2)}) copy-start(bf16[128,512]{1,0:T(8,128)(2,1)} %constant.28.clone.t1) | copy-start | bytes 393220
  157.8 26.9 %copy-start.33 = (bf16[512,128]{1,0:T(8,128)(2,1)S(1)}, bf16[512,128]{1,0:T(8,128)(2,1)}, u32[]{:S(2)}) copy-start(bf16[512,128]{1,0:T(8,128)(2,1)} %constant.26.clone.r3) | copy-start | bytes 393220
  158.8 6.1 %collective-permute-start.15 = (f32[40,8,128]{2,1,0:T(8,128)S(1)}, f32[40,8,128]{2,1,0:T(8,128)S(1)}, u32[]{:S(2)}, u32[]{:S(2)}) collective-permute-start(f32[40,8,128]{2,1,0:T(8,128)S(1)} %get-tuple-element.58), channel_id=1, source_target_pairs={{0,15},{1,0},{2,1},{3,2},{4,3},{5,4},{6,5},{7,6},{8,7},{9,8},{10,9... | collective-permute-start | bytes 491528 | tf_op jit(solution)/shard_map/ppermute | solution.py:639
  161.9 3.0 %collective-permute-start.14 = (f32[40,8,128]{2,1,0:T(8,128)S(1)}, f32[40,8,128]{2,1,0:T(8,128)S(1)}, u32[]{:S(2)}, u32[]{:S(2)}) collective-permute-start(f32[40,8,128]{2,1,0:T(8,128)S(1)} %get-tuple-element.59), channel_id=1, source_target_pairs={{0,1},{1,2},{2,3},{3,4},{4,5},{5,6},{6,7},{7,8},{8,9},{9,10},{10,1... | collective-permute-start | bytes 491528 | tf_op jit(solution)/shard_map/ppermute | solution.py:639
  184.7 1.2 copy-start.5
  (40 other events, 34.6 us)

commit v4 on v3

--- a/solution.py
+++ b/solution.py
@@ -2,7 +2,6 @@
 
 import jax
 import jax.numpy as jnp
-import numpy as np
 from jax import lax
 from jax.experimental import pallas as pl
 from jax.experimental.pallas import tpu as pltpu
@@ -16,7 +15,7 @@
 HY = 12
 PX, RY = TX + 2 * HX, TY + 2 * HY
 CHUNK = 4
-VMEM_BYTES = 24 * 1024 * 1024
+VMEM_BYTES = 56 * 1024 * 1024
 
 
 def cheb_steps(degree, lower):
@@ -36,22 +35,27 @@
 COARSE = cheb_steps(24, 0.05)
 
 
-def lane_map(z):
-    groups = 128 // z
-    out = np.zeros((4, 128, 128), np.float32)
-    for q in range(4):
-        for lane in range(128):
-            cell = (lane // z + groups * q) // 2
-            out[q, lane, cell * (z // 2) + (lane % z) // 2] = 1.0
-    return out
-
-
-def restrict_map(z):
-    return jnp.asarray(lane_map(z).reshape(512, 128), BF16)
-
-
-def prolong_map(z):
-    return jnp.asarray(np.concatenate([m.T for m in lane_map(z)], axis=1), BF16)
+def lane_match(z, q, source, target):
+    cell = (source // z + (128 // z) * q) // 2
+    return jnp.where(cell * (z // 2) + (source % z) // 2 == target, 1.0, 0.0).astype(BF16)
+
+
+def restrict_map(z, planes=(0, 4)):
+    shape = ((planes[1] - planes[0]) * 128, 128)
+    row = lax.broadcasted_iota(jnp.int32, shape, 0)
+    return lane_match(z, planes[0] + row // 128, row % 128, lanes(shape))
+
+
+def prolong_map(z, planes=(0, 4)):
+    shape = (128, (planes[1] - planes[0]) * 128)
+    column = lanes(shape)
+    target = lax.broadcasted_iota(jnp.int32, shape, 0)
+    return lane_match(z, planes[0] + column // 128, column % 128, target)
+
+
+def prolong_one(z, q):
+    shape = (128, 128)
+    return lane_match(z, q, lanes(shape), lax.broadcasted_iota(jnp.int32, shape, 0))
 
 
 def pair_dot(value, matrix):
@@ -218,8 +222,8 @@
     dst[:, HY + TY : RY - 2, :] = above
 
 
-def down_kernel(pos, tile, left, right, below, above, ktile, r0, r1, bx, x, wx, wy, wz, s, rd, one, two, *scratch):
-    kx, d, rs, b1s, x1s, k1s = scratch
+def down_kernel(pos, tile, left, right, below, above, ktile, one, two, *refs):
+    given, (bx, x, wx, wy, wz, s, rd), (kx, d, rs, b1s, x1s, k1s, sems) = refs[:7], refs[7:14], refs[14:]
     gx, gy = pos[0], pos[1]
     inside_at = insider(RY, gx * TX - HX, gy * TY - HY)
     fill_top(bx, tile[...], left[0], right[0], below[0], above[0])
@@ -240,18 +244,22 @@
         x[at] = v
 
     build_top(kx, wx, wy, wz, s, rd, 0, PX, inside_at, begin)
+    keeping = moves((bx, x, wx, wy, wz, s, rd), given, sems)
+    for move in keeping[:1] + keeping[2:]:
+        move.start()
     for keep, gain in steps:
         sweep_top(x, wx, wy, wz, s, 2, PX - 2, advance_top(keep, gain, bx, 0, rd, d, x))
 
     def residual(p, at, v, av):
         d[at] = bx[at] - av
 
+    keeping[1].start()
     sweep_top(x, wx, wy, wz, s, 4, PX - 4, residual)
 
     def coarse(src):
         for c in range(16):
             rs[c] = src[2 + 2 * c] + src[3 + 2 * c]
-        return pair_planes(rs, 8, 4, 24, r0)
+        return pair_planes(rs, 8, 4, 24)
 
     for p in (2, 3, PX - 4, PX - 3):
         d[p] = jnp.zeros((RY, 128), F32)
@@ -265,22 +273,29 @@
     for number, src in enumerate((b1s, x1s, k1s)):
         one[number] = src[2:6, 4:20, :]
     b1s[...] = remain(x1, b1, level, 64)
-    send_all(two, coarse_tile((b1s, k1s), 2, 4, r1))
-
-
-def pair_planes(rs, planes, start, rows, r0):
+    send_all(two, coarse_tile((b1s, k1s), 2, 4))
+    for move in keeping:
+        move.wait()
+
+
+def moves(sources, targets, sems):
+    return [pltpu.make_async_copy(a, b, sems.at[i]) for i, (a, b) in enumerate(zip(sources, targets))]
+
+
+def pair_planes(rs, planes, start, rows):
     flat = [
         jnp.concatenate([pair_rows(rs, 2 * c, start, rows), pair_rows(rs, 2 * c + 1, start, rows)], axis=1)
         for c in range(planes)
     ]
-    return (0.125 * pair_dot(jnp.concatenate(flat, axis=0), r0[...])).reshape(planes, rows, 128)
-
-
-def coarse_tile(sources, plane, row, r1):
+    out = 0.125 * pair_dot(jnp.concatenate(flat, axis=0), restrict_map(128, (1, 3)))
+    return out.reshape(planes, rows, 128)
+
+
+def coarse_tile(sources, plane, row):
     flat = [
         jnp.concatenate([pair_rows(src, plane + q, row, 8) for q in range(4)], axis=1) for src in sources
     ]
-    out = 0.125 * pair_dot(jnp.concatenate(flat, axis=0), r1[...])
+    out = 0.125 * pair_dot(jnp.concatenate(flat, axis=0), restrict_map(64))
     return out.reshape(len(sources), 8, 128)
 
 
@@ -307,28 +322,29 @@
     return advance
 
 
-def call(kernel, outs, scratch, *args, flops=1e7):
-    specs = [pl.BlockSpec(memory_space=pltpu.SMEM)]
-    specs += [pl.BlockSpec(memory_space=pltpu.VMEM)] * (len(args) - 1)
+def call(kernel, outs, scratch, *args, far_in=0, far_out=0, copies=0):
+    near, far = pl.BlockSpec(memory_space=pltpu.VMEM), pl.BlockSpec(memory_space=pl.ANY)
+    specs = [pl.BlockSpec(memory_space=pltpu.SMEM)] + [near] * (len(args) - 1 - far_in) + [far] * far_in
     return pl.pallas_call(
         kernel,
         out_shape=[jax.ShapeDtypeStruct(o, F32) for o in outs],
         in_specs=specs,
-        out_specs=[pl.BlockSpec(memory_space=pltpu.VMEM)] * len(outs),
-        scratch_shapes=[pltpu.VMEM(o, F32) for o in scratch],
+        out_specs=[near] * (len(outs) - far_out) + [far] * far_out,
+        scratch_shapes=[pltpu.VMEM(o, F32) for o in scratch]
+        + ([pltpu.SemaphoreType.DMA((copies,))] if copies else []),
         compiler_params=pltpu.CompilerParams(vmem_limit_bytes=VMEM_BYTES),
-        cost_estimate=pl.CostEstimate(flops=int(flops), bytes_accessed=8 << 20, transcendentals=0),
+        cost_estimate=pl.CostEstimate(flops=10**7, bytes_accessed=8 << 20, transcendentals=0),
     )(*args)
 
 
 def go_down(*args):
     top = (PX, RY, 128)
-    outs = [top] * 7 + [(3, 4, 16, 128), (16, 2, 8, 128)]
-    scratch = [top] * 2 + [(16, RY, 128)] + [(8, 24, 128)] * 3
-    return call(down_kernel, outs, scratch, *args)
-
-
-def one_kernel(pos, mid, left, right, below, above, k1, r1, bout, xout, two, res):
+    outs = [(3, 4, 16, 128), (16, 2, 8, 128)] + [top] * 7
+    scratch = [top] * 9 + [(16, RY, 128)] + [(8, 24, 128)] * 3
+    return call(down_kernel, outs, scratch, *args, far_out=7, copies=7)
+
+
+def one_kernel(pos, mid, left, right, below, above, k1, bout, xout, two, res):
     gx, gy = pos[0], pos[1]
     fill_one(bout, left[:, 0:16], mid[...], right[:, 0:16], below[...], above[...])
     b = bout[...]
@@ -337,7 +353,7 @@
     x = smooth(None, b, level, 64)
     xout[...] = x
     res[...] = remain(x, b, level, 64)
-    send_all(two, coarse_tile((res,), 4, 8, r1))
+    send_all(two, coarse_tile((res,), 4, 8))
 
 
 def fill_one(dst, left, tile, right, below, above):
@@ -355,12 +371,12 @@
 
 def mid_kernel(first, pos, mid, below, above, *refs):
     if first:
-        r2, near, three, k2, x2 = refs[:5]
-        scratch = refs[5:]
+        near, three, k2 = refs[:3]
+        scratch = refs[3:]
     else:
-        k2, r2, near, three = refs[:4]
-        scratch = refs[4:]
-    hold, rs, cs = scratch
+        k2, near, three = refs[:3]
+        scratch = refs[3:]
+    hold, rs, cs, edge = scratch
     gx, gy = pos[0], pos[1]
     shape = (16, 24, 128)
     inside = within(shape, 0, gy * 8 - 8, 32, 64, 128)
@@ -393,13 +409,18 @@
             near[number, i] = jnp.where(ok, hold[number, from_plane], 0.0)
 
     if first:
-        x2[...] = near[1, :, 8:16, :]
+        for i in range(5):
+            edge[0, i : i + 1, :] = near[1, i, 9:10, :]
+            edge[1, i : i + 1, :] = near[1, i, 14:15, :]
+        upper = lax.rem(gy + 1, 16)
+        for g in range(16):
+            three[g, 4] = jnp.where(upper == g, edge[0], edge[1])
 
     def coarse(src, out):
         flat = [
             jnp.concatenate([pair_rows(src, 4 * c + q, 4, 8) for q in range(4)], axis=1) for c in range(4)
         ]
-        cs[...] = (0.125 * pair_dot(jnp.concatenate(flat, axis=0), r2[...])).reshape(4, 8, 128)
+        cs[...] = (0.125 * pair_dot(jnp.concatenate(flat, axis=0), restrict_map(32))).reshape(4, 8, 128)
         for c in range(4):
             part = cs[c, 2:6, :]
             for g in range(16):
@@ -410,11 +431,11 @@
         coarse(k2, 2)
 
 
-def go_mid(first, pos, mid, below, above, k2, r2):
-    outs = [(7, 5, 24, 128), (16, 4 if first else 2, 8, 128)]
-    outs += [(16, 24, 128), (5, 8, 128)] if first else []
-    scratch = [(7, 16, 24, 128), (16, 24, 128), (4, 8, 128)]
-    args = (mid, below, above) + (() if first else (k2,)) + (r2,)
+def go_mid(first, pos, mid, below, above, k2):
+    outs = [(7, 5, 24, 128), (16, 5 if first else 2, 8, 128)]
+    outs += [(16, 24, 128)] if first else []
+    scratch = [(7, 16, 24, 128), (16, 24, 128), (4, 8, 128), (2, 8, 128)]
+    args = (mid, below, above) + (() if first else (k2,))
     return call(functools.partial(mid_kernel, first), outs, scratch, pos, *args)
 
 
@@ -461,7 +482,7 @@
             dst[c, 4 * g : 4 * g + 4, :] = part
 
 
-def solve_three(b_ref, k_ref, owned, s3, r3, t3):
+def solve_three(b_ref, k_ref, owned, s3):
     shape = (4, 64, 128)
     plane = lax.broadcasted_iota(jnp.int32, shape, 0)
     row = lax.broadcasted_iota(jnp.int32, shape, 1)
@@ -474,27 +495,27 @@
     flat = [
         jnp.concatenate([pair_rows(src, q, 0, 32) for q in range(4)], axis=1) for src in (s3, k_ref)
     ]
-    fine = 0.125 * pair_dot(jnp.concatenate(flat, axis=0), r3[...])
+    fine = 0.125 * pair_dot(jnp.concatenate(flat, axis=0), restrict_map(16))
     last = solve_last(fine[:32], fine[32:], owned[...])
-    back = pair_dot(last, t3[...])
+    back = pair_dot(last, prolong_map(16))
     for q in range(4):
         spread_rows(s3, q, 0, back[:, 128 * q : 128 * q + 128])
     s3[...] = smooth(x + s3[...], b, level, 16)
 
 
-def rise_two(gx, gy, near, x2, s3, t2, e2, s2):
+def rise_two(gx, gy, near, x2, s3, e2, s2):
     for i in range(5):
         at = jnp.clip(gx - 2 + i, 0, 15)
-        spread_rows(e2, i, 8, pair_dot(s3[at // 4], t2[at % 4]))
+        spread_rows(e2, i, 8, pair_dot(s3[at // 4], prolong_one(32, at % 4)))
     e = e2[:, pl.ds(pl.multiple_of(gy * 8, 8), 24), :]
     level = tuple(near[number] for number in range(2, 7))
     x = jnp.where(level[4] > 0.0, x2 + e, 0.0)
     s2[...] = smooth(x, near[0], level, 32)
 
 
-def rise_one(x1, b1, k1, inside, s2, t1, s1):
+def rise_one(x1, b1, k1, inside, s2, s1):
     flat = jnp.concatenate([s2[i, 4:20, :] for i in range(1, 4)], axis=0)
-    back = pair_dot(flat, t1[...])
+    back = pair_dot(flat, prolong_map(64))
     for i in range(3):
         for q in range(4):
             spread_rows(s1, 4 * i + q, 0, back[16 * i : 16 * i + 16, 128 * q : 128 * q + 128])
@@ -502,9 +523,9 @@
     s1[...] = smooth(jnp.where(inside, x1 + s1[...], 0.0), b1, level, 64)
 
 
-def spread_one(s1, low, high, t0, e0):
+def spread_one(s1, low, high, e0):
     flat = jnp.concatenate([s1[i, 4:28, :] for i in range(low, high)], axis=0)
-    back = pair_dot(flat, t0[...])
+    back = pair_dot(flat, prolong_map(128, (1, 3)))
     for i in range(high - low):
         for q in range(2):
             part = back[24 * i : 24 * i + 24, 128 * q : 128 * q + 128]
@@ -527,27 +548,41 @@
 
 
 def turn_kernel(
-    pos, owned, three, near, x2low, x2high, one, left, right, below, above, b0, x0, wx, wy, wz, s, rd, r0, r3, t3, t2, t1, t0,
-    k3, k1, xout, rout, x0n, b1n, east, west,
-    b3, s3, e2, s2, x2s, b1s, s1, e0, d, x, rs
+    pos, owned, three, near, one, left, right, below, above, *refs
 ):
     gx, gy = pos[0], pos[1]
+    fars, (x0n, b1n, east, west, *far_outs) = refs[:7], refs[7:15]
+    b3, s3, e2, s2, x2s, b1s, s1, e0, d, x, rs, xout, rout, k3, k1 = refs[15:30]
+    tops, sems = refs[30:37], refs[37]
+    b0, x0, wx, wy, wz, s, rd = tops
+    loads = moves(fars, tops, sems)
+    for move in loads:
+        move.start()
+    xkeep, rkeep, kkeep, k1keep = (
+        pltpu.make_async_copy(a, b, sems.at[7 + i]) for i, (a, b) in enumerate(zip((xout, rout, k3, k1), far_outs))
+    )
     fill_three(b3, three, 0)
     fill_three(k3, three, 2)
-    solve_three(b3, k3, owned, s3, r3, t3)
-    x2s[:, 0:8, :] = x2low[...]
-    x2s[:, 8:16, :] = near[1, :, 8:16, :]
-    x2s[:, 16:24, :] = x2high[...]
-    rise_two(gx, gy, near, x2s[...], s3, t2, e2, s2)
+    kkeep.start()
+    solve_three(b3, k3, owned, s3)
+    x2s[...] = near[1]
+    lower, upper = lax.rem(gy + 15, 16), lax.rem(gy + 1, 16)
+    for i in range(5):
+        x2s[i, 1:2, :] = three[lower, 4, i : i + 1, :]
+        x2s[i, 22:23, :] = three[upper, 4, i : i + 1, :]
+    rise_two(gx, gy, near, x2s[...], s3, e2, s2)
 
     inside = within((12, 32, 128), gx * 8 - 8, gy * 16 - 8, 64, 128, 256)
     for number, dst in enumerate((b1s, s1, k1)):
         part = slice(32 + 12 * number, 44 + 12 * number)
         fill_one(dst, left[number], one[number], right[number], below[part], above[part])
     k1[...] = jnp.where(inside, k1[...], 0.0)
-    rise_one(s1[...], b1s[...], k1[...], inside, s2, t1, s1)
-
-    spread_one(s1, 2, 10, t0, e0)
+    k1keep.start()
+    rise_one(s1[...], b1s[...], k1[...], inside, s2, s1)
+
+    spread_one(s1, 2, 10, e0)
+    for move in loads:
+        move.wait()
     add_top(x0, e0, rd, x, 2, PX - 2)
     start, steps = SMOOTH
     sweep_top(x, wx, wy, wz, s, 4, PX - 4, open_top(b0, 0, rd, d, x))
@@ -559,6 +594,8 @@
 
     sweep_top(x, wx, wy, wz, s, 6, PX - 6, residual)
     xout[...] = x[9 : PX - 9]
+    xkeep.start()
+    rkeep.start()
 
     def begin(i, _):
         at = pl.ds(6 + i * CHUNK, CHUNK)
@@ -578,34 +615,41 @@
     x0n[...] = x[HX : HX + TX, HY : HY + TY, :]
     for c in range(8):
         rs[c] = d[HX + 2 * c] + d[HX + 1 + 2 * c]
-    b1 = pair_planes(rs, 4, HY, 16, r0)
+    b1 = pair_planes(rs, 4, HY, 16)
     b1n[...] = b1
     for side, plane in ((east, HX + TX - 4), (west, HX)):
         side[:, 0:16, :] = b1
         side[:, 16:48, :] = x[plane : plane + 4, HY : HY + TY, :]
+    for move in (xkeep, rkeep, kkeep, k1keep):
+        move.wait()
 
 
 def go_turn(*args):
-    top, wide = (PX, RY, 128), (12, 32, 128)
-    outs = [(4, 64, 128), wide, (TX + 2, RY, 128), (TX + 8, RY, 128), (TX, TY, 128), (4, 16, 128)]
-    outs += [(4, 48, 128)] * 2
-    scratch = [(4, 64, 128)] * 2 + [(5, 144, 128), (5, 24, 128), (5, 24, 128), wide, wide, (16, RY, 128)]
-    return call(turn_kernel, outs, scratch + [top] * 2 + [(8, RY, 128)], *args)
+    top, wide, three = (PX, RY, 128), (12, 32, 128), (4, 64, 128)
+    kept = [(TX + 2, RY, 128), (TX + 8, RY, 128), three, wide]
+    outs = [(TX, TY, 128), (4, 16, 128), (4, 48, 128), (4, 48, 128)] + kept
+    scratch = [three] * 2 + [(5, 144, 128), (5, 24, 128), (5, 24, 128), wide, wide, (16, RY, 128)]
+    scratch += [top] * 2 + [(8, RY, 128)] + kept + [top] * 7
+    return call(turn_kernel, outs, scratch, *args, far_in=7, far_out=4, copies=11)
 
 
 def last_kernel(
-    pos, owned, three, k3, near, b1, x1, k1, x0n, left, right, below, above, r, xbefore,
-    b0, wx, wy, wz, s, rd, r3, t3, t2, t1, t0, xout, rout,
-    b3, s3, e2, s2, s1, e0, d, x
+    pos, owned, three, k3, near, b1, x1, k1, x0n, left, right, below, above, *refs
 ):
     gx, gy = pos[0], pos[1]
+    fars, (xout, rout), (b3, s3, e2, s2, s1, e0, d, x) = refs[:8], refs[8:10], refs[10:18]
+    tops, sems = refs[18:26], refs[26]
+    r, xbefore, b0, wx, wy, wz, s, rd = tops
+    loads = moves(fars, tops, sems)
+    for move in loads:
+        move.start()
     fill_three(b3, three, 0)
-    solve_three(b3, k3, owned, s3, r3, t3)
-    rise_two(gx, gy, near, near[1], s3, t2, e2, s2)
+    solve_three(b3, k3, owned, s3)
+    rise_two(gx, gy, near, near[1], s3, e2, s2)
     inside = within((12, 32, 128), gx * 8 - 8, gy * 16 - 8, 64, 128, 256)
-    rise_one(x1[...], b1[...], k1[...], inside, s2, t1, s1)
-
-    spread_one(s1, 3, 9, t0, e0)
+    rise_one(x1[...], b1[...], k1[...], inside, s2, s1)
+
+    spread_one(s1, 3, 9, e0)
     low, high = HX - 4, HX + TX + 4
     x[low:HX, HY : HY + TY, :] = left[:, 16:48, :]
     x[HX : HX + TX, HY : HY + TY, :] = x0n[...]
@@ -614,6 +658,8 @@
     x[low:high, HY + TY : HY + TY + 8, :] = above[16:40]
     x[low:high, 0 : HY - 8, :] = jnp.zeros((high - low, HY - 8, 128), F32)
     x[low:high, RY - 4 : RY, :] = jnp.zeros((high - low, 4, 128), F32)
+    for move in loads:
+        move.wait()
     add_top(x, e0, rd, x, low, high)
     sweep_top(x, wx, wy, wz, s, low, high, open_top(r, low, rd, d, x))
     for keep, gain in SMOOTH[1]:
@@ -630,8 +676,9 @@
 
 def go_last(*args):
     top, wide, tile = (PX, RY, 128), (12, 32, 128), (TX, TY, 128)
-    scratch = [(4, 64, 128)] * 2 + [(5, 144, 128), (5, 24, 128), wide, (16, RY, 128)]
-    return call(last_kernel, [tile, tile], scratch + [top] * 2, *args)
+    scratch = [(4, 64, 128)] * 2 + [(5, 144, 128), (5, 24, 128), wide, (16, RY, 128)] + [top] * 2
+    scratch += [(TX + 8, RY, 128), (TX + 2, RY, 128)] + [top] * 6
+    return call(last_kernel, [tile, tile], scratch, *args, far_in=8, copies=8)
 
 
 def shift(value, axis, step):
@@ -646,20 +693,13 @@
 def local(right_side, kappa, owners):
     pos = jnp.stack([lax.axis_index("gx"), lax.axis_index("gy")]).astype(jnp.int32)
     owned = jnp.repeat(jnp.repeat(owners.T, 2, 0), 8, 1).astype(F32)
-    r0 = restrict_map(128)[128:384]
-    r1, r2, r3 = restrict_map(64), restrict_map(32), restrict_map(16)
-    t0 = prolong_map(128)[:, 128:384]
-    t1, t3 = prolong_map(64), prolong_map(16)
-    t2 = jnp.asarray(np.transpose(lane_map(32), (0, 2, 1)), BF16)
-
     mid = jnp.stack([right_side, kappa])
     left = shift(mid[:, TX - HX :], "gx", 1)
     right = shift(mid[:, :HX], "gx", -1)
     wide = jnp.concatenate([left, mid, right], axis=1)
     below = shift(wide[:, :, TY - HX :], "gy", 1)
     above = shift(wide[:, :, :HX], "gy", -1)
-    b0, x0, wx, wy, wz, s, rd, one, two = go_down(pos, right_side, left, right, below, above, kappa, r0, r1)
-    top = (wx, wy, wz, s, rd)
+    one, two, b0, x0, *top = go_down(pos, right_side, left, right, below, above, kappa)
     left = shift(one, "gx", 1)
     right = shift(one, "gx", -1)
     two = gather(two, "gx")
@@ -667,13 +707,10 @@
     wide = jnp.concatenate([left, one, right], axis=1)
     below = shift(jnp.concatenate([rows, wide[:, :, 8:].reshape(-1, 8, 128)]), "gy", 1)
     above = shift(jnp.concatenate([rows, wide[:, :, :8].reshape(-1, 8, 128)]), "gy", -1)
-    near, three, k2, x2 = go_mid(True, pos, two, below, above, None, r2)
-    x2low = shift(x2, "gy", 1)
-    x2high = shift(x2, "gy", -1)
+    near, three, k2 = go_mid(True, pos, two, below, above, None)
     three = gather(three, "gy")
-    k3, k1, xbefore, source, x0n, b1n, east, west = go_turn(
-        pos, owned, three, near, x2low, x2high, one, left, right, below, above, b0, x0, *top,
-        r0, r3, t3, t2, t1, t0
+    x0n, b1n, east, west, xbefore, source, k3, k1 = go_turn(
+        pos, owned, three, near, one, left, right, below, above, b0, x0, *top
     )
 
     left = shift(east, "gx", 1)
@@ -681,16 +718,15 @@
     wide = jnp.concatenate([left[:, :16], b1n, right[:, :16]])
     below = shift(wide[:, 8:], "gy", 1)
     above = shift(wide[:, :8], "gy", -1)
-    b1, x1, two = go_one(pos, b1n, left, right, below, above, k1, r1)
+    b1, x1, two = go_one(pos, b1n, left, right, below, above, k1)
     two = gather(two, "gx")
     wide = jnp.concatenate([left[:, 16:], x0n, right[:, 16:]])
     below = shift(jnp.concatenate([two[:, 0], wide[:, 24:]]), "gy", 1)
     above = shift(jnp.concatenate([two[:, 0], wide[:, :8]]), "gy", -1)
-    near, three = go_mid(False, pos, two, below, above, k2, r2)
+    near, three = go_mid(False, pos, two, below, above, k2)
     three = gather(three, "gy")
     field, residual = go_last(
-        pos, owned, three, k3, near, b1, x1, k1, x0n, left, right, below, above, source, xbefore, b0,
-        *top, r3, t3, t2, t1, t0
+        pos, owned, three, k3, near, b1, x1, k1, x0n, left, right, below, above, source, xbefore, b0, *top
     )
     return field, residual
 

time: 207 us -> 185 us (0.89)
  local copies, waits for them, and re-layouts: 44.6 us -> 10.2 us
  Pallas kernels: 40.9 us -> 55.1 us
  starting transfers between devices: 50.1 us -> 47.2 us
    unnamed x140 -> x40, local copies, waits for them, and re-layouts: 41.6 us -> 5.09 us
    pallas_call x6, Pallas kernels: 40.9 us -> 55.1 us  [call(): pl.pallas_call(kernel, out_shape=[jax.ShapeDtypeStruct(o, F32) for o in o...]
    all_to_all x3, waiting for transfers between devices: 13.5 us -> 22.7 us  [gather(): return lax.all_to_all(copies, axis, 0, 0, tiled=True)]
    ppermute x16 -> x14, waiting for transfers between devices: 36.7 us -> 29.1 us  [shift(): lax.ppermute(value, axis, [(i, (i + step) % count) for i in range(count)])]
    ppermute x16 -> x14, starting transfers between devices: 27.8 us -> 26.9 us  [shift(): lax.ppermute(value, axis, [(i, (i + step) % count) for i in range(count)])]
  transfers between devices with their start and end apart: 19 -> 17, of which waited for: 12 -> 11; matrix products, arithmetic and copies ran while one was open for 2% -> 3% of each run, Pallas kernels for 0% -> 0%
where the time goes in v4:
time: 185 us; the launch traced here: 184 us
  Pallas kernels  55.1 us (30%)
  waiting for transfers between devices  51.8 us (28%)
  starting transfers between devices  47.2 us (26%)
  blocking collectives  16.1 us (9%)
  local copies, waits for them, and re-layouts  10.2 us (6%)
  other arithmetic  2.75 us (1%)
    pallas_call x6, Pallas kernels, call(): pl.pallas_call(kernel, out_shape=[jax.ShapeDtypeStruct(o, F32) for o in o...  55.1 us
    ppermute x14, waiting for transfers between devices, shift(): lax.ppermute(value, axis, [(i, (i + step) % count) for i in range(count)])  29.1 us
    ppermute x14, starting transfers between devices, shift(): lax.ppermute(value, axis, [(i, (i + step) % count) for i in range(count)])  26.9 us
    all_to_all x3, waiting for transfers between devices, gather(): return lax.all_to_all(copies, axis, 0, 0, tiled=True)  22.7 us
    all_to_all x3, starting transfers between devices, gather(): return lax.all_to_all(copies, axis, 0, 0, tiled=True)  20.3 us
    all_to_all x1, blocking collectives, gather(): return lax.all_to_all(copies, axis, 0, 0, tiled=True)  16.1 us
    unnamed x40, local copies, waits for them, and re-layouts  5.09 us
  transfers between devices with their start and end apart: 17, of which 11 were waited for; matrix products, arithmetic and copies ran while one was open for 3% of the time, Pallas kernels for 0%

profile of v4, /device:TPU:1, one launch (start us, length us, event | category | flops | bytes accessed | tf_op | source)
XLA Modules:
  0.0 184.3 jit_solution(18384123846450115534)
XLA Ops:
  0.7 1.3 pad_maximum_fusion.3
  1.9 5.8 %collective-permute-start.1 = (f32[2,10,32,128]{3,2,1,0:T(8,128)S(1)}, f32[2,10,32,128]{3,2,1,0:T(8,128)S(1)}, u32[]{:S(2)}, u32[]{:S(2)}) collective-permute-start(f32[2,10,32,128]{3,2,1,0:T(8,128)S(1)} %get-tuple-element.54), channel_id=1, source_target_pairs={{0,240},{16,0},{32,16},{48,32},{64,48},{80,64},{96,80},{112,96},{1... | collective-permute-start | bytes 983048 | tf_op jit(solution)/shard_map/ppermute | solution.py:686
  7.7 6.4 %collective-permute-done.1.right = f32[2,10,32,128]{3,2,1,0:T(8,128)S(1)} collective-permute-done((f32[2,10,32,128]{3,2,1,0:T(8,128)S(1)}, f32[2,10,32,128]{3,2,1,0:T(8,128)S(1)}, u32[]{:S(2)}, u32[]{:S(2)}) %collective-permute-start.1) | collective-permute-done | bytes 327712 | tf_op jit(solution)/shard_map/ppermute | solution.py:686
  14.1 5.2 %collective-permute-done.left = f32[2,10,32,128]{3,2,1,0:T(8,128)S(1)} collective-permute-done((f32[2,10,32,128]{3,2,1,0:T(8,128)S(1)}, f32[2,10,32,128]{3,2,1,0:T(8,128)S(1)}, u32[]{:S(2)}, u32[]{:S(2)}) %collective-permute-start) | collective-permute-done | bytes 327712 | tf_op jit(solution)/shard_map/ppermute | solution.py:686
  19.4 0.7 copy-done.4
  20.1 0.1 fusion.1
  20.2 0.3 copy.23
  20.5 3.4 %collective-permute-start.2 = (f32[2,36,10,128]{3,0,2,1:T(2,128)S(1)}, f32[2,36,10,128]{3,0,2,1:T(2,128)S(1)}, u32[]{:S(2)}, u32[]{:S(2)}) collective-permute-start(f32[2,36,10,128]{3,0,2,1:T(2,128)S(1)} %copy.23), channel_id=1, source_target_pairs={{0,1},{1,2},{2,3},{3,4},{4,5},{5,6},{6,7},{7,8},{8,9},{9,10},{10,1... | collective-permute-start | bytes 1105928 | tf_op jit(solution)/shard_map/ppermute | solution.py:686
  23.9 0.3 copy.24
  24.2 0.6 pad_add_fusion.pos
  24.8 3.6 %collective-permute-done.2 = f32[2,36,10,128]{3,0,2,1:T(2,128)S(1)} collective-permute-done((f32[2,36,10,128]{3,0,2,1:T(2,128)S(1)}, f32[2,36,10,128]{3,0,2,1:T(2,128)S(1)}, u32[]{:S(2)}, u32[]{:S(2)}) %collective-permute-start.2) | collective-permute-done | bytes 368672 | tf_op jit(solution)/shard_map/ppermute | solution.py:686
  28.3 0.9 copy.25.below
  29.3 2.0 %collective-permute-done.3 = f32[2,36,10,128]{3,0,2,1:T(2,128)S(1)} collective-permute-done((f32[2,36,10,128]{3,0,2,1:T(2,128)S(1)}, f32[2,36,10,128]{3,0,2,1:T(2,128)S(1)}, u32[]{:S(2)}, u32[]{:S(2)}) %collective-permute-start.3) | collective-permute-done | bytes 368672 | tf_op jit(solution)/shard_map/ppermute | solution.py:686
  31.3 0.9 copy.26.above
  32.2 9.9 %shard_map.50 = (f32[3,4,16,128]{3,2,1,0:T(8,128)}, f32[16,2,8,128]{3,2,1,0:T(8,128)}, f32[36,56,128]{2,1,0:T(8,128)}, f32[36,56,128]{2,1,0:T(8,128)}, f32[36,56...) custom-call(s32[2]{0:T(128)} %pad_add_fusion.pos, ...), custom_call_target="tpu_custom_call" | custom-call | flops 10000000 | bytes 8388608 | tf_op jit(solution)/shard_map/pallas_call | solution.py:328
  42.2 4.8 %collective-permute-start.5 = (f32[3,4,16,128]{3,2,1,0:T(8,128)}, f32[3,4,16,128]{3,2,1,0:T(8,128)S(1)}, u32[]{:S(2)}, u32[]{:S(2)}) collective-permute-start(f32[3,4,16,128]{3,2,1,0:T(8,128)} %get-tuple-element.28.one), channel_id=1, source_target_pairs={{0,240},{16,0},{32,16},{48,32},{64,48},{80,64},{96,80},{112,96},{1... | collective-permute-start | bytes 294920 | tf_op jit(solution)/shard_map/ppermute | solution.py:686
  47.0 3.5 %all-to-all-start = ((f32[16,2,8,128]{3,2,1,0:T(8,128)}), f32[16,2,8,128]{3,2,1,0:T(8,128)S(1)}, u32[]{:S(2)}, u32[]{:S(2)}) async-start(f32[16,2,8,128]{3,2,1,0:T(8,128)} %get-tuple-element.27), calls=%async_computation | async-start | bytes 262144 | tf_op jit(solution)/shard_map/all_to_all | solution.py:690
  50.5 0.9 constant_dynamic-update-slice_fusion.1
  51.5 5.7 %all-to-all-done.mid = f32[16,2,8,128]{3,2,1,0:T(8,128)S(1)} async-done(((f32[16,2,8,128]{3,2,1,0:T(8,128)}), f32[16,2,8,128]{3,2,1,0:T(8,128)S(1)}, u32[]{:S(2)}, u32[]{:S(2)}) %all-to-all-start) | async-done | bytes 131104 | tf_op jit(solution)/shard_map/all_to_all | solution.py:690
  57.3 2.9 %collective-permute-start.7 = (f32[68,8,128]{2,1,0:T(8,128)S(1)}, f32[68,8,128]{2,1,0:T(8,128)S(1)}, u32[]{:S(2)}, u32[]{:S(2)}) collective-permute-start(f32[68,8,128]{2,1,0:T(8,128)S(1)} %get-tuple-element.60), channel_id=1, source_target_pairs={{0,15},{1,0},{2,1},{3,2},{4,3},{5,4},{6,5},{7,6},{8,7},{9,8},{10,9... | collective-permute-start | bytes 835592 | tf_op jit(solution)/shard_map/ppermute | solution.py:686
  60.3 3.9 %collective-permute-done.7.above = f32[68,8,128]{2,1,0:T(8,128)S(1)} collective-permute-done((f32[68,8,128]{2,1,0:T(8,128)S(1)}, f32[68,8,128]{2,1,0:T(8,128)S(1)}, u32[]{:S(2)}, u32[]{:S(2)}) %collective-permute-start.7) | collective-permute-done | bytes 278560 | tf_op jit(solution)/shard_map/ppermute | solution.py:686
  64.2 0.7 copy-done.6
  64.9 0.7 copy-done.7
  65.6 3.5 %shard_map.51 = (f32[7,5,24,128]{3,2,1,0:T(8,128)}, f32[16,5,8,128]{3,2,1,0:T(8,128)}, f32[16,24,128]{2,1,0:T(8,128)}) custom-call(s32[2]{0:T(128)} %pad_add_fusion.pos, f32[16,2,8,128]{3,2,1,0:T(8,128)} %copy-done.5, f32[68,8,128]{2,1,0:T(8,128)} %copy-done.7, f32[68,8,128]{2,1,0:T(8,128)} %copy-done.6), custom_call_target="tpu_custom_call" | custom-call | flops 10000000 | bytes 8388608 | tf_op jit(solution)/shard_map/pallas_call | solution.py:328
  69.1 10.6 %all-to-all-start.1 = ((f32[16,5,8,128]{3,2,1,0:T(8,128)}), f32[16,5,8,128]{3,2,1,0:T(8,128)S(1)}, u32[]{:S(2)}, u32[]{:S(2)}) async-start(f32[16,5,8,128]{3,2,1,0:T(8,128)} %get-tuple-element.29), calls=%async_computation.1 | async-start | bytes 655360 | tf_op jit(solution)/shard_map/all_to_all | solution.py:690
  79.8 0.7 copy.29.owned
  80.5 12.2 %all-to-all-done.1.three = f32[16,5,8,128]{3,2,1,0:T(8,128)S(1)} async-done(((f32[16,5,8,128]{3,2,1,0:T(8,128)}), f32[16,5,8,128]{3,2,1,0:T(8,128)S(1)}, u32[]{:S(2)}, u32[]{:S(2)}) %all-to-all-start.1) | async-done | bytes 327712 | tf_op jit(solution)/shard_map/all_to_all | solution.py:690
  92.7 0.7 copy-done.2
  93.4 19.8 %shard_map.52 = (f32[16,32,128]{2,1,0:T(8,128)}, f32[4,16,128]{2,1,0:T(8,128)}, f32[4,48,128]{2,1,0:T(8,128)}, f32[4,48,128]{2,1,0:T(8,128)}, f32[18,56,128]{2,1...) custom-call(s32[2]{0:T(128)} %pad_add_fusion.pos, f32[32,128]{1,0:T(8,128)} %copy.29.owned, ...), custom_call_target="tpu_custom_call" | custom-call | flops 10000000 | bytes 8388608 | tf_op jit(solution)/shard_map/pallas_call | solution.py:328
  113.2 0.3 collective-permute-start.8
  113.5 4.6 %collective-permute-start.9 = (f32[4,48,128]{2,1,0:T(8,128)}, f32[4,48,128]{2,1,0:T(8,128)S(1)}, u32[]{:S(2)}, u32[]{:S(2)}) collective-permute-start(f32[4,48,128]{2,1,0:T(8,128)} %get-tuple-element.40), channel_id=1, source_target_pairs={{0,240},{16,0},{32,16},{48,32},{64,48},{80,64},{96,80},{112,96},{1... | collective-permute-start | bytes 294920 | tf_op jit(solution)/shard_map/ppermute | solution.py:686
  118.1 3.3 %collective-permute-done.8.left = f32[4,48,128]{2,1,0:T(8,128)S(1)} collective-permute-done((f32[4,48,128]{2,1,0:T(8,128)}, f32[4,48,128]{2,1,0:T(8,128)S(1)}, u32[]{:S(2)}, u32[]{:S(2)}) %collective-permute-start.8) | collective-permute-done | bytes 98336 | tf_op jit(solution)/shard_map/ppermute | solution.py:686
  121.4 0.8 pad_maximum_fusion.10
  122.2 0.4 collective-permute-start.11
  122.6 1.4 collective-permute-start.10
  124.0 1.8 collective-permute-done.11.above
  125.8 0.6 copy-done.16
  126.4 3.1 %shard_map.53 = (f32[12,32,128]{2,1,0:T(8,128)}, f32[12,32,128]{2,1,0:T(8,128)}, f32[16,1,8,128]{3,2,1,0:T(8,128)}) custom-call(s32[2]{0:T(128)} %pad_add_fusion.pos, f32[4,16,128]{2,1,0:T(8,128)} %get-tuple-element.38.mid, f32[4,48,128]{2,1,0:T(8,128)} %copy-done.9, f32[4,48,128]{2,1,0:T(8,128)} %copy-done.10, f32[12,8,128]{2,1,0:T(8,128)} %copy-done.17, ...), custom_call_target="tpu_custom_call" | custom-call | flops 10000000 | bytes 8388608 | tf_op jit(solution)/shard_map/pallas_call | solution.py:328
  129.5 6.2 %all-to-all-start.2 = ((f32[16,1,8,128]{3,2,1,0:T(8,128)}), f32[16,1,8,128]{3,2,1,0:T(8,128)S(1)}, u32[]{:S(2)}, u32[]{:S(2)}) async-start(f32[16,1,8,128]{3,2,1,0:T(8,128)} %get-tuple-element.42), calls=%async_computation.2 | async-start | bytes 131072 | tf_op jit(solution)/shard_map/all_to_all | solution.py:690
  135.7 0.9 slice.66
  136.6 0.8 slice.67
  137.4 4.8 %all-to-all-done.2.mid = f32[16,1,8,128]{3,2,1,0:T(8,128)S(1)} async-done(((f32[16,1,8,128]{3,2,1,0:T(8,128)}), f32[16,1,8,128]{3,2,1,0:T(8,128)S(1)}, u32[]{:S(2)}, u32[]{:S(2)}) %all-to-all-start.2) | async-done | bytes 65568 | tf_op jit(solution)/shard_map/all_to_all | solution.py:690
  142.3 3.2 %collective-permute-start.13 = (f32[40,8,128]{2,1,0:T(8,128)S(1)}, f32[40,8,128]{2,1,0:T(8,128)S(1)}, u32[]{:S(2)}, u32[]{:S(2)}) collective-permute-start(f32[40,8,128]{2,1,0:T(8,128)S(1)} %get-tuple-element.56), channel_id=1, source_target_pairs={{0,15},{1,0},{2,1},{3,2},{4,3},{5,4},{6,5},{7,6},{8,7},{9,8},{10,9... | collective-permute-start | bytes 491528 | tf_op jit(solution)/shard_map/ppermute | solution.py:686
  145.5 3.0 %collective-permute-done.13.above = f32[40,8,128]{2,1,0:T(8,128)S(1)} collective-permute-done((f32[40,8,128]{2,1,0:T(8,128)S(1)}, f32[40,8,128]{2,1,0:T(8,128)S(1)}, u32[]{:S(2)}, u32[]{:S(2)}) %collective-permute-start.13) | collective-permute-done | bytes 163872 | tf_op jit(solution)/shard_map/ppermute | solution.py:686
  148.5 0.7 copy-done.11
  149.2 3.3 %shard_map.54 = (f32[7,5,24,128]{3,2,1,0:T(8,128)}, f32[16,2,8,128]{3,2,1,0:T(8,128)}) custom-call(s32[2]{0:T(128)} %pad_add_fusion.pos, f32[16,1,8,128]{3,2,1,0:T(8,128)} %copy-done.13, f32[40,8,128]{2,1,0:T(8,128)} %copy-done.12, f32[40,8,128]{2,1,0:T(8,128)} %copy-done.11, f32[16,24,128]{2,1,0:T(8,128)} %get-tuple-element.44.refs_0_), custom_call_target="tpu_custom_call" | custom-call | flops 10000000 | bytes 8388608 | tf_op jit(solution)/shard_map/pallas_call | solution.py:328
  152.4 16.1 %all_to_all.20.three = f32[16,2,8,128]{3,2,1,0:T(8,128)} all-to-all(f32[16,2,8,128]{3,2,1,0:T(8,128)} %get-tuple-element.45), channel_id=1, replica_groups=mesh['gx'=16,'gy'=16] {'gy'}, dimensions={0} | all-to-all | bytes 262144 | tf_op jit(solution)/shard_map/all_to_all | solution.py:690
  168.6 15.6 %shard_map.55 = (f32[16,32,128]{2,1,0:T(8,128)}, f32[16,32,128]{2,1,0:T(8,128)}) custom-call(s32[2]{0:T(128)} %pad_add_fusion.pos, f32[32,128]{1,0:T(8,128)} %copy.29.owned, f32[16,2,8,128]{3,2,1,0:T(8,128)} %all_to_all.20.three, f32[4,64,128]{2,1,0:T(8,128)} %get-tuple-element.46.k3, f32[7,5,24,128]{3,2,1,0:T(8,128)} %get-tuple-element.47.near, ...), custom_call_target="tpu_custom_call" | custom-call | flops 10000000 | bytes 8388608 | tf_op jit(solution)/shard_map/pallas_call | solution.py:328
  (58 shorter events, 0.6 us)
Async XLA Ops:
  0.6 18.7 %copy-start.1 = (f32[16,32,128]{2,1,0:T(8,128)S(1)}, f32[16,32,128]{2,1,0:T(8,128)}, u32[]{:S(2)}) copy-start(f32[16,32,128]{2,1,0:T(8,128)} %ktile.1) | copy-start | bytes 786436
  0.6 18.7 %copy-start = (f32[16,32,128]{2,1,0:T(8,128)S(1)}, f32[16,32,128]{2,1,0:T(8,128)}, u32[]{:S(2)}) copy-start(f32[16,32,128]{2,1,0:T(8,128)} %tile.1) | copy-start | bytes 786436
  1.9 12.2 %collective-permute-start.1 = (f32[2,10,32,128]{3,2,1,0:T(8,128)S(1)}, f32[2,10,32,128]{3,2,1,0:T(8,128)S(1)}, u32[]{:S(2)}, u32[]{:S(2)}) collective-permute-start(f32[2,10,32,128]{3,2,1,0:T(8,128)S(1)} %get-tuple-element.54), channel_id=1, source_target_pairs={{0,240},{16,0},{32,16},{48,32},{64,48},{80,64},{96,80},{112,96},{1... | collective-permute-start | bytes 983048 | tf_op jit(solution)/shard_map/ppermute | solution.py:686
  7.7 11.6 %collective-permute-start = (f32[2,10,32,128]{3,2,1,0:T(8,128)S(1)}, f32[2,10,32,128]{3,2,1,0:T(8,128)S(1)}, u32[]{:S(2)}, u32[]{:S(2)}) collective-permute-start(f32[2,10,32,128]{3,2,1,0:T(8,128)S(1)} %get-tuple-element.55), channel_id=1, source_target_pairs={{0,16},{16,32},{32,48},{48,64},{64,80},{80,96},{96,112},{112,128},... | collective-permute-start | bytes 983048 | tf_op jit(solution)/shard_map/ppermute | solution.py:686
  14.1 5.3 %copy-start.3 = (f32[2,10,32,128]{3,2,1,0:T(8,128)}, f32[2,10,32,128]{3,2,1,0:T(8,128)S(1)}, u32[]{:S(2)}) copy-start(f32[2,10,32,128]{3,2,1,0:T(8,128)S(1)} %collective-permute-done.1.right) | copy-start | bytes 983044
  19.3 0.8 copy-start.4
  20.5 7.9 %collective-permute-start.2 = (f32[2,36,10,128]{3,0,2,1:T(2,128)S(1)}, f32[2,36,10,128]{3,0,2,1:T(2,128)S(1)}, u32[]{:S(2)}, u32[]{:S(2)}) collective-permute-start(f32[2,36,10,128]{3,0,2,1:T(2,128)S(1)} %copy.23), channel_id=1, source_target_pairs={{0,1},{1,2},{2,3},{3,4},{4,5},{5,6},{6,7},{7,8},{8,9},{9,10},{10,1... | collective-permute-start | bytes 1105928 | tf_op jit(solution)/shard_map/ppermute | solution.py:686
  24.2 7.1 %collective-permute-start.3 = (f32[2,36,10,128]{3,0,2,1:T(2,128)S(1)}, f32[2,36,10,128]{3,0,2,1:T(2,128)S(1)}, u32[]{:S(2)}, u32[]{:S(2)}) collective-permute-start(f32[2,36,10,128]{3,0,2,1:T(2,128)S(1)} %copy.24), channel_id=1, source_target_pairs={{0,15},{1,0},{2,1},{3,2},{4,3},{5,4},{6,5},{7,6},{8,7},{9,8},{10,9... | collective-permute-start | bytes 1105928 | tf_op jit(solution)/shard_map/ppermute | solution.py:686
  42.1 8.4 %collective-permute-start.4 = (f32[3,4,16,128]{3,2,1,0:T(8,128)}, f32[3,4,16,128]{3,2,1,0:T(8,128)S(1)}, u32[]{:S(2)}, u32[]{:S(2)}) collective-permute-start(f32[3,4,16,128]{3,2,1,0:T(8,128)} %get-tuple-element.28.one), channel_id=1, source_target_pairs={{0,16},{16,32},{32,48},{48,64},{64,80},{80,96},{96,112},{112,128},... | collective-permute-start | bytes 294920 | tf_op jit(solution)/shard_map/ppermute | solution.py:686
  42.2 9.3 %collective-permute-start.5 = (f32[3,4,16,128]{3,2,1,0:T(8,128)}, f32[3,4,16,128]{3,2,1,0:T(8,128)S(1)}, u32[]{:S(2)}, u32[]{:S(2)}) collective-permute-start(f32[3,4,16,128]{3,2,1,0:T(8,128)} %get-tuple-element.28.one), channel_id=1, source_target_pairs={{0,240},{16,0},{32,16},{48,32},{64,48},{80,64},{96,80},{112,96},{1... | collective-permute-start | bytes 294920 | tf_op jit(solution)/shard_map/ppermute | solution.py:686
  47.0 10.2 %all-to-all-start = ((f32[16,2,8,128]{3,2,1,0:T(8,128)}), f32[16,2,8,128]{3,2,1,0:T(8,128)S(1)}, u32[]{:S(2)}, u32[]{:S(2)}) async-start(f32[16,2,8,128]{3,2,1,0:T(8,128)} %get-tuple-element.27), calls=%async_computation | async-start | bytes 262144 | tf_op jit(solution)/shard_map/all_to_all | solution.py:690
  50.5 6.8 %copy-start.14 = (f32[3,4,16,128]{3,2,1,0:T(8,128)}, f32[3,4,16,128]{3,2,1,0:T(8,128)S(1)}, u32[]{:S(2)}) copy-start(f32[3,4,16,128]{3,2,1,0:T(8,128)S(1)} %collective-permute-done.4.left) | copy-start | bytes 294916
  51.5 17.6 %copy-start.15 = (f32[3,4,16,128]{3,2,1,0:T(8,128)}, f32[3,4,16,128]{3,2,1,0:T(8,128)S(1)}, u32[]{:S(2)}) copy-start(f32[3,4,16,128]{3,2,1,0:T(8,128)S(1)} %collective-permute-done.5.right) | copy-start | bytes 294916
  57.2 6.9 %copy-start.5 = (f32[16,2,8,128]{3,2,1,0:T(8,128)}, f32[16,2,8,128]{3,2,1,0:T(8,128)S(1)}, u32[]{:S(2)}) copy-start(f32[16,2,8,128]{3,2,1,0:T(8,128)S(1)} %all-to-all-done.mid) | copy-start | bytes 393220
  57.3 22.4 %copy-start.18 = (s32[16,16]{1,0:T(8,128)S(1)}, s32[16,16]{1,0:T(8,128)}, u32[]{:S(2)}) copy-start(s32[16,16]{1,0:T(8,128)} %param.5) | copy-start | bytes 3076
  57.3 6.8 %collective-permute-start.7 = (f32[68,8,128]{2,1,0:T(8,128)S(1)}, f32[68,8,128]{2,1,0:T(8,128)S(1)}, u32[]{:S(2)}, u32[]{:S(2)}) collective-permute-start(f32[68,8,128]{2,1,0:T(8,128)S(1)} %get-tuple-element.60), channel_id=1, source_target_pairs={{0,15},{1,0},{2,1},{3,2},{4,3},{5,4},{6,5},{7,6},{8,7},{9,8},{10,9... | collective-permute-start | bytes 835592 | tf_op jit(solution)/shard_map/ppermute | solution.py:686
  60.3 3.9 %collective-permute-start.6 = (f32[68,8,128]{2,1,0:T(8,128)S(1)}, f32[68,8,128]{2,1,0:T(8,128)S(1)}, u32[]{:S(2)}, u32[]{:S(2)}) collective-permute-start(f32[68,8,128]{2,1,0:T(8,128)S(1)} %get-tuple-element.61), channel_id=1, source_target_pairs={{0,1},{1,2},{2,3},{3,4},{4,5},{5,6},{6,7},{7,8},{8,9},{9,10},{10,1... | collective-permute-start | bytes 835592 | tf_op jit(solution)/shard_map/ppermute | solution.py:686
  64.2 0.7 copy-start.6
  64.8 0.7 copy-start.7
  69.1 23.6 %all-to-all-start.1 = ((f32[16,5,8,128]{3,2,1,0:T(8,128)}), f32[16,5,8,128]{3,2,1,0:T(8,128)S(1)}, u32[]{:S(2)}, u32[]{:S(2)}) async-start(f32[16,5,8,128]{3,2,1,0:T(8,128)} %get-tuple-element.29), calls=%async_computation.1 | async-start | bytes 655360 | tf_op jit(solution)/shard_map/all_to_all | solution.py:690
  92.7 0.7 copy-start.2
  113.2 29.0 %copy-start.8 = (f32[16,32,128]{2,1,0:T(8,128)S(1)}, f32[16,32,128]{2,1,0:T(8,128)}, u32[]{:S(2)}) copy-start(f32[16,32,128]{2,1,0:T(8,128)} %get-tuple-element.43.x0n) | copy-start | bytes 786436
  113.2 8.2 %collective-permute-start.8 = (f32[4,48,128]{2,1,0:T(8,128)}, f32[4,48,128]{2,1,0:T(8,128)S(1)}, u32[]{:S(2)}, u32[]{:S(2)}) collective-permute-start(f32[4,48,128]{2,1,0:T(8,128)} %get-tuple-element.39), channel_id=1, source_target_pairs={{0,16},{16,32},{32,48},{48,64},{64,80},{80,96},{96,112},{112,128},... | collective-permute-start | bytes 294920 | tf_op jit(solution)/shard_map/ppermute | solution.py:686
  113.5 7.9 %collective-permute-start.9 = (f32[4,48,128]{2,1,0:T(8,128)}, f32[4,48,128]{2,1,0:T(8,128)S(1)}, u32[]{:S(2)}, u32[]{:S(2)}) collective-permute-start(f32[4,48,128]{2,1,0:T(8,128)} %get-tuple-element.40), channel_id=1, source_target_pairs={{0,240},{16,0},{32,16},{48,32},{64,48},{80,64},{96,80},{112,96},{1... | collective-permute-start | bytes 294920 | tf_op jit(solution)/shard_map/ppermute | solution.py:686
  121.4 4.4 %copy-start.9 = (f32[4,48,128]{2,1,0:T(8,128)}, f32[4,48,128]{2,1,0:T(8,128)S(1)}, u32[]{:S(2)}) copy-start(f32[4,48,128]{2,1,0:T(8,128)S(1)} %collective-permute-done.8.left) | copy-start | bytes 294916
  121.4 4.4 %copy-start.10 = (f32[4,48,128]{2,1,0:T(8,128)}, f32[4,48,128]{2,1,0:T(8,128)S(1)}, u32[]{:S(2)}) copy-start(f32[4,48,128]{2,1,0:T(8,128)S(1)} %collective-permute-done.9.right) | copy-start | bytes 294916
  122.2 3.5 %collective-permute-start.11 = (f32[12,8,128]{2,1,0:T(8,128)S(1)}, f32[12,8,128]{2,1,0:T(8,128)S(1)}, u32[]{:S(2)}, u32[]{:S(2)}) collective-permute-start(f32[12,8,128]{2,1,0:T(8,128)S(1)} %get-tuple-element.62), channel_id=1, source_target_pairs={{0,15},{1,0},{2,1},{3,2},{4,3},{5,4},{6,5},{7,6},{8,7},{9,8},{10,9... | collective-permute-start | bytes 147464 | tf_op jit(solution)/shard_map/ppermute | solution.py:686
  122.6 3.1 %collective-permute-start.10 = (f32[12,8,128]{2,1,0:T(8,128)S(1)}, f32[12,8,128]{2,1,0:T(8,128)S(1)}, u32[]{:S(2)}, u32[]{:S(2)}) collective-permute-start(f32[12,8,128]{2,1,0:T(8,128)S(1)} %get-tuple-element.63), channel_id=1, source_target_pairs={{0,1},{1,2},{2,3},{3,4},{4,5},{5,6},{6,7},{7,8},{8,9},{9,10},{10,1... | collective-permute-start | bytes 147464 | tf_op jit(solution)/shard_map/ppermute | solution.py:686
  125.8 0.6 copy-start.16
  125.8 0.6 copy-start.17
  129.5 12.7 %all-to-all-start.2 = ((f32[16,1,8,128]{3,2,1,0:T(8,128)}), f32[16,1,8,128]{3,2,1,0:T(8,128)S(1)}, u32[]{:S(2)}, u32[]{:S(2)}) async-start(f32[16,1,8,128]{3,2,1,0:T(8,128)} %get-tuple-element.42), calls=%async_computation.2 | async-start | bytes 131072 | tf_op jit(solution)/shard_map/all_to_all | solution.py:690
  142.2 6.2 %copy-start.13 = (f32[16,1,8,128]{3,2,1,0:T(8,128)}, f32[16,1,8,128]{3,2,1,0:T(8,128)S(1)}, u32[]{:S(2)}) copy-start(f32[16,1,8,128]{3,2,1,0:T(8,128)S(1)} %all-to-all-done.2.mid) | copy-start | bytes 196612
  142.3 6.2 %collective-permute-start.13 = (f32[40,8,128]{2,1,0:T(8,128)S(1)}, f32[40,8,128]{2,1,0:T(8,128)S(1)}, u32[]{:S(2)}, u32[]{:S(2)}) collective-permute-start(f32[40,8,128]{2,1,0:T(8,128)S(1)} %get-tuple-element.56), channel_id=1, source_target_pairs={{0,15},{1,0},{2,1},{3,2},{4,3},{5,4},{6,5},{7,6},{8,7},{9,8},{10,9... | collective-permute-start | bytes 491528 | tf_op jit(solution)/shard_map/ppermute | solution.py:686
  145.5 3.0 %collective-permute-start.12 = (f32[40,8,128]{2,1,0:T(8,128)S(1)}, f32[40,8,128]{2,1,0:T(8,128)S(1)}, u32[]{:S(2)}, u32[]{:S(2)}) collective-permute-start(f32[40,8,128]{2,1,0:T(8,128)S(1)} %get-tuple-element.57), channel_id=1, source_target_pairs={{0,1},{1,2},{2,3},{3,4},{4,5},{5,6},{6,7},{7,8},{8,9},{9,10},{10,1... | collective-permute-start | bytes 491528 | tf_op jit(solution)/shard_map/ppermute | solution.py:686
  148.4 0.7 copy-start.11
  148.4 0.7 copy-start.12

commit v5 on v4

--- a/solution.py
+++ b/solution.py
@@ -15,6 +15,7 @@
 HY = 12
 PX, RY = TX + 2 * HX, TY + 2 * HY
 CHUNK = 4
+PARTS = 2
 VMEM_BYTES = 56 * 1024 * 1024
 
 
@@ -36,21 +37,23 @@
 
 
 def lane_match(z, q, source, target):
-    cell = (source // z + (128 // z) * q) // 2
-    return jnp.where(cell * (z // 2) + (source % z) // 2 == target, 1.0, 0.0).astype(BF16)
+    bits = z.bit_length() - 1
+    cell = (lax.shift_right_logical(source, bits) + (128 // z) * q) & -2
+    inner = lax.shift_right_logical(source & (z - 1), 1)
+    return jnp.where(cell * (z // 4) + inner == target, 1.0, 0.0).astype(BF16)
 
 
 def restrict_map(z, planes=(0, 4)):
     shape = ((planes[1] - planes[0]) * 128, 128)
     row = lax.broadcasted_iota(jnp.int32, shape, 0)
-    return lane_match(z, planes[0] + row // 128, row % 128, lanes(shape))
+    return lane_match(z, planes[0] + lax.shift_right_logical(row, 7), row & 127, lanes(shape))
 
 
 def prolong_map(z, planes=(0, 4)):
     shape = (128, (planes[1] - planes[0]) * 128)
     column = lanes(shape)
     target = lax.broadcasted_iota(jnp.int32, shape, 0)
-    return lane_match(z, planes[0] + column // 128, column % 128, target)
+    return lane_match(z, planes[0] + lax.shift_right_logical(column, 7), column & 127, target)
 
 
 def prolong_one(z, q):
@@ -59,12 +62,13 @@
 
 
 def pair_dot(value, matrix):
-    high = value.astype(BF16)
-    rest = value - high.astype(F32)
-    mid = rest.astype(BF16)
-    low = (rest - mid.astype(F32)).astype(BF16)
-    dot = functools.partial(jnp.dot, preferred_element_type=F32)
-    return dot(high, matrix) + (dot(mid, matrix) + dot(low, matrix))
+    rows = value.shape[0]
+    high = value.astype(BF16).astype(F32)
+    rest = value - high
+    mid = rest.astype(BF16).astype(F32)
+    parts = jnp.concatenate([high, mid, rest - mid], axis=0).astype(BF16)
+    out = jnp.dot(parts, matrix, preferred_element_type=F32)
+    return out[:rows] + (out[rows : 2 * rows] + out[2 * rows :])
 
 
 def lanes(shape):
@@ -144,7 +148,7 @@
 
 def within(shape, first_x, first_y, z, size_x, size_y):
     plane = lax.broadcasted_iota(jnp.int32, shape, 0)
-    cx = first_x + plane * (128 // z) + lanes(shape) // z
+    cx = first_x + plane * (128 // z) + lax.shift_right_logical(lanes(shape), z.bit_length() - 1)
     cy = first_y + lax.broadcasted_iota(jnp.int32, shape, 1)
     return (cx >= 0) & (cx < size_x) & (cy >= 0) & (cy < size_y)
 
@@ -193,13 +197,14 @@
 
 
 def sweep_top(x, wx, wy, wz, s, low, high, body):
+    size = (high - low) // PARTS
     fx0 = wx[low - 1 : low] * (x[low : low + 1] - x[low - 1 : low])
 
     def step(i, fxp):
-        p = low + i * CHUNK
-        at = pl.ds(p, CHUNK)
+        p = low + i * size
+        at = pl.ds(p, size)
         v = x[at]
-        vn = jnp.concatenate([v[1:], x[pl.ds(p + CHUNK, 1)]], axis=0)
+        vn = jnp.concatenate([v[1:], x[pl.ds(p + size, 1)]], axis=0)
         fx = wx[at] * (vn - v)
         fy = wy[at] * (turn(v, -1, 1) - v)
         fz = wz[at] * (turn(v, -1, 2) - v)
@@ -208,8 +213,8 @@
         body(p, at, v, s[at] * v - total)
         return fx[-1:]
 
-    assert (high - low) % CHUNK == 0
-    lax.fori_loop(0, (high - low) // CHUNK, step, fx0)
+    assert (high - low) % PARTS == 0
+    lax.fori_loop(0, PARTS, step, fx0, unroll=True)
 
 
 def fill_top(dst, tile, left, right, below, above):
@@ -223,7 +228,8 @@
 
 
 def down_kernel(pos, tile, left, right, below, above, ktile, one, two, *refs):
-    given, (bx, x, wx, wy, wz, s, rd), (kx, d, rs, b1s, x1s, k1s, sems) = refs[:7], refs[7:14], refs[14:]
+    given, (bx, kx, x, wx, wy, wz, s, rd, d, rs, b1s, x1s, k1s, sems) = refs[:3], refs[3:]
+    keeping = moves((bx, kx, x), given, sems)
     gx, gy = pos[0], pos[1]
     inside_at = insider(RY, gx * TX - HX, gy * TY - HY)
     fill_top(bx, tile[...], left[0], right[0], below[0], above[0])
@@ -235,6 +241,8 @@
         return 0
 
     lax.fori_loop(0, PX // CHUNK, clear, 0)
+    for move in keeping[:2]:
+        move.start()
     start, steps = SMOOTH
 
     def begin(p, rdv):
@@ -244,16 +252,13 @@
         x[at] = v
 
     build_top(kx, wx, wy, wz, s, rd, 0, PX, inside_at, begin)
-    keeping = moves((bx, x, wx, wy, wz, s, rd), given, sems)
-    for move in keeping[:1] + keeping[2:]:
-        move.start()
     for keep, gain in steps:
         sweep_top(x, wx, wy, wz, s, 2, PX - 2, advance_top(keep, gain, bx, 0, rd, d, x))
 
     def residual(p, at, v, av):
         d[at] = bx[at] - av
 
-    keeping[1].start()
+    keeping[2].start()
     sweep_top(x, wx, wy, wz, s, 4, PX - 4, residual)
 
     def coarse(src):
@@ -306,7 +311,7 @@
 
 def advance_top(keep, gain, b, shift_b, rd, d, x):
     def advance(p, at, v, av):
-        dv = keep * d[at] + gain * ((b[pl.ds(p - shift_b, CHUNK)] - av) * rd[at])
+        dv = keep * d[at] + gain * ((b[pl.ds(p - shift_b, v.shape[0])] - av) * rd[at])
         d[at] = dv
         x[at] = v + dv
 
@@ -315,7 +320,7 @@
 
 def open_top(b, shift_b, rd, d, x):
     def advance(p, at, v, av):
-        dv = ((b[pl.ds(p - shift_b, CHUNK)] - av) * rd[at]) * SMOOTH[0]
+        dv = ((b[pl.ds(p - shift_b, v.shape[0])] - av) * rd[at]) * SMOOTH[0]
         d[at] = dv
         x[at] = v + dv
 
@@ -339,9 +344,9 @@
 
 def go_down(*args):
     top = (PX, RY, 128)
-    outs = [(3, 4, 16, 128), (16, 2, 8, 128)] + [top] * 7
+    outs = [(3, 4, 16, 128), (16, 2, 8, 128)] + [top] * 3
     scratch = [top] * 9 + [(16, RY, 128)] + [(8, 24, 128)] * 3
-    return call(down_kernel, outs, scratch, *args, far_out=7, copies=7)
+    return call(down_kernel, outs, scratch, *args, far_out=3, copies=3)
 
 
 def one_kernel(pos, mid, left, right, below, above, k1, bout, xout, two, res):
@@ -399,13 +404,13 @@
     level = build(k, 0.25**2, 32, inside, edge_x)
     x = smooth(None, b, level, 32)
     rs[...] = remain(x, b, level, 32)
-    for number, value in enumerate((b, x) + level):
+    for number, value in enumerate((b, x, k)):
         hold[number] = value
     for i in range(5):
         at = gx - 2 + i
         ok = (at >= 0) & (at < 16)
         from_plane = jnp.clip(at, 0, 15)
-        for number in range(7):
+        for number in range(3):
             near[number, i] = jnp.where(ok, hold[number, from_plane], 0.0)
 
     if first:
@@ -432,9 +437,9 @@
 
 
 def go_mid(first, pos, mid, below, above, k2):
-    outs = [(7, 5, 24, 128), (16, 5 if first else 2, 8, 128)]
+    outs = [(3, 5, 24, 128), (16, 5 if first else 2, 8, 128)]
     outs += [(16, 24, 128)] if first else []
-    scratch = [(7, 16, 24, 128), (16, 24, 128), (4, 8, 128), (2, 8, 128)]
+    scratch = [(3, 16, 24, 128), (16, 24, 128), (4, 8, 128), (2, 8, 128)]
     args = (mid, below, above) + (() if first else (k2,))
     return call(functools.partial(mid_kernel, first), outs, scratch, pos, *args)
 
@@ -491,26 +496,29 @@
     level = build(k_ref[...], 0.25**3, 16, None, edge_x, (row == 0, row == 63))
     b = b_ref[...]
     x = smooth(None, b, level, 16)
-    s3[...] = remain(x, b, level, 16)
+    s3[:, 8:72, :] = remain(x, b, level, 16)
     flat = [
-        jnp.concatenate([pair_rows(src, q, 0, 32) for q in range(4)], axis=1) for src in (s3, k_ref)
+        jnp.concatenate([pair_rows(src, q, row0, 32) for q in range(4)], axis=1) for src, row0 in ((s3, 8), (k_ref, 0))
     ]
     fine = 0.125 * pair_dot(jnp.concatenate(flat, axis=0), restrict_map(16))
     last = solve_last(fine[:32], fine[32:], owned[...])
     back = pair_dot(last, prolong_map(16))
     for q in range(4):
-        spread_rows(s3, q, 0, back[:, 128 * q : 128 * q + 128])
-    s3[...] = smooth(x + s3[...], b, level, 16)
+        spread_rows(s3, q, 8, back[:, 128 * q : 128 * q + 128])
+    s3[:, 8:72, :] = smooth(x + s3[:, 8:72, :], b, level, 16)
 
 
 def rise_two(gx, gy, near, x2, s3, e2, s2):
+    pair = lax.shift_right_logical(gy + 1, 1)
+    rows = pl.ds(pl.multiple_of(pair * 8, 8), 24)
     for i in range(5):
         at = jnp.clip(gx - 2 + i, 0, 15)
-        spread_rows(e2, i, 8, pair_dot(s3[at // 4], prolong_one(32, at % 4)))
-    e = e2[:, pl.ds(pl.multiple_of(gy * 8, 8), 24), :]
-    level = tuple(near[number] for number in range(2, 7))
-    x = jnp.where(level[4] > 0.0, x2 + e, 0.0)
-    s2[...] = smooth(x, near[0], level, 32)
+        spread_rows(e2, i, 0, pair_dot(s3[at // 4, rows, :], prolong_one(32, at % 4)))
+    e = e2[:, pl.ds(pl.multiple_of((gy + 1 - 2 * pair) * 8, 8), 24), :]
+    shape = (5, 24, 128)
+    inside = within(shape, gx * 4 - 8, gy * 8 - 8, 32, 64, 128)
+    level = build(near[2], 0.25**2, 32, inside)
+    s2[...] = smooth(jnp.where(inside, x2 + e, 0.0), near[0], level, 32)
 
 
 def rise_one(x1, b1, k1, inside, s2, s1):
@@ -534,32 +542,30 @@
     e0[:, RY - 4 : RY, :] = jnp.zeros((16, 4, 128), F32)
 
 
-def add_top(x0, e0, rd, x, low, high):
-    def step(i, _):
-        p = low + i * CHUNK
+def add_top(x0, e0, x):
+    def begin(p, rdv):
         c = (p - 2) // 2
         pair = (e0[pl.ds(c, 1)], e0[pl.ds(c + 1, 1)])
         correction = jnp.concatenate([pair[0], pair[0], pair[1], pair[1]], axis=0)
         at = pl.ds(p, CHUNK)
-        x[at] = jnp.where(rd[at] > 0.0, x0[at] + correction, 0.0)
-        return 0
-
-    lax.fori_loop(0, (high - low) // CHUNK, step, 0)
+        x[at] = jnp.where(rdv > 0.0, x0[at] + correction, 0.0)
+
+    return begin
 
 
 def turn_kernel(
     pos, owned, three, near, one, left, right, below, above, *refs
 ):
     gx, gy = pos[0], pos[1]
-    fars, (x0n, b1n, east, west, *far_outs) = refs[:7], refs[7:15]
-    b3, s3, e2, s2, x2s, b1s, s1, e0, d, x, rs, xout, rout, k3, k1 = refs[15:30]
-    tops, sems = refs[30:37], refs[37]
-    b0, x0, wx, wy, wz, s, rd = tops
+    fars, (x0n, b1n, east, west, *far_outs) = refs[:3], refs[3:11]
+    b3, s3, e2, s2, x2s, b1s, s1, e0, d, x, rs, xout, rout, k3, k1 = refs[11:26]
+    tops, sems = refs[26:29], refs[34]
+    (b0, k0, x0), (wx, wy, wz, s, rd) = tops, refs[29:34]
     loads = moves(fars, tops, sems)
     for move in loads:
         move.start()
     xkeep, rkeep, kkeep, k1keep = (
-        pltpu.make_async_copy(a, b, sems.at[7 + i]) for i, (a, b) in enumerate(zip((xout, rout, k3, k1), far_outs))
+        pltpu.make_async_copy(a, b, sems.at[3 + i]) for i, (a, b) in enumerate(zip((xout, rout, k3, k1), far_outs))
     )
     fill_three(b3, three, 0)
     fill_three(k3, three, 2)
@@ -583,14 +589,15 @@
     spread_one(s1, 2, 10, e0)
     for move in loads:
         move.wait()
-    add_top(x0, e0, rd, x, 2, PX - 2)
+    inside_at = insider(RY, gx * TX - HX, gy * TY - HY)
+    build_top(k0, wx, wy, wz, s, rd, 2, PX - 2, inside_at, add_top(x0, e0, x))
     start, steps = SMOOTH
     sweep_top(x, wx, wy, wz, s, 4, PX - 4, open_top(b0, 0, rd, d, x))
     for (keep, gain), edge in zip(steps, (4, 6)):
         sweep_top(x, wx, wy, wz, s, edge, PX - edge, advance_top(keep, gain, b0, 0, rd, d, x))
 
     def residual(p, at, v, av):
-        rout[pl.ds(p - 6, CHUNK)] = b0[at] - av
+        rout[pl.ds(p - 6, v.shape[0])] = b0[at] - av
 
     sweep_top(x, wx, wy, wz, s, 6, PX - 6, residual)
     xout[...] = x[9 : PX - 9]
@@ -609,7 +616,7 @@
         sweep_top(x, wx, wy, wz, s, 8, PX - 8, advance_top(keep, gain, rout, 6, rd, d, x))
 
     def again(p, at, v, av):
-        d[at] = rout[pl.ds(p - 6, CHUNK)] - av
+        d[at] = rout[pl.ds(p - 6, v.shape[0])] - av
 
     sweep_top(x, wx, wy, wz, s, HX, HX + TX, again)
     x0n[...] = x[HX : HX + TX, HY : HY + TY, :]
@@ -628,18 +635,18 @@
     top, wide, three = (PX, RY, 128), (12, 32, 128), (4, 64, 128)
     kept = [(TX + 2, RY, 128), (TX + 8, RY, 128), three, wide]
     outs = [(TX, TY, 128), (4, 16, 128), (4, 48, 128), (4, 48, 128)] + kept
-    scratch = [three] * 2 + [(5, 144, 128), (5, 24, 128), (5, 24, 128), wide, wide, (16, RY, 128)]
-    scratch += [top] * 2 + [(8, RY, 128)] + kept + [top] * 7
-    return call(turn_kernel, outs, scratch, *args, far_in=7, far_out=4, copies=11)
+    scratch = [three, (4, 88, 128), (5, 48, 128), (5, 24, 128), (5, 24, 128), wide, wide, (16, RY, 128)]
+    scratch += [top] * 2 + [(8, RY, 128)] + kept + [top] * 8
+    return call(turn_kernel, outs, scratch, *args, far_in=3, far_out=4, copies=7)
 
 
 def last_kernel(
-    pos, owned, three, k3, near, b1, x1, k1, x0n, left, right, below, above, *refs
+    pos, owned, three, k3, near, b1, x1, k1, x0n, left, right, below, above, borig, *refs
 ):
     gx, gy = pos[0], pos[1]
-    fars, (xout, rout), (b3, s3, e2, s2, s1, e0, d, x) = refs[:8], refs[8:10], refs[10:18]
-    tops, sems = refs[18:26], refs[26]
-    r, xbefore, b0, wx, wy, wz, s, rd = tops
+    fars, (xout, rout), (b3, s3, e2, s2, s1, e0, d, x) = refs[:3], refs[3:5], refs[5:13]
+    tops, sems = refs[13:16], refs[21]
+    (r, xbefore, k0), (wx, wy, wz, s, rd) = tops, refs[16:21]
     loads = moves(fars, tops, sems)
     for move in loads:
         move.start()
@@ -660,25 +667,26 @@
     x[low:high, RY - 4 : RY, :] = jnp.zeros((high - low, 4, 128), F32)
     for move in loads:
         move.wait()
-    add_top(x, e0, rd, x, low, high)
+    inside_at = insider(RY, gx * TX - HX, gy * TY - HY)
+    build_top(k0, wx, wy, wz, s, rd, low, high, inside_at, add_top(x, e0, x))
     sweep_top(x, wx, wy, wz, s, low, high, open_top(r, low, rd, d, x))
     for keep, gain in SMOOTH[1]:
         sweep_top(x, wx, wy, wz, s, 8, PX - 8, advance_top(keep, gain, r, low, rd, d, x))
     x[9 : PX - 9] = x[9 : PX - 9] + xbefore[...]
 
     def residual(p, at, v, av):
-        d[at] = b0[at] - av
+        d[at] = av
 
     sweep_top(x, wx, wy, wz, s, HX, HX + TX, residual)
     xout[...] = x[HX : HX + TX, HY : HY + TY, :]
-    rout[...] = d[HX : HX + TX, HY : HY + TY, :]
+    rout[...] = borig[...] - d[HX : HX + TX, HY : HY + TY, :]
 
 
 def go_last(*args):
     top, wide, tile = (PX, RY, 128), (12, 32, 128), (TX, TY, 128)
-    scratch = [(4, 64, 128)] * 2 + [(5, 144, 128), (5, 24, 128), wide, (16, RY, 128)] + [top] * 2
+    scratch = [(4, 64, 128), (4, 88, 128), (5, 48, 128), (5, 24, 128), wide, (16, RY, 128)] + [top] * 2
     scratch += [(TX + 8, RY, 128), (TX + 2, RY, 128)] + [top] * 6
-    return call(last_kernel, [tile, tile], scratch, *args, far_in=8, copies=8)
+    return call(last_kernel, [tile, tile], scratch, *args, far_in=3, copies=3)
 
 
 def shift(value, axis, step):
@@ -699,7 +707,7 @@
     wide = jnp.concatenate([left, mid, right], axis=1)
     below = shift(wide[:, :, TY - HX :], "gy", 1)
     above = shift(wide[:, :, :HX], "gy", -1)
-    one, two, b0, x0, *top = go_down(pos, right_side, left, right, below, above, kappa)
+    one, two, b0, k0, x0 = go_down(pos, right_side, left, right, below, above, kappa)
     left = shift(one, "gx", 1)
     right = shift(one, "gx", -1)
     two = gather(two, "gx")
@@ -710,7 +718,7 @@
     near, three, k2 = go_mid(True, pos, two, below, above, None)
     three = gather(three, "gy")
     x0n, b1n, east, west, xbefore, source, k3, k1 = go_turn(
-        pos, owned, three, near, one, left, right, below, above, b0, x0, *top
+        pos, owned, three, near, one, left, right, below, above, b0, k0, x0
     )
 
     left = shift(east, "gx", 1)
@@ -726,7 +734,7 @@
     near, three = go_mid(False, pos, two, below, above, k2)
     three = gather(three, "gy")
     field, residual = go_last(
-        pos, owned, three, k3, near, b1, x1, k1, x0n, left, right, below, above, source, xbefore, b0, *top
+        pos, owned, three, k3, near, b1, x1, k1, x0n, left, right, below, above, right_side, source, xbefore, k0
     )
     return field, residual
 

time: 185 us -> 175 us (0.946)
  Pallas kernels: 55.1 us -> 45.1 us
    pallas_call x6, Pallas kernels: 55.1 us -> 45.1 us  [call(): pl.pallas_call(kernel, out_shape=[jax.ShapeDtypeStruct(o, F32) for o in o...]
where the time goes in v5:
time: 175 us; the launch traced here: 174 us
  waiting for transfers between devices  51.8 us (30%)
  starting transfers between devices  47.1 us (27%)
  Pallas kernels  45.1 us (26%)
  blocking collectives  16.2 us (9%)
  local copies, waits for them, and re-layouts  10.1 us (6%)
  other arithmetic  2.86 us (2%)
    pallas_call x6, Pallas kernels, call(): pl.pallas_call(kernel, out_shape=[jax.ShapeDtypeStruct(o, F32) for o in o...  45.1 us
    ppermute x14, waiting for transfers between devices, shift(): lax.ppermute(value, axis, [(i, (i + step) % count) for i in range(count)])  29.1 us
    ppermute x14, starting transfers between devices, shift(): lax.ppermute(value, axis, [(i, (i + step) % count) for i in range(count)])  26.9 us
    all_to_all x3, waiting for transfers between devices, gather(): return lax.all_to_all(copies, axis, 0, 0, tiled=True)  22.7 us
    all_to_all x3, starting transfers between devices, gather(): return lax.all_to_all(copies, axis, 0, 0, tiled=True)  20.2 us
    all_to_all x1, blocking collectives, gather(): return lax.all_to_all(copies, axis, 0, 0, tiled=True)  16.2 us
    unnamed x40, local copies, waits for them, and re-layouts  5.09 us
  transfers between devices with their start and end apart: 17, of which 11 were waited for; matrix products, arithmetic and copies ran while one was open for 3% of the time, Pallas kernels for 0%

profile of v5, /device:TPU:1, one launch (start us, length us, event | category | flops | bytes accessed | tf_op | source)
XLA Modules:
  0.0 174.2 jit_solution(271219035844561430)
XLA Ops:
  0.7 1.3 pad_maximum_fusion.3
  1.9 5.8 %collective-permute-start.1 = (f32[2,10,32,128]{3,2,1,0:T(8,128)S(1)}, f32[2,10,32,128]{3,2,1,0:T(8,128)S(1)}, u32[]{:S(2)}, u32[]{:S(2)}) collective-permute-start(f32[2,10,32,128]{3,2,1,0:T(8,128)S(1)} %get-tuple-element.46), channel_id=1, source_target_pairs={{0,240},{16,0},{32,16},{48,32},{64,48},{80,64},{96,80},{112,96},{1... | collective-permute-start | bytes 983048 | tf_op jit(solution)/shard_map/ppermute | solution.py:694
  7.7 6.4 %collective-permute-done.1.right = f32[2,10,32,128]{3,2,1,0:T(8,128)S(1)} collective-permute-done((f32[2,10,32,128]{3,2,1,0:T(8,128)S(1)}, f32[2,10,32,128]{3,2,1,0:T(8,128)S(1)}, u32[]{:S(2)}, u32[]{:S(2)}) %collective-permute-start.1) | collective-permute-done | bytes 327712 | tf_op jit(solution)/shard_map/ppermute | solution.py:694
  14.1 5.2 %collective-permute-done.left = f32[2,10,32,128]{3,2,1,0:T(8,128)S(1)} collective-permute-done((f32[2,10,32,128]{3,2,1,0:T(8,128)S(1)}, f32[2,10,32,128]{3,2,1,0:T(8,128)S(1)}, u32[]{:S(2)}, u32[]{:S(2)}) %collective-permute-start) | collective-permute-done | bytes 327712 | tf_op jit(solution)/shard_map/ppermute | solution.py:694
  19.4 0.6 copy-done.3
  20.1 0.1 fusion.1
  20.2 0.3 copy.23
  20.5 3.4 %collective-permute-start.2 = (f32[2,36,10,128]{3,0,2,1:T(2,128)S(1)}, f32[2,36,10,128]{3,0,2,1:T(2,128)S(1)}, u32[]{:S(2)}, u32[]{:S(2)}) collective-permute-start(f32[2,36,10,128]{3,0,2,1:T(2,128)S(1)} %copy.23), channel_id=1, source_target_pairs={{0,1},{1,2},{2,3},{3,4},{4,5},{5,6},{6,7},{7,8},{8,9},{9,10},{10,1... | collective-permute-start | bytes 1105928 | tf_op jit(solution)/shard_map/ppermute | solution.py:694
  23.9 0.3 copy.24
  24.2 0.7 pad_add_fusion.pos
  24.8 3.5 %collective-permute-done.2 = f32[2,36,10,128]{3,0,2,1:T(2,128)S(1)} collective-permute-done((f32[2,36,10,128]{3,0,2,1:T(2,128)S(1)}, f32[2,36,10,128]{3,0,2,1:T(2,128)S(1)}, u32[]{:S(2)}, u32[]{:S(2)}) %collective-permute-start.2) | collective-permute-done | bytes 368672 | tf_op jit(solution)/shard_map/ppermute | solution.py:694
  28.3 0.9 copy.25.below
  29.2 2.0 %collective-permute-done.3 = f32[2,36,10,128]{3,0,2,1:T(2,128)S(1)} collective-permute-done((f32[2,36,10,128]{3,0,2,1:T(2,128)S(1)}, f32[2,36,10,128]{3,0,2,1:T(2,128)S(1)}, u32[]{:S(2)}, u32[]{:S(2)}) %collective-permute-start.3) | collective-permute-done | bytes 368672 | tf_op jit(solution)/shard_map/ppermute | solution.py:694
  31.2 0.9 copy.26.above
  32.1 7.8 %shard_map.50 = (f32[3,4,16,128]{3,2,1,0:T(8,128)}, f32[16,2,8,128]{3,2,1,0:T(8,128)}, f32[36,56,128]{2,1,0:T(8,128)}, f32[36,56,128]{2,1,0:T(8,128)}, f32[36,56,128]{2,1,0:T(8,128)}) custom-call(s32[2]{0:T(128)} %pad_add_fusion.pos, f32[16,32,128]{2,1,0:T(8,128)} %borig.1, f32[2,10,32,128]{3,2,1,0:T(8,128)} %copy-done.3, f32[2,10,32,128]{3,2,1,0:T(8,128)} %copy-done.2, ...), custom_call_target="tpu_custom_call" | custom-call | flops 10000000 | bytes 8388608 | tf_op jit(solution)/shard_map/pallas_call | solution.py:333
  40.1 4.8 %collective-permute-start.5 = (f32[3,4,16,128]{3,2,1,0:T(8,128)}, f32[3,4,16,128]{3,2,1,0:T(8,128)S(1)}, u32[]{:S(2)}, u32[]{:S(2)}) collective-permute-start(f32[3,4,16,128]{3,2,1,0:T(8,128)} %get-tuple-element.24.one), channel_id=1, source_target_pairs={{0,240},{16,0},{32,16},{48,32},{64,48},{80,64},{96,80},{112,96},{1... | collective-permute-start | bytes 294920 | tf_op jit(solution)/shard_map/ppermute | solution.py:694
  44.8 3.5 %all-to-all-start = ((f32[16,2,8,128]{3,2,1,0:T(8,128)}), f32[16,2,8,128]{3,2,1,0:T(8,128)S(1)}, u32[]{:S(2)}, u32[]{:S(2)}) async-start(f32[16,2,8,128]{3,2,1,0:T(8,128)} %get-tuple-element.23), calls=%async_computation | async-start | bytes 262144 | tf_op jit(solution)/shard_map/all_to_all | solution.py:698
  48.4 0.9 constant_dynamic-update-slice_fusion.1
  49.4 5.7 %all-to-all-done.mid = f32[16,2,8,128]{3,2,1,0:T(8,128)S(1)} async-done(((f32[16,2,8,128]{3,2,1,0:T(8,128)}), f32[16,2,8,128]{3,2,1,0:T(8,128)S(1)}, u32[]{:S(2)}, u32[]{:S(2)}) %all-to-all-start) | async-done | bytes 131104 | tf_op jit(solution)/shard_map/all_to_all | solution.py:698
  55.2 2.9 %collective-permute-start.7 = (f32[68,8,128]{2,1,0:T(8,128)S(1)}, f32[68,8,128]{2,1,0:T(8,128)S(1)}, u32[]{:S(2)}, u32[]{:S(2)}) collective-permute-start(f32[68,8,128]{2,1,0:T(8,128)S(1)} %get-tuple-element.52), channel_id=1, source_target_pairs={{0,15},{1,0},{2,1},{3,2},{4,3},{5,4},{6,5},{7,6},{8,7},{9,8},{10,9... | collective-permute-start | bytes 835592 | tf_op jit(solution)/shard_map/ppermute | solution.py:694
  58.1 3.9 %collective-permute-done.7.above = f32[68,8,128]{2,1,0:T(8,128)S(1)} collective-permute-done((f32[68,8,128]{2,1,0:T(8,128)S(1)}, f32[68,8,128]{2,1,0:T(8,128)S(1)}, u32[]{:S(2)}, u32[]{:S(2)}) %collective-permute-start.7) | collective-permute-done | bytes 278560 | tf_op jit(solution)/shard_map/ppermute | solution.py:694
  62.0 0.7 copy-done.6
  62.7 0.7 copy-done.7
  63.4 3.3 %shard_map.51 = (f32[3,5,24,128]{3,2,1,0:T(8,128)}, f32[16,5,8,128]{3,2,1,0:T(8,128)}, f32[16,24,128]{2,1,0:T(8,128)}) custom-call(s32[2]{0:T(128)} %pad_add_fusion.pos, f32[16,2,8,128]{3,2,1,0:T(8,128)} %copy-done.5, f32[68,8,128]{2,1,0:T(8,128)} %copy-done.7, f32[68,8,128]{2,1,0:T(8,128)} %copy-done.6), custom_call_target="tpu_custom_call" | custom-call | flops 10000000 | bytes 8388608 | tf_op jit(solution)/shard_map/pallas_call | solution.py:333
  66.7 10.5 %all-to-all-start.1 = ((f32[16,5,8,128]{3,2,1,0:T(8,128)}), f32[16,5,8,128]{3,2,1,0:T(8,128)S(1)}, u32[]{:S(2)}, u32[]{:S(2)}) async-start(f32[16,5,8,128]{3,2,1,0:T(8,128)} %get-tuple-element.25), calls=%async_computation.1 | async-start | bytes 655360 | tf_op jit(solution)/shard_map/all_to_all | solution.py:698
  77.4 0.7 copy.29.owned
  78.1 12.2 %all-to-all-done.1.three = f32[16,5,8,128]{3,2,1,0:T(8,128)S(1)} async-done(((f32[16,5,8,128]{3,2,1,0:T(8,128)}), f32[16,5,8,128]{3,2,1,0:T(8,128)S(1)}, u32[]{:S(2)}, u32[]{:S(2)}) %all-to-all-start.1) | async-done | bytes 327712 | tf_op jit(solution)/shard_map/all_to_all | solution.py:698
  90.3 0.7 copy-done.4
  91.0 15.5 %shard_map.52 = (f32[16,32,128]{2,1,0:T(8,128)}, f32[4,16,128]{2,1,0:T(8,128)}, f32[4,48,128]{2,1,0:T(8,128)}, f32[4,48,128]{2,1,0:T(8,128)}, f32[18,56,128]{2,1...) custom-call(s32[2]{0:T(128)} %pad_add_fusion.pos, f32[32,128]{1,0:T(8,128)} %copy.29.owned, ...), custom_call_target="tpu_custom_call" | custom-call | flops 10000000 | bytes 8388608 | tf_op jit(solution)/shard_map/pallas_call | solution.py:333
  106.5 0.3 collective-permute-start.8
  106.8 4.6 %collective-permute-start.9 = (f32[4,48,128]{2,1,0:T(8,128)}, f32[4,48,128]{2,1,0:T(8,128)S(1)}, u32[]{:S(2)}, u32[]{:S(2)}) collective-permute-start(f32[4,48,128]{2,1,0:T(8,128)} %get-tuple-element.32), channel_id=1, source_target_pairs={{0,240},{16,0},{32,16},{48,32},{64,48},{80,64},{96,80},{112,96},{1... | collective-permute-start | bytes 294920 | tf_op jit(solution)/shard_map/ppermute | solution.py:694
  111.4 3.3 %collective-permute-done.8.left = f32[4,48,128]{2,1,0:T(8,128)S(1)} collective-permute-done((f32[4,48,128]{2,1,0:T(8,128)}, f32[4,48,128]{2,1,0:T(8,128)S(1)}, u32[]{:S(2)}, u32[]{:S(2)}) %collective-permute-start.8) | collective-permute-done | bytes 98336 | tf_op jit(solution)/shard_map/ppermute | solution.py:694
  114.7 0.8 pad_maximum_fusion.10
  115.5 0.4 collective-permute-start.11
  116.0 1.4 collective-permute-start.10
  117.3 1.8 %collective-permute-done.11.above = f32[12,8,128]{2,1,0:T(8,128)S(1)} collective-permute-done((f32[12,8,128]{2,1,0:T(8,128)S(1)}, f32[12,8,128]{2,1,0:T(8,128)S(1)}, u32[]{:S(2)}, u32[]{:S(2)}) %collective-permute-start.11) | collective-permute-done | bytes 49184 | tf_op jit(solution)/shard_map/ppermute | solution.py:694
  119.1 0.6 copy-done.16
  119.7 2.9 %shard_map.53 = (f32[12,32,128]{2,1,0:T(8,128)}, f32[12,32,128]{2,1,0:T(8,128)}, f32[16,1,8,128]{3,2,1,0:T(8,128)}) custom-call(s32[2]{0:T(128)} %pad_add_fusion.pos, f32[4,16,128]{2,1,0:T(8,128)} %get-tuple-element.30.mid, f32[4,48,128]{2,1,0:T(8,128)} %copy-done.9, f32[4,48,128]{2,1,0:T(8,128)} %copy-done.10, f32[12,8,128]{2,1,0:T(8,128)} %copy-done.17, ...), custom_call_target="tpu_custom_call" | custom-call | flops 10000000 | bytes 8388608 | tf_op jit(solution)/shard_map/pallas_call | solution.py:333
  122.6 6.2 %all-to-all-start.2 = ((f32[16,1,8,128]{3,2,1,0:T(8,128)}), f32[16,1,8,128]{3,2,1,0:T(8,128)S(1)}, u32[]{:S(2)}, u32[]{:S(2)}) async-start(f32[16,1,8,128]{3,2,1,0:T(8,128)} %get-tuple-element.34), calls=%async_computation.2 | async-start | bytes 131072 | tf_op jit(solution)/shard_map/all_to_all | solution.py:698
  128.8 0.9 slice.66
  129.7 0.8 slice.67
  130.5 4.8 %all-to-all-done.2.mid = f32[16,1,8,128]{3,2,1,0:T(8,128)S(1)} async-done(((f32[16,1,8,128]{3,2,1,0:T(8,128)}), f32[16,1,8,128]{3,2,1,0:T(8,128)S(1)}, u32[]{:S(2)}, u32[]{:S(2)}) %all-to-all-start.2) | async-done | bytes 65568 | tf_op jit(solution)/shard_map/all_to_all | solution.py:698
  135.4 3.2 %collective-permute-start.13 = (f32[40,8,128]{2,1,0:T(8,128)S(1)}, f32[40,8,128]{2,1,0:T(8,128)S(1)}, u32[]{:S(2)}, u32[]{:S(2)}) collective-permute-start(f32[40,8,128]{2,1,0:T(8,128)S(1)} %get-tuple-element.48), channel_id=1, source_target_pairs={{0,15},{1,0},{2,1},{3,2},{4,3},{5,4},{6,5},{7,6},{8,7},{9,8},{10,9... | collective-permute-start | bytes 491528 | tf_op jit(solution)/shard_map/ppermute | solution.py:694
  138.6 2.9 %collective-permute-done.13.above = f32[40,8,128]{2,1,0:T(8,128)S(1)} collective-permute-done((f32[40,8,128]{2,1,0:T(8,128)S(1)}, f32[40,8,128]{2,1,0:T(8,128)S(1)}, u32[]{:S(2)}, u32[]{:S(2)}) %collective-permute-start.13) | collective-permute-done | bytes 163872 | tf_op jit(solution)/shard_map/ppermute | solution.py:694
  141.6 0.7 copy-done.11
  142.3 3.1 %shard_map.54 = (f32[3,5,24,128]{3,2,1,0:T(8,128)}, f32[16,2,8,128]{3,2,1,0:T(8,128)}) custom-call(s32[2]{0:T(128)} %pad_add_fusion.pos, f32[16,1,8,128]{3,2,1,0:T(8,128)} %copy-done.13, f32[40,8,128]{2,1,0:T(8,128)} %copy-done.12, f32[40,8,128]{2,1,0:T(8,128)} %copy-done.11, f32[16,24,128]{2,1,0:T(8,128)} %get-tuple-element.36.refs_0_), custom_call_target="tpu_custom_call" | custom-call | flops 10000000 | bytes 8388608 | tf_op jit(solution)/shard_map/pallas_call | solution.py:333
  145.4 16.2 %all_to_all.20.three = f32[16,2,8,128]{3,2,1,0:T(8,128)} all-to-all(f32[16,2,8,128]{3,2,1,0:T(8,128)} %get-tuple-element.37), channel_id=1, replica_groups=mesh['gx'=16,'gy'=16] {'gy'}, dimensions={0} | all-to-all | bytes 262144 | tf_op jit(solution)/shard_map/all_to_all | solution.py:698
  161.5 12.5 %shard_map.55 = (f32[16,32,128]{2,1,0:T(8,128)}, f32[16,32,128]{2,1,0:T(8,128)}) custom-call(s32[2]{0:T(128)} %pad_add_fusion.pos, f32[32,128]{1,0:T(8,128)} %copy.29.owned, f32[16,2,8,128]{3,2,1,0:T(8,128)} %all_to_all.20.three, f32[4,64,128]{2,1,0:T(8,128)} %get-tuple-element.38.k3, f32[3,5,24,128]{3,2,1,0:T(8,128)} %get-tuple-element.39.near, ...), custom_call_target="tpu_custom_call" | custom-call | flops 10000000 | bytes 8388608 | tf_op jit(solution)/shard_map/pallas_call | solution.py:333
  (58 shorter events, 0.6 us)
Async XLA Ops:
  0.6 18.7 %copy-start = (f32[16,32,128]{2,1,0:T(8,128)S(1)}, f32[16,32,128]{2,1,0:T(8,128)}, u32[]{:S(2)}) copy-start(f32[16,32,128]{2,1,0:T(8,128)} %borig.1) | copy-start | bytes 786436
  0.6 18.7 %copy-start.1 = (f32[16,32,128]{2,1,0:T(8,128)S(1)}, f32[16,32,128]{2,1,0:T(8,128)}, u32[]{:S(2)}) copy-start(f32[16,32,128]{2,1,0:T(8,128)} %ktile.1) | copy-start | bytes 786436
  1.9 12.2 %collective-permute-start.1 = (f32[2,10,32,128]{3,2,1,0:T(8,128)S(1)}, f32[2,10,32,128]{3,2,1,0:T(8,128)S(1)}, u32[]{:S(2)}, u32[]{:S(2)}) collective-permute-start(f32[2,10,32,128]{3,2,1,0:T(8,128)S(1)} %get-tuple-element.46), channel_id=1, source_target_pairs={{0,240},{16,0},{32,16},{48,32},{64,48},{80,64},{96,80},{112,96},{1... | collective-permute-start | bytes 983048 | tf_op jit(solution)/shard_map/ppermute | solution.py:694
  7.7 11.6 %collective-permute-start = (f32[2,10,32,128]{3,2,1,0:T(8,128)S(1)}, f32[2,10,32,128]{3,2,1,0:T(8,128)S(1)}, u32[]{:S(2)}, u32[]{:S(2)}) collective-permute-start(f32[2,10,32,128]{3,2,1,0:T(8,128)S(1)} %get-tuple-element.47), channel_id=1, source_target_pairs={{0,16},{16,32},{32,48},{48,64},{64,80},{80,96},{96,112},{112,128},... | collective-permute-start | bytes 983048 | tf_op jit(solution)/shard_map/ppermute | solution.py:694
  14.1 5.3 %copy-start.2 = (f32[2,10,32,128]{3,2,1,0:T(8,128)}, f32[2,10,32,128]{3,2,1,0:T(8,128)S(1)}, u32[]{:S(2)}) copy-start(f32[2,10,32,128]{3,2,1,0:T(8,128)S(1)} %collective-permute-done.1.right) | copy-start | bytes 983044
  19.3 0.7 copy-start.3
  20.5 7.9 %collective-permute-start.2 = (f32[2,36,10,128]{3,0,2,1:T(2,128)S(1)}, f32[2,36,10,128]{3,0,2,1:T(2,128)S(1)}, u32[]{:S(2)}, u32[]{:S(2)}) collective-permute-start(f32[2,36,10,128]{3,0,2,1:T(2,128)S(1)} %copy.23), channel_id=1, source_target_pairs={{0,1},{1,2},{2,3},{3,4},{4,5},{5,6},{6,7},{7,8},{8,9},{9,10},{10,1... | collective-permute-start | bytes 1105928 | tf_op jit(solution)/shard_map/ppermute | solution.py:694
  24.1 7.1 %collective-permute-start.3 = (f32[2,36,10,128]{3,0,2,1:T(2,128)S(1)}, f32[2,36,10,128]{3,0,2,1:T(2,128)S(1)}, u32[]{:S(2)}, u32[]{:S(2)}) collective-permute-start(f32[2,36,10,128]{3,0,2,1:T(2,128)S(1)} %copy.24), channel_id=1, source_target_pairs={{0,15},{1,0},{2,1},{3,2},{4,3},{5,4},{6,5},{7,6},{8,7},{9,8},{10,9... | collective-permute-start | bytes 1105928 | tf_op jit(solution)/shard_map/ppermute | solution.py:694
  40.0 8.4 %collective-permute-start.4 = (f32[3,4,16,128]{3,2,1,0:T(8,128)}, f32[3,4,16,128]{3,2,1,0:T(8,128)S(1)}, u32[]{:S(2)}, u32[]{:S(2)}) collective-permute-start(f32[3,4,16,128]{3,2,1,0:T(8,128)} %get-tuple-element.24.one), channel_id=1, source_target_pairs={{0,16},{16,32},{32,48},{48,64},{64,80},{80,96},{96,112},{112,128},... | collective-permute-start | bytes 294920 | tf_op jit(solution)/shard_map/ppermute | solution.py:694
  40.1 9.3 %collective-permute-start.5 = (f32[3,4,16,128]{3,2,1,0:T(8,128)}, f32[3,4,16,128]{3,2,1,0:T(8,128)S(1)}, u32[]{:S(2)}, u32[]{:S(2)}) collective-permute-start(f32[3,4,16,128]{3,2,1,0:T(8,128)} %get-tuple-element.24.one), channel_id=1, source_target_pairs={{0,240},{16,0},{32,16},{48,32},{64,48},{80,64},{96,80},{112,96},{1... | collective-permute-start | bytes 294920 | tf_op jit(solution)/shard_map/ppermute | solution.py:694
  44.8 10.3 %all-to-all-start = ((f32[16,2,8,128]{3,2,1,0:T(8,128)}), f32[16,2,8,128]{3,2,1,0:T(8,128)S(1)}, u32[]{:S(2)}, u32[]{:S(2)}) async-start(f32[16,2,8,128]{3,2,1,0:T(8,128)} %get-tuple-element.23), calls=%async_computation | async-start | bytes 262144 | tf_op jit(solution)/shard_map/all_to_all | solution.py:698
  48.4 6.8 %copy-start.14 = (f32[3,4,16,128]{3,2,1,0:T(8,128)}, f32[3,4,16,128]{3,2,1,0:T(8,128)S(1)}, u32[]{:S(2)}) copy-start(f32[3,4,16,128]{3,2,1,0:T(8,128)S(1)} %collective-permute-done.4.left) | copy-start | bytes 294916
  49.3 17.4 %copy-start.15 = (f32[3,4,16,128]{3,2,1,0:T(8,128)}, f32[3,4,16,128]{3,2,1,0:T(8,128)S(1)}, u32[]{:S(2)}) copy-start(f32[3,4,16,128]{3,2,1,0:T(8,128)S(1)} %collective-permute-done.5.right) | copy-start | bytes 294916
  55.1 6.9 %copy-start.5 = (f32[16,2,8,128]{3,2,1,0:T(8,128)}, f32[16,2,8,128]{3,2,1,0:T(8,128)S(1)}, u32[]{:S(2)}) copy-start(f32[16,2,8,128]{3,2,1,0:T(8,128)S(1)} %all-to-all-done.mid) | copy-start | bytes 393220
  55.1 22.2 %copy-start.18 = (s32[16,16]{1,0:T(8,128)S(1)}, s32[16,16]{1,0:T(8,128)}, u32[]{:S(2)}) copy-start(s32[16,16]{1,0:T(8,128)} %param.5) | copy-start | bytes 3076
  55.2 6.8 %collective-permute-start.7 = (f32[68,8,128]{2,1,0:T(8,128)S(1)}, f32[68,8,128]{2,1,0:T(8,128)S(1)}, u32[]{:S(2)}, u32[]{:S(2)}) collective-permute-start(f32[68,8,128]{2,1,0:T(8,128)S(1)} %get-tuple-element.52), channel_id=1, source_target_pairs={{0,15},{1,0},{2,1},{3,2},{4,3},{5,4},{6,5},{7,6},{8,7},{9,8},{10,9... | collective-permute-start | bytes 835592 | tf_op jit(solution)/shard_map/ppermute | solution.py:694
  58.1 3.9 %collective-permute-start.6 = (f32[68,8,128]{2,1,0:T(8,128)S(1)}, f32[68,8,128]{2,1,0:T(8,128)S(1)}, u32[]{:S(2)}, u32[]{:S(2)}) collective-permute-start(f32[68,8,128]{2,1,0:T(8,128)S(1)} %get-tuple-element.53), channel_id=1, source_target_pairs={{0,1},{1,2},{2,3},{3,4},{4,5},{5,6},{6,7},{7,8},{8,9},{9,10},{10,1... | collective-permute-start | bytes 835592 | tf_op jit(solution)/shard_map/ppermute | solution.py:694
  62.0 0.7 copy-start.6
  62.7 0.7 copy-start.7
  66.7 23.6 %all-to-all-start.1 = ((f32[16,5,8,128]{3,2,1,0:T(8,128)}), f32[16,5,8,128]{3,2,1,0:T(8,128)S(1)}, u32[]{:S(2)}, u32[]{:S(2)}) async-start(f32[16,5,8,128]{3,2,1,0:T(8,128)} %get-tuple-element.25), calls=%async_computation.1 | async-start | bytes 655360 | tf_op jit(solution)/shard_map/all_to_all | solution.py:698
  90.3 0.7 copy-start.4
  106.5 28.8 %copy-start.8 = (f32[16,32,128]{2,1,0:T(8,128)S(1)}, f32[16,32,128]{2,1,0:T(8,128)}, u32[]{:S(2)}) copy-start(f32[16,32,128]{2,1,0:T(8,128)} %get-tuple-element.35.x0n) | copy-start | bytes 786436
  106.5 8.2 %collective-permute-start.8 = (f32[4,48,128]{2,1,0:T(8,128)}, f32[4,48,128]{2,1,0:T(8,128)S(1)}, u32[]{:S(2)}, u32[]{:S(2)}) collective-permute-start(f32[4,48,128]{2,1,0:T(8,128)} %get-tuple-element.31), channel_id=1, source_target_pairs={{0,16},{16,32},{32,48},{48,64},{64,80},{80,96},{96,112},{112,128},... | collective-permute-start | bytes 294920 | tf_op jit(solution)/shard_map/ppermute | solution.py:694
  106.8 7.9 %collective-permute-start.9 = (f32[4,48,128]{2,1,0:T(8,128)}, f32[4,48,128]{2,1,0:T(8,128)S(1)}, u32[]{:S(2)}, u32[]{:S(2)}) collective-permute-start(f32[4,48,128]{2,1,0:T(8,128)} %get-tuple-element.32), channel_id=1, source_target_pairs={{0,240},{16,0},{32,16},{48,32},{64,48},{80,64},{96,80},{112,96},{1... | collective-permute-start | bytes 294920 | tf_op jit(solution)/shard_map/ppermute | solution.py:694
  114.7 4.4 %copy-start.9 = (f32[4,48,128]{2,1,0:T(8,128)}, f32[4,48,128]{2,1,0:T(8,128)S(1)}, u32[]{:S(2)}) copy-start(f32[4,48,128]{2,1,0:T(8,128)S(1)} %collective-permute-done.8.left) | copy-start | bytes 294916
  114.7 4.4 %copy-start.10 = (f32[4,48,128]{2,1,0:T(8,128)}, f32[4,48,128]{2,1,0:T(8,128)S(1)}, u32[]{:S(2)}) copy-start(f32[4,48,128]{2,1,0:T(8,128)S(1)} %collective-permute-done.9.right) | copy-start | bytes 294916
  115.5 3.5 %collective-permute-start.11 = (f32[12,8,128]{2,1,0:T(8,128)S(1)}, f32[12,8,128]{2,1,0:T(8,128)S(1)}, u32[]{:S(2)}, u32[]{:S(2)}) collective-permute-start(f32[12,8,128]{2,1,0:T(8,128)S(1)} %get-tuple-element.54), channel_id=1, source_target_pairs={{0,15},{1,0},{2,1},{3,2},{4,3},{5,4},{6,5},{7,6},{8,7},{9,8},{10,9... | collective-permute-start | bytes 147464 | tf_op jit(solution)/shard_map/ppermute | solution.py:694
  116.0 3.1 %collective-permute-start.10 = (f32[12,8,128]{2,1,0:T(8,128)S(1)}, f32[12,8,128]{2,1,0:T(8,128)S(1)}, u32[]{:S(2)}, u32[]{:S(2)}) collective-permute-start(f32[12,8,128]{2,1,0:T(8,128)S(1)} %get-tuple-element.55), channel_id=1, source_target_pairs={{0,1},{1,2},{2,3},{3,4},{4,5},{5,6},{6,7},{7,8},{8,9},{9,10},{10,1... | collective-permute-start | bytes 147464 | tf_op jit(solution)/shard_map/ppermute | solution.py:694
  119.1 0.6 copy-start.16
  119.1 0.6 copy-start.17
  122.6 12.7 %all-to-all-start.2 = ((f32[16,1,8,128]{3,2,1,0:T(8,128)}), f32[16,1,8,128]{3,2,1,0:T(8,128)S(1)}, u32[]{:S(2)}, u32[]{:S(2)}) async-start(f32[16,1,8,128]{3,2,1,0:T(8,128)} %get-tuple-element.34), calls=%async_computation.2 | async-start | bytes 131072 | tf_op jit(solution)/shard_map/all_to_all | solution.py:698
  135.3 6.2 %copy-start.13 = (f32[16,1,8,128]{3,2,1,0:T(8,128)}, f32[16,1,8,128]{3,2,1,0:T(8,128)S(1)}, u32[]{:S(2)}) copy-start(f32[16,1,8,128]{3,2,1,0:T(8,128)S(1)} %all-to-all-done.2.mid) | copy-start | bytes 196612
  135.4 6.2 %collective-permute-start.13 = (f32[40,8,128]{2,1,0:T(8,128)S(1)}, f32[40,8,128]{2,1,0:T(8,128)S(1)}, u32[]{:S(2)}, u32[]{:S(2)}) collective-permute-start(f32[40,8,128]{2,1,0:T(8,128)S(1)} %get-tuple-element.48), channel_id=1, source_target_pairs={{0,15},{1,0},{2,1},{3,2},{4,3},{5,4},{6,5},{7,6},{8,7},{9,8},{10,9... | collective-permute-start | bytes 491528 | tf_op jit(solution)/shard_map/ppermute | solution.py:694
  138.6 3.0 %collective-permute-start.12 = (f32[40,8,128]{2,1,0:T(8,128)S(1)}, f32[40,8,128]{2,1,0:T(8,128)S(1)}, u32[]{:S(2)}, u32[]{:S(2)}) collective-permute-start(f32[40,8,128]{2,1,0:T(8,128)S(1)} %get-tuple-element.49), channel_id=1, source_target_pairs={{0,1},{1,2},{2,3},{3,4},{4,5},{5,6},{6,7},{7,8},{8,9},{9,10},{10,1... | collective-permute-start | bytes 491528 | tf_op jit(solution)/shard_map/ppermute | solution.py:694
  141.5 0.7 copy-start.11
  141.6 0.7 copy-start.12

commit v6 on v5

--- a/solution.py
+++ b/solution.py
@@ -217,23 +217,37 @@
     lax.fori_loop(0, PARTS, step, fx0, unroll=True)
 
 
-def fill_top(dst, tile, left, right, below, above):
+class Pick:
+    def __init__(self, take_first, first, second):
+        self.take_first, self.first, self.second = take_first, first, second
+
+    def __getitem__(self, index):
+        return jnp.where(self.take_first, self.first[index], self.second[index])
+
+
+def sides(at, first, second):
+    odd = (at & 1) == 1
+    return Pick(odd, first, second), Pick(odd, second, first)
+
+
+def fill_top(dst, number, wide, below, above):
     dst[:, 0:2, :] = jnp.zeros((PX, 2, 128), F32)
     dst[:, RY - 2 : RY, :] = jnp.zeros((PX, 2, 128), F32)
-    dst[0:HX, HY : HY + TY, :] = left
-    dst[HX : HX + TX, HY : HY + TY, :] = tile
-    dst[HX + TX :, HY : HY + TY, :] = right
-    dst[:, 2:HY, :] = below
-    dst[:, HY + TY : RY - 2, :] = above
-
-
-def down_kernel(pos, tile, left, right, below, above, ktile, one, two, *refs):
+    dst[:, HY : HY + TY, :] = wide[number]
+    for p in range(PX):
+        part = slice(HX * (PX * number + p), HX * (PX * number + p + 1))
+        dst[p, 2:HY, :] = below[part]
+        dst[p, HY + TY : RY - 2, :] = above[part]
+
+
+def down_kernel(pos, wide, by_y, by_y2, one, two, *refs):
     given, (bx, kx, x, wx, wy, wz, s, rd, d, rs, b1s, x1s, k1s, sems) = refs[:3], refs[3:]
     keeping = moves((bx, kx, x), given, sems)
     gx, gy = pos[0], pos[1]
     inside_at = insider(RY, gx * TX - HX, gy * TY - HY)
-    fill_top(bx, tile[...], left[0], right[0], below[0], above[0])
-    fill_top(kx, ktile[...], left[1], right[1], below[1], above[1])
+    below, above = sides(gy, by_y, by_y2)
+    fill_top(bx, 0, wide, below, above)
+    fill_top(kx, 1, wide, below, above)
 
     def clear(i, _):
         at = pl.ds(i * CHUNK, CHUNK)
@@ -349,9 +363,12 @@
     return call(down_kernel, outs, scratch, *args, far_out=3, copies=3)
 
 
-def one_kernel(pos, mid, left, right, below, above, k1, bout, xout, two, res):
+def one_kernel(pos, mid, by_x, by_x2, by_y, by_y2, k1, bout, xout, two, res):
     gx, gy = pos[0], pos[1]
-    fill_one(bout, left[:, 0:16], mid[...], right[:, 0:16], below[...], above[...])
+    left, right = sides(gx, by_x, by_x2)
+    below, above = sides(gy, by_y, by_y2)
+    head = (slice(None), slice(0, 16))
+    fill_one(bout, left[head], mid[...], right[head], below[...], above[...])
     b = bout[...]
     inside = within(b.shape, gx * 8 - 8, gy * 16 - 8, 64, 128, 256)
     level = build(k1[...], 0.25, 64, inside)
@@ -374,7 +391,7 @@
     return call(one_kernel, [wide, wide, (16, 1, 8, 128)], [wide], *args)
 
 
-def mid_kernel(first, pos, mid, below, above, *refs):
+def mid_kernel(first, pos, mid, by_y, by_y2, *refs):
     if first:
         near, three, k2 = refs[:3]
         scratch = refs[3:]
@@ -383,6 +400,7 @@
         scratch = refs[3:]
     hold, rs, cs, edge = scratch
     gx, gy = pos[0], pos[1]
+    below, above = sides(gy, by_y, by_y2)
     shape = (16, 24, 128)
     inside = within(shape, 0, gy * 8 - 8, 32, 64, 128)
 
@@ -554,10 +572,12 @@
 
 
 def turn_kernel(
-    pos, owned, three, near, one, left, right, below, above, *refs
+    pos, owned, three, near, one, by_x, by_x2, by_y, by_y2, *refs
 ):
     gx, gy = pos[0], pos[1]
-    fars, (x0n, b1n, east, west, *far_outs) = refs[:3], refs[3:11]
+    left, right = sides(gx, by_x, by_x2)
+    below, above = sides(gy, by_y, by_y2)
+    fars, (x0n, b1n, send, send2, *far_outs) = refs[:3], refs[3:11]
     b3, s3, e2, s2, x2s, b1s, s1, e0, d, x, rs, xout, rout, k3, k1 = refs[11:26]
     tops, sems = refs[26:29], refs[34]
     (b0, k0, x0), (wx, wy, wz, s, rd) = tops, refs[29:34]
@@ -624,9 +644,10 @@
         rs[c] = d[HX + 2 * c] + d[HX + 1 + 2 * c]
     b1 = pair_planes(rs, 4, HY, 16)
     b1n[...] = b1
-    for side, plane in ((east, HX + TX - 4), (west, HX)):
+    odd = (gx & 1) == 1
+    for side, of_odd, of_even in ((send, HX, HX + TX - 4), (send2, HX + TX - 4, HX)):
         side[:, 0:16, :] = b1
-        side[:, 16:48, :] = x[plane : plane + 4, HY : HY + TY, :]
+        side[:, 16:48, :] = x[pl.ds(jnp.where(odd, of_odd, of_even), 4), HY : HY + TY, :]
     for move in (xkeep, rkeep, kkeep, k1keep):
         move.wait()
 
@@ -641,9 +662,11 @@
 
 
 def last_kernel(
-    pos, owned, three, k3, near, b1, x1, k1, x0n, left, right, below, above, borig, *refs
+    pos, owned, three, k3, near, b1, x1, k1, x0n, by_x, by_x2, by_y, by_y2, borig, *refs
 ):
     gx, gy = pos[0], pos[1]
+    left, right = sides(gx, by_x, by_x2)
+    below, above = sides(gy, by_y, by_y2)
     fars, (xout, rout), (b3, s3, e2, s2, s1, e0, d, x) = refs[:3], refs[3:5], refs[5:13]
     tops, sems = refs[13:16], refs[21]
     (r, xbefore, k0), (wx, wy, wz, s, rd) = tops, refs[16:21]
@@ -689,9 +712,20 @@
     return call(last_kernel, [tile, tile], scratch, *args, far_in=3, copies=3)
 
 
-def shift(value, axis, step):
+def swap(low, high, axis):
     count = lax.axis_size(axis)
-    return lax.ppermute(value, axis, [(i, (i + step) % count) for i in range(count)])
+    odd = lax.axis_index(axis) % 2 == 1
+    first = jnp.where(odd, low, high) if low is not high else low
+    second = jnp.where(odd, high, low) if low is not high else low
+    return (
+        lax.ppermute(first, axis, [(i, i ^ 1) for i in range(count)]),
+        lax.ppermute(second, axis, [(i, (i + 1 if i % 2 else i - 1) % count) for i in range(count)]),
+    )
+
+
+def apart(first, second, axis):
+    odd = lax.axis_index(axis) % 2 == 1
+    return jnp.where(odd, first, second), jnp.where(odd, second, first)
 
 
 def gather(copies, axis):
@@ -702,39 +736,40 @@
     pos = jnp.stack([lax.axis_index("gx"), lax.axis_index("gy")]).astype(jnp.int32)
     owned = jnp.repeat(jnp.repeat(owners.T, 2, 0), 8, 1).astype(F32)
     mid = jnp.stack([right_side, kappa])
-    left = shift(mid[:, TX - HX :], "gx", 1)
-    right = shift(mid[:, :HX], "gx", -1)
+    left, right = apart(*swap(mid[:, :HX], mid[:, TX - HX :], "gx"), "gx")
     wide = jnp.concatenate([left, mid, right], axis=1)
-    below = shift(wide[:, :, TY - HX :], "gy", 1)
-    above = shift(wide[:, :, :HX], "gy", -1)
-    one, two, b0, k0, x0 = go_down(pos, right_side, left, right, below, above, kappa)
-    left = shift(one, "gx", 1)
-    right = shift(one, "gx", -1)
+    low, high = (part.reshape(-1, 128) for part in (wide[:, :, :HX], wide[:, :, TY - HX :]))
+    one, two, b0, k0, x0 = go_down(pos, wide, *swap(low, high, "gy"))
+    by_x = swap(one, one, "gx")
     two = gather(two, "gx")
+    left, right = apart(*by_x, "gx")
     rows = jnp.swapaxes(two, 0, 1).reshape(-1, 8, 128)
     wide = jnp.concatenate([left, one, right], axis=1)
-    below = shift(jnp.concatenate([rows, wide[:, :, 8:].reshape(-1, 8, 128)]), "gy", 1)
-    above = shift(jnp.concatenate([rows, wide[:, :, :8].reshape(-1, 8, 128)]), "gy", -1)
-    near, three, k2 = go_mid(True, pos, two, below, above, None)
+    low, high = (
+        jnp.concatenate([rows, part.reshape(-1, 8, 128)]) for part in (wide[:, :, :8], wide[:, :, 8:])
+    )
+    by_y = swap(low, high, "gy")
+    near, three, k2 = go_mid(True, pos, two, *by_y, None)
     three = gather(three, "gy")
-    x0n, b1n, east, west, xbefore, source, k3, k1 = go_turn(
-        pos, owned, three, near, one, left, right, below, above, b0, k0, x0
+    x0n, b1n, send, send2, xbefore, source, k3, k1 = go_turn(
+        pos, owned, three, near, one, *by_x, *by_y, b0, k0, x0
     )
 
-    left = shift(east, "gx", 1)
-    right = shift(west, "gx", -1)
+    by_x = (
+        lax.ppermute(send, "gx", [(i, i ^ 1) for i in range(16)]),
+        lax.ppermute(send2, "gx", [(i, (i + 1 if i % 2 else i - 1) % 16) for i in range(16)]),
+    )
+    left, right = apart(*by_x, "gx")
     wide = jnp.concatenate([left[:, :16], b1n, right[:, :16]])
-    below = shift(wide[:, 8:], "gy", 1)
-    above = shift(wide[:, :8], "gy", -1)
-    b1, x1, two = go_one(pos, b1n, left, right, below, above, k1)
+    b1, x1, two = go_one(pos, b1n, *by_x, *swap(wide[:, :8], wide[:, 8:], "gy"), k1)
     two = gather(two, "gx")
     wide = jnp.concatenate([left[:, 16:], x0n, right[:, 16:]])
-    below = shift(jnp.concatenate([two[:, 0], wide[:, 24:]]), "gy", 1)
-    above = shift(jnp.concatenate([two[:, 0], wide[:, :8]]), "gy", -1)
-    near, three = go_mid(False, pos, two, below, above, k2)
+    low, high = (jnp.concatenate([two[:, 0], part]) for part in (wide[:, :8], wide[:, 24:]))
+    by_y = swap(low, high, "gy")
+    near, three = go_mid(False, pos, two, *by_y, k2)
     three = gather(three, "gy")
     field, residual = go_last(
-        pos, owned, three, k3, near, b1, x1, k1, x0n, left, right, below, above, right_side, source, xbefore, k0
+        pos, owned, three, k3, near, b1, x1, k1, x0n, *by_x, *by_y, right_side, source, xbefore, k0
     )
     return field, residual
 

time: 175 us -> 166 us (0.949)
  local copies, waits for them, and re-layouts: 10.1 us -> 5.46 us
  waiting for transfers between devices: 51.8 us -> 48.3 us
    ppermute x14, waiting for transfers between devices: 29.1 us -> 24.4 us  [the longest x6 14.7 us: swap(): lax.ppermute(second, axis, [(i, (i + 1 if i % 2 else i - 1) % count) for...]
    all_to_all x3, starting transfers between devices: 20.2 us -> 17.6 us  [gather(): return lax.all_to_all(copies, axis, 0, 0, tiled=True)]
    ppermute x2 -> x0, local copies, waits for them, and re-layouts: 1.76 us -> none  [shift(): lax.ppermute(value, axis, [(i, (i + step) % count) for i in range(count)])]
  transfers between devices with their start and end apart: 17 -> 17, of which waited for: 11 -> 12; matrix products, arithmetic and copies ran while one was open for 3% -> 1% of each run, Pallas kernels for 0% -> 0%
where the time goes in v6:
time: 166 us
  waiting for transfers between devices  48.3 us (29%)
  starting transfers between devices  45.7 us (28%)
  Pallas kernels  43.6 us (26%)
  blocking collectives  17.4 us (10%)
  local copies, waits for them, and re-layouts  5.46 us (3%)
  other arithmetic  4.06 us (2%)
    pallas_call x6, Pallas kernels, call(): pl.pallas_call(kernel, out_shape=[jax.ShapeDtypeStruct(o, F32) for o in o...  43.6 us
    all_to_all x3, waiting for transfers between devices, gather(): return lax.all_to_all(copies, axis, 0, 0, tiled=True)  23.9 us
    all_to_all x3, starting transfers between devices, gather(): return lax.all_to_all(copies, axis, 0, 0, tiled=True)  17.6 us
    all_to_all x1, blocking collectives, gather(): return lax.all_to_all(copies, axis, 0, 0, tiled=True)  17.4 us
    ppermute x6, waiting for transfers between devices, swap(): lax.ppermute(second, axis, [(i, (i + 1 if i % 2 else i - 1) % count) for...  14.7 us
    ppermute x6, starting transfers between devices, swap(): lax.ppermute(second, axis, [(i, (i + 1 if i % 2 else i - 1) % count) for...  14.5 us
    ppermute x6, starting transfers between devices, swap(): lax.ppermute(first, axis, [(i, i ^ 1) for i in range(count)])  11.5 us
    unnamed x40, local copies, waits for them, and re-layouts  4.49 us
  transfers between devices with their start and end apart: 17, of which 12 were waited for; matrix products, arithmetic and copies ran while one was open for 1% of the time, Pallas kernels for 0%

profile of v6, /device:TPU:1, one launch (start us, length us, event | category | flops | bytes accessed | tf_op | source)
XLA Modules:
  0.0 165.7 jit_solution(18015320198351015454)
XLA Ops:
  0.7 1.4 fusion.3
  2.1 2.2 %collective-permute-start = (f32[2,10,32,128]{3,2,1,0:T(8,128)S(1)}, f32[2,10,32,128]{3,2,1,0:T(8,128)S(1)}, u32[]{:S(2)}, u32[]{:S(2)}) collective-permute-start(f32[2,10,32,128]{3,2,1,0:T(8,128)S(1)} %get-tuple-element.48), channel_id=1, source_target_pairs={{0,16},{16,0},{32,48},{48,32},{64,80},{80,64},{96,112},{112,96},{1... | collective-permute-start | bytes 983048 | tf_op jit(solution)/shard_map/ppermute | solution.py:721
  4.3 4.1 %collective-permute-start.1 = (f32[2,10,32,128]{3,2,1,0:T(8,128)S(1)}, f32[2,10,32,128]{3,2,1,0:T(8,128)S(1)}, u32[]{:S(2)}, u32[]{:S(2)}) collective-permute-start(f32[2,10,32,128]{3,2,1,0:T(8,128)S(1)} %get-tuple-element.49), channel_id=1, source_target_pairs={{0,240},{16,32},{32,16},{48,64},{64,48},{80,96},{96,80},{112,128},... | collective-permute-start | bytes 983048 | tf_op jit(solution)/shard_map/ppermute | solution.py:722
  8.4 2.1 %collective-permute-done = f32[2,10,32,128]{3,2,1,0:T(8,128)S(1)} collective-permute-done((f32[2,10,32,128]{3,2,1,0:T(8,128)S(1)}, f32[2,10,32,128]{3,2,1,0:T(8,128)S(1)}, u32[]{:S(2)}, u32[]{:S(2)}) %collective-permute-start) | collective-permute-done | bytes 327712 | tf_op jit(solution)/shard_map/ppermute | solution.py:721
  10.5 5.1 %collective-permute-done.1 = f32[2,10,32,128]{3,2,1,0:T(8,128)S(1)} collective-permute-done((f32[2,10,32,128]{3,2,1,0:T(8,128)S(1)}, f32[2,10,32,128]{3,2,1,0:T(8,128)S(1)}, u32[]{:S(2)}, u32[]{:S(2)}) %collective-permute-start.1) | collective-permute-done | bytes 327712 | tf_op jit(solution)/shard_map/ppermute | solution.py:722
  15.7 0.1 pad_maximum_fusion.wide
  15.8 0.1 slice_select_fusion
  15.9 0.9 copy-done
  16.9 2.2 %collective-permute-start.2 = (f32[720,128]{1,0:T(8,128)S(1)}, f32[720,128]{1,0:T(8,128)S(1)}, u32[]{:S(2)}, u32[]{:S(2)}) collective-permute-start(f32[720,128]{1,0:T(8,128)S(1)} %select_n.130), channel_id=1, source_target_pairs={{0,1},{1,0},{2,3},{3,2},{4,5},{5,4},{6,7},{7,6},{8,9},{9,8},{10,11... | collective-permute-start | bytes 1105928 | tf_op jit(solution)/shard_map/ppermute | solution.py:721
  19.1 1.6 collective-permute-start.3
  20.8 0.6 pad_add_fusion.pos
  21.3 5.0 %collective-permute-done.3.by_y2 = f32[720,128]{1,0:T(8,128)S(1)} collective-permute-done((f32[720,128]{1,0:T(8,128)S(1)}, f32[720,128]{1,0:T(8,128)S(1)}, u32[]{:S(2)}, u32[]{:S(2)}) %collective-permute-start.3) | collective-permute-done | bytes 368672 | tf_op jit(solution)/shard_map/ppermute | solution.py:722
  26.4 0.7 copy-done.16
  27.1 7.7 %shard_map.50 = (f32[3,4,16,128]{3,2,1,0:T(8,128)}, f32[16,2,8,128]{3,2,1,0:T(8,128)}, f32[36,56,128]{2,1,0:T(8,128)}, f32[36,56,128]{2,1,0:T(8,128)}, f32[36,56,128]{2,1,0:T(8,128)}) custom-call(s32[2]{0:T(128)} %pad_add_fusion.pos, f32[2,36,32,128]{3,2,1,0:T(8,128)} %copy-done, f32[720,128]{1,0:T(8,128)} %copy-done.15, f32[720,128]{1,0:T(8,128)} %copy-done.16), custom_call_target="tpu_custom_call" | custom-call | flops 10000000 | bytes 8388608 | tf_op jit(solution)/shard_map/pallas_call | solution.py:347
  34.8 4.2 %collective-permute-start.5 = (f32[3,4,16,128]{3,2,1,0:T(8,128)}, f32[3,4,16,128]{3,2,1,0:T(8,128)S(1)}, u32[]{:S(2)}, u32[]{:S(2)}) collective-permute-start(f32[3,4,16,128]{3,2,1,0:T(8,128)} %get-tuple-element.24.one), channel_id=1, source_target_pairs={{0,240},{16,32},{32,16},{48,64},{64,48},{80,96},{96,80},{112,128},... | collective-permute-start | bytes 294920 | tf_op jit(solution)/shard_map/ppermute | solution.py:722
  39.0 3.5 %all-to-all-start = ((f32[16,2,8,128]{3,2,1,0:T(8,128)}), f32[16,2,8,128]{3,2,1,0:T(8,128)S(1)}, u32[]{:S(2)}, u32[]{:S(2)}) async-start(f32[16,2,8,128]{3,2,1,0:T(8,128)} %get-tuple-element.23), calls=%async_computation | async-start | bytes 262144 | tf_op jit(solution)/shard_map/all_to_all | solution.py:732
  42.5 0.1 collective-permute-done.4.by_x
  42.7 0.9 pad_maximum_fusion.4
  43.7 5.5 %all-to-all-done.mid = f32[16,2,8,128]{3,2,1,0:T(8,128)S(1)} async-done(((f32[16,2,8,128]{3,2,1,0:T(8,128)}), f32[16,2,8,128]{3,2,1,0:T(8,128)S(1)}, u32[]{:S(2)}, u32[]{:S(2)}) %all-to-all-start) | async-done | bytes 131104 | tf_op jit(solution)/shard_map/all_to_all | solution.py:732
  49.3 3.2 %collective-permute-start.7 = (f32[68,8,128]{2,1,0:T(8,128)S(1)}, f32[68,8,128]{2,1,0:T(8,128)S(1)}, u32[]{:S(2)}, u32[]{:S(2)}) collective-permute-start(f32[68,8,128]{2,1,0:T(8,128)S(1)} %get-tuple-element.52), channel_id=1, source_target_pairs={{0,15},{1,2},{2,1},{3,4},{4,3},{5,6},{6,5},{7,8},{8,7},{9,10},{10,... | collective-permute-start | bytes 835592 | tf_op jit(solution)/shard_map/ppermute | solution.py:722
  52.5 4.5 %collective-permute-start.6 = (f32[68,8,128]{2,1,0:T(8,128)S(1)}, f32[68,8,128]{2,1,0:T(8,128)S(1)}, u32[]{:S(2)}, u32[]{:S(2)}) collective-permute-start(f32[68,8,128]{2,1,0:T(8,128)S(1)} %get-tuple-element.53), channel_id=1, source_target_pairs={{0,1},{1,0},{2,3},{3,2},{4,5},{5,4},{6,7},{7,6},{8,9},{9,8},{10,11... | collective-permute-start | bytes 835592 | tf_op jit(solution)/shard_map/ppermute | solution.py:721
  57.0 1.2 collective-permute-done.6.by_y
  58.2 0.7 copy-done.5
  58.9 3.3 %shard_map.51 = (f32[3,5,24,128]{3,2,1,0:T(8,128)}, f32[16,5,8,128]{3,2,1,0:T(8,128)}, f32[16,24,128]{2,1,0:T(8,128)}) custom-call(s32[2]{0:T(128)} %pad_add_fusion.pos, f32[16,2,8,128]{3,2,1,0:T(8,128)} %copy-done.3, f32[68,8,128]{2,1,0:T(8,128)} %copy-done.5, f32[68,8,128]{2,1,0:T(8,128)} %copy-done.4), custom_call_target="tpu_custom_call" | custom-call | flops 10000000 | bytes 8388608 | tf_op jit(solution)/shard_map/pallas_call | solution.py:347
  62.2 10.3 %all-to-all-start.1 = ((f32[16,5,8,128]{3,2,1,0:T(8,128)}), f32[16,5,8,128]{3,2,1,0:T(8,128)S(1)}, u32[]{:S(2)}, u32[]{:S(2)}) async-start(f32[16,5,8,128]{3,2,1,0:T(8,128)} %get-tuple-element.25), calls=%async_computation.1 | async-start | bytes 655360 | tf_op jit(solution)/shard_map/all_to_all | solution.py:732
  72.7 0.7 copy.25.owned
  73.3 12.2 %all-to-all-done.1.three = f32[16,5,8,128]{3,2,1,0:T(8,128)S(1)} async-done(((f32[16,5,8,128]{3,2,1,0:T(8,128)}), f32[16,5,8,128]{3,2,1,0:T(8,128)S(1)}, u32[]{:S(2)}, u32[]{:S(2)}) %all-to-all-start.1) | async-done | bytes 327712 | tf_op jit(solution)/shard_map/all_to_all | solution.py:732
  85.6 0.7 copy-done.2
  86.3 15.4 %shard_map.52 = (f32[16,32,128]{2,1,0:T(8,128)}, f32[4,16,128]{2,1,0:T(8,128)}, f32[4,48,128]{2,1,0:T(8,128)}, f32[4,48,128]{2,1,0:T(8,128)}, f32[18,56,128]{2,1...) custom-call(s32[2]{0:T(128)} %pad_add_fusion.pos, f32[32,128]{1,0:T(8,128)} %copy.25.owned, ...), custom_call_target="tpu_custom_call" | custom-call | flops 10000000 | bytes 8388608 | tf_op jit(solution)/shard_map/pallas_call | solution.py:347
  101.8 0.3 collective-permute-start.8
  102.0 1.8 %collective-permute-start.9 = (f32[4,48,128]{2,1,0:T(8,128)}, f32[4,48,128]{2,1,0:T(8,128)S(1)}, u32[]{:S(2)}, u32[]{:S(2)}) collective-permute-start(f32[4,48,128]{2,1,0:T(8,128)} %get-tuple-element.32), channel_id=1, source_target_pairs={{0,240},{16,32},{32,16},{48,64},{64,48},{80,96},{96,80},{112,128},... | collective-permute-start | bytes 294920 | tf_op jit(solution)/shard_map/ppermute | solution.py:760
  103.9 2.8 %collective-permute-done.8.by_x = f32[4,48,128]{2,1,0:T(8,128)S(1)} collective-permute-done((f32[4,48,128]{2,1,0:T(8,128)}, f32[4,48,128]{2,1,0:T(8,128)S(1)}, u32[]{:S(2)}, u32[]{:S(2)}) %collective-permute-start.8) | collective-permute-done | bytes 98336 | tf_op jit(solution)/shard_map/ppermute | solution.py:759
  106.7 3.6 %collective-permute-done.9.by_x2 = f32[4,48,128]{2,1,0:T(8,128)S(1)} collective-permute-done((f32[4,48,128]{2,1,0:T(8,128)}, f32[4,48,128]{2,1,0:T(8,128)S(1)}, u32[]{:S(2)}, u32[]{:S(2)}) %collective-permute-start.9) | collective-permute-done | bytes 98336 | tf_op jit(solution)/shard_map/ppermute | solution.py:760
  110.3 0.8 pad_maximum_fusion.11
  111.1 0.1 collective-permute-start.11
  111.2 0.7 collective-permute-start.10
  111.8 2.8 %collective-permute-done.11.by_y2 = f32[12,8,128]{2,1,0:T(8,128)S(1)} collective-permute-done((f32[12,8,128]{2,1,0:T(8,128)S(1)}, f32[12,8,128]{2,1,0:T(8,128)S(1)}, u32[]{:S(2)}, u32[]{:S(2)}) %collective-permute-start.11) | collective-permute-done | bytes 49184 | tf_op jit(solution)/shard_map/ppermute | solution.py:722
  114.7 0.6 copy-done.17
  115.3 2.9 %shard_map.53 = (f32[12,32,128]{2,1,0:T(8,128)}, f32[12,32,128]{2,1,0:T(8,128)}, f32[16,1,8,128]{3,2,1,0:T(8,128)}) custom-call(s32[2]{0:T(128)} %pad_add_fusion.pos, f32[4,16,128]{2,1,0:T(8,128)} %get-tuple-element.30.mid, f32[4,48,128]{2,1,0:T(8,128)} %copy-done.8, f32[4,48,128]{2,1,0:T(8,128)} %copy-done.9, f32[12,8,128]{2,1,0:T(8,128)} %copy-done.18, ...), custom_call_target="tpu_custom_call" | custom-call | flops 10000000 | bytes 8388608 | tf_op jit(solution)/shard_map/pallas_call | solution.py:347
  118.2 3.7 %all-to-all-start.2 = ((f32[16,1,8,128]{3,2,1,0:T(8,128)}), f32[16,1,8,128]{3,2,1,0:T(8,128)S(1)}, u32[]{:S(2)}, u32[]{:S(2)}) async-start(f32[16,1,8,128]{3,2,1,0:T(8,128)} %get-tuple-element.34), calls=%async_computation.2 | async-start | bytes 131072 | tf_op jit(solution)/shard_map/all_to_all | solution.py:732
  122.0 6.2 %all-to-all-done.2.mid = f32[16,1,8,128]{3,2,1,0:T(8,128)S(1)} async-done(((f32[16,1,8,128]{3,2,1,0:T(8,128)}), f32[16,1,8,128]{3,2,1,0:T(8,128)S(1)}, u32[]{:S(2)}, u32[]{:S(2)}) %all-to-all-start.2) | async-done | bytes 65568 | tf_op jit(solution)/shard_map/all_to_all | solution.py:732
  128.2 1.3 collective-permute-start.13
  129.5 1.9 %collective-permute-start.12 = (f32[40,8,128]{2,1,0:T(8,128)S(1)}, f32[40,8,128]{2,1,0:T(8,128)S(1)}, u32[]{:S(2)}, u32[]{:S(2)}) collective-permute-start(f32[40,8,128]{2,1,0:T(8,128)S(1)} %get-tuple-element.51), channel_id=1, source_target_pairs={{0,1},{1,0},{2,3},{3,2},{4,5},{5,4},{6,7},{7,6},{8,9},{9,8},{10,11... | collective-permute-start | bytes 491528 | tf_op jit(solution)/shard_map/ppermute | solution.py:721
  131.4 1.6 collective-permute-done.13.by_y2
  133.1 0.7 copy-done.10
  133.8 3.1 %shard_map.54 = (f32[3,5,24,128]{3,2,1,0:T(8,128)}, f32[16,2,8,128]{3,2,1,0:T(8,128)}) custom-call(s32[2]{0:T(128)} %pad_add_fusion.pos, f32[16,1,8,128]{3,2,1,0:T(8,128)} %copy-done.12, f32[40,8,128]{2,1,0:T(8,128)} %copy-done.11, f32[40,8,128]{2,1,0:T(8,128)} %copy-done.10, f32[16,24,128]{2,1,0:T(8,128)} %get-tuple-element.36.refs_0_), custom_call_target="tpu_custom_call" | custom-call | flops 10000000 | bytes 8388608 | tf_op jit(solution)/shard_map/pallas_call | solution.py:347
  136.9 17.4 %all_to_all.20.three = f32[16,2,8,128]{3,2,1,0:T(8,128)} all-to-all(f32[16,2,8,128]{3,2,1,0:T(8,128)} %get-tuple-element.37), channel_id=1, replica_groups=mesh['gx'=16,'gy'=16] {'gy'}, dimensions={0} | all-to-all | bytes 262144 | tf_op jit(solution)/shard_map/all_to_all | solution.py:732
  154.3 11.2 %shard_map.55 = (f32[16,32,128]{2,1,0:T(8,128)}, f32[16,32,128]{2,1,0:T(8,128)}) custom-call(s32[2]{0:T(128)} %pad_add_fusion.pos, f32[32,128]{1,0:T(8,128)} %copy.25.owned, f32[16,2,8,128]{3,2,1,0:T(8,128)} %all_to_all.20.three, f32[4,64,128]{2,1,0:T(8,128)} %get-tuple-element.38.k3, f32[3,5,24,128]{3,2,1,0:T(8,128)} %get-tuple-element.39.near, ...), custom_call_target="tpu_custom_call" | custom-call | flops 10000000 | bytes 8388608 | tf_op jit(solution)/shard_map/pallas_call | solution.py:347
  (59 shorter events, 0.6 us)
Async XLA Ops:
  0.6 15.0 %copy-start.1 = (f32[16,32,128]{2,1,0:T(8,128)S(1)}, f32[16,32,128]{2,1,0:T(8,128)}, u32[]{:S(2)}) copy-start(f32[16,32,128]{2,1,0:T(8,128)} %borig.1) | copy-start | bytes 786436
  0.7 15.0 %copy-start.6 = (f32[16,32,128]{2,1,0:T(8,128)S(1)}, f32[16,32,128]{2,1,0:T(8,128)}, u32[]{:S(2)}) copy-start(f32[16,32,128]{2,1,0:T(8,128)} %param.4) | copy-start | bytes 786436
  2.1 8.4 %collective-permute-start = (f32[2,10,32,128]{3,2,1,0:T(8,128)S(1)}, f32[2,10,32,128]{3,2,1,0:T(8,128)S(1)}, u32[]{:S(2)}, u32[]{:S(2)}) collective-permute-start(f32[2,10,32,128]{3,2,1,0:T(8,128)S(1)} %get-tuple-element.48), channel_id=1, source_target_pairs={{0,16},{16,0},{32,48},{48,32},{64,80},{80,64},{96,112},{112,96},{1... | collective-permute-start | bytes 983048 | tf_op jit(solution)/shard_map/ppermute | solution.py:721
  4.3 11.3 %collective-permute-start.1 = (f32[2,10,32,128]{3,2,1,0:T(8,128)S(1)}, f32[2,10,32,128]{3,2,1,0:T(8,128)S(1)}, u32[]{:S(2)}, u32[]{:S(2)}) collective-permute-start(f32[2,10,32,128]{3,2,1,0:T(8,128)S(1)} %get-tuple-element.49), channel_id=1, source_target_pairs={{0,240},{16,32},{32,16},{48,64},{64,48},{80,96},{96,80},{112,128},... | collective-permute-start | bytes 983048 | tf_op jit(solution)/shard_map/ppermute | solution.py:722
  15.8 1.0 copy-start
  16.9 4.4 %collective-permute-start.2 = (f32[720,128]{1,0:T(8,128)S(1)}, f32[720,128]{1,0:T(8,128)S(1)}, u32[]{:S(2)}, u32[]{:S(2)}) collective-permute-start(f32[720,128]{1,0:T(8,128)S(1)} %select_n.130), channel_id=1, source_target_pairs={{0,1},{1,0},{2,3},{3,2},{4,5},{5,4},{6,7},{7,6},{8,9},{9,8},{10,11... | collective-permute-start | bytes 1105928 | tf_op jit(solution)/shard_map/ppermute | solution.py:721
  19.1 7.2 %collective-permute-start.3 = (f32[720,128]{1,0:T(8,128)S(1)}, f32[720,128]{1,0:T(8,128)S(1)}, u32[]{:S(2)}, u32[]{:S(2)}) collective-permute-start(f32[720,128]{1,0:T(8,128)S(1)} %select_n.132), channel_id=1, source_target_pairs={{0,15},{1,2},{2,1},{3,4},{4,3},{5,6},{6,5},{7,8},{8,7},{9,10},{10,... | collective-permute-start | bytes 1105928 | tf_op jit(solution)/shard_map/ppermute | solution.py:722
  21.3 5.0 %copy-start.15 = (f32[720,128]{1,0:T(8,128)}, f32[720,128]{1,0:T(8,128)S(1)}, u32[]{:S(2)}) copy-start(f32[720,128]{1,0:T(8,128)S(1)} %collective-permute-done.2.by_y) | copy-start | bytes 1105924
  26.4 0.7 copy-start.16
  34.8 7.7 %collective-permute-start.5 = (f32[3,4,16,128]{3,2,1,0:T(8,128)}, f32[3,4,16,128]{3,2,1,0:T(8,128)S(1)}, u32[]{:S(2)}, u32[]{:S(2)}) collective-permute-start(f32[3,4,16,128]{3,2,1,0:T(8,128)} %get-tuple-element.24.one), channel_id=1, source_target_pairs={{0,240},{16,32},{32,16},{48,64},{64,48},{80,96},{96,80},{112,128},... | collective-permute-start | bytes 294920 | tf_op jit(solution)/shard_map/ppermute | solution.py:722
  39.0 3.7 %collective-permute-start.4 = (f32[3,4,16,128]{3,2,1,0:T(8,128)}, f32[3,4,16,128]{3,2,1,0:T(8,128)S(1)}, u32[]{:S(2)}, u32[]{:S(2)}) collective-permute-start(f32[3,4,16,128]{3,2,1,0:T(8,128)} %get-tuple-element.24.one), channel_id=1, source_target_pairs={{0,16},{16,0},{32,48},{48,32},{64,80},{80,64},{96,112},{112,96},{1... | collective-permute-start | bytes 294920 | tf_op jit(solution)/shard_map/ppermute | solution.py:721
  39.0 10.2 %all-to-all-start = ((f32[16,2,8,128]{3,2,1,0:T(8,128)}), f32[16,2,8,128]{3,2,1,0:T(8,128)S(1)}, u32[]{:S(2)}, u32[]{:S(2)}) async-start(f32[16,2,8,128]{3,2,1,0:T(8,128)} %get-tuple-element.23), calls=%async_computation | async-start | bytes 262144 | tf_op jit(solution)/shard_map/all_to_all | solution.py:732
  42.5 6.7 %copy-start.13 = (f32[3,4,16,128]{3,2,1,0:T(8,128)}, f32[3,4,16,128]{3,2,1,0:T(8,128)S(1)}, u32[]{:S(2)}) copy-start(f32[3,4,16,128]{3,2,1,0:T(8,128)S(1)} %collective-permute-done.5.by_x2) | copy-start | bytes 294916
  42.7 6.6 %copy-start.14 = (f32[3,4,16,128]{3,2,1,0:T(8,128)}, f32[3,4,16,128]{3,2,1,0:T(8,128)S(1)}, u32[]{:S(2)}) copy-start(f32[3,4,16,128]{3,2,1,0:T(8,128)S(1)} %collective-permute-done.4.by_x) | copy-start | bytes 294916
  49.2 9.0 %copy-start.3 = (f32[16,2,8,128]{3,2,1,0:T(8,128)}, f32[16,2,8,128]{3,2,1,0:T(8,128)S(1)}, u32[]{:S(2)}) copy-start(f32[16,2,8,128]{3,2,1,0:T(8,128)S(1)} %all-to-all-done.mid) | copy-start | bytes 393220
  49.2 23.3 %copy-start.19 = (s32[16,16]{1,0:T(8,128)S(1)}, s32[16,16]{1,0:T(8,128)}, u32[]{:S(2)}) copy-start(s32[16,16]{1,0:T(8,128)} %param.5) | copy-start | bytes 3076
  49.3 7.7 %collective-permute-start.7 = (f32[68,8,128]{2,1,0:T(8,128)S(1)}, f32[68,8,128]{2,1,0:T(8,128)S(1)}, u32[]{:S(2)}, u32[]{:S(2)}) collective-permute-start(f32[68,8,128]{2,1,0:T(8,128)S(1)} %get-tuple-element.52), channel_id=1, source_target_pairs={{0,15},{1,2},{2,1},{3,4},{4,3},{5,6},{6,5},{7,8},{8,7},{9,10},{10,... | collective-permute-start | bytes 835592 | tf_op jit(solution)/shard_map/ppermute | solution.py:722
  52.5 5.7 %collective-permute-start.6 = (f32[68,8,128]{2,1,0:T(8,128)S(1)}, f32[68,8,128]{2,1,0:T(8,128)S(1)}, u32[]{:S(2)}, u32[]{:S(2)}) collective-permute-start(f32[68,8,128]{2,1,0:T(8,128)S(1)} %get-tuple-element.53), channel_id=1, source_target_pairs={{0,1},{1,0},{2,3},{3,2},{4,5},{5,4},{6,7},{7,6},{8,9},{9,8},{10,11... | collective-permute-start | bytes 835592 | tf_op jit(solution)/shard_map/ppermute | solution.py:721
  57.0 1.2 copy-start.4
  58.2 0.7 copy-start.5
  62.2 23.4 %all-to-all-start.1 = ((f32[16,5,8,128]{3,2,1,0:T(8,128)}), f32[16,5,8,128]{3,2,1,0:T(8,128)S(1)}, u32[]{:S(2)}, u32[]{:S(2)}) async-start(f32[16,5,8,128]{3,2,1,0:T(8,128)} %get-tuple-element.25), calls=%async_computation.1 | async-start | bytes 655360 | tf_op jit(solution)/shard_map/all_to_all | solution.py:732
  85.6 0.7 copy-start.2
  101.8 26.4 %copy-start.7 = (f32[16,32,128]{2,1,0:T(8,128)S(1)}, f32[16,32,128]{2,1,0:T(8,128)}, u32[]{:S(2)}) copy-start(f32[16,32,128]{2,1,0:T(8,128)} %get-tuple-element.35.x0n) | copy-start | bytes 786436
  101.8 4.9 %collective-permute-start.8 = (f32[4,48,128]{2,1,0:T(8,128)}, f32[4,48,128]{2,1,0:T(8,128)S(1)}, u32[]{:S(2)}, u32[]{:S(2)}) collective-permute-start(f32[4,48,128]{2,1,0:T(8,128)} %get-tuple-element.31), channel_id=1, source_target_pairs={{0,16},{16,0},{32,48},{48,32},{64,80},{80,64},{96,112},{112,96},{1... | collective-permute-start | bytes 294920 | tf_op jit(solution)/shard_map/ppermute | solution.py:759
  102.0 8.2 %collective-permute-start.9 = (f32[4,48,128]{2,1,0:T(8,128)}, f32[4,48,128]{2,1,0:T(8,128)S(1)}, u32[]{:S(2)}, u32[]{:S(2)}) collective-permute-start(f32[4,48,128]{2,1,0:T(8,128)} %get-tuple-element.32), channel_id=1, source_target_pairs={{0,240},{16,32},{32,16},{48,64},{64,48},{80,96},{96,80},{112,128},... | collective-permute-start | bytes 294920 | tf_op jit(solution)/shard_map/ppermute | solution.py:760
  106.7 8.0 %copy-start.8 = (f32[4,48,128]{2,1,0:T(8,128)}, f32[4,48,128]{2,1,0:T(8,128)S(1)}, u32[]{:S(2)}) copy-start(f32[4,48,128]{2,1,0:T(8,128)S(1)} %collective-permute-done.8.by_x) | copy-start | bytes 294916
  110.2 4.5 %copy-start.9 = (f32[4,48,128]{2,1,0:T(8,128)}, f32[4,48,128]{2,1,0:T(8,128)S(1)}, u32[]{:S(2)}) copy-start(f32[4,48,128]{2,1,0:T(8,128)S(1)} %collective-permute-done.9.by_x2) | copy-start | bytes 294916
  111.1 3.6 %collective-permute-start.11 = (f32[12,8,128]{2,1,0:T(8,128)S(1)}, f32[12,8,128]{2,1,0:T(8,128)S(1)}, u32[]{:S(2)}, u32[]{:S(2)}) collective-permute-start(f32[12,8,128]{2,1,0:T(8,128)S(1)} %get-tuple-element.60), channel_id=1, source_target_pairs={{0,15},{1,2},{2,1},{3,4},{4,3},{5,6},{6,5},{7,8},{8,7},{9,10},{10,... | collective-permute-start | bytes 147464 | tf_op jit(solution)/shard_map/ppermute | solution.py:722
  111.2 3.5 %collective-permute-start.10 = (f32[12,8,128]{2,1,0:T(8,128)S(1)}, f32[12,8,128]{2,1,0:T(8,128)S(1)}, u32[]{:S(2)}, u32[]{:S(2)}) collective-permute-start(f32[12,8,128]{2,1,0:T(8,128)S(1)} %get-tuple-element.61), channel_id=1, source_target_pairs={{0,1},{1,0},{2,3},{3,2},{4,5},{5,4},{6,7},{7,6},{8,9},{9,8},{10,11... | collective-permute-start | bytes 147464 | tf_op jit(solution)/shard_map/ppermute | solution.py:721
  114.7 0.6 copy-start.17
  114.7 0.6 copy-start.18
  118.2 10.0 %all-to-all-start.2 = ((f32[16,1,8,128]{3,2,1,0:T(8,128)}), f32[16,1,8,128]{3,2,1,0:T(8,128)S(1)}, u32[]{:S(2)}, u32[]{:S(2)}) async-start(f32[16,1,8,128]{3,2,1,0:T(8,128)} %get-tuple-element.34), calls=%async_computation.2 | async-start | bytes 131072 | tf_op jit(solution)/shard_map/all_to_all | solution.py:732
  128.2 4.9 %copy-start.12 = (f32[16,1,8,128]{3,2,1,0:T(8,128)}, f32[16,1,8,128]{3,2,1,0:T(8,128)S(1)}, u32[]{:S(2)}) copy-start(f32[16,1,8,128]{3,2,1,0:T(8,128)S(1)} %all-to-all-done.2.mid) | copy-start | bytes 196612
  128.2 4.8 %collective-permute-start.13 = (f32[40,8,128]{2,1,0:T(8,128)S(1)}, f32[40,8,128]{2,1,0:T(8,128)S(1)}, u32[]{:S(2)}, u32[]{:S(2)}) collective-permute-start(f32[40,8,128]{2,1,0:T(8,128)S(1)} %get-tuple-element.50), channel_id=1, source_target_pairs={{0,15},{1,2},{2,1},{3,4},{4,3},{5,6},{6,5},{7,8},{8,7},{9,10},{10,... | collective-permute-start | bytes 491528 | tf_op jit(solution)/shard_map/ppermute | solution.py:722
  129.5 3.5 %collective-permute-start.12 = (f32[40,8,128]{2,1,0:T(8,128)S(1)}, f32[40,8,128]{2,1,0:T(8,128)S(1)}, u32[]{:S(2)}, u32[]{:S(2)}) collective-permute-start(f32[40,8,128]{2,1,0:T(8,128)S(1)} %get-tuple-element.51), channel_id=1, source_target_pairs={{0,1},{1,0},{2,3},{3,2},{4,5},{5,4},{6,7},{7,6},{8,9},{9,8},{10,11... | collective-permute-start | bytes 491528 | tf_op jit(solution)/shard_map/ppermute | solution.py:721
  133.0 0.7 copy-start.10
  133.0 0.7 copy-start.11

commit v7 on v6

--- a/solution.py
+++ b/solution.py
@@ -572,25 +572,28 @@
 
 
 def turn_kernel(
-    pos, owned, three, near, one, by_x, by_x2, by_y, by_y2, *refs
+    pos, owned, three, *refs
 ):
     gx, gy = pos[0], pos[1]
+    fars, (b1n, send, send2, *far_outs) = refs[:9], refs[9:17]
+    b3, s3, e2, s2, x2s, b1s, s1, e0, d, x, rs, xout, rout, k3, k1, x0n = refs[17:33]
+    tops, (wx, wy, wz, s, rd), sems = refs[33:42], refs[42:47], refs[47]
+    near, one, by_x, by_x2, by_y, by_y2, b0, k0, x0 = tops
     left, right = sides(gx, by_x, by_x2)
     below, above = sides(gy, by_y, by_y2)
-    fars, (x0n, b1n, send, send2, *far_outs) = refs[:3], refs[3:11]
-    b3, s3, e2, s2, x2s, b1s, s1, e0, d, x, rs, xout, rout, k3, k1 = refs[11:26]
-    tops, sems = refs[26:29], refs[34]
-    (b0, k0, x0), (wx, wy, wz, s, rd) = tops, refs[29:34]
-    loads = moves(fars, tops, sems)
+    part = pl.ds(32, 36)
+    loads = moves(fars[:4] + (fars[4].at[part], fars[5].at[part]) + fars[6:], tops, sems)
     for move in loads:
         move.start()
-    xkeep, rkeep, kkeep, k1keep = (
-        pltpu.make_async_copy(a, b, sems.at[3 + i]) for i, (a, b) in enumerate(zip((xout, rout, k3, k1), far_outs))
-    )
+    keeps = xkeep, rkeep, kkeep, k1keep, x0keep = [
+        pltpu.make_async_copy(a, b, sems.at[9 + i])
+        for i, (a, b) in enumerate(zip((xout, rout, k3, k1, x0n), far_outs))
+    ]
     fill_three(b3, three, 0)
     fill_three(k3, three, 2)
     kkeep.start()
     solve_three(b3, k3, owned, s3)
+    loads[0].wait()
     x2s[...] = near[1]
     lower, upper = lax.rem(gy + 15, 16), lax.rem(gy + 1, 16)
     for i in range(5):
@@ -598,16 +601,18 @@
         x2s[i, 22:23, :] = three[upper, 4, i : i + 1, :]
     rise_two(gx, gy, near, x2s[...], s3, e2, s2)
 
+    for move in loads[1:6]:
+        move.wait()
     inside = within((12, 32, 128), gx * 8 - 8, gy * 16 - 8, 64, 128, 256)
     for number, dst in enumerate((b1s, s1, k1)):
-        part = slice(32 + 12 * number, 44 + 12 * number)
+        part = slice(12 * number, 12 * number + 12)
         fill_one(dst, left[number], one[number], right[number], below[part], above[part])
     k1[...] = jnp.where(inside, k1[...], 0.0)
     k1keep.start()
     rise_one(s1[...], b1s[...], k1[...], inside, s2, s1)
 
     spread_one(s1, 2, 10, e0)
-    for move in loads:
+    for move in loads[6:]:
         move.wait()
     inside_at = insider(RY, gx * TX - HX, gy * TY - HY)
     build_top(k0, wx, wy, wz, s, rd, 2, PX - 2, inside_at, add_top(x0, e0, x))
@@ -638,8 +643,9 @@
     def again(p, at, v, av):
         d[at] = rout[pl.ds(p - 6, v.shape[0])] - av
 
+    x0n[...] = x[HX : HX + TX, HY : HY + TY, :]
+    x0keep.start()
     sweep_top(x, wx, wy, wz, s, HX, HX + TX, again)
-    x0n[...] = x[HX : HX + TX, HY : HY + TY, :]
     for c in range(8):
         rs[c] = d[HX + 2 * c] + d[HX + 1 + 2 * c]
     b1 = pair_planes(rs, 4, HY, 16)
@@ -648,48 +654,55 @@
     for side, of_odd, of_even in ((send, HX, HX + TX - 4), (send2, HX + TX - 4, HX)):
         side[:, 0:16, :] = b1
         side[:, 16:48, :] = x[pl.ds(jnp.where(odd, of_odd, of_even), 4), HY : HY + TY, :]
-    for move in (xkeep, rkeep, kkeep, k1keep):
+    for move in keeps:
         move.wait()
 
 
 def go_turn(*args):
-    top, wide, three = (PX, RY, 128), (12, 32, 128), (4, 64, 128)
-    kept = [(TX + 2, RY, 128), (TX + 8, RY, 128), three, wide]
-    outs = [(TX, TY, 128), (4, 16, 128), (4, 48, 128), (4, 48, 128)] + kept
+    top, wide, three, one = (PX, RY, 128), (12, 32, 128), (4, 64, 128), (3, 4, 16, 128)
+    kept = [(TX + 2, RY, 128), (TX + 8, RY, 128), three, wide, (TX, TY, 128)]
+    outs = [(4, 16, 128), (4, 48, 128), (4, 48, 128)] + kept
     scratch = [three, (4, 88, 128), (5, 48, 128), (5, 24, 128), (5, 24, 128), wide, wide, (16, RY, 128)]
-    scratch += [top] * 2 + [(8, RY, 128)] + kept + [top] * 8
-    return call(turn_kernel, outs, scratch, *args, far_in=3, far_out=4, copies=7)
+    scratch += [top] * 2 + [(8, RY, 128)] + kept + [(3, 5, 24, 128)] + [one] * 3 + [(36, 8, 128)] * 2 + [top] * 8
+    return call(turn_kernel, outs, scratch, *args, far_in=9, far_out=5, copies=14)
 
 
 def last_kernel(
-    pos, owned, three, k3, near, b1, x1, k1, x0n, by_x, by_x2, by_y, by_y2, borig, *refs
+    pos, owned, three, k3, *refs
 ):
     gx, gy = pos[0], pos[1]
+    fars, far_outs, (b3, s3, e2, s2, s1, e0, d, x) = refs[:13], refs[13:15], refs[15:23]
+    tops, (wx, wy, wz, s, rd, xout, rout), sems = refs[23:36], refs[36:43], refs[43]
+    near, b1, x1, k1, by_x, by_x2, by_y, by_y2, x0n, k0, r, xbefore, borig = tops
     left, right = sides(gx, by_x, by_x2)
     below, above = sides(gy, by_y, by_y2)
-    fars, (xout, rout), (b3, s3, e2, s2, s1, e0, d, x) = refs[:3], refs[3:5], refs[5:13]
-    tops, sems = refs[13:16], refs[21]
-    (r, xbefore, k0), (wx, wy, wz, s, rd) = tops, refs[16:21]
-    loads = moves(fars, tops, sems)
+    part = pl.ds(16, 24)
+    loads = moves(fars[:6] + (fars[6].at[part], fars[7].at[part]) + fars[8:], tops, sems)
     for move in loads:
         move.start()
+    keeps = [
+        pltpu.make_async_copy(a, b, sems.at[13 + i]) for i, (a, b) in enumerate(zip((xout, rout), far_outs))
+    ]
     fill_three(b3, three, 0)
     solve_three(b3, k3, owned, s3)
+    loads[0].wait()
     rise_two(gx, gy, near, near[1], s3, e2, s2)
+    for move in loads[1:4]:
+        move.wait()
     inside = within((12, 32, 128), gx * 8 - 8, gy * 16 - 8, 64, 128, 256)
     rise_one(x1[...], b1[...], k1[...], inside, s2, s1)
 
     spread_one(s1, 3, 9, e0)
+    for move in loads[4:]:
+        move.wait()
     low, high = HX - 4, HX + TX + 4
     x[low:HX, HY : HY + TY, :] = left[:, 16:48, :]
     x[HX : HX + TX, HY : HY + TY, :] = x0n[...]
     x[HX + TX : high, HY : HY + TY, :] = right[:, 16:48, :]
-    x[low:high, HY - 8 : HY, :] = below[16:40]
-    x[low:high, HY + TY : HY + TY + 8, :] = above[16:40]
+    x[low:high, HY - 8 : HY, :] = below[...]
+    x[low:high, HY + TY : HY + TY + 8, :] = above[...]
     x[low:high, 0 : HY - 8, :] = jnp.zeros((high - low, HY - 8, 128), F32)
     x[low:high, RY - 4 : RY, :] = jnp.zeros((high - low, 4, 128), F32)
-    for move in loads:
-        move.wait()
     inside_at = insider(RY, gx * TX - HX, gy * TY - HY)
     build_top(k0, wx, wy, wz, s, rd, low, high, inside_at, add_top(x, e0, x))
     sweep_top(x, wx, wy, wz, s, low, high, open_top(r, low, rd, d, x))
@@ -700,16 +713,21 @@
     def residual(p, at, v, av):
         d[at] = av
 
+    xout[...] = x[HX : HX + TX, HY : HY + TY, :]
+    keeps[0].start()
     sweep_top(x, wx, wy, wz, s, HX, HX + TX, residual)
-    xout[...] = x[HX : HX + TX, HY : HY + TY, :]
     rout[...] = borig[...] - d[HX : HX + TX, HY : HY + TY, :]
+    keeps[1].start()
+    for move in keeps:
+        move.wait()
 
 
 def go_last(*args):
     top, wide, tile = (PX, RY, 128), (12, 32, 128), (TX, TY, 128)
     scratch = [(4, 64, 128), (4, 88, 128), (5, 48, 128), (5, 24, 128), wide, (16, RY, 128)] + [top] * 2
-    scratch += [(TX + 8, RY, 128), (TX + 2, RY, 128)] + [top] * 6
-    return call(last_kernel, [tile, tile], scratch, *args, far_in=3, copies=3)
+    scratch += [(3, 5, 24, 128)] + [wide] * 3 + [(4, 48, 128)] * 2 + [(24, 8, 128)] * 2
+    scratch += [tile, top, (TX + 8, RY, 128), (TX + 2, RY, 128), tile] + [top] * 5 + [tile] * 2
+    return call(last_kernel, [tile, tile], scratch, *args, far_in=13, far_out=2, copies=15)
 
 
 def swap(low, high, axis):
@@ -751,7 +769,7 @@
     by_y = swap(low, high, "gy")
     near, three, k2 = go_mid(True, pos, two, *by_y, None)
     three = gather(three, "gy")
-    x0n, b1n, send, send2, xbefore, source, k3, k1 = go_turn(
+    b1n, send, send2, xbefore, source, k3, k1, x0n = go_turn(
         pos, owned, three, near, one, *by_x, *by_y, b0, k0, x0
     )
 
@@ -769,7 +787,7 @@
     near, three = go_mid(False, pos, two, *by_y, k2)
     three = gather(three, "gy")
     field, residual = go_last(
-        pos, owned, three, k3, near, b1, x1, k1, x0n, *by_x, *by_y, right_side, source, xbefore, k0
+        pos, owned, three, k3, near, b1, x1, k1, *by_x, *by_y, x0n, k0, source, xbefore, right_side
     )
     return field, residual
 

time: 166 us -> 165 us (level)
  no operation moved by 1% of the time
where the time goes in v7:
time: 165 us
  waiting for transfers between devices  48.3 us (29%)
  starting transfers between devices  45.7 us (28%)
  Pallas kernels  42.5 us (26%)
  blocking collectives  17.4 us (11%)
  local copies, waits for them, and re-layouts  5.46 us (3%)
  other arithmetic  4.06 us (2%)
    pallas_call x6, Pallas kernels, call(): pl.pallas_call(kernel, out_shape=[jax.ShapeDtypeStruct(o, F32) for o in o...  42.5 us
    all_to_all x3, waiting for transfers between devices, gather(): return lax.all_to_all(copies, axis, 0, 0, tiled=True)  23.9 us
    all_to_all x3, starting transfers between devices, gather(): return lax.all_to_all(copies, axis, 0, 0, tiled=True)  17.6 us
    all_to_all x1, blocking collectives, gather(): return lax.all_to_all(copies, axis, 0, 0, tiled=True)  17.4 us
    ppermute x6, waiting for transfers between devices, swap(): lax.ppermute(second, axis, [(i, (i + 1 if i % 2 else i - 1) % count) for...  14.6 us
    ppermute x6, starting transfers between devices, swap(): lax.ppermute(second, axis, [(i, (i + 1 if i % 2 else i - 1) % count) for...  14.5 us
    ppermute x6, starting transfers between devices, swap(): lax.ppermute(first, axis, [(i, i ^ 1) for i in range(count)])  11.5 us
    unnamed x40, local copies, waits for them, and re-layouts  4.49 us
  transfers between devices with their start and end apart: 17, of which 12 were waited for; matrix products, arithmetic and copies ran while one was open for 1% of the time, Pallas kernels for 0%

profile of v7, /device:TPU:1, one launch (start us, length us, event | category | flops | bytes accessed | tf_op | source)
XLA Modules:
  0.0 164.5 jit_solution(2862770919513915160)
XLA Ops:
  0.7 1.4 fusion.3
  2.1 2.2 %collective-permute-start = (f32[2,10,32,128]{3,2,1,0:T(8,128)S(1)}, f32[2,10,32,128]{3,2,1,0:T(8,128)S(1)}, u32[]{:S(2)}, u32[]{:S(2)}) collective-permute-start(f32[2,10,32,128]{3,2,1,0:T(8,128)S(1)} %get-tuple-element.48), channel_id=1, source_target_pairs={{0,16},{16,0},{32,48},{48,32},{64,80},{80,64},{96,112},{112,96},{1... | collective-permute-start | bytes 983048 | tf_op jit(solution)/shard_map/ppermute | solution.py:739
  4.3 4.1 %collective-permute-start.1 = (f32[2,10,32,128]{3,2,1,0:T(8,128)S(1)}, f32[2,10,32,128]{3,2,1,0:T(8,128)S(1)}, u32[]{:S(2)}, u32[]{:S(2)}) collective-permute-start(f32[2,10,32,128]{3,2,1,0:T(8,128)S(1)} %get-tuple-element.49), channel_id=1, source_target_pairs={{0,240},{16,32},{32,16},{48,64},{64,48},{80,96},{96,80},{112,128},... | collective-permute-start | bytes 983048 | tf_op jit(solution)/shard_map/ppermute | solution.py:740
  8.4 2.1 %collective-permute-done = f32[2,10,32,128]{3,2,1,0:T(8,128)S(1)} collective-permute-done((f32[2,10,32,128]{3,2,1,0:T(8,128)S(1)}, f32[2,10,32,128]{3,2,1,0:T(8,128)S(1)}, u32[]{:S(2)}, u32[]{:S(2)}) %collective-permute-start) | collective-permute-done | bytes 327712 | tf_op jit(solution)/shard_map/ppermute | solution.py:739
  10.5 5.1 %collective-permute-done.1 = f32[2,10,32,128]{3,2,1,0:T(8,128)S(1)} collective-permute-done((f32[2,10,32,128]{3,2,1,0:T(8,128)S(1)}, f32[2,10,32,128]{3,2,1,0:T(8,128)S(1)}, u32[]{:S(2)}, u32[]{:S(2)}) %collective-permute-start.1) | collective-permute-done | bytes 327712 | tf_op jit(solution)/shard_map/ppermute | solution.py:740
  15.7 0.1 pad_maximum_fusion.wide
  15.8 0.1 slice_select_fusion
  15.9 0.9 copy-done
  16.9 2.2 %collective-permute-start.2 = (f32[720,128]{1,0:T(8,128)S(1)}, f32[720,128]{1,0:T(8,128)S(1)}, u32[]{:S(2)}, u32[]{:S(2)}) collective-permute-start(f32[720,128]{1,0:T(8,128)S(1)} %select_n.130), channel_id=1, source_target_pairs={{0,1},{1,0},{2,3},{3,2},{4,5},{5,4},{6,7},{7,6},{8,9},{9,8},{10,11... | collective-permute-start | bytes 1105928 | tf_op jit(solution)/shard_map/ppermute | solution.py:739
  19.1 1.6 collective-permute-start.3
  20.8 0.6 pad_add_fusion.pos
  21.3 5.0 %collective-permute-done.3.by_y2 = f32[720,128]{1,0:T(8,128)S(1)} collective-permute-done((f32[720,128]{1,0:T(8,128)S(1)}, f32[720,128]{1,0:T(8,128)S(1)}, u32[]{:S(2)}, u32[]{:S(2)}) %collective-permute-start.3) | collective-permute-done | bytes 368672 | tf_op jit(solution)/shard_map/ppermute | solution.py:740
  26.4 0.7 copy-done.16
  27.1 7.7 %shard_map.50 = (f32[3,4,16,128]{3,2,1,0:T(8,128)}, f32[16,2,8,128]{3,2,1,0:T(8,128)}, f32[36,56,128]{2,1,0:T(8,128)}, f32[36,56,128]{2,1,0:T(8,128)}, f32[36,56,128]{2,1,0:T(8,128)}) custom-call(s32[2]{0:T(128)} %pad_add_fusion.pos, f32[2,36,32,128]{3,2,1,0:T(8,128)} %copy-done, f32[720,128]{1,0:T(8,128)} %copy-done.15, f32[720,128]{1,0:T(8,128)} %copy-done.16), custom_call_target="tpu_custom_call" | custom-call | flops 10000000 | bytes 8388608 | tf_op jit(solution)/shard_map/pallas_call | solution.py:347
  34.8 4.2 %collective-permute-start.5 = (f32[3,4,16,128]{3,2,1,0:T(8,128)}, f32[3,4,16,128]{3,2,1,0:T(8,128)S(1)}, u32[]{:S(2)}, u32[]{:S(2)}) collective-permute-start(f32[3,4,16,128]{3,2,1,0:T(8,128)} %get-tuple-element.24.refs_1_), channel_id=1, source_target_pairs={{0,240},{16,32},{32,16},{48,64},{64,48},{80,96},{96,80},{112,128},... | collective-permute-start | bytes 294920 | tf_op jit(solution)/shard_map/ppermute | solution.py:740
  39.0 3.5 %all-to-all-start = ((f32[16,2,8,128]{3,2,1,0:T(8,128)}), f32[16,2,8,128]{3,2,1,0:T(8,128)S(1)}, u32[]{:S(2)}, u32[]{:S(2)}) async-start(f32[16,2,8,128]{3,2,1,0:T(8,128)} %get-tuple-element.23), calls=%async_computation | async-start | bytes 262144 | tf_op jit(solution)/shard_map/all_to_all | solution.py:750
  42.5 0.1 collective-permute-done.4.refs_2_
  42.7 0.9 pad_maximum_fusion.4
  43.7 5.5 %all-to-all-done.mid = f32[16,2,8,128]{3,2,1,0:T(8,128)S(1)} async-done(((f32[16,2,8,128]{3,2,1,0:T(8,128)}), f32[16,2,8,128]{3,2,1,0:T(8,128)S(1)}, u32[]{:S(2)}, u32[]{:S(2)}) %all-to-all-start) | async-done | bytes 131104 | tf_op jit(solution)/shard_map/all_to_all | solution.py:750
  49.3 3.2 %collective-permute-start.7 = (f32[68,8,128]{2,1,0:T(8,128)S(1)}, f32[68,8,128]{2,1,0:T(8,128)S(1)}, u32[]{:S(2)}, u32[]{:S(2)}) collective-permute-start(f32[68,8,128]{2,1,0:T(8,128)S(1)} %get-tuple-element.52), channel_id=1, source_target_pairs={{0,15},{1,2},{2,1},{3,4},{4,3},{5,6},{6,5},{7,8},{8,7},{9,10},{10,... | collective-permute-start | bytes 835592 | tf_op jit(solution)/shard_map/ppermute | solution.py:740
  52.5 4.5 %collective-permute-start.6 = (f32[68,8,128]{2,1,0:T(8,128)S(1)}, f32[68,8,128]{2,1,0:T(8,128)S(1)}, u32[]{:S(2)}, u32[]{:S(2)}) collective-permute-start(f32[68,8,128]{2,1,0:T(8,128)S(1)} %get-tuple-element.53), channel_id=1, source_target_pairs={{0,1},{1,0},{2,3},{3,2},{4,5},{5,4},{6,7},{7,6},{8,9},{9,8},{10,11... | collective-permute-start | bytes 835592 | tf_op jit(solution)/shard_map/ppermute | solution.py:739
  57.0 1.2 collective-permute-done.6.by_y.refs_4_
  58.2 0.7 copy-done.5
  58.9 3.3 %shard_map.51 = (f32[3,5,24,128]{3,2,1,0:T(8,128)}, f32[16,5,8,128]{3,2,1,0:T(8,128)}, f32[16,24,128]{2,1,0:T(8,128)}) custom-call(s32[2]{0:T(128)} %pad_add_fusion.pos, f32[16,2,8,128]{3,2,1,0:T(8,128)} %copy-done.3, f32[68,8,128]{2,1,0:T(8,128)} %copy-done.5, f32[68,8,128]{2,1,0:T(8,128)} %copy-done.4), custom_call_target="tpu_custom_call" | custom-call | flops 10000000 | bytes 8388608 | tf_op jit(solution)/shard_map/pallas_call | solution.py:347
  62.2 10.3 %all-to-all-start.1 = ((f32[16,5,8,128]{3,2,1,0:T(8,128)}), f32[16,5,8,128]{3,2,1,0:T(8,128)S(1)}, u32[]{:S(2)}, u32[]{:S(2)}) async-start(f32[16,5,8,128]{3,2,1,0:T(8,128)} %get-tuple-element.25), calls=%async_computation.1 | async-start | bytes 655360 | tf_op jit(solution)/shard_map/all_to_all | solution.py:750
  72.7 0.7 copy.25.owned
  73.3 12.2 %all-to-all-done.1.three = f32[16,5,8,128]{3,2,1,0:T(8,128)S(1)} async-done(((f32[16,5,8,128]{3,2,1,0:T(8,128)}), f32[16,5,8,128]{3,2,1,0:T(8,128)S(1)}, u32[]{:S(2)}, u32[]{:S(2)}) %all-to-all-start.1) | async-done | bytes 327712 | tf_op jit(solution)/shard_map/all_to_all | solution.py:750
  85.6 0.7 copy-done.2
  86.3 14.6 %shard_map.52 = (f32[4,16,128]{2,1,0:T(8,128)}, f32[4,48,128]{2,1,0:T(8,128)}, f32[4,48,128]{2,1,0:T(8,128)}, f32[18,56,128]{2,1,0:T(8,128)}, f32[24,56,128]{2,1...) custom-call(s32[2]{0:T(128)} %pad_add_fusion.pos, f32[32,128]{1,0:T(8,128)} %copy.25.owned, ...), custom_call_target="tpu_custom_call" | custom-call | flops 10000000 | bytes 8388608 | tf_op jit(solution)/shard_map/pallas_call | solution.py:347
  100.9 0.3 collective-permute-start.8
  101.2 1.9 %collective-permute-start.9 = (f32[4,48,128]{2,1,0:T(8,128)}, f32[4,48,128]{2,1,0:T(8,128)S(1)}, u32[]{:S(2)}, u32[]{:S(2)}) collective-permute-start(f32[4,48,128]{2,1,0:T(8,128)} %get-tuple-element.32), channel_id=1, source_target_pairs={{0,240},{16,32},{32,16},{48,64},{64,48},{80,96},{96,80},{112,128},... | collective-permute-start | bytes 294920 | tf_op jit(solution)/shard_map/ppermute | solution.py:778
  103.0 2.8 %collective-permute-done.8.by_x.refs_4_ = f32[4,48,128]{2,1,0:T(8,128)S(1)} collective-permute-done((f32[4,48,128]{2,1,0:T(8,128)}, f32[4,48,128]{2,1,0:T(8,128)S(1)}, u32[]{:S(2)}, u32[]{:S(2)}) %collective-permute-start.8) | collective-permute-done | bytes 98336 | tf_op jit(solution)/shard_map/ppermute | solution.py:777
  105.8 3.6 %collective-permute-done.9.by_x2.refs_5_ = f32[4,48,128]{2,1,0:T(8,128)S(1)} collective-permute-done((f32[4,48,128]{2,1,0:T(8,128)}, f32[4,48,128]{2,1,0:T(8,128)S(1)}, u32[]{:S(2)}, u32[]{:S(2)}) %collective-permute-start.9) | collective-permute-done | bytes 98336 | tf_op jit(solution)/shard_map/ppermute | solution.py:778
  109.4 0.8 pad_maximum_fusion.11
  110.2 0.1 collective-permute-start.11
  110.3 0.7 collective-permute-start.10
  111.0 2.8 %collective-permute-done.11.by_y2 = f32[12,8,128]{2,1,0:T(8,128)S(1)} collective-permute-done((f32[12,8,128]{2,1,0:T(8,128)S(1)}, f32[12,8,128]{2,1,0:T(8,128)S(1)}, u32[]{:S(2)}, u32[]{:S(2)}) %collective-permute-start.11) | collective-permute-done | bytes 49184 | tf_op jit(solution)/shard_map/ppermute | solution.py:740
  113.8 0.6 copy-done.17
  114.4 2.9 %shard_map.53 = (f32[12,32,128]{2,1,0:T(8,128)}, f32[12,32,128]{2,1,0:T(8,128)}, f32[16,1,8,128]{3,2,1,0:T(8,128)}) custom-call(s32[2]{0:T(128)} %pad_add_fusion.pos, f32[4,16,128]{2,1,0:T(8,128)} %get-tuple-element.30.mid, f32[4,48,128]{2,1,0:T(8,128)} %copy-done.8, f32[4,48,128]{2,1,0:T(8,128)} %copy-done.9, f32[12,8,128]{2,1,0:T(8,128)} %copy-done.18, ...), custom_call_target="tpu_custom_call" | custom-call | flops 10000000 | bytes 8388608 | tf_op jit(solution)/shard_map/pallas_call | solution.py:347
  117.4 3.7 %all-to-all-start.2 = ((f32[16,1,8,128]{3,2,1,0:T(8,128)}), f32[16,1,8,128]{3,2,1,0:T(8,128)S(1)}, u32[]{:S(2)}, u32[]{:S(2)}) async-start(f32[16,1,8,128]{3,2,1,0:T(8,128)} %get-tuple-element.34), calls=%async_computation.2 | async-start | bytes 131072 | tf_op jit(solution)/shard_map/all_to_all | solution.py:750
  121.1 6.2 %all-to-all-done.2.mid = f32[16,1,8,128]{3,2,1,0:T(8,128)S(1)} async-done(((f32[16,1,8,128]{3,2,1,0:T(8,128)}), f32[16,1,8,128]{3,2,1,0:T(8,128)S(1)}, u32[]{:S(2)}, u32[]{:S(2)}) %all-to-all-start.2) | async-done | bytes 65568 | tf_op jit(solution)/shard_map/all_to_all | solution.py:750
  127.4 1.3 collective-permute-start.13
  128.7 1.9 %collective-permute-start.12 = (f32[40,8,128]{2,1,0:T(8,128)S(1)}, f32[40,8,128]{2,1,0:T(8,128)S(1)}, u32[]{:S(2)}, u32[]{:S(2)}) collective-permute-start(f32[40,8,128]{2,1,0:T(8,128)S(1)} %get-tuple-element.51), channel_id=1, source_target_pairs={{0,1},{1,0},{2,3},{3,2},{4,5},{5,4},{6,7},{7,6},{8,9},{9,8},{10,11... | collective-permute-start | bytes 491528 | tf_op jit(solution)/shard_map/ppermute | solution.py:739
  130.5 1.6 %collective-permute-done.13.by_y2.refs_7_ = f32[40,8,128]{2,1,0:T(8,128)S(1)} collective-permute-done((f32[40,8,128]{2,1,0:T(8,128)S(1)}, f32[40,8,128]{2,1,0:T(8,128)S(1)}, u32[]{:S(2)}, u32[]{:S(2)}) %collective-permute-start.13) | collective-permute-done | bytes 163872 | tf_op jit(solution)/shard_map/ppermute | solution.py:740
  132.2 0.7 copy-done.10
  132.9 3.1 %shard_map.54 = (f32[3,5,24,128]{3,2,1,0:T(8,128)}, f32[16,2,8,128]{3,2,1,0:T(8,128)}) custom-call(s32[2]{0:T(128)} %pad_add_fusion.pos, f32[16,1,8,128]{3,2,1,0:T(8,128)} %copy-done.12, f32[40,8,128]{2,1,0:T(8,128)} %copy-done.11, f32[40,8,128]{2,1,0:T(8,128)} %copy-done.10, f32[16,24,128]{2,1,0:T(8,128)} %get-tuple-element.36.refs_0_), custom_call_target="tpu_custom_call" | custom-call | flops 10000000 | bytes 8388608 | tf_op jit(solution)/shard_map/pallas_call | solution.py:347
  136.0 17.4 %all_to_all.20.three = f32[16,2,8,128]{3,2,1,0:T(8,128)} all-to-all(f32[16,2,8,128]{3,2,1,0:T(8,128)} %get-tuple-element.37), channel_id=1, replica_groups=mesh['gx'=16,'gy'=16] {'gy'}, dimensions={0} | all-to-all | bytes 262144 | tf_op jit(solution)/shard_map/all_to_all | solution.py:750
  153.4 10.9 %shard_map.55 = (f32[16,32,128]{2,1,0:T(8,128)}, f32[16,32,128]{2,1,0:T(8,128)}) custom-call(s32[2]{0:T(128)} %pad_add_fusion.pos, f32[32,128]{1,0:T(8,128)} %copy.25.owned, f32[16,2,8,128]{3,2,1,0:T(8,128)} %all_to_all.20.three, f32[4,64,128]{2,1,0:T(8,128)} %get-tuple-element.38.k3, f32[3,5,24,128]{3,2,1,0:T(8,128)} %get-tuple-element.39.refs_0_, ...), custom_call_target="tpu_custom_call" | custom-call | flops 10000000 | bytes 8388608 | tf_op jit(solution)/shard_map/pallas_call | solution.py:347
  (59 shorter events, 0.6 us)
Async XLA Ops:
  0.6 15.0 %copy-start.1 = (f32[16,32,128]{2,1,0:T(8,128)S(1)}, f32[16,32,128]{2,1,0:T(8,128)}, u32[]{:S(2)}) copy-start(f32[16,32,128]{2,1,0:T(8,128)} %refs_12_.1) | copy-start | bytes 786436
  0.7 15.0 %copy-start.6 = (f32[16,32,128]{2,1,0:T(8,128)S(1)}, f32[16,32,128]{2,1,0:T(8,128)}, u32[]{:S(2)}) copy-start(f32[16,32,128]{2,1,0:T(8,128)} %param.4) | copy-start | bytes 786436
  2.1 8.4 %collective-permute-start = (f32[2,10,32,128]{3,2,1,0:T(8,128)S(1)}, f32[2,10,32,128]{3,2,1,0:T(8,128)S(1)}, u32[]{:S(2)}, u32[]{:S(2)}) collective-permute-start(f32[2,10,32,128]{3,2,1,0:T(8,128)S(1)} %get-tuple-element.48), channel_id=1, source_target_pairs={{0,16},{16,0},{32,48},{48,32},{64,80},{80,64},{96,112},{112,96},{1... | collective-permute-start | bytes 983048 | tf_op jit(solution)/shard_map/ppermute | solution.py:739
  4.3 11.3 %collective-permute-start.1 = (f32[2,10,32,128]{3,2,1,0:T(8,128)S(1)}, f32[2,10,32,128]{3,2,1,0:T(8,128)S(1)}, u32[]{:S(2)}, u32[]{:S(2)}) collective-permute-start(f32[2,10,32,128]{3,2,1,0:T(8,128)S(1)} %get-tuple-element.49), channel_id=1, source_target_pairs={{0,240},{16,32},{32,16},{48,64},{64,48},{80,96},{96,80},{112,128},... | collective-permute-start | bytes 983048 | tf_op jit(solution)/shard_map/ppermute | solution.py:740
  15.8 1.0 copy-start
  16.9 4.4 %collective-permute-start.2 = (f32[720,128]{1,0:T(8,128)S(1)}, f32[720,128]{1,0:T(8,128)S(1)}, u32[]{:S(2)}, u32[]{:S(2)}) collective-permute-start(f32[720,128]{1,0:T(8,128)S(1)} %select_n.130), channel_id=1, source_target_pairs={{0,1},{1,0},{2,3},{3,2},{4,5},{5,4},{6,7},{7,6},{8,9},{9,8},{10,11... | collective-permute-start | bytes 1105928 | tf_op jit(solution)/shard_map/ppermute | solution.py:739
  19.1 7.2 %collective-permute-start.3 = (f32[720,128]{1,0:T(8,128)S(1)}, f32[720,128]{1,0:T(8,128)S(1)}, u32[]{:S(2)}, u32[]{:S(2)}) collective-permute-start(f32[720,128]{1,0:T(8,128)S(1)} %select_n.132), channel_id=1, source_target_pairs={{0,15},{1,2},{2,1},{3,4},{4,3},{5,6},{6,5},{7,8},{8,7},{9,10},{10,... | collective-permute-start | bytes 1105928 | tf_op jit(solution)/shard_map/ppermute | solution.py:740
  21.3 5.0 %copy-start.15 = (f32[720,128]{1,0:T(8,128)}, f32[720,128]{1,0:T(8,128)S(1)}, u32[]{:S(2)}) copy-start(f32[720,128]{1,0:T(8,128)S(1)} %collective-permute-done.2.by_y) | copy-start | bytes 1105924
  26.4 0.7 copy-start.16
  34.8 7.7 %collective-permute-start.5 = (f32[3,4,16,128]{3,2,1,0:T(8,128)}, f32[3,4,16,128]{3,2,1,0:T(8,128)S(1)}, u32[]{:S(2)}, u32[]{:S(2)}) collective-permute-start(f32[3,4,16,128]{3,2,1,0:T(8,128)} %get-tuple-element.24.refs_1_), channel_id=1, source_target_pairs={{0,240},{16,32},{32,16},{48,64},{64,48},{80,96},{96,80},{112,128},... | collective-permute-start | bytes 294920 | tf_op jit(solution)/shard_map/ppermute | solution.py:740
  39.0 3.7 %collective-permute-start.4 = (f32[3,4,16,128]{3,2,1,0:T(8,128)}, f32[3,4,16,128]{3,2,1,0:T(8,128)S(1)}, u32[]{:S(2)}, u32[]{:S(2)}) collective-permute-start(f32[3,4,16,128]{3,2,1,0:T(8,128)} %get-tuple-element.24.refs_1_), channel_id=1, source_target_pairs={{0,16},{16,0},{32,48},{48,32},{64,80},{80,64},{96,112},{112,96},{1... | collective-permute-start | bytes 294920 | tf_op jit(solution)/shard_map/ppermute | solution.py:739
  39.0 10.2 %all-to-all-start = ((f32[16,2,8,128]{3,2,1,0:T(8,128)}), f32[16,2,8,128]{3,2,1,0:T(8,128)S(1)}, u32[]{:S(2)}, u32[]{:S(2)}) async-start(f32[16,2,8,128]{3,2,1,0:T(8,128)} %get-tuple-element.23), calls=%async_computation | async-start | bytes 262144 | tf_op jit(solution)/shard_map/all_to_all | solution.py:750
  42.5 6.7 %copy-start.13 = (f32[3,4,16,128]{3,2,1,0:T(8,128)}, f32[3,4,16,128]{3,2,1,0:T(8,128)S(1)}, u32[]{:S(2)}) copy-start(f32[3,4,16,128]{3,2,1,0:T(8,128)S(1)} %collective-permute-done.5.refs_3_) | copy-start | bytes 294916
  42.7 6.6 %copy-start.14 = (f32[3,4,16,128]{3,2,1,0:T(8,128)}, f32[3,4,16,128]{3,2,1,0:T(8,128)S(1)}, u32[]{:S(2)}) copy-start(f32[3,4,16,128]{3,2,1,0:T(8,128)S(1)} %collective-permute-done.4.refs_2_) | copy-start | bytes 294916
  49.2 9.0 %copy-start.3 = (f32[16,2,8,128]{3,2,1,0:T(8,128)}, f32[16,2,8,128]{3,2,1,0:T(8,128)S(1)}, u32[]{:S(2)}) copy-start(f32[16,2,8,128]{3,2,1,0:T(8,128)S(1)} %all-to-all-done.mid) | copy-start | bytes 393220
  49.2 23.3 %copy-start.19 = (s32[16,16]{1,0:T(8,128)S(1)}, s32[16,16]{1,0:T(8,128)}, u32[]{:S(2)}) copy-start(s32[16,16]{1,0:T(8,128)} %param.5) | copy-start | bytes 3076
  49.3 7.7 %collective-permute-start.7 = (f32[68,8,128]{2,1,0:T(8,128)S(1)}, f32[68,8,128]{2,1,0:T(8,128)S(1)}, u32[]{:S(2)}, u32[]{:S(2)}) collective-permute-start(f32[68,8,128]{2,1,0:T(8,128)S(1)} %get-tuple-element.52), channel_id=1, source_target_pairs={{0,15},{1,2},{2,1},{3,4},{4,3},{5,6},{6,5},{7,8},{8,7},{9,10},{10,... | collective-permute-start | bytes 835592 | tf_op jit(solution)/shard_map/ppermute | solution.py:740
  52.5 5.7 %collective-permute-start.6 = (f32[68,8,128]{2,1,0:T(8,128)S(1)}, f32[68,8,128]{2,1,0:T(8,128)S(1)}, u32[]{:S(2)}, u32[]{:S(2)}) collective-permute-start(f32[68,8,128]{2,1,0:T(8,128)S(1)} %get-tuple-element.53), channel_id=1, source_target_pairs={{0,1},{1,0},{2,3},{3,2},{4,5},{5,4},{6,7},{7,6},{8,9},{9,8},{10,11... | collective-permute-start | bytes 835592 | tf_op jit(solution)/shard_map/ppermute | solution.py:739
  57.0 1.2 copy-start.4
  58.2 0.7 copy-start.5
  62.2 23.4 %all-to-all-start.1 = ((f32[16,5,8,128]{3,2,1,0:T(8,128)}), f32[16,5,8,128]{3,2,1,0:T(8,128)S(1)}, u32[]{:S(2)}, u32[]{:S(2)}) async-start(f32[16,5,8,128]{3,2,1,0:T(8,128)} %get-tuple-element.25), calls=%async_computation.1 | async-start | bytes 655360 | tf_op jit(solution)/shard_map/all_to_all | solution.py:750
  85.6 0.7 copy-start.2
  100.9 26.4 %copy-start.7 = (f32[16,32,128]{2,1,0:T(8,128)S(1)}, f32[16,32,128]{2,1,0:T(8,128)}, u32[]{:S(2)}) copy-start(f32[16,32,128]{2,1,0:T(8,128)} %get-tuple-element.35.refs_8_) | copy-start | bytes 786436
  100.9 4.9 %collective-permute-start.8 = (f32[4,48,128]{2,1,0:T(8,128)}, f32[4,48,128]{2,1,0:T(8,128)S(1)}, u32[]{:S(2)}, u32[]{:S(2)}) collective-permute-start(f32[4,48,128]{2,1,0:T(8,128)} %get-tuple-element.31), channel_id=1, source_target_pairs={{0,16},{16,0},{32,48},{48,32},{64,80},{80,64},{96,112},{112,96},{1... | collective-permute-start | bytes 294920 | tf_op jit(solution)/shard_map/ppermute | solution.py:777
  101.2 8.2 %collective-permute-start.9 = (f32[4,48,128]{2,1,0:T(8,128)}, f32[4,48,128]{2,1,0:T(8,128)S(1)}, u32[]{:S(2)}, u32[]{:S(2)}) collective-permute-start(f32[4,48,128]{2,1,0:T(8,128)} %get-tuple-element.32), channel_id=1, source_target_pairs={{0,240},{16,32},{32,16},{48,64},{64,48},{80,96},{96,80},{112,128},... | collective-permute-start | bytes 294920 | tf_op jit(solution)/shard_map/ppermute | solution.py:778
  105.8 8.0 %copy-start.8 = (f32[4,48,128]{2,1,0:T(8,128)}, f32[4,48,128]{2,1,0:T(8,128)S(1)}, u32[]{:S(2)}) copy-start(f32[4,48,128]{2,1,0:T(8,128)S(1)} %collective-permute-done.8.by_x.refs_4_) | copy-start | bytes 294916
  109.4 4.5 %copy-start.9 = (f32[4,48,128]{2,1,0:T(8,128)}, f32[4,48,128]{2,1,0:T(8,128)S(1)}, u32[]{:S(2)}) copy-start(f32[4,48,128]{2,1,0:T(8,128)S(1)} %collective-permute-done.9.by_x2.refs_5_) | copy-start | bytes 294916
  110.2 3.6 %collective-permute-start.11 = (f32[12,8,128]{2,1,0:T(8,128)S(1)}, f32[12,8,128]{2,1,0:T(8,128)S(1)}, u32[]{:S(2)}, u32[]{:S(2)}) collective-permute-start(f32[12,8,128]{2,1,0:T(8,128)S(1)} %get-tuple-element.60), channel_id=1, source_target_pairs={{0,15},{1,2},{2,1},{3,4},{4,3},{5,6},{6,5},{7,8},{8,7},{9,10},{10,... | collective-permute-start | bytes 147464 | tf_op jit(solution)/shard_map/ppermute | solution.py:740
  110.3 3.5 %collective-permute-start.10 = (f32[12,8,128]{2,1,0:T(8,128)S(1)}, f32[12,8,128]{2,1,0:T(8,128)S(1)}, u32[]{:S(2)}, u32[]{:S(2)}) collective-permute-start(f32[12,8,128]{2,1,0:T(8,128)S(1)} %get-tuple-element.61), channel_id=1, source_target_pairs={{0,1},{1,0},{2,3},{3,2},{4,5},{5,4},{6,7},{7,6},{8,9},{9,8},{10,11... | collective-permute-start | bytes 147464 | tf_op jit(solution)/shard_map/ppermute | solution.py:739
  113.8 0.6 copy-start.17
  113.8 0.6 copy-start.18
  117.4 10.0 %all-to-all-start.2 = ((f32[16,1,8,128]{3,2,1,0:T(8,128)}), f32[16,1,8,128]{3,2,1,0:T(8,128)S(1)}, u32[]{:S(2)}, u32[]{:S(2)}) async-start(f32[16,1,8,128]{3,2,1,0:T(8,128)} %get-tuple-element.34), calls=%async_computation.2 | async-start | bytes 131072 | tf_op jit(solution)/shard_map/all_to_all | solution.py:750
  127.3 4.9 %copy-start.12 = (f32[16,1,8,128]{3,2,1,0:T(8,128)}, f32[16,1,8,128]{3,2,1,0:T(8,128)S(1)}, u32[]{:S(2)}) copy-start(f32[16,1,8,128]{3,2,1,0:T(8,128)S(1)} %all-to-all-done.2.mid) | copy-start | bytes 196612
  127.4 4.8 %collective-permute-start.13 = (f32[40,8,128]{2,1,0:T(8,128)S(1)}, f32[40,8,128]{2,1,0:T(8,128)S(1)}, u32[]{:S(2)}, u32[]{:S(2)}) collective-permute-start(f32[40,8,128]{2,1,0:T(8,128)S(1)} %get-tuple-element.50), channel_id=1, source_target_pairs={{0,15},{1,2},{2,1},{3,4},{4,3},{5,6},{6,5},{7,8},{8,7},{9,10},{10,... | collective-permute-start | bytes 491528 | tf_op jit(solution)/shard_map/ppermute | solution.py:740
  128.7 3.5 %collective-permute-start.12 = (f32[40,8,128]{2,1,0:T(8,128)S(1)}, f32[40,8,128]{2,1,0:T(8,128)S(1)}, u32[]{:S(2)}, u32[]{:S(2)}) collective-permute-start(f32[40,8,128]{2,1,0:T(8,128)S(1)} %get-tuple-element.51), channel_id=1, source_target_pairs={{0,1},{1,0},{2,3},{3,2},{4,5},{5,4},{6,7},{7,6},{8,9},{9,8},{10,11... | collective-permute-start | bytes 491528 | tf_op jit(solution)/shard_map/ppermute | solution.py:739
  132.2 0.7 copy-start.10
  132.2 0.7 copy-start.11

commit v8 on v7

--- a/solution.py
+++ b/solution.py
@@ -193,7 +193,7 @@
         return fx[-1:]
 
     assert (high - low) % CHUNK == 0
-    lax.fori_loop(0, (high - low) // CHUNK, step, jnp.zeros((1, rows, 128), F32))
+    lax.fori_loop(0, (high - low) // CHUNK, step, jnp.zeros((1, rows, 128), F32), unroll=True)
 
 
 def sweep_top(x, wx, wy, wz, s, low, high, body):
@@ -254,7 +254,7 @@
         kx[at] = jnp.where(inside_at(i * CHUNK), kx[at], 0.0)
         return 0
 
-    lax.fori_loop(0, PX // CHUNK, clear, 0)
+    lax.fori_loop(0, PX // CHUNK, clear, 0, unroll=True)
     for move in keeping[:2]:
         move.start()
     start, steps = SMOOTH
@@ -636,7 +636,7 @@
         x[at] = v
         return 0
 
-    lax.fori_loop(0, (PX - 12) // CHUNK, begin, 0)
+    lax.fori_loop(0, (PX - 12) // CHUNK, begin, 0, unroll=True)
     for keep, gain in steps:
         sweep_top(x, wx, wy, wz, s, 8, PX - 8, advance_top(keep, gain, rout, 6, rd, d, x))
 

time: 165 us -> 164 us (level)
  no operation moved by 1% of the time
where the time goes in v8:
time: 164 us; the launch traced here: 163 us
  waiting for transfers between devices  48.3 us (29%)
  starting transfers between devices  45.7 us (28%)
  Pallas kernels  40.9 us (25%)
  blocking collectives  17.4 us (11%)
  local copies, waits for them, and re-layouts  5.46 us (3%)
  other arithmetic  4.06 us (2%)
    pallas_call x6, Pallas kernels, call(): pl.pallas_call(kernel, out_shape=[jax.ShapeDtypeStruct(o, F32) for o in o...  40.9 us
    all_to_all x3, waiting for transfers between devices, gather(): return lax.all_to_all(copies, axis, 0, 0, tiled=True)  24.1 us
    all_to_all x1, blocking collectives, gather(): return lax.all_to_all(copies, axis, 0, 0, tiled=True)  17.4 us
    all_to_all x3, starting transfers between devices, gather(): return lax.all_to_all(copies, axis, 0, 0, tiled=True)  17.4 us
    ppermute x6, starting transfers between devices, swap(): lax.ppermute(second, axis, [(i, (i + 1 if i % 2 else i - 1) % count) for...  14.5 us
    ppermute x6, waiting for transfers between devices, swap(): lax.ppermute(second, axis, [(i, (i + 1 if i % 2 else i - 1) % count) for...  14.4 us
    ppermute x6, starting transfers between devices, swap(): lax.ppermute(first, axis, [(i, i ^ 1) for i in range(count)])  11.7 us
    unnamed x40, local copies, waits for them, and re-layouts  4.49 us
  transfers between devices with their start and end apart: 17, of which 12 were waited for; matrix products, arithmetic and copies ran while one was open for 1% of the time, Pallas kernels for 0%

profile of v8, /device:TPU:1, one launch (start us, length us, event | category | flops | bytes accessed | tf_op | source)
XLA Modules:
  0.0 162.9 jit_solution(3306120927364208692)
XLA Ops:
  0.7 1.4 fusion.3
  2.1 2.2 %collective-permute-start = (f32[2,10,32,128]{3,2,1,0:T(8,128)S(1)}, f32[2,10,32,128]{3,2,1,0:T(8,128)S(1)}, u32[]{:S(2)}, u32[]{:S(2)}) collective-permute-start(f32[2,10,32,128]{3,2,1,0:T(8,128)S(1)} %get-tuple-element.48), channel_id=1, source_target_pairs={{0,16},{16,0},{32,48},{48,32},{64,80},{80,64},{96,112},{112,96},{1... | collective-permute-start | bytes 983048 | tf_op jit(solution)/shard_map/ppermute | solution.py:739
  4.3 4.1 %collective-permute-start.1 = (f32[2,10,32,128]{3,2,1,0:T(8,128)S(1)}, f32[2,10,32,128]{3,2,1,0:T(8,128)S(1)}, u32[]{:S(2)}, u32[]{:S(2)}) collective-permute-start(f32[2,10,32,128]{3,2,1,0:T(8,128)S(1)} %get-tuple-element.49), channel_id=1, source_target_pairs={{0,240},{16,32},{32,16},{48,64},{64,48},{80,96},{96,80},{112,128},... | collective-permute-start | bytes 983048 | tf_op jit(solution)/shard_map/ppermute | solution.py:740
  8.4 2.1 %collective-permute-done = f32[2,10,32,128]{3,2,1,0:T(8,128)S(1)} collective-permute-done((f32[2,10,32,128]{3,2,1,0:T(8,128)S(1)}, f32[2,10,32,128]{3,2,1,0:T(8,128)S(1)}, u32[]{:S(2)}, u32[]{:S(2)}) %collective-permute-start) | collective-permute-done | bytes 327712 | tf_op jit(solution)/shard_map/ppermute | solution.py:739
  10.5 5.1 %collective-permute-done.1 = f32[2,10,32,128]{3,2,1,0:T(8,128)S(1)} collective-permute-done((f32[2,10,32,128]{3,2,1,0:T(8,128)S(1)}, f32[2,10,32,128]{3,2,1,0:T(8,128)S(1)}, u32[]{:S(2)}, u32[]{:S(2)}) %collective-permute-start.1) | collective-permute-done | bytes 327712 | tf_op jit(solution)/shard_map/ppermute | solution.py:740
  15.7 0.1 pad_maximum_fusion.wide
  15.8 0.1 slice_select_fusion
  15.9 0.9 copy-done
  16.9 2.2 %collective-permute-start.2 = (f32[720,128]{1,0:T(8,128)S(1)}, f32[720,128]{1,0:T(8,128)S(1)}, u32[]{:S(2)}, u32[]{:S(2)}) collective-permute-start(f32[720,128]{1,0:T(8,128)S(1)} %select_n.130), channel_id=1, source_target_pairs={{0,1},{1,0},{2,3},{3,2},{4,5},{5,4},{6,7},{7,6},{8,9},{9,8},{10,11... | collective-permute-start | bytes 1105928 | tf_op jit(solution)/shard_map/ppermute | solution.py:739
  19.1 1.6 collective-permute-start.3
  20.8 0.6 pad_add_fusion.pos
  21.3 5.0 %collective-permute-done.3.by_y2 = f32[720,128]{1,0:T(8,128)S(1)} collective-permute-done((f32[720,128]{1,0:T(8,128)S(1)}, f32[720,128]{1,0:T(8,128)S(1)}, u32[]{:S(2)}, u32[]{:S(2)}) %collective-permute-start.3) | collective-permute-done | bytes 368672 | tf_op jit(solution)/shard_map/ppermute | solution.py:740
  26.4 0.7 copy-done.16
  27.1 7.0 %shard_map.50 = (f32[3,4,16,128]{3,2,1,0:T(8,128)}, f32[16,2,8,128]{3,2,1,0:T(8,128)}, f32[36,56,128]{2,1,0:T(8,128)}, f32[36,56,128]{2,1,0:T(8,128)}, f32[36,56,128]{2,1,0:T(8,128)}) custom-call(s32[2]{0:T(128)} %pad_add_fusion.pos, f32[2,36,32,128]{3,2,1,0:T(8,128)} %copy-done, f32[720,128]{1,0:T(8,128)} %copy-done.15, f32[720,128]{1,0:T(8,128)} %copy-done.16), custom_call_target="tpu_custom_call" | custom-call | flops 10000000 | bytes 8388608 | tf_op jit(solution)/shard_map/pallas_call | solution.py:347
  34.1 4.2 %collective-permute-start.5 = (f32[3,4,16,128]{3,2,1,0:T(8,128)}, f32[3,4,16,128]{3,2,1,0:T(8,128)S(1)}, u32[]{:S(2)}, u32[]{:S(2)}) collective-permute-start(f32[3,4,16,128]{3,2,1,0:T(8,128)} %get-tuple-element.24.refs_1_), channel_id=1, source_target_pairs={{0,240},{16,32},{32,16},{48,64},{64,48},{80,96},{96,80},{112,128},... | collective-permute-start | bytes 294920 | tf_op jit(solution)/shard_map/ppermute | solution.py:740
  38.3 3.5 %all-to-all-start = ((f32[16,2,8,128]{3,2,1,0:T(8,128)}), f32[16,2,8,128]{3,2,1,0:T(8,128)S(1)}, u32[]{:S(2)}, u32[]{:S(2)}) async-start(f32[16,2,8,128]{3,2,1,0:T(8,128)} %get-tuple-element.23), calls=%async_computation | async-start | bytes 262144 | tf_op jit(solution)/shard_map/all_to_all | solution.py:750
  41.9 0.1 collective-permute-done.4.refs_2_
  42.0 0.9 pad_maximum_fusion.4
  43.0 5.5 %all-to-all-done.mid = f32[16,2,8,128]{3,2,1,0:T(8,128)S(1)} async-done(((f32[16,2,8,128]{3,2,1,0:T(8,128)}), f32[16,2,8,128]{3,2,1,0:T(8,128)S(1)}, u32[]{:S(2)}, u32[]{:S(2)}) %all-to-all-start) | async-done | bytes 131104 | tf_op jit(solution)/shard_map/all_to_all | solution.py:750
  48.6 3.2 %collective-permute-start.7 = (f32[68,8,128]{2,1,0:T(8,128)S(1)}, f32[68,8,128]{2,1,0:T(8,128)S(1)}, u32[]{:S(2)}, u32[]{:S(2)}) collective-permute-start(f32[68,8,128]{2,1,0:T(8,128)S(1)} %get-tuple-element.52), channel_id=1, source_target_pairs={{0,15},{1,2},{2,1},{3,4},{4,3},{5,6},{6,5},{7,8},{8,7},{9,10},{10,... | collective-permute-start | bytes 835592 | tf_op jit(solution)/shard_map/ppermute | solution.py:740
  51.8 4.5 %collective-permute-start.6 = (f32[68,8,128]{2,1,0:T(8,128)S(1)}, f32[68,8,128]{2,1,0:T(8,128)S(1)}, u32[]{:S(2)}, u32[]{:S(2)}) collective-permute-start(f32[68,8,128]{2,1,0:T(8,128)S(1)} %get-tuple-element.53), channel_id=1, source_target_pairs={{0,1},{1,0},{2,3},{3,2},{4,5},{5,4},{6,7},{7,6},{8,9},{9,8},{10,11... | collective-permute-start | bytes 835592 | tf_op jit(solution)/shard_map/ppermute | solution.py:739
  56.3 1.2 collective-permute-done.6.by_y.refs_4_
  57.5 0.7 copy-done.5
  58.2 3.3 %shard_map.51 = (f32[3,5,24,128]{3,2,1,0:T(8,128)}, f32[16,5,8,128]{3,2,1,0:T(8,128)}, f32[16,24,128]{2,1,0:T(8,128)}) custom-call(s32[2]{0:T(128)} %pad_add_fusion.pos, f32[16,2,8,128]{3,2,1,0:T(8,128)} %copy-done.3, f32[68,8,128]{2,1,0:T(8,128)} %copy-done.5, f32[68,8,128]{2,1,0:T(8,128)} %copy-done.4), custom_call_target="tpu_custom_call" | custom-call | flops 10000000 | bytes 8388608 | tf_op jit(solution)/shard_map/pallas_call | solution.py:347
  61.5 10.3 %all-to-all-start.1 = ((f32[16,5,8,128]{3,2,1,0:T(8,128)}), f32[16,5,8,128]{3,2,1,0:T(8,128)S(1)}, u32[]{:S(2)}, u32[]{:S(2)}) async-start(f32[16,5,8,128]{3,2,1,0:T(8,128)} %get-tuple-element.25), calls=%async_computation.1 | async-start | bytes 655360 | tf_op jit(solution)/shard_map/all_to_all | solution.py:750
  72.0 0.7 copy.25.owned
  72.6 12.2 %all-to-all-done.1.three = f32[16,5,8,128]{3,2,1,0:T(8,128)S(1)} async-done(((f32[16,5,8,128]{3,2,1,0:T(8,128)}), f32[16,5,8,128]{3,2,1,0:T(8,128)S(1)}, u32[]{:S(2)}, u32[]{:S(2)}) %all-to-all-start.1) | async-done | bytes 327712 | tf_op jit(solution)/shard_map/all_to_all | solution.py:750
  84.9 0.7 copy-done.2
  85.6 14.2 %shard_map.52 = (f32[4,16,128]{2,1,0:T(8,128)}, f32[4,48,128]{2,1,0:T(8,128)}, f32[4,48,128]{2,1,0:T(8,128)}, f32[18,56,128]{2,1,0:T(8,128)}, f32[24,56,128]{2,1...) custom-call(s32[2]{0:T(128)} %pad_add_fusion.pos, f32[32,128]{1,0:T(8,128)} %copy.25.owned, ...), custom_call_target="tpu_custom_call" | custom-call | flops 10000000 | bytes 8388608 | tf_op jit(solution)/shard_map/pallas_call | solution.py:347
  99.8 0.3 collective-permute-start.8
  100.1 1.8 %collective-permute-start.9 = (f32[4,48,128]{2,1,0:T(8,128)}, f32[4,48,128]{2,1,0:T(8,128)S(1)}, u32[]{:S(2)}, u32[]{:S(2)}) collective-permute-start(f32[4,48,128]{2,1,0:T(8,128)} %get-tuple-element.32), channel_id=1, source_target_pairs={{0,240},{16,32},{32,16},{48,64},{64,48},{80,96},{96,80},{112,128},... | collective-permute-start | bytes 294920 | tf_op jit(solution)/shard_map/ppermute | solution.py:778
  101.9 2.8 %collective-permute-done.8.by_x.refs_4_ = f32[4,48,128]{2,1,0:T(8,128)S(1)} collective-permute-done((f32[4,48,128]{2,1,0:T(8,128)}, f32[4,48,128]{2,1,0:T(8,128)S(1)}, u32[]{:S(2)}, u32[]{:S(2)}) %collective-permute-start.8) | collective-permute-done | bytes 98336 | tf_op jit(solution)/shard_map/ppermute | solution.py:777
  104.7 3.6 %collective-permute-done.9.by_x2.refs_5_ = f32[4,48,128]{2,1,0:T(8,128)S(1)} collective-permute-done((f32[4,48,128]{2,1,0:T(8,128)}, f32[4,48,128]{2,1,0:T(8,128)S(1)}, u32[]{:S(2)}, u32[]{:S(2)}) %collective-permute-start.9) | collective-permute-done | bytes 98336 | tf_op jit(solution)/shard_map/ppermute | solution.py:778
  108.3 0.8 pad_maximum_fusion.11
  109.1 0.1 collective-permute-start.11
  109.2 0.9 collective-permute-start.10
  110.1 2.6 %collective-permute-done.11.by_y2 = f32[12,8,128]{2,1,0:T(8,128)S(1)} collective-permute-done((f32[12,8,128]{2,1,0:T(8,128)S(1)}, f32[12,8,128]{2,1,0:T(8,128)S(1)}, u32[]{:S(2)}, u32[]{:S(2)}) %collective-permute-start.11) | collective-permute-done | bytes 49184 | tf_op jit(solution)/shard_map/ppermute | solution.py:740
  112.7 0.6 copy-done.17
  113.3 2.9 %shard_map.53 = (f32[12,32,128]{2,1,0:T(8,128)}, f32[12,32,128]{2,1,0:T(8,128)}, f32[16,1,8,128]{3,2,1,0:T(8,128)}) custom-call(s32[2]{0:T(128)} %pad_add_fusion.pos, f32[4,16,128]{2,1,0:T(8,128)} %get-tuple-element.30.mid, f32[4,48,128]{2,1,0:T(8,128)} %copy-done.8, f32[4,48,128]{2,1,0:T(8,128)} %copy-done.9, f32[12,8,128]{2,1,0:T(8,128)} %copy-done.18, ...), custom_call_target="tpu_custom_call" | custom-call | flops 10000000 | bytes 8388608 | tf_op jit(solution)/shard_map/pallas_call | solution.py:347
  116.2 3.5 %all-to-all-start.2 = ((f32[16,1,8,128]{3,2,1,0:T(8,128)}), f32[16,1,8,128]{3,2,1,0:T(8,128)S(1)}, u32[]{:S(2)}, u32[]{:S(2)}) async-start(f32[16,1,8,128]{3,2,1,0:T(8,128)} %get-tuple-element.34), calls=%async_computation.2 | async-start | bytes 131072 | tf_op jit(solution)/shard_map/all_to_all | solution.py:750
  119.8 6.4 %all-to-all-done.2.mid = f32[16,1,8,128]{3,2,1,0:T(8,128)S(1)} async-done(((f32[16,1,8,128]{3,2,1,0:T(8,128)}), f32[16,1,8,128]{3,2,1,0:T(8,128)S(1)}, u32[]{:S(2)}, u32[]{:S(2)}) %all-to-all-start.2) | async-done | bytes 65568 | tf_op jit(solution)/shard_map/all_to_all | solution.py:750
  126.2 1.3 collective-permute-start.13
  127.6 1.9 %collective-permute-start.12 = (f32[40,8,128]{2,1,0:T(8,128)S(1)}, f32[40,8,128]{2,1,0:T(8,128)S(1)}, u32[]{:S(2)}, u32[]{:S(2)}) collective-permute-start(f32[40,8,128]{2,1,0:T(8,128)S(1)} %get-tuple-element.51), channel_id=1, source_target_pairs={{0,1},{1,0},{2,3},{3,2},{4,5},{5,4},{6,7},{7,6},{8,9},{9,8},{10,11... | collective-permute-start | bytes 491528 | tf_op jit(solution)/shard_map/ppermute | solution.py:739
  129.4 1.7 %collective-permute-done.13.by_y2.refs_7_ = f32[40,8,128]{2,1,0:T(8,128)S(1)} collective-permute-done((f32[40,8,128]{2,1,0:T(8,128)S(1)}, f32[40,8,128]{2,1,0:T(8,128)S(1)}, u32[]{:S(2)}, u32[]{:S(2)}) %collective-permute-start.13) | collective-permute-done | bytes 163872 | tf_op jit(solution)/shard_map/ppermute | solution.py:740
  131.1 0.7 copy-done.10
  131.8 3.1 %shard_map.54 = (f32[3,5,24,128]{3,2,1,0:T(8,128)}, f32[16,2,8,128]{3,2,1,0:T(8,128)}) custom-call(s32[2]{0:T(128)} %pad_add_fusion.pos, f32[16,1,8,128]{3,2,1,0:T(8,128)} %copy-done.12, f32[40,8,128]{2,1,0:T(8,128)} %copy-done.11, f32[40,8,128]{2,1,0:T(8,128)} %copy-done.10, f32[16,24,128]{2,1,0:T(8,128)} %get-tuple-element.36.refs_0_), custom_call_target="tpu_custom_call" | custom-call | flops 10000000 | bytes 8388608 | tf_op jit(solution)/shard_map/pallas_call | solution.py:347
  134.9 17.4 %all_to_all.20.three = f32[16,2,8,128]{3,2,1,0:T(8,128)} all-to-all(f32[16,2,8,128]{3,2,1,0:T(8,128)} %get-tuple-element.37), channel_id=1, replica_groups=mesh['gx'=16,'gy'=16] {'gy'}, dimensions={0} | all-to-all | bytes 262144 | tf_op jit(solution)/shard_map/all_to_all | solution.py:750
  152.3 10.4 %shard_map.55 = (f32[16,32,128]{2,1,0:T(8,128)}, f32[16,32,128]{2,1,0:T(8,128)}) custom-call(s32[2]{0:T(128)} %pad_add_fusion.pos, f32[32,128]{1,0:T(8,128)} %copy.25.owned, f32[16,2,8,128]{3,2,1,0:T(8,128)} %all_to_all.20.three, f32[4,64,128]{2,1,0:T(8,128)} %get-tuple-element.38.k3, f32[3,5,24,128]{3,2,1,0:T(8,128)} %get-tuple-element.39.refs_0_, ...), custom_call_target="tpu_custom_call" | custom-call | flops 10000000 | bytes 8388608 | tf_op jit(solution)/shard_map/pallas_call | solution.py:347
  (59 shorter events, 0.6 us)
Async XLA Ops:
  0.6 15.0 %copy-start.1 = (f32[16,32,128]{2,1,0:T(8,128)S(1)}, f32[16,32,128]{2,1,0:T(8,128)}, u32[]{:S(2)}) copy-start(f32[16,32,128]{2,1,0:T(8,128)} %refs_12_.1) | copy-start | bytes 786436
  0.7 15.0 %copy-start.6 = (f32[16,32,128]{2,1,0:T(8,128)S(1)}, f32[16,32,128]{2,1,0:T(8,128)}, u32[]{:S(2)}) copy-start(f32[16,32,128]{2,1,0:T(8,128)} %param.4) | copy-start | bytes 786436
  2.1 8.4 %collective-permute-start = (f32[2,10,32,128]{3,2,1,0:T(8,128)S(1)}, f32[2,10,32,128]{3,2,1,0:T(8,128)S(1)}, u32[]{:S(2)}, u32[]{:S(2)}) collective-permute-start(f32[2,10,32,128]{3,2,1,0:T(8,128)S(1)} %get-tuple-element.48), channel_id=1, source_target_pairs={{0,16},{16,0},{32,48},{48,32},{64,80},{80,64},{96,112},{112,96},{1... | collective-permute-start | bytes 983048 | tf_op jit(solution)/shard_map/ppermute | solution.py:739
  4.3 11.3 %collective-permute-start.1 = (f32[2,10,32,128]{3,2,1,0:T(8,128)S(1)}, f32[2,10,32,128]{3,2,1,0:T(8,128)S(1)}, u32[]{:S(2)}, u32[]{:S(2)}) collective-permute-start(f32[2,10,32,128]{3,2,1,0:T(8,128)S(1)} %get-tuple-element.49), channel_id=1, source_target_pairs={{0,240},{16,32},{32,16},{48,64},{64,48},{80,96},{96,80},{112,128},... | collective-permute-start | bytes 983048 | tf_op jit(solution)/shard_map/ppermute | solution.py:740
  15.8 1.0 copy-start
  16.9 4.4 %collective-permute-start.2 = (f32[720,128]{1,0:T(8,128)S(1)}, f32[720,128]{1,0:T(8,128)S(1)}, u32[]{:S(2)}, u32[]{:S(2)}) collective-permute-start(f32[720,128]{1,0:T(8,128)S(1)} %select_n.130), channel_id=1, source_target_pairs={{0,1},{1,0},{2,3},{3,2},{4,5},{5,4},{6,7},{7,6},{8,9},{9,8},{10,11... | collective-permute-start | bytes 1105928 | tf_op jit(solution)/shard_map/ppermute | solution.py:739
  19.1 7.2 %collective-permute-start.3 = (f32[720,128]{1,0:T(8,128)S(1)}, f32[720,128]{1,0:T(8,128)S(1)}, u32[]{:S(2)}, u32[]{:S(2)}) collective-permute-start(f32[720,128]{1,0:T(8,128)S(1)} %select_n.132), channel_id=1, source_target_pairs={{0,15},{1,2},{2,1},{3,4},{4,3},{5,6},{6,5},{7,8},{8,7},{9,10},{10,... | collective-permute-start | bytes 1105928 | tf_op jit(solution)/shard_map/ppermute | solution.py:740
  21.3 5.0 %copy-start.15 = (f32[720,128]{1,0:T(8,128)}, f32[720,128]{1,0:T(8,128)S(1)}, u32[]{:S(2)}) copy-start(f32[720,128]{1,0:T(8,128)S(1)} %collective-permute-done.2.by_y) | copy-start | bytes 1105924
  26.4 0.7 copy-start.16
  34.1 7.7 %collective-permute-start.5 = (f32[3,4,16,128]{3,2,1,0:T(8,128)}, f32[3,4,16,128]{3,2,1,0:T(8,128)S(1)}, u32[]{:S(2)}, u32[]{:S(2)}) collective-permute-start(f32[3,4,16,128]{3,2,1,0:T(8,128)} %get-tuple-element.24.refs_1_), channel_id=1, source_target_pairs={{0,240},{16,32},{32,16},{48,64},{64,48},{80,96},{96,80},{112,128},... | collective-permute-start | bytes 294920 | tf_op jit(solution)/shard_map/ppermute | solution.py:740
  38.3 3.7 %collective-permute-start.4 = (f32[3,4,16,128]{3,2,1,0:T(8,128)}, f32[3,4,16,128]{3,2,1,0:T(8,128)S(1)}, u32[]{:S(2)}, u32[]{:S(2)}) collective-permute-start(f32[3,4,16,128]{3,2,1,0:T(8,128)} %get-tuple-element.24.refs_1_), channel_id=1, source_target_pairs={{0,16},{16,0},{32,48},{48,32},{64,80},{80,64},{96,112},{112,96},{1... | collective-permute-start | bytes 294920 | tf_op jit(solution)/shard_map/ppermute | solution.py:739
  38.3 10.2 %all-to-all-start = ((f32[16,2,8,128]{3,2,1,0:T(8,128)}), f32[16,2,8,128]{3,2,1,0:T(8,128)S(1)}, u32[]{:S(2)}, u32[]{:S(2)}) async-start(f32[16,2,8,128]{3,2,1,0:T(8,128)} %get-tuple-element.23), calls=%async_computation | async-start | bytes 262144 | tf_op jit(solution)/shard_map/all_to_all | solution.py:750
  41.8 6.7 %copy-start.13 = (f32[3,4,16,128]{3,2,1,0:T(8,128)}, f32[3,4,16,128]{3,2,1,0:T(8,128)S(1)}, u32[]{:S(2)}) copy-start(f32[3,4,16,128]{3,2,1,0:T(8,128)S(1)} %collective-permute-done.5.refs_3_) | copy-start | bytes 294916
  42.0 6.6 %copy-start.14 = (f32[3,4,16,128]{3,2,1,0:T(8,128)}, f32[3,4,16,128]{3,2,1,0:T(8,128)S(1)}, u32[]{:S(2)}) copy-start(f32[3,4,16,128]{3,2,1,0:T(8,128)S(1)} %collective-permute-done.4.refs_2_) | copy-start | bytes 294916
  48.5 9.0 %copy-start.3 = (f32[16,2,8,128]{3,2,1,0:T(8,128)}, f32[16,2,8,128]{3,2,1,0:T(8,128)S(1)}, u32[]{:S(2)}) copy-start(f32[16,2,8,128]{3,2,1,0:T(8,128)S(1)} %all-to-all-done.mid) | copy-start | bytes 393220
  48.5 23.3 %copy-start.19 = (s32[16,16]{1,0:T(8,128)S(1)}, s32[16,16]{1,0:T(8,128)}, u32[]{:S(2)}) copy-start(s32[16,16]{1,0:T(8,128)} %param.5) | copy-start | bytes 3076
  48.6 7.7 %collective-permute-start.7 = (f32[68,8,128]{2,1,0:T(8,128)S(1)}, f32[68,8,128]{2,1,0:T(8,128)S(1)}, u32[]{:S(2)}, u32[]{:S(2)}) collective-permute-start(f32[68,8,128]{2,1,0:T(8,128)S(1)} %get-tuple-element.52), channel_id=1, source_target_pairs={{0,15},{1,2},{2,1},{3,4},{4,3},{5,6},{6,5},{7,8},{8,7},{9,10},{10,... | collective-permute-start | bytes 835592 | tf_op jit(solution)/shard_map/ppermute | solution.py:740
  51.8 5.7 %collective-permute-start.6 = (f32[68,8,128]{2,1,0:T(8,128)S(1)}, f32[68,8,128]{2,1,0:T(8,128)S(1)}, u32[]{:S(2)}, u32[]{:S(2)}) collective-permute-start(f32[68,8,128]{2,1,0:T(8,128)S(1)} %get-tuple-element.53), channel_id=1, source_target_pairs={{0,1},{1,0},{2,3},{3,2},{4,5},{5,4},{6,7},{7,6},{8,9},{9,8},{10,11... | collective-permute-start | bytes 835592 | tf_op jit(solution)/shard_map/ppermute | solution.py:739
  56.3 1.2 copy-start.4
  57.5 0.7 copy-start.5
  61.5 23.4 %all-to-all-start.1 = ((f32[16,5,8,128]{3,2,1,0:T(8,128)}), f32[16,5,8,128]{3,2,1,0:T(8,128)S(1)}, u32[]{:S(2)}, u32[]{:S(2)}) async-start(f32[16,5,8,128]{3,2,1,0:T(8,128)} %get-tuple-element.25), calls=%async_computation.1 | async-start | bytes 655360 | tf_op jit(solution)/shard_map/all_to_all | solution.py:750
  84.9 0.7 copy-start.2
  99.8 26.4 %copy-start.7 = (f32[16,32,128]{2,1,0:T(8,128)S(1)}, f32[16,32,128]{2,1,0:T(8,128)}, u32[]{:S(2)}) copy-start(f32[16,32,128]{2,1,0:T(8,128)} %get-tuple-element.35.refs_8_) | copy-start | bytes 786436
  99.8 4.9 %collective-permute-start.8 = (f32[4,48,128]{2,1,0:T(8,128)}, f32[4,48,128]{2,1,0:T(8,128)S(1)}, u32[]{:S(2)}, u32[]{:S(2)}) collective-permute-start(f32[4,48,128]{2,1,0:T(8,128)} %get-tuple-element.31), channel_id=1, source_target_pairs={{0,16},{16,0},{32,48},{48,32},{64,80},{80,64},{96,112},{112,96},{1... | collective-permute-start | bytes 294920 | tf_op jit(solution)/shard_map/ppermute | solution.py:777
  100.1 8.2 %collective-permute-start.9 = (f32[4,48,128]{2,1,0:T(8,128)}, f32[4,48,128]{2,1,0:T(8,128)S(1)}, u32[]{:S(2)}, u32[]{:S(2)}) collective-permute-start(f32[4,48,128]{2,1,0:T(8,128)} %get-tuple-element.32), channel_id=1, source_target_pairs={{0,240},{16,32},{32,16},{48,64},{64,48},{80,96},{96,80},{112,128},... | collective-permute-start | bytes 294920 | tf_op jit(solution)/shard_map/ppermute | solution.py:778
  104.7 8.0 %copy-start.8 = (f32[4,48,128]{2,1,0:T(8,128)}, f32[4,48,128]{2,1,0:T(8,128)S(1)}, u32[]{:S(2)}) copy-start(f32[4,48,128]{2,1,0:T(8,128)S(1)} %collective-permute-done.8.by_x.refs_4_) | copy-start | bytes 294916
  108.3 4.5 %copy-start.9 = (f32[4,48,128]{2,1,0:T(8,128)}, f32[4,48,128]{2,1,0:T(8,128)S(1)}, u32[]{:S(2)}) copy-start(f32[4,48,128]{2,1,0:T(8,128)S(1)} %collective-permute-done.9.by_x2.refs_5_) | copy-start | bytes 294916
  109.1 3.6 %collective-permute-start.11 = (f32[12,8,128]{2,1,0:T(8,128)S(1)}, f32[12,8,128]{2,1,0:T(8,128)S(1)}, u32[]{:S(2)}, u32[]{:S(2)}) collective-permute-start(f32[12,8,128]{2,1,0:T(8,128)S(1)} %get-tuple-element.60), channel_id=1, source_target_pairs={{0,15},{1,2},{2,1},{3,4},{4,3},{5,6},{6,5},{7,8},{8,7},{9,10},{10,... | collective-permute-start | bytes 147464 | tf_op jit(solution)/shard_map/ppermute | solution.py:740
  109.2 3.5 %collective-permute-start.10 = (f32[12,8,128]{2,1,0:T(8,128)S(1)}, f32[12,8,128]{2,1,0:T(8,128)S(1)}, u32[]{:S(2)}, u32[]{:S(2)}) collective-permute-start(f32[12,8,128]{2,1,0:T(8,128)S(1)} %get-tuple-element.61), channel_id=1, source_target_pairs={{0,1},{1,0},{2,3},{3,2},{4,5},{5,4},{6,7},{7,6},{8,9},{9,8},{10,11... | collective-permute-start | bytes 147464 | tf_op jit(solution)/shard_map/ppermute | solution.py:739
  112.7 0.6 copy-start.17
  112.7 0.6 copy-start.18
  116.2 10.0 %all-to-all-start.2 = ((f32[16,1,8,128]{3,2,1,0:T(8,128)}), f32[16,1,8,128]{3,2,1,0:T(8,128)S(1)}, u32[]{:S(2)}, u32[]{:S(2)}) async-start(f32[16,1,8,128]{3,2,1,0:T(8,128)} %get-tuple-element.34), calls=%async_computation.2 | async-start | bytes 131072 | tf_op jit(solution)/shard_map/all_to_all | solution.py:750
  126.2 4.9 %copy-start.12 = (f32[16,1,8,128]{3,2,1,0:T(8,128)}, f32[16,1,8,128]{3,2,1,0:T(8,128)S(1)}, u32[]{:S(2)}) copy-start(f32[16,1,8,128]{3,2,1,0:T(8,128)S(1)} %all-to-all-done.2.mid) | copy-start | bytes 196612
  126.2 4.8 %collective-permute-start.13 = (f32[40,8,128]{2,1,0:T(8,128)S(1)}, f32[40,8,128]{2,1,0:T(8,128)S(1)}, u32[]{:S(2)}, u32[]{:S(2)}) collective-permute-start(f32[40,8,128]{2,1,0:T(8,128)S(1)} %get-tuple-element.50), channel_id=1, source_target_pairs={{0,15},{1,2},{2,1},{3,4},{4,3},{5,6},{6,5},{7,8},{8,7},{9,10},{10,... | collective-permute-start | bytes 491528 | tf_op jit(solution)/shard_map/ppermute | solution.py:740
  127.6 3.5 %collective-permute-start.12 = (f32[40,8,128]{2,1,0:T(8,128)S(1)}, f32[40,8,128]{2,1,0:T(8,128)S(1)}, u32[]{:S(2)}, u32[]{:S(2)}) collective-permute-start(f32[40,8,128]{2,1,0:T(8,128)S(1)} %get-tuple-element.51), channel_id=1, source_target_pairs={{0,1},{1,0},{2,3},{3,2},{4,5},{5,4},{6,7},{7,6},{8,9},{9,8},{10,11... | collective-permute-start | bytes 491528 | tf_op jit(solution)/shard_map/ppermute | solution.py:739
  131.1 0.7 copy-start.10
  131.1 0.7 copy-start.11

commit v9 on v8

--- a/solution.py
+++ b/solution.py
@@ -341,7 +341,7 @@
     return advance
 
 
-def call(kernel, outs, scratch, *args, far_in=0, far_out=0, copies=0):
+def call(kernel, outs, scratch, *args, far_in=0, far_out=0, copies=0, grant=VMEM_BYTES):
     near, far = pl.BlockSpec(memory_space=pltpu.VMEM), pl.BlockSpec(memory_space=pl.ANY)
     specs = [pl.BlockSpec(memory_space=pltpu.SMEM)] + [near] * (len(args) - 1 - far_in) + [far] * far_in
     return pl.pallas_call(
@@ -351,7 +351,7 @@
         out_specs=[near] * (len(outs) - far_out) + [far] * far_out,
         scratch_shapes=[pltpu.VMEM(o, F32) for o in scratch]
         + ([pltpu.SemaphoreType.DMA((copies,))] if copies else []),
-        compiler_params=pltpu.CompilerParams(vmem_limit_bytes=VMEM_BYTES),
+        compiler_params=pltpu.CompilerParams(vmem_limit_bytes=grant),
         cost_estimate=pl.CostEstimate(flops=10**7, bytes_accessed=8 << 20, transcendentals=0),
     )(*args)
 
@@ -459,7 +459,8 @@
     outs += [(16, 24, 128)] if first else []
     scratch = [(3, 16, 24, 128), (16, 24, 128), (4, 8, 128), (2, 8, 128)]
     args = (mid, below, above) + (() if first else (k2,))
-    return call(functools.partial(mid_kernel, first), outs, scratch, pos, *args)
+    grant = VMEM_BYTES if first else VMEM_BYTES // 4
+    return call(functools.partial(mid_kernel, first), outs, scratch, pos, *args, grant=grant)
 
 
 def solve_last(b, k, owned):

time: 164 us -> 161 us (0.982)
    unnamed x40 -> x44, local copies, waits for them, and re-layouts: 4.49 us -> 4.44 us
  transfers between devices with their start and end apart: 17 -> 17, of which waited for: 12 -> 12; matrix products, arithmetic and copies ran while one was open for 1% -> 2% of each run, Pallas kernels for 0% -> 0%
where the time goes in v9:
time: 161 us
  waiting for transfers between devices  48.2 us (30%)
  starting transfers between devices  45.7 us (28%)
  Pallas kernels  39.6 us (25%)
  blocking collectives  16.5 us (10%)
  local copies, waits for them, and re-layouts  5.4 us (3%)
  other arithmetic  4.18 us (3%)
    pallas_call x6, Pallas kernels, call(): pl.pallas_call(kernel, out_shape=[jax.ShapeDtypeStruct(o, F32) for o in o...  39.6 us
    all_to_all x3, waiting for transfers between devices, gather(): return lax.all_to_all(copies, axis, 0, 0, tiled=True)  24.1 us
    all_to_all x3, starting transfers between devices, gather(): return lax.all_to_all(copies, axis, 0, 0, tiled=True)  17.4 us
    all_to_all x1, blocking collectives, gather(): return lax.all_to_all(copies, axis, 0, 0, tiled=True)  16.5 us
    ppermute x6, starting transfers between devices, swap(): lax.ppermute(second, axis, [(i, (i + 1 if i % 2 else i - 1) % count) for...  14.5 us
    ppermute x6, waiting for transfers between devices, swap(): lax.ppermute(second, axis, [(i, (i + 1 if i % 2 else i - 1) % count) for...  14.4 us
    ppermute x6, starting transfers between devices, swap(): lax.ppermute(first, axis, [(i, i ^ 1) for i in range(count)])  11.7 us
    unnamed x44, local copies, waits for them, and re-layouts  4.44 us
  transfers between devices with their start and end apart: 17, of which 12 were waited for; matrix products, arithmetic and copies ran while one was open for 2% of the time, Pallas kernels for 0%

profile of v9, /device:TPU:1, one launch (start us, length us, event | category | flops | bytes accessed | tf_op | source)
XLA Modules:
  0.0 160.8 jit_solution(17882628079648689025)
XLA Ops:
  0.7 1.4 fusion.3
  2.1 2.2 %collective-permute-start = (f32[2,10,32,128]{3,2,1,0:T(8,128)S(1)}, f32[2,10,32,128]{3,2,1,0:T(8,128)S(1)}, u32[]{:S(2)}, u32[]{:S(2)}) collective-permute-start(f32[2,10,32,128]{3,2,1,0:T(8,128)S(1)} %get-tuple-element.48), channel_id=1, source_target_pairs={{0,16},{16,0},{32,48},{48,32},{64,80},{80,64},{96,112},{112,96},{1... | collective-permute-start | bytes 983048 | tf_op jit(solution)/shard_map/ppermute | solution.py:740
  4.3 4.1 %collective-permute-start.1 = (f32[2,10,32,128]{3,2,1,0:T(8,128)S(1)}, f32[2,10,32,128]{3,2,1,0:T(8,128)S(1)}, u32[]{:S(2)}, u32[]{:S(2)}) collective-permute-start(f32[2,10,32,128]{3,2,1,0:T(8,128)S(1)} %get-tuple-element.49), channel_id=1, source_target_pairs={{0,240},{16,32},{32,16},{48,64},{64,48},{80,96},{96,80},{112,128},... | collective-permute-start | bytes 983048 | tf_op jit(solution)/shard_map/ppermute | solution.py:741
  8.4 2.1 %collective-permute-done = f32[2,10,32,128]{3,2,1,0:T(8,128)S(1)} collective-permute-done((f32[2,10,32,128]{3,2,1,0:T(8,128)S(1)}, f32[2,10,32,128]{3,2,1,0:T(8,128)S(1)}, u32[]{:S(2)}, u32[]{:S(2)}) %collective-permute-start) | collective-permute-done | bytes 327712 | tf_op jit(solution)/shard_map/ppermute | solution.py:740
  10.5 5.1 %collective-permute-done.1 = f32[2,10,32,128]{3,2,1,0:T(8,128)S(1)} collective-permute-done((f32[2,10,32,128]{3,2,1,0:T(8,128)S(1)}, f32[2,10,32,128]{3,2,1,0:T(8,128)S(1)}, u32[]{:S(2)}, u32[]{:S(2)}) %collective-permute-start.1) | collective-permute-done | bytes 327712 | tf_op jit(solution)/shard_map/ppermute | solution.py:741
  15.7 0.1 pad_maximum_fusion.wide
  15.8 0.1 slice_select_fusion
  15.9 0.9 copy-done.5
  16.9 2.2 %collective-permute-start.2 = (f32[720,128]{1,0:T(8,128)S(1)}, f32[720,128]{1,0:T(8,128)S(1)}, u32[]{:S(2)}, u32[]{:S(2)}) collective-permute-start(f32[720,128]{1,0:T(8,128)S(1)} %select_n.130), channel_id=1, source_target_pairs={{0,1},{1,0},{2,3},{3,2},{4,5},{5,4},{6,7},{7,6},{8,9},{9,8},{10,11... | collective-permute-start | bytes 1105928 | tf_op jit(solution)/shard_map/ppermute | solution.py:740
  19.1 1.6 %collective-permute-start.3 = (f32[720,128]{1,0:T(8,128)S(1)}, f32[720,128]{1,0:T(8,128)S(1)}, u32[]{:S(2)}, u32[]{:S(2)}) collective-permute-start(f32[720,128]{1,0:T(8,128)S(1)} %select_n.132), channel_id=1, source_target_pairs={{0,15},{1,2},{2,1},{3,4},{4,3},{5,6},{6,5},{7,8},{8,7},{9,10},{10,... | collective-permute-start | bytes 1105928 | tf_op jit(solution)/shard_map/ppermute | solution.py:741
  20.8 0.6 pad_add_fusion.pos
  21.4 5.0 %collective-permute-done.3.by_y2 = f32[720,128]{1,0:T(8,128)S(1)} collective-permute-done((f32[720,128]{1,0:T(8,128)S(1)}, f32[720,128]{1,0:T(8,128)S(1)}, u32[]{:S(2)}, u32[]{:S(2)}) %collective-permute-start.3) | collective-permute-done | bytes 368672 | tf_op jit(solution)/shard_map/ppermute | solution.py:741
  26.4 0.8 copy-done.18
  27.1 7.0 %shard_map.50 = (f32[3,4,16,128]{3,2,1,0:T(8,128)}, f32[16,2,8,128]{3,2,1,0:T(8,128)}, f32[36,56,128]{2,1,0:T(8,128)}, f32[36,56,128]{2,1,0:T(8,128)}, f32[36,56,128]{2,1,0:T(8,128)}) custom-call(s32[2]{0:T(128)} %pad_add_fusion.pos, f32[2,36,32,128]{3,2,1,0:T(8,128)} %copy-done.5, f32[720,128]{1,0:T(8,128)} %copy-done.17, f32[720,128]{1,0:T(8,128)} %copy-done.18), custom_call_target="tpu_custom_call" | custom-call | flops 10000000 | bytes 8388608 | tf_op jit(solution)/shard_map/pallas_call | solution.py:347
  34.1 4.2 %collective-permute-start.5 = (f32[3,4,16,128]{3,2,1,0:T(8,128)}, f32[3,4,16,128]{3,2,1,0:T(8,128)S(1)}, u32[]{:S(2)}, u32[]{:S(2)}) collective-permute-start(f32[3,4,16,128]{3,2,1,0:T(8,128)} %get-tuple-element.24.refs_1_), channel_id=1, source_target_pairs={{0,240},{16,32},{32,16},{48,64},{64,48},{80,96},{96,80},{112,128},... | collective-permute-start | bytes 294920 | tf_op jit(solution)/shard_map/ppermute | solution.py:741
  38.3 3.5 %all-to-all-start = ((f32[16,2,8,128]{3,2,1,0:T(8,128)}), f32[16,2,8,128]{3,2,1,0:T(8,128)S(1)}, u32[]{:S(2)}, u32[]{:S(2)}) async-start(f32[16,2,8,128]{3,2,1,0:T(8,128)} %get-tuple-element.23), calls=%async_computation | async-start | bytes 262144 | tf_op jit(solution)/shard_map/all_to_all | solution.py:751
  41.9 0.1 collective-permute-done.4.refs_2_
  42.0 0.9 pad_maximum_fusion.4
  43.0 5.5 %all-to-all-done.mid = f32[16,2,8,128]{3,2,1,0:T(8,128)S(1)} async-done(((f32[16,2,8,128]{3,2,1,0:T(8,128)}), f32[16,2,8,128]{3,2,1,0:T(8,128)S(1)}, u32[]{:S(2)}, u32[]{:S(2)}) %all-to-all-start) | async-done | bytes 131104 | tf_op jit(solution)/shard_map/all_to_all | solution.py:751
  48.6 3.2 %collective-permute-start.7 = (f32[68,8,128]{2,1,0:T(8,128)S(1)}, f32[68,8,128]{2,1,0:T(8,128)S(1)}, u32[]{:S(2)}, u32[]{:S(2)}) collective-permute-start(f32[68,8,128]{2,1,0:T(8,128)S(1)} %get-tuple-element.52), channel_id=1, source_target_pairs={{0,15},{1,2},{2,1},{3,4},{4,3},{5,6},{6,5},{7,8},{8,7},{9,10},{10,... | collective-permute-start | bytes 835592 | tf_op jit(solution)/shard_map/ppermute | solution.py:741
  51.8 4.5 %collective-permute-start.6 = (f32[68,8,128]{2,1,0:T(8,128)S(1)}, f32[68,8,128]{2,1,0:T(8,128)S(1)}, u32[]{:S(2)}, u32[]{:S(2)}) collective-permute-start(f32[68,8,128]{2,1,0:T(8,128)S(1)} %get-tuple-element.53), channel_id=1, source_target_pairs={{0,1},{1,0},{2,3},{3,2},{4,5},{5,4},{6,7},{7,6},{8,9},{9,8},{10,11... | collective-permute-start | bytes 835592 | tf_op jit(solution)/shard_map/ppermute | solution.py:740
  56.3 1.2 collective-permute-done.6.by_y.refs_4_
  57.5 0.7 copy-done.10
  58.2 3.3 %shard_map.51 = (f32[3,5,24,128]{3,2,1,0:T(8,128)}, f32[16,5,8,128]{3,2,1,0:T(8,128)}, f32[16,24,128]{2,1,0:T(8,128)}) custom-call(s32[2]{0:T(128)} %pad_add_fusion.pos, f32[16,2,8,128]{3,2,1,0:T(8,128)} %copy-done.8, f32[68,8,128]{2,1,0:T(8,128)} %copy-done.10, f32[68,8,128]{2,1,0:T(8,128)} %copy-done.9), custom_call_target="tpu_custom_call" | custom-call | flops 10000000 | bytes 8388608 | tf_op jit(solution)/shard_map/pallas_call | solution.py:347
  61.5 10.3 %all-to-all-start.1 = ((f32[16,5,8,128]{3,2,1,0:T(8,128)}), f32[16,5,8,128]{3,2,1,0:T(8,128)S(1)}, u32[]{:S(2)}, u32[]{:S(2)}) async-start(f32[16,5,8,128]{3,2,1,0:T(8,128)} %get-tuple-element.25), calls=%async_computation.1 | async-start | bytes 655360 | tf_op jit(solution)/shard_map/all_to_all | solution.py:751
  72.0 0.7 copy.25.owned
  72.7 12.2 %all-to-all-done.1.three = f32[16,5,8,128]{3,2,1,0:T(8,128)S(1)} async-done(((f32[16,5,8,128]{3,2,1,0:T(8,128)}), f32[16,5,8,128]{3,2,1,0:T(8,128)S(1)}, u32[]{:S(2)}, u32[]{:S(2)}) %all-to-all-start.1) | async-done | bytes 327712 | tf_op jit(solution)/shard_map/all_to_all | solution.py:751
  84.9 0.7 copy-done.7
  85.6 14.2 %shard_map.52 = (f32[4,16,128]{2,1,0:T(8,128)}, f32[4,48,128]{2,1,0:T(8,128)}, f32[4,48,128]{2,1,0:T(8,128)}, f32[18,56,128]{2,1,0:T(8,128)}, f32[24,56,128]{2,1...) custom-call(s32[2]{0:T(128)} %pad_add_fusion.pos, f32[32,128]{1,0:T(8,128)} %copy.25.owned, ...), custom_call_target="tpu_custom_call" | custom-call | flops 10000000 | bytes 8388608 | tf_op jit(solution)/shard_map/pallas_call | solution.py:347
  99.8 0.3 collective-permute-start.8
  100.1 1.8 %collective-permute-start.9 = (f32[4,48,128]{2,1,0:T(8,128)}, f32[4,48,128]{2,1,0:T(8,128)S(1)}, u32[]{:S(2)}, u32[]{:S(2)}) collective-permute-start(f32[4,48,128]{2,1,0:T(8,128)} %get-tuple-element.32), channel_id=1, source_target_pairs={{0,240},{16,32},{32,16},{48,64},{64,48},{80,96},{96,80},{112,128},... | collective-permute-start | bytes 294920 | tf_op jit(solution)/shard_map/ppermute | solution.py:779
  101.9 2.8 %collective-permute-done.8.by_x.refs_4_ = f32[4,48,128]{2,1,0:T(8,128)S(1)} collective-permute-done((f32[4,48,128]{2,1,0:T(8,128)}, f32[4,48,128]{2,1,0:T(8,128)S(1)}, u32[]{:S(2)}, u32[]{:S(2)}) %collective-permute-start.8) | collective-permute-done | bytes 98336 | tf_op jit(solution)/shard_map/ppermute | solution.py:778
  104.7 3.6 %collective-permute-done.9.by_x2.refs_5_ = f32[4,48,128]{2,1,0:T(8,128)S(1)} collective-permute-done((f32[4,48,128]{2,1,0:T(8,128)}, f32[4,48,128]{2,1,0:T(8,128)S(1)}, u32[]{:S(2)}, u32[]{:S(2)}) %collective-permute-start.9) | collective-permute-done | bytes 98336 | tf_op jit(solution)/shard_map/ppermute | solution.py:779
  108.3 0.9 pad_maximum_fusion.11
  109.2 0.1 collective-permute-start.11
  109.3 0.9 collective-permute-start.10
  110.2 2.6 %collective-permute-done.11.by_y2 = f32[12,8,128]{2,1,0:T(8,128)S(1)} collective-permute-done((f32[12,8,128]{2,1,0:T(8,128)S(1)}, f32[12,8,128]{2,1,0:T(8,128)S(1)}, u32[]{:S(2)}, u32[]{:S(2)}) %collective-permute-start.11) | collective-permute-done | bytes 49184 | tf_op jit(solution)/shard_map/ppermute | solution.py:741
  112.8 0.6 copy-done.19
  113.4 2.9 %shard_map.53 = (f32[12,32,128]{2,1,0:T(8,128)}, f32[12,32,128]{2,1,0:T(8,128)}, f32[16,1,8,128]{3,2,1,0:T(8,128)}) custom-call(s32[2]{0:T(128)} %pad_add_fusion.pos, f32[4,16,128]{2,1,0:T(8,128)} %get-tuple-element.30.mid, f32[4,48,128]{2,1,0:T(8,128)} %copy-done.13, f32[4,48,128]{2,1,0:T(8,128)} %copy-done.14, f32[12,8,128]{2,1,0:T(8,128)} %copy-done.20, ...), custom_call_target="tpu_custom_call" | custom-call | flops 10000000 | bytes 8388608 | tf_op jit(solution)/shard_map/pallas_call | solution.py:347
  116.3 3.5 %all-to-all-start.2 = ((f32[16,1,8,128]{3,2,1,0:T(8,128)}), f32[16,1,8,128]{3,2,1,0:T(8,128)S(1)}, u32[]{:S(2)}, u32[]{:S(2)}) async-start(f32[16,1,8,128]{3,2,1,0:T(8,128)} %get-tuple-element.34), calls=%async_computation.2 | async-start | bytes 131072 | tf_op jit(solution)/shard_map/all_to_all | solution.py:751
  119.9 6.4 %all-to-all-done.2.mid = f32[16,1,8,128]{3,2,1,0:T(8,128)S(1)} async-done(((f32[16,1,8,128]{3,2,1,0:T(8,128)}), f32[16,1,8,128]{3,2,1,0:T(8,128)S(1)}, u32[]{:S(2)}, u32[]{:S(2)}) %all-to-all-start.2) | async-done | bytes 65568 | tf_op jit(solution)/shard_map/all_to_all | solution.py:751
  126.3 1.3 collective-permute-start.13
  127.6 1.9 %collective-permute-start.12 = (f32[40,8,128]{2,1,0:T(8,128)S(1)}, f32[40,8,128]{2,1,0:T(8,128)S(1)}, u32[]{:S(2)}, u32[]{:S(2)}) collective-permute-start(f32[40,8,128]{2,1,0:T(8,128)S(1)} %get-tuple-element.51), channel_id=1, source_target_pairs={{0,1},{1,0},{2,3},{3,2},{4,5},{5,4},{6,7},{7,6},{8,9},{9,8},{10,11... | collective-permute-start | bytes 491528 | tf_op jit(solution)/shard_map/ppermute | solution.py:740
  129.5 1.6 %collective-permute-done.13.by_y2.refs_7_ = f32[40,8,128]{2,1,0:T(8,128)S(1)} collective-permute-done((f32[40,8,128]{2,1,0:T(8,128)S(1)}, f32[40,8,128]{2,1,0:T(8,128)S(1)}, u32[]{:S(2)}, u32[]{:S(2)}) %collective-permute-start.13) | collective-permute-done | bytes 163872 | tf_op jit(solution)/shard_map/ppermute | solution.py:741
  131.2 1.8 %shard_map.54 = (f32[3,5,24,128]{3,2,1,0:T(8,128)S(1)}, f32[16,2,8,128]{3,2,1,0:T(8,128)S(1)}) custom-call(s32[2]{0:T(128)S(1)} %copy-done.4, f32[16,1,8,128]{3,2,1,0:T(8,128)S(1)} %all-to-all-done.2.mid, f32[40,8,128]{2,1,0:T(8,128)S(1)} %collective-permute-done.12.by_y.refs_6_, f32[40,8,128]{2,1,0:T(8,128)S(1)} %collective-permute-done.13.by_y2.refs_7_, ...), custom_call_target="tpu_custom_call" | custom-call | flops 10000000 | bytes 8388608 | tf_op jit(solution)/shard_map/pallas_call | solution.py:347
  133.0 0.7 copy-done.3
  133.7 16.5 %all_to_all.20.three = f32[16,2,8,128]{3,2,1,0:T(8,128)} all-to-all(f32[16,2,8,128]{3,2,1,0:T(8,128)S(1)} %get-tuple-element.37), channel_id=1, replica_groups=mesh['gx'=16,'gy'=16] {'gy'}, dimensions={0} | all-to-all | bytes 262144 | tf_op jit(solution)/shard_map/all_to_all | solution.py:751
  150.2 10.4 %shard_map.55 = (f32[16,32,128]{2,1,0:T(8,128)}, f32[16,32,128]{2,1,0:T(8,128)}) custom-call(s32[2]{0:T(128)} %pad_add_fusion.pos, f32[32,128]{1,0:T(8,128)} %copy.25.owned, f32[16,2,8,128]{3,2,1,0:T(8,128)} %all_to_all.20.three, f32[4,64,128]{2,1,0:T(8,128)} %get-tuple-element.38.k3, f32[3,5,24,128]{3,2,1,0:T(8,128)} %copy-done.3, ...), custom_call_target="tpu_custom_call" | custom-call | flops 10000000 | bytes 8388608 | tf_op jit(solution)/shard_map/pallas_call | solution.py:347
  (63 shorter events, 0.6 us)
Async XLA Ops:
  0.6 15.0 %copy-start.6 = (f32[16,32,128]{2,1,0:T(8,128)S(1)}, f32[16,32,128]{2,1,0:T(8,128)}, u32[]{:S(2)}) copy-start(f32[16,32,128]{2,1,0:T(8,128)} %refs_12_.1) | copy-start | bytes 786436
  0.7 15.0 %copy-start.11 = (f32[16,32,128]{2,1,0:T(8,128)S(1)}, f32[16,32,128]{2,1,0:T(8,128)}, u32[]{:S(2)}) copy-start(f32[16,32,128]{2,1,0:T(8,128)} %param.4) | copy-start | bytes 786436
  2.1 8.4 %collective-permute-start = (f32[2,10,32,128]{3,2,1,0:T(8,128)S(1)}, f32[2,10,32,128]{3,2,1,0:T(8,128)S(1)}, u32[]{:S(2)}, u32[]{:S(2)}) collective-permute-start(f32[2,10,32,128]{3,2,1,0:T(8,128)S(1)} %get-tuple-element.48), channel_id=1, source_target_pairs={{0,16},{16,0},{32,48},{48,32},{64,80},{80,64},{96,112},{112,96},{1... | collective-permute-start | bytes 983048 | tf_op jit(solution)/shard_map/ppermute | solution.py:740
  4.3 11.3 %collective-permute-start.1 = (f32[2,10,32,128]{3,2,1,0:T(8,128)S(1)}, f32[2,10,32,128]{3,2,1,0:T(8,128)S(1)}, u32[]{:S(2)}, u32[]{:S(2)}) collective-permute-start(f32[2,10,32,128]{3,2,1,0:T(8,128)S(1)} %get-tuple-element.49), channel_id=1, source_target_pairs={{0,240},{16,32},{32,16},{48,64},{64,48},{80,96},{96,80},{112,128},... | collective-permute-start | bytes 983048 | tf_op jit(solution)/shard_map/ppermute | solution.py:741
  15.8 1.0 copy-start.5
  16.9 4.5 %collective-permute-start.2 = (f32[720,128]{1,0:T(8,128)S(1)}, f32[720,128]{1,0:T(8,128)S(1)}, u32[]{:S(2)}, u32[]{:S(2)}) collective-permute-start(f32[720,128]{1,0:T(8,128)S(1)} %select_n.130), channel_id=1, source_target_pairs={{0,1},{1,0},{2,3},{3,2},{4,5},{5,4},{6,7},{7,6},{8,9},{9,8},{10,11... | collective-permute-start | bytes 1105928 | tf_op jit(solution)/shard_map/ppermute | solution.py:740
  19.1 7.2 %collective-permute-start.3 = (f32[720,128]{1,0:T(8,128)S(1)}, f32[720,128]{1,0:T(8,128)S(1)}, u32[]{:S(2)}, u32[]{:S(2)}) collective-permute-start(f32[720,128]{1,0:T(8,128)S(1)} %select_n.132), channel_id=1, source_target_pairs={{0,15},{1,2},{2,1},{3,4},{4,3},{5,6},{6,5},{7,8},{8,7},{9,10},{10,... | collective-permute-start | bytes 1105928 | tf_op jit(solution)/shard_map/ppermute | solution.py:741
  21.4 5.0 %copy-start.17 = (f32[720,128]{1,0:T(8,128)}, f32[720,128]{1,0:T(8,128)S(1)}, u32[]{:S(2)}) copy-start(f32[720,128]{1,0:T(8,128)S(1)} %collective-permute-done.2.by_y) | copy-start | bytes 1105924
  26.4 0.8 copy-start.18
  34.1 7.7 %collective-permute-start.5 = (f32[3,4,16,128]{3,2,1,0:T(8,128)}, f32[3,4,16,128]{3,2,1,0:T(8,128)S(1)}, u32[]{:S(2)}, u32[]{:S(2)}) collective-permute-start(f32[3,4,16,128]{3,2,1,0:T(8,128)} %get-tuple-element.24.refs_1_), channel_id=1, source_target_pairs={{0,240},{16,32},{32,16},{48,64},{64,48},{80,96},{96,80},{112,128},... | collective-permute-start | bytes 294920 | tf_op jit(solution)/shard_map/ppermute | solution.py:741
  38.3 3.7 %collective-permute-start.4 = (f32[3,4,16,128]{3,2,1,0:T(8,128)}, f32[3,4,16,128]{3,2,1,0:T(8,128)S(1)}, u32[]{:S(2)}, u32[]{:S(2)}) collective-permute-start(f32[3,4,16,128]{3,2,1,0:T(8,128)} %get-tuple-element.24.refs_1_), channel_id=1, source_target_pairs={{0,16},{16,0},{32,48},{48,32},{64,80},{80,64},{96,112},{112,96},{1... | collective-permute-start | bytes 294920 | tf_op jit(solution)/shard_map/ppermute | solution.py:740
  38.3 10.2 %all-to-all-start = ((f32[16,2,8,128]{3,2,1,0:T(8,128)}), f32[16,2,8,128]{3,2,1,0:T(8,128)S(1)}, u32[]{:S(2)}, u32[]{:S(2)}) async-start(f32[16,2,8,128]{3,2,1,0:T(8,128)} %get-tuple-element.23), calls=%async_computation | async-start | bytes 262144 | tf_op jit(solution)/shard_map/all_to_all | solution.py:751
  41.8 6.7 %copy-start.15 = (f32[3,4,16,128]{3,2,1,0:T(8,128)}, f32[3,4,16,128]{3,2,1,0:T(8,128)S(1)}, u32[]{:S(2)}) copy-start(f32[3,4,16,128]{3,2,1,0:T(8,128)S(1)} %collective-permute-done.5.refs_3_) | copy-start | bytes 294916
  42.0 6.6 %copy-start.16 = (f32[3,4,16,128]{3,2,1,0:T(8,128)}, f32[3,4,16,128]{3,2,1,0:T(8,128)S(1)}, u32[]{:S(2)}) copy-start(f32[3,4,16,128]{3,2,1,0:T(8,128)S(1)} %collective-permute-done.4.refs_2_) | copy-start | bytes 294916
  48.5 9.0 %copy-start.8 = (f32[16,2,8,128]{3,2,1,0:T(8,128)}, f32[16,2,8,128]{3,2,1,0:T(8,128)S(1)}, u32[]{:S(2)}) copy-start(f32[16,2,8,128]{3,2,1,0:T(8,128)S(1)} %all-to-all-done.mid) | copy-start | bytes 393220
  48.5 23.3 %copy-start.21 = (s32[16,16]{1,0:T(8,128)S(1)}, s32[16,16]{1,0:T(8,128)}, u32[]{:S(2)}) copy-start(s32[16,16]{1,0:T(8,128)} %param.5) | copy-start | bytes 3076
  48.6 7.7 %collective-permute-start.7 = (f32[68,8,128]{2,1,0:T(8,128)S(1)}, f32[68,8,128]{2,1,0:T(8,128)S(1)}, u32[]{:S(2)}, u32[]{:S(2)}) collective-permute-start(f32[68,8,128]{2,1,0:T(8,128)S(1)} %get-tuple-element.52), channel_id=1, source_target_pairs={{0,15},{1,2},{2,1},{3,4},{4,3},{5,6},{6,5},{7,8},{8,7},{9,10},{10,... | collective-permute-start | bytes 835592 | tf_op jit(solution)/shard_map/ppermute | solution.py:741
  51.8 5.7 %collective-permute-start.6 = (f32[68,8,128]{2,1,0:T(8,128)S(1)}, f32[68,8,128]{2,1,0:T(8,128)S(1)}, u32[]{:S(2)}, u32[]{:S(2)}) collective-permute-start(f32[68,8,128]{2,1,0:T(8,128)S(1)} %get-tuple-element.53), channel_id=1, source_target_pairs={{0,1},{1,0},{2,3},{3,2},{4,5},{5,4},{6,7},{7,6},{8,9},{9,8},{10,11... | collective-permute-start | bytes 835592 | tf_op jit(solution)/shard_map/ppermute | solution.py:740
  56.3 1.2 copy-start.9
  57.5 0.7 copy-start.10
  61.5 23.4 %all-to-all-start.1 = ((f32[16,5,8,128]{3,2,1,0:T(8,128)}), f32[16,5,8,128]{3,2,1,0:T(8,128)S(1)}, u32[]{:S(2)}, u32[]{:S(2)}) async-start(f32[16,5,8,128]{3,2,1,0:T(8,128)} %get-tuple-element.25), calls=%async_computation.1 | async-start | bytes 655360 | tf_op jit(solution)/shard_map/all_to_all | solution.py:751
  84.9 0.7 copy-start.7
  99.8 26.5 %copy-start.12 = (f32[16,32,128]{2,1,0:T(8,128)S(1)}, f32[16,32,128]{2,1,0:T(8,128)}, u32[]{:S(2)}) copy-start(f32[16,32,128]{2,1,0:T(8,128)} %get-tuple-element.35.refs_8_) | copy-start | bytes 786436
  99.8 4.9 %collective-permute-start.8 = (f32[4,48,128]{2,1,0:T(8,128)}, f32[4,48,128]{2,1,0:T(8,128)S(1)}, u32[]{:S(2)}, u32[]{:S(2)}) collective-permute-start(f32[4,48,128]{2,1,0:T(8,128)} %get-tuple-element.31), channel_id=1, source_target_pairs={{0,16},{16,0},{32,48},{48,32},{64,80},{80,64},{96,112},{112,96},{1... | collective-permute-start | bytes 294920 | tf_op jit(solution)/shard_map/ppermute | solution.py:778
  100.1 8.2 %collective-permute-start.9 = (f32[4,48,128]{2,1,0:T(8,128)}, f32[4,48,128]{2,1,0:T(8,128)S(1)}, u32[]{:S(2)}, u32[]{:S(2)}) collective-permute-start(f32[4,48,128]{2,1,0:T(8,128)} %get-tuple-element.32), channel_id=1, source_target_pairs={{0,240},{16,32},{32,16},{48,64},{64,48},{80,96},{96,80},{112,128},... | collective-permute-start | bytes 294920 | tf_op jit(solution)/shard_map/ppermute | solution.py:779
  104.7 8.1 %copy-start.13 = (f32[4,48,128]{2,1,0:T(8,128)}, f32[4,48,128]{2,1,0:T(8,128)S(1)}, u32[]{:S(2)}) copy-start(f32[4,48,128]{2,1,0:T(8,128)S(1)} %collective-permute-done.8.by_x.refs_4_) | copy-start | bytes 294916
  108.2 4.6 %copy-start.14 = (f32[4,48,128]{2,1,0:T(8,128)}, f32[4,48,128]{2,1,0:T(8,128)S(1)}, u32[]{:S(2)}) copy-start(f32[4,48,128]{2,1,0:T(8,128)S(1)} %collective-permute-done.9.by_x2.refs_5_) | copy-start | bytes 294916
  108.3 22.9 %copy-start.2 = (f32[16,24,128]{2,1,0:T(8,128)S(1)}, f32[16,24,128]{2,1,0:T(8,128)}, u32[]{:S(2)}) copy-start(f32[16,24,128]{2,1,0:T(8,128)} %get-tuple-element.36.refs_0_) | copy-start | bytes 589828
  108.3 22.9 %copy-start.4 = (s32[2]{0:T(128)S(1)}, s32[2]{0:T(128)}, u32[]{:S(2)}) copy-start(s32[2]{0:T(128)} %pad_add_fusion.pos) | copy-start | bytes 28
  109.2 3.6 %collective-permute-start.11 = (f32[12,8,128]{2,1,0:T(8,128)S(1)}, f32[12,8,128]{2,1,0:T(8,128)S(1)}, u32[]{:S(2)}, u32[]{:S(2)}) collective-permute-start(f32[12,8,128]{2,1,0:T(8,128)S(1)} %get-tuple-element.60), channel_id=1, source_target_pairs={{0,15},{1,2},{2,1},{3,4},{4,3},{5,6},{6,5},{7,8},{8,7},{9,10},{10,... | collective-permute-start | bytes 147464 | tf_op jit(solution)/shard_map/ppermute | solution.py:741
  109.3 3.5 %collective-permute-start.10 = (f32[12,8,128]{2,1,0:T(8,128)S(1)}, f32[12,8,128]{2,1,0:T(8,128)S(1)}, u32[]{:S(2)}, u32[]{:S(2)}) collective-permute-start(f32[12,8,128]{2,1,0:T(8,128)S(1)} %get-tuple-element.61), channel_id=1, source_target_pairs={{0,1},{1,0},{2,3},{3,2},{4,5},{5,4},{6,7},{7,6},{8,9},{9,8},{10,11... | collective-permute-start | bytes 147464 | tf_op jit(solution)/shard_map/ppermute | solution.py:740
  112.8 0.6 copy-start.19
  112.8 0.6 copy-start.20
  116.3 10.0 %all-to-all-start.2 = ((f32[16,1,8,128]{3,2,1,0:T(8,128)}), f32[16,1,8,128]{3,2,1,0:T(8,128)S(1)}, u32[]{:S(2)}, u32[]{:S(2)}) async-start(f32[16,1,8,128]{3,2,1,0:T(8,128)} %get-tuple-element.34), calls=%async_computation.2 | async-start | bytes 131072 | tf_op jit(solution)/shard_map/all_to_all | solution.py:751
  126.3 4.8 %collective-permute-start.13 = (f32[40,8,128]{2,1,0:T(8,128)S(1)}, f32[40,8,128]{2,1,0:T(8,128)S(1)}, u32[]{:S(2)}, u32[]{:S(2)}) collective-permute-start(f32[40,8,128]{2,1,0:T(8,128)S(1)} %get-tuple-element.50), channel_id=1, source_target_pairs={{0,15},{1,2},{2,1},{3,4},{4,3},{5,6},{6,5},{7,8},{8,7},{9,10},{10,... | collective-permute-start | bytes 491528 | tf_op jit(solution)/shard_map/ppermute | solution.py:741
  127.6 3.5 %collective-permute-start.12 = (f32[40,8,128]{2,1,0:T(8,128)S(1)}, f32[40,8,128]{2,1,0:T(8,128)S(1)}, u32[]{:S(2)}, u32[]{:S(2)}) collective-permute-start(f32[40,8,128]{2,1,0:T(8,128)S(1)} %get-tuple-element.51), channel_id=1, source_target_pairs={{0,1},{1,0},{2,3},{3,2},{4,5},{5,4},{6,7},{7,6},{8,9},{9,8},{10,11... | collective-permute-start | bytes 491528 | tf_op jit(solution)/shard_map/ppermute | solution.py:740
  131.2 19.0 %copy-start = (f32[40,8,128]{2,1,0:T(8,128)}, f32[40,8,128]{2,1,0:T(8,128)S(1)}, u32[]{:S(2)}) copy-start(f32[40,8,128]{2,1,0:T(8,128)S(1)} %collective-permute-done.13.by_y2.refs_7_) | copy-start | bytes 491524
  131.2 19.0 %copy-start.1 = (f32[40,8,128]{2,1,0:T(8,128)}, f32[40,8,128]{2,1,0:T(8,128)S(1)}, u32[]{:S(2)}) copy-start(f32[40,8,128]{2,1,0:T(8,128)S(1)} %collective-permute-done.12.by_y.refs_6_) | copy-start | bytes 491524
  133.0 0.7 copy-start.3

commit v10 on v9

--- a/solution.py
+++ b/solution.py
@@ -459,7 +459,7 @@
     outs += [(16, 24, 128)] if first else []
     scratch = [(3, 16, 24, 128), (16, 24, 128), (4, 8, 128), (2, 8, 128)]
     args = (mid, below, above) + (() if first else (k2,))
-    grant = VMEM_BYTES if first else VMEM_BYTES // 4
+    grant = VMEM_BYTES // 4
     return call(functools.partial(mid_kernel, first), outs, scratch, pos, *args, grant=grant)
 
 

time: 161 us -> 159 us (0.988)
  no operation moved by 1% of the time
where the time goes in v10:
time: 159 us
  waiting for transfers between devices  48.3 us (30%)
  starting transfers between devices  45 us (28%)
  Pallas kernels  39.1 us (25%)
  blocking collectives  16.5 us (10%)
  local copies, waits for them, and re-layouts  4.69 us (3%)
  other arithmetic  4.09 us (3%)
    pallas_call x6, Pallas kernels, call(): pl.pallas_call(kernel, out_shape=[jax.ShapeDtypeStruct(o, F32) for o in o...  39.1 us
    all_to_all x3, waiting for transfers between devices, gather(): return lax.all_to_all(copies, axis, 0, 0, tiled=True)  24.1 us
    all_to_all x3, starting transfers between devices, gather(): return lax.all_to_all(copies, axis, 0, 0, tiled=True)  16.7 us
    all_to_all x1, blocking collectives, gather(): return lax.all_to_all(copies, axis, 0, 0, tiled=True)  16.5 us
    ppermute x6, starting transfers between devices, swap(): lax.ppermute(second, axis, [(i, (i + 1 if i % 2 else i - 1) % count) for...  14.5 us
    ppermute x6, waiting for transfers between devices, swap(): lax.ppermute(second, axis, [(i, (i + 1 if i % 2 else i - 1) % count) for...  14.4 us
    ppermute x6, starting transfers between devices, swap(): lax.ppermute(first, axis, [(i, i ^ 1) for i in range(count)])  11.7 us
    unnamed x44, local copies, waits for them, and re-layouts  3.72 us
  transfers between devices with their start and end apart: 17, of which 12 were waited for; matrix products, arithmetic and copies ran while one was open for 2% of the time, Pallas kernels for 0%

profile of v10, /device:TPU:1, one launch (start us, length us, event | category | flops | bytes accessed | tf_op | source)
XLA Modules:
  0.0 158.8 jit_solution(17917207896824275497)
XLA Ops:
  0.7 1.4 fusion.3
  2.1 2.2 %collective-permute-start = (f32[2,10,32,128]{3,2,1,0:T(8,128)S(1)}, f32[2,10,32,128]{3,2,1,0:T(8,128)S(1)}, u32[]{:S(2)}, u32[]{:S(2)}) collective-permute-start(f32[2,10,32,128]{3,2,1,0:T(8,128)S(1)} %get-tuple-element.48), channel_id=1, source_target_pairs={{0,16},{16,0},{32,48},{48,32},{64,80},{80,64},{96,112},{112,96},{1... | collective-permute-start | bytes 983048 | tf_op jit(solution)/shard_map/ppermute | solution.py:740
  4.3 4.1 %collective-permute-start.1 = (f32[2,10,32,128]{3,2,1,0:T(8,128)S(1)}, f32[2,10,32,128]{3,2,1,0:T(8,128)S(1)}, u32[]{:S(2)}, u32[]{:S(2)}) collective-permute-start(f32[2,10,32,128]{3,2,1,0:T(8,128)S(1)} %get-tuple-element.49), channel_id=1, source_target_pairs={{0,240},{16,32},{32,16},{48,64},{64,48},{80,96},{96,80},{112,128},... | collective-permute-start | bytes 983048 | tf_op jit(solution)/shard_map/ppermute | solution.py:741
  8.4 2.1 %collective-permute-done = f32[2,10,32,128]{3,2,1,0:T(8,128)S(1)} collective-permute-done((f32[2,10,32,128]{3,2,1,0:T(8,128)S(1)}, f32[2,10,32,128]{3,2,1,0:T(8,128)S(1)}, u32[]{:S(2)}, u32[]{:S(2)}) %collective-permute-start) | collective-permute-done | bytes 327712 | tf_op jit(solution)/shard_map/ppermute | solution.py:740
  10.5 5.1 %collective-permute-done.1 = f32[2,10,32,128]{3,2,1,0:T(8,128)S(1)} collective-permute-done((f32[2,10,32,128]{3,2,1,0:T(8,128)S(1)}, f32[2,10,32,128]{3,2,1,0:T(8,128)S(1)}, u32[]{:S(2)}, u32[]{:S(2)}) %collective-permute-start.1) | collective-permute-done | bytes 327712 | tf_op jit(solution)/shard_map/ppermute | solution.py:741
  15.7 0.1 pad_maximum_fusion.wide
  15.8 0.1 slice_select_fusion
  15.9 0.9 copy-done.8
  16.9 2.2 %collective-permute-start.2 = (f32[720,128]{1,0:T(8,128)S(1)}, f32[720,128]{1,0:T(8,128)S(1)}, u32[]{:S(2)}, u32[]{:S(2)}) collective-permute-start(f32[720,128]{1,0:T(8,128)S(1)} %select_n.130), channel_id=1, source_target_pairs={{0,1},{1,0},{2,3},{3,2},{4,5},{5,4},{6,7},{7,6},{8,9},{9,8},{10,11... | collective-permute-start | bytes 1105928 | tf_op jit(solution)/shard_map/ppermute | solution.py:740
  19.1 1.6 %collective-permute-start.3 = (f32[720,128]{1,0:T(8,128)S(1)}, f32[720,128]{1,0:T(8,128)S(1)}, u32[]{:S(2)}, u32[]{:S(2)}) collective-permute-start(f32[720,128]{1,0:T(8,128)S(1)} %select_n.132), channel_id=1, source_target_pairs={{0,15},{1,2},{2,1},{3,4},{4,3},{5,6},{6,5},{7,8},{8,7},{9,10},{10,... | collective-permute-start | bytes 1105928 | tf_op jit(solution)/shard_map/ppermute | solution.py:741
  20.8 0.6 pad_add_fusion.pos
  21.4 5.0 %collective-permute-done.3.by_y2 = f32[720,128]{1,0:T(8,128)S(1)} collective-permute-done((f32[720,128]{1,0:T(8,128)S(1)}, f32[720,128]{1,0:T(8,128)S(1)}, u32[]{:S(2)}, u32[]{:S(2)}) %collective-permute-start.3) | collective-permute-done | bytes 368672 | tf_op jit(solution)/shard_map/ppermute | solution.py:741
  26.4 0.7 copy-done.18
  27.1 7.0 %shard_map.50 = (f32[3,4,16,128]{3,2,1,0:T(8,128)}, f32[16,2,8,128]{3,2,1,0:T(8,128)}, f32[36,56,128]{2,1,0:T(8,128)}, f32[36,56,128]{2,1,0:T(8,128)}, f32[36,56,128]{2,1,0:T(8,128)}) custom-call(s32[2]{0:T(128)} %pad_add_fusion.pos, f32[2,36,32,128]{3,2,1,0:T(8,128)} %copy-done.8, f32[720,128]{1,0:T(8,128)} %copy-done.17, f32[720,128]{1,0:T(8,128)} %copy-done.18), custom_call_target="tpu_custom_call" | custom-call | flops 10000000 | bytes 8388608 | tf_op jit(solution)/shard_map/pallas_call | solution.py:347
  34.1 4.2 %collective-permute-start.5 = (f32[3,4,16,128]{3,2,1,0:T(8,128)}, f32[3,4,16,128]{3,2,1,0:T(8,128)S(1)}, u32[]{:S(2)}, u32[]{:S(2)}) collective-permute-start(f32[3,4,16,128]{3,2,1,0:T(8,128)} %get-tuple-element.24.refs_1_), channel_id=1, source_target_pairs={{0,240},{16,32},{32,16},{48,64},{64,48},{80,96},{96,80},{112,128},... | collective-permute-start | bytes 294920 | tf_op jit(solution)/shard_map/ppermute | solution.py:741
  38.3 3.5 %all-to-all-start = ((f32[16,2,8,128]{3,2,1,0:T(8,128)}), f32[16,2,8,128]{3,2,1,0:T(8,128)S(1)}, u32[]{:S(2)}, u32[]{:S(2)}) async-start(f32[16,2,8,128]{3,2,1,0:T(8,128)} %get-tuple-element.23), calls=%async_computation | async-start | bytes 262144 | tf_op jit(solution)/shard_map/all_to_all | solution.py:751
  41.8 0.1 collective-permute-done.4.refs_2_
  42.0 0.9 pad_maximum_fusion.4
  43.0 5.5 %all-to-all-done.mid = f32[16,2,8,128]{3,2,1,0:T(8,128)S(1)} async-done(((f32[16,2,8,128]{3,2,1,0:T(8,128)}), f32[16,2,8,128]{3,2,1,0:T(8,128)S(1)}, u32[]{:S(2)}, u32[]{:S(2)}) %all-to-all-start) | async-done | bytes 131104 | tf_op jit(solution)/shard_map/all_to_all | solution.py:751
  48.5 3.2 %collective-permute-start.7 = (f32[68,8,128]{2,1,0:T(8,128)S(1)}, f32[68,8,128]{2,1,0:T(8,128)S(1)}, u32[]{:S(2)}, u32[]{:S(2)}) collective-permute-start(f32[68,8,128]{2,1,0:T(8,128)S(1)} %get-tuple-element.52), channel_id=1, source_target_pairs={{0,15},{1,2},{2,1},{3,4},{4,3},{5,6},{6,5},{7,8},{8,7},{9,10},{10,... | collective-permute-start | bytes 835592 | tf_op jit(solution)/shard_map/ppermute | solution.py:741
  51.8 4.5 %collective-permute-start.6 = (f32[68,8,128]{2,1,0:T(8,128)S(1)}, f32[68,8,128]{2,1,0:T(8,128)S(1)}, u32[]{:S(2)}, u32[]{:S(2)}) collective-permute-start(f32[68,8,128]{2,1,0:T(8,128)S(1)} %get-tuple-element.53), channel_id=1, source_target_pairs={{0,1},{1,0},{2,3},{3,2},{4,5},{5,4},{6,7},{7,6},{8,9},{9,8},{10,11... | collective-permute-start | bytes 835592 | tf_op jit(solution)/shard_map/ppermute | solution.py:740
  56.3 1.2 collective-permute-done.6.by_y.refs_4_
  57.5 2.7 %shard_map.51 = (f32[3,5,24,128]{3,2,1,0:T(8,128)S(1)}, f32[16,5,8,128]{3,2,1,0:T(8,128)}, f32[16,24,128]{2,1,0:T(8,128)S(1)}) custom-call(s32[2]{0:T(128)S(1)} %copy-done.6, f32[16,2,8,128]{3,2,1,0:T(8,128)S(1)} %all-to-all-done.mid, f32[68,8,128]{2,1,0:T(8,128)S(1)} %collective-permute-done.6.by_y.refs_4_, ...), custom_call_target="tpu_custom_call" | custom-call | flops 10000000 | bytes 8388608 | tf_op jit(solution)/shard_map/pallas_call | solution.py:347
  60.2 0.7 copy-done.4
  60.8 9.7 %all-to-all-start.1 = ((f32[16,5,8,128]{3,2,1,0:T(8,128)}), f32[16,5,8,128]{3,2,1,0:T(8,128)S(1)}, u32[]{:S(2)}, u32[]{:S(2)}) async-start(f32[16,5,8,128]{3,2,1,0:T(8,128)} %get-tuple-element.25), calls=%async_computation.1 | async-start | bytes 655360 | tf_op jit(solution)/shard_map/all_to_all | solution.py:751
  70.5 0.1 copy.21
  70.7 0.7 copy.25.owned
  71.3 12.2 %all-to-all-done.1.three = f32[16,5,8,128]{3,2,1,0:T(8,128)S(1)} async-done(((f32[16,5,8,128]{3,2,1,0:T(8,128)}), f32[16,5,8,128]{3,2,1,0:T(8,128)S(1)}, u32[]{:S(2)}, u32[]{:S(2)}) %all-to-all-start.1) | async-done | bytes 327712 | tf_op jit(solution)/shard_map/all_to_all | solution.py:751
  83.6 0.7 copy-done.10
  84.3 14.2 %shard_map.52 = (f32[4,16,128]{2,1,0:T(8,128)}, f32[4,48,128]{2,1,0:T(8,128)}, f32[4,48,128]{2,1,0:T(8,128)}, f32[18,56,128]{2,1,0:T(8,128)}, f32[24,56,128]{2,1...) custom-call(s32[2]{0:T(128)} %pad_add_fusion.pos, f32[32,128]{1,0:T(8,128)} %copy.25.owned, ...), custom_call_target="tpu_custom_call" | custom-call | flops 10000000 | bytes 8388608 | tf_op jit(solution)/shard_map/pallas_call | solution.py:347
  98.5 0.3 collective-permute-start.8
  98.8 1.8 %collective-permute-start.9 = (f32[4,48,128]{2,1,0:T(8,128)}, f32[4,48,128]{2,1,0:T(8,128)S(1)}, u32[]{:S(2)}, u32[]{:S(2)}) collective-permute-start(f32[4,48,128]{2,1,0:T(8,128)} %get-tuple-element.32), channel_id=1, source_target_pairs={{0,240},{16,32},{32,16},{48,64},{64,48},{80,96},{96,80},{112,128},... | collective-permute-start | bytes 294920 | tf_op jit(solution)/shard_map/ppermute | solution.py:779
  100.6 2.8 %collective-permute-done.8.by_x.refs_4_ = f32[4,48,128]{2,1,0:T(8,128)S(1)} collective-permute-done((f32[4,48,128]{2,1,0:T(8,128)}, f32[4,48,128]{2,1,0:T(8,128)S(1)}, u32[]{:S(2)}, u32[]{:S(2)}) %collective-permute-start.8) | collective-permute-done | bytes 98336 | tf_op jit(solution)/shard_map/ppermute | solution.py:778
  103.4 3.6 %collective-permute-done.9.by_x2.refs_5_ = f32[4,48,128]{2,1,0:T(8,128)S(1)} collective-permute-done((f32[4,48,128]{2,1,0:T(8,128)}, f32[4,48,128]{2,1,0:T(8,128)S(1)}, u32[]{:S(2)}, u32[]{:S(2)}) %collective-permute-start.9) | collective-permute-done | bytes 98336 | tf_op jit(solution)/shard_map/ppermute | solution.py:779
  107.0 0.8 pad_maximum_fusion.11
  107.8 0.1 collective-permute-start.11
  107.9 0.9 collective-permute-start.10
  108.8 2.6 %collective-permute-done.11.by_y2 = f32[12,8,128]{2,1,0:T(8,128)S(1)} collective-permute-done((f32[12,8,128]{2,1,0:T(8,128)S(1)}, f32[12,8,128]{2,1,0:T(8,128)S(1)}, u32[]{:S(2)}, u32[]{:S(2)}) %collective-permute-start.11) | collective-permute-done | bytes 49184 | tf_op jit(solution)/shard_map/ppermute | solution.py:741
  111.4 0.6 copy-done.19
  112.0 2.9 %shard_map.53 = (f32[12,32,128]{2,1,0:T(8,128)}, f32[12,32,128]{2,1,0:T(8,128)}, f32[16,1,8,128]{3,2,1,0:T(8,128)}) custom-call(s32[2]{0:T(128)} %pad_add_fusion.pos, f32[4,16,128]{2,1,0:T(8,128)} %get-tuple-element.30.mid, f32[4,48,128]{2,1,0:T(8,128)} %copy-done.13, f32[4,48,128]{2,1,0:T(8,128)} %copy-done.14, f32[12,8,128]{2,1,0:T(8,128)} %copy-done.20, ...), custom_call_target="tpu_custom_call" | custom-call | flops 10000000 | bytes 8388608 | tf_op jit(solution)/shard_map/pallas_call | solution.py:347
  114.9 3.5 %all-to-all-start.2 = ((f32[16,1,8,128]{3,2,1,0:T(8,128)}), f32[16,1,8,128]{3,2,1,0:T(8,128)S(1)}, u32[]{:S(2)}, u32[]{:S(2)}) async-start(f32[16,1,8,128]{3,2,1,0:T(8,128)} %get-tuple-element.34), calls=%async_computation.2 | async-start | bytes 131072 | tf_op jit(solution)/shard_map/all_to_all | solution.py:751
  118.5 6.4 %all-to-all-done.2.mid = f32[16,1,8,128]{3,2,1,0:T(8,128)S(1)} async-done(((f32[16,1,8,128]{3,2,1,0:T(8,128)}), f32[16,1,8,128]{3,2,1,0:T(8,128)S(1)}, u32[]{:S(2)}, u32[]{:S(2)}) %all-to-all-start.2) | async-done | bytes 65568 | tf_op jit(solution)/shard_map/all_to_all | solution.py:751
  124.9 1.3 collective-permute-start.13
  126.2 1.9 %collective-permute-start.12 = (f32[40,8,128]{2,1,0:T(8,128)S(1)}, f32[40,8,128]{2,1,0:T(8,128)S(1)}, u32[]{:S(2)}, u32[]{:S(2)}) collective-permute-start(f32[40,8,128]{2,1,0:T(8,128)S(1)} %get-tuple-element.51), channel_id=1, source_target_pairs={{0,1},{1,0},{2,3},{3,2},{4,5},{5,4},{6,7},{7,6},{8,9},{9,8},{10,11... | collective-permute-start | bytes 491528 | tf_op jit(solution)/shard_map/ppermute | solution.py:740
  128.1 1.7 %collective-permute-done.13.by_y2.refs_7_ = f32[40,8,128]{2,1,0:T(8,128)S(1)} collective-permute-done((f32[40,8,128]{2,1,0:T(8,128)S(1)}, f32[40,8,128]{2,1,0:T(8,128)S(1)}, u32[]{:S(2)}, u32[]{:S(2)}) %collective-permute-start.13) | collective-permute-done | bytes 163872 | tf_op jit(solution)/shard_map/ppermute | solution.py:741
  129.8 1.8 %shard_map.54 = (f32[3,5,24,128]{3,2,1,0:T(8,128)S(1)}, f32[16,2,8,128]{3,2,1,0:T(8,128)S(1)}) custom-call(s32[2]{0:T(128)S(1)} %copy-done.7, f32[16,1,8,128]{3,2,1,0:T(8,128)S(1)} %all-to-all-done.2.mid, f32[40,8,128]{2,1,0:T(8,128)S(1)} %collective-permute-done.12.by_y.refs_6_, f32[40,8,128]{2,1,0:T(8,128)S(1)} %collective-permute-done.13.by_y2.refs_7_, ...), custom_call_target="tpu_custom_call" | custom-call | flops 10000000 | bytes 8388608 | tf_op jit(solution)/shard_map/pallas_call | solution.py:347
  131.6 16.5 %all_to_all.20.three = f32[16,2,8,128]{3,2,1,0:T(8,128)} all-to-all(f32[16,2,8,128]{3,2,1,0:T(8,128)S(1)} %get-tuple-element.37), channel_id=1, replica_groups=mesh['gx'=16,'gy'=16] {'gy'}, dimensions={0} | all-to-all | bytes 262144 | tf_op jit(solution)/shard_map/all_to_all | solution.py:751
  148.1 10.5 %shard_map.55 = (f32[16,32,128]{2,1,0:T(8,128)}, f32[16,32,128]{2,1,0:T(8,128)}) custom-call(s32[2]{0:T(128)} %pad_add_fusion.pos, f32[32,128]{1,0:T(8,128)} %copy.25.owned, f32[16,2,8,128]{3,2,1,0:T(8,128)} %all_to_all.20.three, f32[4,64,128]{2,1,0:T(8,128)} %get-tuple-element.38.k3, f32[3,5,24,128]{3,2,1,0:T(8,128)} %copy-done.5, ...), custom_call_target="tpu_custom_call" | custom-call | flops 10000000 | bytes 8388608 | tf_op jit(solution)/shard_map/pallas_call | solution.py:347
  (63 shorter events, 0.5 us)
Async XLA Ops:
  0.6 15.0 %copy-start.9 = (f32[16,32,128]{2,1,0:T(8,128)S(1)}, f32[16,32,128]{2,1,0:T(8,128)}, u32[]{:S(2)}) copy-start(f32[16,32,128]{2,1,0:T(8,128)} %refs_12_.1) | copy-start | bytes 786436
  0.7 15.0 %copy-start.11 = (f32[16,32,128]{2,1,0:T(8,128)S(1)}, f32[16,32,128]{2,1,0:T(8,128)}, u32[]{:S(2)}) copy-start(f32[16,32,128]{2,1,0:T(8,128)} %param.4) | copy-start | bytes 786436
  2.1 8.4 %collective-permute-start = (f32[2,10,32,128]{3,2,1,0:T(8,128)S(1)}, f32[2,10,32,128]{3,2,1,0:T(8,128)S(1)}, u32[]{:S(2)}, u32[]{:S(2)}) collective-permute-start(f32[2,10,32,128]{3,2,1,0:T(8,128)S(1)} %get-tuple-element.48), channel_id=1, source_target_pairs={{0,16},{16,0},{32,48},{48,32},{64,80},{80,64},{96,112},{112,96},{1... | collective-permute-start | bytes 983048 | tf_op jit(solution)/shard_map/ppermute | solution.py:740
  4.3 11.3 %collective-permute-start.1 = (f32[2,10,32,128]{3,2,1,0:T(8,128)S(1)}, f32[2,10,32,128]{3,2,1,0:T(8,128)S(1)}, u32[]{:S(2)}, u32[]{:S(2)}) collective-permute-start(f32[2,10,32,128]{3,2,1,0:T(8,128)S(1)} %get-tuple-element.49), channel_id=1, source_target_pairs={{0,240},{16,32},{32,16},{48,64},{64,48},{80,96},{96,80},{112,128},... | collective-permute-start | bytes 983048 | tf_op jit(solution)/shard_map/ppermute | solution.py:741
  15.8 1.0 copy-start.8
  16.9 4.5 %collective-permute-start.2 = (f32[720,128]{1,0:T(8,128)S(1)}, f32[720,128]{1,0:T(8,128)S(1)}, u32[]{:S(2)}, u32[]{:S(2)}) collective-permute-start(f32[720,128]{1,0:T(8,128)S(1)} %select_n.130), channel_id=1, source_target_pairs={{0,1},{1,0},{2,3},{3,2},{4,5},{5,4},{6,7},{7,6},{8,9},{9,8},{10,11... | collective-permute-start | bytes 1105928 | tf_op jit(solution)/shard_map/ppermute | solution.py:740
  19.1 7.2 %collective-permute-start.3 = (f32[720,128]{1,0:T(8,128)S(1)}, f32[720,128]{1,0:T(8,128)S(1)}, u32[]{:S(2)}, u32[]{:S(2)}) collective-permute-start(f32[720,128]{1,0:T(8,128)S(1)} %select_n.132), channel_id=1, source_target_pairs={{0,15},{1,2},{2,1},{3,4},{4,3},{5,6},{6,5},{7,8},{8,7},{9,10},{10,... | collective-permute-start | bytes 1105928 | tf_op jit(solution)/shard_map/ppermute | solution.py:741
  21.4 5.0 %copy-start.17 = (f32[720,128]{1,0:T(8,128)}, f32[720,128]{1,0:T(8,128)S(1)}, u32[]{:S(2)}) copy-start(f32[720,128]{1,0:T(8,128)S(1)} %collective-permute-done.2.by_y) | copy-start | bytes 1105924
  26.4 0.7 copy-start.18
  34.1 7.7 %collective-permute-start.5 = (f32[3,4,16,128]{3,2,1,0:T(8,128)}, f32[3,4,16,128]{3,2,1,0:T(8,128)S(1)}, u32[]{:S(2)}, u32[]{:S(2)}) collective-permute-start(f32[3,4,16,128]{3,2,1,0:T(8,128)} %get-tuple-element.24.refs_1_), channel_id=1, source_target_pairs={{0,240},{16,32},{32,16},{48,64},{64,48},{80,96},{96,80},{112,128},... | collective-permute-start | bytes 294920 | tf_op jit(solution)/shard_map/ppermute | solution.py:741
  38.3 3.7 %collective-permute-start.4 = (f32[3,4,16,128]{3,2,1,0:T(8,128)}, f32[3,4,16,128]{3,2,1,0:T(8,128)S(1)}, u32[]{:S(2)}, u32[]{:S(2)}) collective-permute-start(f32[3,4,16,128]{3,2,1,0:T(8,128)} %get-tuple-element.24.refs_1_), channel_id=1, source_target_pairs={{0,16},{16,0},{32,48},{48,32},{64,80},{80,64},{96,112},{112,96},{1... | collective-permute-start | bytes 294920 | tf_op jit(solution)/shard_map/ppermute | solution.py:740
  38.3 10.2 %all-to-all-start = ((f32[16,2,8,128]{3,2,1,0:T(8,128)}), f32[16,2,8,128]{3,2,1,0:T(8,128)S(1)}, u32[]{:S(2)}, u32[]{:S(2)}) async-start(f32[16,2,8,128]{3,2,1,0:T(8,128)} %get-tuple-element.23), calls=%async_computation | async-start | bytes 262144 | tf_op jit(solution)/shard_map/all_to_all | solution.py:751
  41.8 6.7 %copy-start.15 = (f32[3,4,16,128]{3,2,1,0:T(8,128)}, f32[3,4,16,128]{3,2,1,0:T(8,128)S(1)}, u32[]{:S(2)}) copy-start(f32[3,4,16,128]{3,2,1,0:T(8,128)S(1)} %collective-permute-done.5.refs_3_) | copy-start | bytes 294916
  42.0 6.6 %copy-start.16 = (f32[3,4,16,128]{3,2,1,0:T(8,128)}, f32[3,4,16,128]{3,2,1,0:T(8,128)S(1)}, u32[]{:S(2)}) copy-start(f32[3,4,16,128]{3,2,1,0:T(8,128)S(1)} %collective-permute-done.4.refs_2_) | copy-start | bytes 294916
  42.0 15.5 %copy-start.6 = (s32[2]{0:T(128)S(1)}, s32[2]{0:T(128)}, u32[]{:S(2)}) copy-start(s32[2]{0:T(128)} %pad_add_fusion.pos) | copy-start | bytes 28
  48.5 22.0 %copy-start.21 = (s32[16,16]{1,0:T(8,128)S(1)}, s32[16,16]{1,0:T(8,128)}, u32[]{:S(2)}) copy-start(s32[16,16]{1,0:T(8,128)} %param.5) | copy-start | bytes 3076
  48.5 7.7 %collective-permute-start.7 = (f32[68,8,128]{2,1,0:T(8,128)S(1)}, f32[68,8,128]{2,1,0:T(8,128)S(1)}, u32[]{:S(2)}, u32[]{:S(2)}) collective-permute-start(f32[68,8,128]{2,1,0:T(8,128)S(1)} %get-tuple-element.52), channel_id=1, source_target_pairs={{0,15},{1,2},{2,1},{3,4},{4,3},{5,6},{6,5},{7,8},{8,7},{9,10},{10,... | collective-permute-start | bytes 835592 | tf_op jit(solution)/shard_map/ppermute | solution.py:741
  51.8 5.7 %collective-permute-start.6 = (f32[68,8,128]{2,1,0:T(8,128)S(1)}, f32[68,8,128]{2,1,0:T(8,128)S(1)}, u32[]{:S(2)}, u32[]{:S(2)}) collective-permute-start(f32[68,8,128]{2,1,0:T(8,128)S(1)} %get-tuple-element.53), channel_id=1, source_target_pairs={{0,1},{1,0},{2,3},{3,2},{4,5},{5,4},{6,7},{7,6},{8,9},{9,8},{10,11... | collective-permute-start | bytes 835592 | tf_op jit(solution)/shard_map/ppermute | solution.py:740
  56.3 27.3 %copy-start = (f32[68,8,128]{2,1,0:T(8,128)}, f32[68,8,128]{2,1,0:T(8,128)S(1)}, u32[]{:S(2)}) copy-start(f32[68,8,128]{2,1,0:T(8,128)S(1)} %collective-permute-done.7.by_y2.refs_5_) | copy-start | bytes 835588
  57.5 26.1 %copy-start.1 = (f32[68,8,128]{2,1,0:T(8,128)}, f32[68,8,128]{2,1,0:T(8,128)S(1)}, u32[]{:S(2)}) copy-start(f32[68,8,128]{2,1,0:T(8,128)S(1)} %collective-permute-done.6.by_y.refs_4_) | copy-start | bytes 835588
  60.2 0.7 copy-start.4
  60.8 22.7 %all-to-all-start.1 = ((f32[16,5,8,128]{3,2,1,0:T(8,128)}), f32[16,5,8,128]{3,2,1,0:T(8,128)S(1)}, u32[]{:S(2)}, u32[]{:S(2)}) async-start(f32[16,5,8,128]{3,2,1,0:T(8,128)} %get-tuple-element.25), calls=%async_computation.1 | async-start | bytes 655360 | tf_op jit(solution)/shard_map/all_to_all | solution.py:751
  83.6 0.7 copy-start.10
  98.5 26.4 %copy-start.12 = (f32[16,32,128]{2,1,0:T(8,128)S(1)}, f32[16,32,128]{2,1,0:T(8,128)}, u32[]{:S(2)}) copy-start(f32[16,32,128]{2,1,0:T(8,128)} %get-tuple-element.35.refs_8_) | copy-start | bytes 786436
  98.5 4.9 %collective-permute-start.8 = (f32[4,48,128]{2,1,0:T(8,128)}, f32[4,48,128]{2,1,0:T(8,128)S(1)}, u32[]{:S(2)}, u32[]{:S(2)}) collective-permute-start(f32[4,48,128]{2,1,0:T(8,128)} %get-tuple-element.31), channel_id=1, source_target_pairs={{0,16},{16,0},{32,48},{48,32},{64,80},{80,64},{96,112},{112,96},{1... | collective-permute-start | bytes 294920 | tf_op jit(solution)/shard_map/ppermute | solution.py:778
  98.8 8.2 %collective-permute-start.9 = (f32[4,48,128]{2,1,0:T(8,128)}, f32[4,48,128]{2,1,0:T(8,128)S(1)}, u32[]{:S(2)}, u32[]{:S(2)}) collective-permute-start(f32[4,48,128]{2,1,0:T(8,128)} %get-tuple-element.32), channel_id=1, source_target_pairs={{0,240},{16,32},{32,16},{48,64},{64,48},{80,96},{96,80},{112,128},... | collective-permute-start | bytes 294920 | tf_op jit(solution)/shard_map/ppermute | solution.py:779
  103.4 8.0 %copy-start.13 = (f32[4,48,128]{2,1,0:T(8,128)}, f32[4,48,128]{2,1,0:T(8,128)S(1)}, u32[]{:S(2)}) copy-start(f32[4,48,128]{2,1,0:T(8,128)S(1)} %collective-permute-done.8.by_x.refs_4_) | copy-start | bytes 294916
  106.9 4.5 %copy-start.14 = (f32[4,48,128]{2,1,0:T(8,128)}, f32[4,48,128]{2,1,0:T(8,128)S(1)}, u32[]{:S(2)}) copy-start(f32[4,48,128]{2,1,0:T(8,128)S(1)} %collective-permute-done.9.by_x2.refs_5_) | copy-start | bytes 294916
  107.0 22.8 %copy-start.7 = (s32[2]{0:T(128)S(1)}, s32[2]{0:T(128)}, u32[]{:S(2)}) copy-start(s32[2]{0:T(128)} %pad_add_fusion.pos) | copy-start | bytes 28
  107.8 3.6 %collective-permute-start.11 = (f32[12,8,128]{2,1,0:T(8,128)S(1)}, f32[12,8,128]{2,1,0:T(8,128)S(1)}, u32[]{:S(2)}, u32[]{:S(2)}) collective-permute-start(f32[12,8,128]{2,1,0:T(8,128)S(1)} %get-tuple-element.60), channel_id=1, source_target_pairs={{0,15},{1,2},{2,1},{3,4},{4,3},{5,6},{6,5},{7,8},{8,7},{9,10},{10,... | collective-permute-start | bytes 147464 | tf_op jit(solution)/shard_map/ppermute | solution.py:741
  107.9 3.5 %collective-permute-start.10 = (f32[12,8,128]{2,1,0:T(8,128)S(1)}, f32[12,8,128]{2,1,0:T(8,128)S(1)}, u32[]{:S(2)}, u32[]{:S(2)}) collective-permute-start(f32[12,8,128]{2,1,0:T(8,128)S(1)} %get-tuple-element.61), channel_id=1, source_target_pairs={{0,1},{1,0},{2,3},{3,2},{4,5},{5,4},{6,7},{7,6},{8,9},{9,8},{10,11... | collective-permute-start | bytes 147464 | tf_op jit(solution)/shard_map/ppermute | solution.py:740
  111.4 0.6 copy-start.19
  111.4 0.6 copy-start.20
  114.9 10.0 %all-to-all-start.2 = ((f32[16,1,8,128]{3,2,1,0:T(8,128)}), f32[16,1,8,128]{3,2,1,0:T(8,128)S(1)}, u32[]{:S(2)}, u32[]{:S(2)}) async-start(f32[16,1,8,128]{3,2,1,0:T(8,128)} %get-tuple-element.34), calls=%async_computation.2 | async-start | bytes 131072 | tf_op jit(solution)/shard_map/all_to_all | solution.py:751
  124.9 4.8 %collective-permute-start.13 = (f32[40,8,128]{2,1,0:T(8,128)S(1)}, f32[40,8,128]{2,1,0:T(8,128)S(1)}, u32[]{:S(2)}, u32[]{:S(2)}) collective-permute-start(f32[40,8,128]{2,1,0:T(8,128)S(1)} %get-tuple-element.50), channel_id=1, source_target_pairs={{0,15},{1,2},{2,1},{3,4},{4,3},{5,6},{6,5},{7,8},{8,7},{9,10},{10,... | collective-permute-start | bytes 491528 | tf_op jit(solution)/shard_map/ppermute | solution.py:741
  126.2 3.5 %collective-permute-start.12 = (f32[40,8,128]{2,1,0:T(8,128)S(1)}, f32[40,8,128]{2,1,0:T(8,128)S(1)}, u32[]{:S(2)}, u32[]{:S(2)}) collective-permute-start(f32[40,8,128]{2,1,0:T(8,128)S(1)} %get-tuple-element.51), channel_id=1, source_target_pairs={{0,1},{1,0},{2,3},{3,2},{4,5},{5,4},{6,7},{7,6},{8,9},{9,8},{10,11... | collective-permute-start | bytes 491528 | tf_op jit(solution)/shard_map/ppermute | solution.py:740
  129.8 18.4 %copy-start.2 = (f32[40,8,128]{2,1,0:T(8,128)}, f32[40,8,128]{2,1,0:T(8,128)S(1)}, u32[]{:S(2)}) copy-start(f32[40,8,128]{2,1,0:T(8,128)S(1)} %collective-permute-done.13.by_y2.refs_7_) | copy-start | bytes 491524
  129.8 18.4 %copy-start.3 = (f32[40,8,128]{2,1,0:T(8,128)}, f32[40,8,128]{2,1,0:T(8,128)S(1)}, u32[]{:S(2)}) copy-start(f32[40,8,128]{2,1,0:T(8,128)S(1)} %collective-permute-done.12.by_y.refs_6_) | copy-start | bytes 491524
  131.6 16.5 %copy-start.5 = (f32[3,5,24,128]{3,2,1,0:T(8,128)}, f32[3,5,24,128]{3,2,1,0:T(8,128)S(1)}, u32[]{:S(2)}) copy-start(f32[3,5,24,128]{3,2,1,0:T(8,128)S(1)} %get-tuple-element.39.refs_0_) | copy-start | bytes 552964
